TPU v7x, 32 devices: a whole 2x2x4 slice. The times are simulated.
32 devices in a mesh: group: 4 (over x, core), dev: 8 (over z, y).
Axes of the slice: x: 2, y: 2, z: 4, core: 2. Of those that a mesh axis runs over, the one named last changes fastest.
Arguments:
- queries: bfloat16 [256, 32, 128], P(('group', 'dev')), may hold values from -0.5390625 to 0.5390625
- passages: bfloat16 [512, 256, 128], P(('group', 'dev')), may hold values from -6 to 6
- candidates: int32 [256, 16], P(('group', 'dev')), may hold values from 0 to 511, as said below
- location: int32 [512], replicated, may hold values from 0 to 511, as said below
Outputs:
- loss: float32 [256], P(('group', 'dev'))
- query_grad: float32 [256, 32, 128], P(('group', 'dev'))
Inputs may be any that keep to these rules, and one draw needn't show every extreme that they name: `candidates`: for each device holding queries and each device holding passage rows (rows of passages split evenly over group+dev in order), at most 12 of the sending device's pairs (query, listed document) have their document's row on that device. In every draw one device receives exactly 12 such pairs from every device. `location`: A permutation of the documents.
All inputs are finite; a program needn't handle non-finite values.
Results may differ from a plain program's by a relative error of at most 0.011.
Values may be sent and summed in bfloat16 or wider, within the bound.
No kernel may reach another device: no remote copies, remote signals or barrier semaphores. Data moves between devices by JAX's collectives and lax.ppermute only.
A program may use at most 64 MiB of HBM per device.

v0:
```python
import jax
import jax.numpy as jnp
from jax import lax
from jax.sharding import PartitionSpec as P

SOFTNESS = 0.02
EPSILON = 1e-06


def normalize(values):
    floats = values.astype(jnp.float32)
    scale = lax.rsqrt(jnp.sum(floats * floats, axis=-1, keepdims=True) + EPSILON)
    return (floats * scale, scale)


def local(queries, passages, candidates, location):
    group_count = lax.axis_size("group")
    dev_count = lax.axis_size("dev")
    device_total = group_count * dev_count
    query_count, query_len, feat_width = queries.shape
    pass_count = passages.shape[0]
    list_len = candidates.shape[1]
    pair_count = query_count * list_len
    slot_cap = max(2, (3 * pair_count + device_total - 1) // device_total)
    slot_total = device_total * slot_cap
    query_unit, query_scale = normalize(queries)
    query_send = query_unit.astype(jnp.bfloat16)
    passage_unit = normalize(passages)[0].astype(jnp.bfloat16)
    rows = jnp.take(location, candidates.reshape(-1), axis=0)
    target = rows // pass_count
    local_row = rows % pass_count
    same_target = target[:, None] == target[None, :]
    positions = jnp.arange(pair_count, dtype=jnp.int32)
    earlier = positions[None, :] < positions[:, None]
    before = jnp.sum(same_target & earlier, axis=1)
    slot_index = target * slot_cap + before
    query_owner = positions // list_len
    outgoing = jnp.zeros((slot_total, query_len, feat_width), jnp.bfloat16)
    outgoing = outgoing.at[slot_index].set(query_send[query_owner])
    labels = (
        jnp.zeros((slot_total,), jnp.bfloat16).at[slot_index].set(local_row.astype(jnp.bfloat16))
    )
    outgoing = outgoing.reshape(group_count, dev_count, slot_cap, query_len, feat_width)
    labels = labels.reshape(group_count, dev_count, slot_cap)
    mid_queries, mid_labels = (
        lax.all_to_all(outgoing, "dev", split_axis=1, concat_axis=1, tiled=True),
        lax.all_to_all(labels, "dev", split_axis=1, concat_axis=1, tiled=True),
    )
    arrived, tags = (
        lax.all_to_all(mid_queries, "group", split_axis=0, concat_axis=0, tiled=True),
        lax.all_to_all(mid_labels, "group", split_axis=0, concat_axis=0, tiled=True),
    )
    block_rows = dev_count * slot_cap
    arrived = arrived.reshape(group_count, block_rows, query_len, feat_width)
    tags = tags.reshape(group_count, block_rows).astype(jnp.int32)

    def score_block(inputs):
        query_block, tag_block = inputs
        passage_block = jnp.take(passage_unit, tag_block, axis=0)
        logits = (
            jnp.einsum(
                "bqe,bpe->bqp", query_block, passage_block, preferred_element_type=jnp.float32
            )
            / SOFTNESS
        )
        exp_terms = jnp.exp(logits)
        token_mass = jnp.sum(exp_terms, axis=-1, keepdims=True)
        pair_score = jnp.sum(SOFTNESS * jnp.log(token_mass[..., 0]), axis=-1)
        attention = (exp_terms / token_mass).astype(jnp.bfloat16)
        pulled = jnp.einsum(
            "bqp,bpe->bqe", attention, passage_block, preferred_element_type=jnp.float32
        )
        return (pulled.astype(jnp.bfloat16), pair_score)

    pulled, scores = lax.map(score_block, (arrived, tags))
    pulled = pulled.reshape(group_count, dev_count, slot_cap, query_len, feat_width)
    scores = scores.reshape(group_count, dev_count, slot_cap)
    mid_pulled = lax.all_to_all(pulled, "dev", split_axis=1, concat_axis=1, tiled=True)
    pulled_back = lax.all_to_all(mid_pulled, "group", split_axis=0, concat_axis=0, tiled=True)
    mid_scores = lax.all_to_all(scores, "dev", split_axis=1, concat_axis=1, tiled=True)
    scores_back = lax.all_to_all(mid_scores, "group", split_axis=0, concat_axis=0, tiled=True)
    pulled_flat = pulled_back.reshape(slot_total, query_len, feat_width)
    scores_flat = scores_back.reshape(slot_total)
    pair_pulled = jnp.take(pulled_flat, slot_index, axis=0).reshape(
        query_count, list_len, query_len, feat_width
    )
    pair_score = jnp.take(scores_flat, slot_index, axis=0).reshape(query_count, list_len)
    exp_scores = jnp.exp(pair_score)
    total = jnp.sum(exp_scores, axis=-1, keepdims=True)
    loss = jnp.log(total[:, 0]) - pair_score[:, 0]
    first = (jnp.arange(list_len) == 0).astype(jnp.float32)
    coeff = exp_scores / total - first[None, :]
    unit_grad = jnp.einsum("bk,bkqe->bqe", coeff, pair_pulled.astype(jnp.float32))
    along = jnp.sum(query_unit * unit_grad, axis=-1, keepdims=True)
    query_grad = (unit_grad - query_unit * along) * query_scale
    return (loss, query_grad)


def solution(mesh):
    placed = (
        P(("group", "dev"), None, None),
        P(("group", "dev"), None, None),
        P(("group", "dev"), None),
        P(),
    )
    return jax.shard_map(
        local,
        mesh=mesh,
        in_specs=placed,
        out_specs=(P(("group", "dev")), P(("group", "dev"), None, None)),
        check_vma=False,
    )
```

profile of v0, /device:TPU:0, one launch (start us, length us, event | category | flops | bytes accessed | tf_op | source)
XLA Modules:
  0.0 347.9 jit_solution(1722824978734313704)
XLA Ops:
  0.6 0.8 reshape.314
  1.4 0.8 reshape.315
  2.2 1.3 gather_fusion.1
  3.5 0.2 convert_reduce_fusion
  3.7 1.3 scatter_custom_fusion.1
  5.1 0.1 reshape.318
  5.2 0.6 copy.24
  5.8 7.3 %all-to-all-start.2 = ((bf16[4,8,12]{2,0,1:T(4,128)(2,1)}), bf16[4,8,12]{2,0,1:T(4,128)(2,1)S(1)}, u32[]{:S(2)}, u32[]{:S(2)}) async-start(bf16[4,8,12]{2,0,1:T(4,128)(2,1)} %copy.24), calls=%async_computation.2 | async-start | bytes 16384 | tf_op jit(solution)/shard_map/all_to_all | solution.py:47
  13.1 0.9 fusion.27
  14.1 0.9 fusion.24
  15.0 1.7 gather_fusion.2
  16.7 0.4 broadcast_in_dim.73
  17.1 9.7 %scatter_fusion = bf16[384,32,128]{2,1,0:T(8,128)(2,1)S(1)} fusion(bf16[384,32,128]{2,1,0:T(8,128)(2,1)S(1)} %broadcast_in_dim.73, s32[128]{0:T(128)S(1)} %fusion.36, bf16[128,32,128]{2,1,0:T(8,128)(2,1)} %gather_fusion.2), kind=kCustom, calls=%fused_computation.5 | custom fusion | bytes 3146240 | tf_op jit(solution)/shard_map/scatter | solution.py:39
  26.8 2.2 copy.22
  29.0 6.0 %all-to-all-start = ((bf16[4,8,12,32,128]{4,3,2,0,1:T(8,128)(2,1)}), bf16[4,8,12,32,128]{4,3,2,0,1:T(8,128)(2,1)S(1)}, u32[]{:S(2)}, u32[]{:S(2)}) async-start(bf16[4,8,12,32,128]{4,3,2,0,1:T(8,128)(2,1)} %copy.22), calls=%async_computation | async-start | bytes 6291456 | tf_op jit(solution)/shard_map/all_to_all | solution.py:46
  35.0 0.6 copy.25
  35.6 69.5 %all-to-all-done = bf16[4,8,12,32,128]{4,3,2,0,1:T(8,128)(2,1)S(1)} async-done(((bf16[4,8,12,32,128]{4,3,2,0,1:T(8,128)(2,1)}), bf16[4,8,12,32,128]{4,3,2,0,1:T(8,128)(2,1)S(1)}, u32[]{:S(2)}, u32[]{:S(2)}) %all-to-all-start) | async-done | bytes 3145760 | tf_op jit(solution)/shard_map/all_to_all | solution.py:46
  105.2 3.2 all-to-all-start.3
  108.5 2.2 copy.23
  110.7 1.6 all-to-all-done.3
  112.2 4.6 %all-to-all-start.1 = ((bf16[4,8,12,32,128]{4,3,2,1,0:T(8,128)(2,1)}), bf16[4,8,12,32,128]{4,3,2,1,0:T(8,128)(2,1)}, u32[]{:S(2)}, u32[]{:S(2)}) async-start(bf16[4,8,12,32,128]{4,3,2,1,0:T(8,128)(2,1)} %copy.23), calls=%async_computation.1 | async-start | bytes 6291456 | tf_op jit(solution)/shard_map/all_to_all | solution.py:50
  116.9 0.6 fusion.16
  117.6 0.7 fusion.17
  118.3 0.1 reshape.323
  118.4 35.5 %all-to-all-done.1 = bf16[4,8,12,32,128]{4,3,2,1,0:T(8,128)(2,1)} async-done(((bf16[4,8,12,32,128]{4,3,2,1,0:T(8,128)(2,1)}), bf16[4,8,12,32,128]{4,3,2,1,0:T(8,128)(2,1)}, u32[]{:S(2)}, u32[]{:S(2)}) %all-to-all-start.1) | async-done | bytes 3145760 | tf_op jit(solution)/shard_map/all_to_all | solution.py:50
  153.9 56.2 %while.12 = (s32[]{:T(128)}, bf16[4,96,32,128]{3,2,1,0:T(8,128)(2,1)}, f32[4,96]{1,0:T(4,128)S(1)}, bf16[4,96,32,128]{3,2,1,0:T(8,128)(2,1)}, s32[4,96]{1,0:T(4,...) while((s32[]{:T(128)}, bf16[4,96,32,128]{3,2,1,0:T(8,128)(2,1)}, ...), condition=%wide.region_8.9_spmd, body=%wide.region_5.8_spmd.sunk | while | flops 413274880 | bytes 58241436 | solution.py:75
  153.9 5.9 %gather_fusion = bf16[96,256,128]{2,1,0:T(8,128)(2,1)} fusion(bf16[16,256,128]{2,1,0:T(8,128)(2,1)S(1)} %get-tuple-element.118, s32[1024]{0:T(1024)S(1)} %pad_clamp_fusion.5), kind=kCustom, calls=%fused_computation.clone.1 | custom fusion | bytes 12583296 | tf_op jit(solution)/shard_map/while/body/eval_jaxpr/jit(_take)/gather | solution.py:59
  159.8 5.5 %fusion.45 = (f32[96,32]{1,0:T(8,128)S(1)}, f32[96,32,256]{2,1,0:T(8,128)S(1)}) fusion(bf16[96,256,128]{2,1,0:T(8,128)(2,1)} %gather_fusion, pred[96]{0:T(512)(128)(4,1)S(1)} %compare_and_fusion.4, bf16[4,96,32,128]{3,2,1,0:T(8,128)(2,1)} %get-tuple-element.116, s32[]{:T(128)} %get-tuple-element.105), kind=kOutput, calls=%fused_computation.10.clone.1 | convolution fusion | flops 206042112 | bytes 10236512 | tf_op jit(solution)/shard_map/while/body/eval_jaxpr/bqe,bpe->bqp/dot_general | solution.py:61
  165.4 2.4 fusion.46
  167.8 0.1 multiply_reduce_fusion.2
  167.9 5.9 %gather_fusion = bf16[96,256,128]{2,1,0:T(8,128)(2,1)} fusion(bf16[16,256,128]{2,1,0:T(8,128)(2,1)S(1)} %get-tuple-element.118, s32[1024]{0:T(1024)S(1)} %pad_clamp_fusion.5), kind=kCustom, calls=%fused_computation.clone.1 | custom fusion | bytes 12583296 | tf_op jit(solution)/shard_map/while/body/eval_jaxpr/jit(_take)/gather | solution.py:59
  173.9 5.5 %fusion.45 = (f32[96,32]{1,0:T(8,128)S(1)}, f32[96,32,256]{2,1,0:T(8,128)S(1)}) fusion(bf16[96,256,128]{2,1,0:T(8,128)(2,1)} %gather_fusion, pred[96]{0:T(512)(128)(4,1)S(1)} %compare_and_fusion.4, bf16[4,96,32,128]{3,2,1,0:T(8,128)(2,1)} %get-tuple-element.116, s32[]{:T(128)} %get-tuple-element.105), kind=kOutput, calls=%fused_computation.10.clone.1 | convolution fusion | flops 206042112 | bytes 10236512 | tf_op jit(solution)/shard_map/while/body/eval_jaxpr/bqe,bpe->bqp/dot_general | solution.py:61
  179.4 2.4 fusion.46
  181.8 0.1 multiply_reduce_fusion.2
  182.0 5.9 %gather_fusion = bf16[96,256,128]{2,1,0:T(8,128)(2,1)} fusion(bf16[16,256,128]{2,1,0:T(8,128)(2,1)S(1)} %get-tuple-element.118, s32[1024]{0:T(1024)S(1)} %pad_clamp_fusion.5), kind=kCustom, calls=%fused_computation.clone.1 | custom fusion | bytes 12583296 | tf_op jit(solution)/shard_map/while/body/eval_jaxpr/jit(_take)/gather | solution.py:59
  188.0 5.5 %fusion.45 = (f32[96,32]{1,0:T(8,128)S(1)}, f32[96,32,256]{2,1,0:T(8,128)S(1)}) fusion(bf16[96,256,128]{2,1,0:T(8,128)(2,1)} %gather_fusion, pred[96]{0:T(512)(128)(4,1)S(1)} %compare_and_fusion.4, bf16[4,96,32,128]{3,2,1,0:T(8,128)(2,1)} %get-tuple-element.116, s32[]{:T(128)} %get-tuple-element.105), kind=kOutput, calls=%fused_computation.10.clone.1 | convolution fusion | flops 206042112 | bytes 10236512 | tf_op jit(solution)/shard_map/while/body/eval_jaxpr/bqe,bpe->bqp/dot_general | solution.py:61
  193.5 2.4 fusion.46
  195.9 0.1 multiply_reduce_fusion.2
  196.1 5.9 %gather_fusion = bf16[96,256,128]{2,1,0:T(8,128)(2,1)} fusion(bf16[16,256,128]{2,1,0:T(8,128)(2,1)S(1)} %get-tuple-element.118, s32[1024]{0:T(1024)S(1)} %pad_clamp_fusion.5), kind=kCustom, calls=%fused_computation.clone.1 | custom fusion | bytes 12583296 | tf_op jit(solution)/shard_map/while/body/eval_jaxpr/jit(_take)/gather | solution.py:59
  202.0 5.5 %fusion.45 = (f32[96,32]{1,0:T(8,128)S(1)}, f32[96,32,256]{2,1,0:T(8,128)S(1)}) fusion(bf16[96,256,128]{2,1,0:T(8,128)(2,1)} %gather_fusion, pred[96]{0:T(512)(128)(4,1)S(1)} %compare_and_fusion.4, bf16[4,96,32,128]{3,2,1,0:T(8,128)(2,1)} %get-tuple-element.116, s32[]{:T(128)} %get-tuple-element.105), kind=kOutput, calls=%fused_computation.10.clone.1 | convolution fusion | flops 206042112 | bytes 10236512 | tf_op jit(solution)/shard_map/while/body/eval_jaxpr/bqe,bpe->bqp/dot_general | solution.py:61
  207.6 2.4 fusion.46
  210.0 0.1 multiply_reduce_fusion.2
  210.1 0.1 reshape.319
  210.2 0.6 copy.26
  210.8 3.7 %all-to-all-start.4 = ((f32[4,8,12]{2,0,1:T(4,128)}), f32[4,8,12]{2,0,1:T(4,128)S(1)}, u32[]{:S(2)}, u32[]{:S(2)}) async-start(f32[4,8,12]{2,0,1:T(4,128)} %copy.26), calls=%async_computation.4 | async-start | bytes 32768 | tf_op jit(solution)/shard_map/all_to_all | solution.py:80
  214.5 4.4 %copy.28 = bf16[4,8,12,32,128]{4,3,2,0,1:T(8,128)(2,1)} copy(bf16[4,8,12,32,128]{4,3,2,1,0:T(8,128)(2,1)} %bitcast.56) | data formatting | bytes 6291456 | tf_op jit(solution)/shard_map/reshape | solution.py:76
  218.9 2.1 all-to-all-done.4
  221.1 3.9 %all-to-all-start.6 = ((bf16[4,8,12,32,128]{4,3,2,0,1:T(8,128)(2,1)}), bf16[4,8,12,32,128]{4,3,2,0,1:T(8,128)(2,1)S(1)}, u32[]{:S(2)}, u32[]{:S(2)}) async-start(bf16[4,8,12,32,128]{4,3,2,0,1:T(8,128)(2,1)} %copy.28), calls=%async_computation.6 | async-start | bytes 6291456 | tf_op jit(solution)/shard_map/all_to_all | solution.py:78
  224.9 0.6 copy.27
  225.5 69.3 %all-to-all-done.6 = bf16[4,8,12,32,128]{4,3,2,0,1:T(8,128)(2,1)S(1)} async-done(((bf16[4,8,12,32,128]{4,3,2,0,1:T(8,128)(2,1)}), bf16[4,8,12,32,128]{4,3,2,0,1:T(8,128)(2,1)S(1)}, u32[]{:S(2)}, u32[]{:S(2)}) %all-to-all-start.6) | async-done | bytes 3145760 | tf_op jit(solution)/shard_map/all_to_all | solution.py:78
  294.9 3.3 all-to-all-start.5
  298.1 2.2 copy.29
  300.3 1.6 all-to-all-done.5
  302.0 3.7 %all-to-all-start.7 = ((bf16[4,8,12,32,128]{4,3,2,1,0:T(8,128)(2,1)}), bf16[4,8,12,32,128]{4,3,2,1,0:T(8,128)(2,1)S(1)}, u32[]{:S(2)}, u32[]{:S(2)}) async-start(bf16[4,8,12,32,128]{4,3,2,1,0:T(8,128)(2,1)} %copy.29), calls=%async_computation.7 | async-start | bytes 6291456 | tf_op jit(solution)/shard_map/all_to_all | solution.py:79
  305.9 0.1 reshape.320
  306.0 1.3 gather_fusion.3
  307.3 0.1 exponential_reduce_fusion
  307.4 0.1 slice_reduce_fusion
  307.6 0.5 log_subtract_fusion
  308.2 34.4 %all-to-all-done.7 = bf16[4,8,12,32,128]{4,3,2,1,0:T(8,128)(2,1)S(1)} async-done(((bf16[4,8,12,32,128]{4,3,2,1,0:T(8,128)(2,1)}), bf16[4,8,12,32,128]{4,3,2,1,0:T(8,128)(2,1)S(1)}, u32[]{:S(2)}, u32[]{:S(2)}) %all-to-all-start.7) | async-done | bytes 3145760 | tf_op jit(solution)/shard_map/all_to_all | solution.py:79
  342.6 1.7 gather_fusion.4
  344.3 1.4 broadcast_select_fusion.9
  345.7 0.4 fusion.21
  346.1 1.8 fusion.20
  (51 shorter events, 0.7 us)
Async XLA Ops:
  0.6 1.6 copy-start
  5.8 23.2 %all-to-all-start.2 = ((bf16[4,8,12]{2,0,1:T(4,128)(2,1)}), bf16[4,8,12]{2,0,1:T(4,128)(2,1)S(1)}, u32[]{:S(2)}, u32[]{:S(2)}) async-start(bf16[4,8,12]{2,0,1:T(4,128)(2,1)} %copy.24), calls=%async_computation.2 | async-start | bytes 16384 | tf_op jit(solution)/shard_map/all_to_all | solution.py:47
  29.0 76.1 %all-to-all-start = ((bf16[4,8,12,32,128]{4,3,2,0,1:T(8,128)(2,1)}), bf16[4,8,12,32,128]{4,3,2,0,1:T(8,128)(2,1)S(1)}, u32[]{:S(2)}, u32[]{:S(2)}) async-start(bf16[4,8,12,32,128]{4,3,2,0,1:T(8,128)(2,1)} %copy.22), calls=%async_computation | async-start | bytes 6291456 | tf_op jit(solution)/shard_map/all_to_all | solution.py:46
  105.2 7.0 %all-to-all-start.3 = ((bf16[4,8,12]{2,1,0:T(8,128)(2,1)}), bf16[4,8,12]{2,1,0:T(8,128)(2,1)S(1)}, u32[]{:S(2)}, u32[]{:S(2)}) async-start(bf16[4,8,12]{2,1,0:T(8,128)(2,1)} %copy.25), calls=%async_computation.3 | async-start | bytes 16384 | tf_op jit(solution)/shard_map/all_to_all | solution.py:51
  110.7 6.2 %copy-start.2 = (bf16[16,256,128]{2,1,0:T(8,128)(2,1)S(1)}, bf16[16,256,128]{2,1,0:T(8,128)(2,1)}, u32[]{:S(2)}) copy-start(bf16[16,256,128]{2,1,0:T(8,128)(2,1)} %param.7) | copy-start | bytes 3145732
  112.2 41.7 %all-to-all-start.1 = ((bf16[4,8,12,32,128]{4,3,2,1,0:T(8,128)(2,1)}), bf16[4,8,12,32,128]{4,3,2,1,0:T(8,128)(2,1)}, u32[]{:S(2)}, u32[]{:S(2)}) async-start(bf16[4,8,12,32,128]{4,3,2,1,0:T(8,128)(2,1)} %copy.23), calls=%async_computation.1 | async-start | bytes 6291456 | tf_op jit(solution)/shard_map/all_to_all | solution.py:50
  159.8 5.5 %copy-start.1 = (bf16[96,256,128]{2,1,0:T(8,128)(2,1)S(1)}, bf16[96,256,128]{2,1,0:T(8,128)(2,1)}, u32[]{:S(2)}) copy-start(bf16[96,256,128]{2,1,0:T(8,128)(2,1)} %gather_fusion) | copy-start | bytes 18874372 | tf_op jit(solution)/shard_map/while
  173.9 5.5 %copy-start.1 = (bf16[96,256,128]{2,1,0:T(8,128)(2,1)S(1)}, bf16[96,256,128]{2,1,0:T(8,128)(2,1)}, u32[]{:S(2)}) copy-start(bf16[96,256,128]{2,1,0:T(8,128)(2,1)} %gather_fusion) | copy-start | bytes 18874372 | tf_op jit(solution)/shard_map/while
  188.0 5.5 %copy-start.1 = (bf16[96,256,128]{2,1,0:T(8,128)(2,1)S(1)}, bf16[96,256,128]{2,1,0:T(8,128)(2,1)}, u32[]{:S(2)}) copy-start(bf16[96,256,128]{2,1,0:T(8,128)(2,1)} %gather_fusion) | copy-start | bytes 18874372 | tf_op jit(solution)/shard_map/while
  202.0 5.5 %copy-start.1 = (bf16[96,256,128]{2,1,0:T(8,128)(2,1)S(1)}, bf16[96,256,128]{2,1,0:T(8,128)(2,1)}, u32[]{:S(2)}) copy-start(bf16[96,256,128]{2,1,0:T(8,128)(2,1)} %gather_fusion) | copy-start | bytes 18874372 | tf_op jit(solution)/shard_map/while
  210.8 10.3 %all-to-all-start.4 = ((f32[4,8,12]{2,0,1:T(4,128)}), f32[4,8,12]{2,0,1:T(4,128)S(1)}, u32[]{:S(2)}, u32[]{:S(2)}) async-start(f32[4,8,12]{2,0,1:T(4,128)} %copy.26), calls=%async_computation.4 | async-start | bytes 32768 | tf_op jit(solution)/shard_map/all_to_all | solution.py:80
  221.1 73.8 %all-to-all-start.6 = ((bf16[4,8,12,32,128]{4,3,2,0,1:T(8,128)(2,1)}), bf16[4,8,12,32,128]{4,3,2,0,1:T(8,128)(2,1)S(1)}, u32[]{:S(2)}, u32[]{:S(2)}) async-start(bf16[4,8,12,32,128]{4,3,2,0,1:T(8,128)(2,1)} %copy.28), calls=%async_computation.6 | async-start | bytes 6291456 | tf_op jit(solution)/shard_map/all_to_all | solution.py:78
  294.9 7.1 %all-to-all-start.5 = ((f32[4,8,12]{2,1,0:T(8,128)}), f32[4,8,12]{2,1,0:T(8,128)S(1)}, u32[]{:S(2)}, u32[]{:S(2)}) async-start(f32[4,8,12]{2,1,0:T(8,128)} %copy.27), calls=%async_computation.5 | async-start | bytes 32768 | tf_op jit(solution)/shard_map/all_to_all | solution.py:81
  300.3 7.0 %copy-start.4 = (s32[8,16]{1,0:T(8,128)S(1)}, s32[8,16]{1,0:T(8,128)}, u32[]{:S(2)}) copy-start(s32[8,16]{1,0:T(8,128)} %param.8) | copy-start | bytes 1540
  302.0 40.6 %all-to-all-start.7 = ((bf16[4,8,12,32,128]{4,3,2,1,0:T(8,128)(2,1)}), bf16[4,8,12,32,128]{4,3,2,1,0:T(8,128)(2,1)S(1)}, u32[]{:S(2)}, u32[]{:S(2)}) async-start(bf16[4,8,12,32,128]{4,3,2,1,0:T(8,128)(2,1)} %copy.29), calls=%async_computation.7 | async-start | bytes 6291456 | tf_op jit(solution)/shard_map/all_to_all | solution.py:79
  305.7 40.4 %copy-start.3 = (bf16[8,32,128]{2,1,0:T(8,128)(2,1)S(1)}, bf16[8,32,128]{2,1,0:T(8,128)(2,1)}, u32[]{:S(2)}) copy-start(bf16[8,32,128]{2,1,0:T(8,128)(2,1)} %param.6) | copy-start | bytes 196612
where the time goes:
time: 349 us; the launch traced here: 348 us
  waiting for transfers between devices  214 us (61%)
  local copies, waits for them, and re-layouts  57 us (16%)
  starting transfers between devices  35.7 us (10%)
  matrix products  32.1 us (9%)
  other arithmetic  8.01 us (2%)
    all_to_all x1, waiting for transfers between devices, local(): lax.all_to_all(outgoing, 'dev', split_axis=1, concat_axis=1, tiled=True)  69.5 us
    all_to_all x1, waiting for transfers between devices, local(): lax.all_to_all(pulled, 'dev', split_axis=1, concat_axis=1, tiled=True)  69.3 us
    all_to_all x1, waiting for transfers between devices, local(): lax.all_to_all(mid_queries, 'group', split_axis=0, concat_axis=0, tiled=T...  35.5 us
    all_to_all x1, waiting for transfers between devices, local(): lax.all_to_all(mid_pulled, 'group', split_axis=0, concat_axis=0, tiled=True)  34.4 us
    gather x4, local copies, waits for them, and re-layouts, score_block(): passage_block = jnp.take(passage_unit, tag_block, axis=0)  23.7 us
    dot_general x4, matrix products, score_block(): jnp.einsum('bqe,bpe->bqp', query_block, passage_block, preferred_element_...  22.1 us
    scatter x1, local copies, waits for them, and re-layouts, local(): outgoing = outgoing.at[slot_index].set(query_send[query_owner])  9.71 us
    dot_general x4, matrix products, score_block(): jnp.einsum('bqp,bpe->bqe', attention, passage_block, preferred_element_ty...  9.55 us
  transfers between devices with their start and end apart: 8, of which 7 were waited for; matrix products, arithmetic and copies ran while one was open for 9% of the time, Pallas kernels for 0%

commit v1 on v0

v1 whole, which is shorter than its diff:
```python
import functools

import jax
import jax.numpy as jnp
from jax import lax
from jax.experimental import pallas as pl
from jax.experimental.pallas import tpu as pltpu
from jax.sharding import PartitionSpec as P

SOFTNESS = 0.02
EPSILON = 1e-06
LANES = 128
TAIL = 16
BASE = 256
UNROLL = 4
F32 = jnp.float32
BF16 = jnp.bfloat16


def call(body, out_shape, name, flops=0, in_specs=None, scratch=()):
    kwargs = {} if in_specs is None else {"in_specs": in_specs}
    return pl.pallas_call(
        body,
        out_shape=out_shape,
        scratch_shapes=list(scratch),
        name=name,
        cost_estimate=pl.CostEstimate(flops=flops, bytes_accessed=1 << 20, transcendentals=0),
        compiler_params=pltpu.CompilerParams(vmem_limit_bytes=48 * 1024 * 1024),
        **kwargs,
    )


def unit(values):
    floats = values.astype(F32)
    scale = lax.rsqrt(jnp.sum(floats * floats, axis=-1, keepdims=True) + EPSILON)
    return floats * scale, scale


def pack_body(queries_ref, cand_ref, out_ref):
    count, length, width = queries_ref.shape
    rows = count * length
    out_ref[:rows] = unit(queries_ref[...])[0].astype(BF16).reshape(rows, width)
    ids = jnp.broadcast_to(cand_ref[...], (TAIL, LANES))
    high = ids // BASE
    low = ids - high * BASE
    place = lax.broadcasted_iota(jnp.int32, (TAIL, LANES), 0)
    digits = jnp.where(place == 0, high, jnp.where(place == 1, low, 0))
    out_ref[rows:] = digits.astype(F32).astype(BF16)


def unit_body(passages_ref, out_ref):
    def step(index, carry):
        out_ref[index] = unit(passages_ref[index])[0].astype(BF16)
        return carry

    lax.fori_loop(0, passages_ref.shape[0], step, 0)


def route_body(docs_ref, pay_ref, out_ref, *, rows, near_count, slots):
    blocks = pay_ref.shape[0]
    ids = []
    for block in range(blocks):
        tile = pay_ref[block, rows : rows + TAIL].astype(F32)
        ids.append((tile[0:1] * BASE + tile[1:2]).astype(jnp.int32))
    ids = jnp.concatenate(ids, axis=0)
    pair = lax.broadcasted_iota(jnp.int32, (blocks, LANES), 0) * LANES
    pair = pair + lax.broadcasted_iota(jnp.int32, (blocks, LANES), 1)
    upper = lax.broadcasted_iota(jnp.int32, (LANES, LANES), 0)
    lane = lax.broadcasted_iota(jnp.int32, (LANES, LANES), 1)
    triangle = (upper <= lane).astype(F32)
    diagonal = upper == lane
    place = lax.broadcasted_iota(jnp.int32, (slots, LANES), 0).astype(F32)
    for half in range(2):
        local = jnp.full((blocks, LANES), -1, jnp.int32)
        for index in range(near_count):
            local = jnp.where(ids == docs_ref[half * near_count + index], index, local)
        mask = local >= 0
        code = (local * (blocks * LANES) + pair).astype(F32)
        ranks = jnp.dot(mask.astype(F32), triangle, preferred_element_type=F32)
        before = jnp.zeros((1, 1), F32)
        found = jnp.zeros((slots, LANES), F32)
        for block in range(blocks):
            row = ranks[block : block + 1]
            slot = jnp.where(mask[block : block + 1], before + row - 1.0, -1.0)
            found = found + jnp.where(place == slot, code[block : block + 1], 0.0)
            before = before + row[:, LANES - 1 : LANES]
        packed = jnp.sum(found, axis=1, keepdims=True)
        for part in range(slots // LANES):
            piece = packed[part * LANES : (part + 1) * LANES]
            line = jnp.sum(jnp.where(diagonal, piece, 0.0), axis=0, keepdims=True)
            out_ref[half, part : part + 1] = line.astype(jnp.int32)
        out_ref[half, slots // LANES : slots // LANES + 1] = jnp.broadcast_to(
            before, (1, LANES)
        ).astype(jnp.int32)


def score_pairs(list_ref, pay_ref, pass_ref, acc_ref, sums_ref, *, length, list_len):
    parts = list_ref.shape[0] - 1
    blocks = pay_ref.shape[0]
    per_block = LANES // list_len
    queries = blocks * per_block
    count = list_ref[parts, 0]
    ones = jnp.ones((pass_ref.shape[1], LANES), BF16)

    def step(index, carry):
        done = []
        for offset in range(UNROLL):
            slot = index * UNROLL + offset
            code = list_ref[slot // LANES, slot % LANES]
            local = code // (blocks * LANES)
            pair = code % (blocks * LANES)
            query = pair // list_len
            first = (pair % list_len) == 0
            weight = jnp.where(slot < count, 1.0, 0.0).astype(F32)
            row = pl.multiple_of((query % per_block) * length, length)
            tokens = pay_ref[query // per_block, pl.ds(row, length)]
            passage = pass_ref[local]
            logits = lax.dot_general(
                tokens, passage, (((1,), (1,)), ((), ())), preferred_element_type=F32
            )
            terms = jnp.exp(logits * (1.0 / SOFTNESS)).astype(BF16)
            pulled = jnp.dot(terms, passage, preferred_element_type=F32)
            mass = jnp.dot(terms, ones, preferred_element_type=F32)
            pulled = pulled / mass
            score = SOFTNESS * jnp.sum(jnp.log(mass), axis=0, keepdims=True)
            exp_score = jnp.exp(score)
            target = jnp.where(first, queries, 0) + query
            factor = jnp.where(first, 1.0, exp_score) * weight
            value = jnp.where(first, score, exp_score) * weight
            done.append((target, pulled * factor, value))
        for target, product, value in done:
            at = pl.ds(pl.multiple_of(target * length, length), length)
            acc_ref[at] = acc_ref[at] + product
            sums_ref[pl.ds(target, 1)] = sums_ref[pl.ds(target, 1)] + value
        return carry

    lax.fori_loop(0, (count + UNROLL - 1) // UNROLL, step, 0)


def near_body(list_ref, pay_ref, pass_ref, acc_ref, sums_ref, *, length, list_len):
    acc_ref[...] = jnp.zeros_like(acc_ref)
    sums_ref[...] = jnp.zeros_like(sums_ref)
    score_pairs(list_ref, pay_ref, pass_ref, acc_ref, sums_ref, length=length, list_len=list_len)


def far_body(
    list_ref, pay_ref, pass_ref, acc_in, sums_in, send_ref, keep_ref, sums_ref, acc_ref,
    *, length, list_len,
):
    acc_ref[...] = acc_in[...]
    sums_ref[...] = sums_in[...]
    score_pairs(list_ref, pay_ref, pass_ref, acc_ref, sums_ref, length=length, list_len=list_len)
    half = send_ref.shape[1]
    for kind in range(2):
        start = kind * 2 * half
        keep_ref[kind] = acc_ref[start : start + half]
        send_ref[kind] = acc_ref[start + half : start + 2 * half].astype(BF16)


def merge_body(keep_ref, got_ref, sums_ref, send_ref, rest_ref, *, length):
    queries = sums_ref.shape[1]

    def part(index):
        at = pl.ds(pl.multiple_of(index * length, length), length)
        others = keep_ref[0, at] + got_ref[0, at].astype(F32)
        first = keep_ref[1, at] + got_ref[1, at].astype(F32)
        return others - sums_ref[0, pl.ds(index, 1)] * first

    def step(index, carry):
        at = pl.ds(pl.multiple_of(index * length, length), length)
        rest_ref[at] = part(index)
        send_ref[at] = part(index + queries // 2).astype(BF16)
        return carry

    lax.fori_loop(0, queries // 2, step, 0)


def last_body(queries_ref, keep_ref, got_ref, sums_ref, grad_ref, loss_ref, *, length):
    for index in range(queries_ref.shape[0]):
        at = slice(index * length, (index + 1) * length)
        spread = sums_ref[0, index : index + 1]
        score = sums_ref[1, index : index + 1]
        total = spread + jnp.exp(score)
        loss_ref[index : index + 1] = jnp.log(total) - score
        gradient = (keep_ref[at] + got_ref[at].astype(F32)) / total
        query_unit, query_scale = unit(queries_ref[index])
        along = jnp.sum(query_unit * gradient, axis=-1, keepdims=True)
        grad_ref[index] = (gradient - query_unit * along) * query_scale


def swap(value, axis, bit):
    size = lax.axis_size(axis)
    return lax.ppermute(value, axis, [(index, index ^ bit) for index in range(size)])


def bits_of(size):
    return [1 << power for power in reversed(range(size.bit_length() - 1))]


def local(queries, passages, candidates, location):
    group_count = lax.axis_size("group")
    dev_count = lax.axis_size("dev")
    device_total = group_count * dev_count
    query_count, length, width = queries.shape
    pass_count, pass_len, _ = passages.shape
    list_len = candidates.shape[1]
    pair_count = query_count * list_len
    rows = query_count * length
    slot_cap = max(2, (3 * pair_count + device_total - 1) // device_total)
    group = lax.axis_index("group")
    dev = lax.axis_index("dev")
    shape = jax.ShapeDtypeStruct

    units = call(unit_body, shape(passages.shape, BF16), "passage_units")(passages)
    payload = call(pack_body, shape((rows + TAIL, width), BF16), "query_units")(
        queries, candidates.reshape(1, pair_count)
    )

    held, offsets = [units], [0]
    for bit in bits_of(group_count):
        held = held + [swap(block, "group", bit) for block in held]
        offsets = offsets + [offset ^ bit for offset in offsets]
    half_bit = group_count // 2
    order = [index for index, offset in enumerate(offsets) if not offset & half_bit]
    order += [index for index, offset in enumerate(offsets) if offset & half_bit]
    near_blocks = len(order) // 2
    near = jnp.concatenate([held[index] for index in order[:near_blocks]], axis=0)
    far = jnp.concatenate([held[index] for index in order[near_blocks:]], axis=0)

    owners = (group ^ jnp.array([offsets[index] for index in order], jnp.int32)) * dev_count + dev
    held_rows = owners[:, None] * pass_count + jnp.arange(pass_count, dtype=jnp.int32)[None, :]
    hits = location[None, :] == held_rows.reshape(-1, 1)
    documents = jnp.arange(location.shape[0], dtype=jnp.int32)
    docs = jnp.sum(jnp.where(hits, documents[None, :], 0), axis=1)

    pay = payload[None]
    for bit in bits_of(dev_count):
        pay = jnp.concatenate([pay, swap(pay, "dev", bit)], axis=0)

    near_count = near_blocks * pass_count
    most = dev_count * min(pair_count, near_blocks * slot_cap)
    slots = -(-most // LANES) * LANES
    lists = call(
        functools.partial(route_body, rows=rows, near_count=near_count, slots=slots),
        shape((2, slots // LANES + 1, LANES), jnp.int32),
        "route",
        in_specs=[pl.BlockSpec(memory_space=pltpu.SMEM), pl.BlockSpec(memory_space=pltpu.VMEM)],
    )(docs, pay)

    all_queries = dev_count * query_count
    flops = dev_count * pair_count // 4 * length * pass_len * width * 4
    mem = [pl.BlockSpec(memory_space=pltpu.SMEM)] + [pl.BlockSpec(memory_space=pltpu.VMEM)] * 4
    sizes = dict(length=length, list_len=list_len)
    acc, sums = call(
        functools.partial(near_body, **sizes),
        [shape((2 * all_queries * length, width), F32), shape((2 * all_queries, LANES), F32)],
        "score_near",
        flops,
        mem[:3],
    )(lists[0], pay, near)
    half_rows = all_queries * length // 2
    send, keep, sums = call(
        functools.partial(far_body, **sizes),
        [
            shape((2, half_rows, width), BF16),
            shape((2, half_rows, width), F32),
            shape((2 * all_queries, LANES), F32),
        ],
        "score_far",
        flops,
        mem,
        [pltpu.VMEM((2 * all_queries * length, width), F32)],
    )(lists[1], pay, far, acc, sums)

    steps = bits_of(dev_count)[::-1]
    sums = sums.reshape((2, 2, all_queries // 2, LANES))
    sums = sums[:, 0] + swap(sums[:, 1], "dev", steps[0])
    got = swap(send, "dev", steps[0])
    levels = len(steps) - 1
    sums = sums.reshape((2,) + (2,) * levels + (query_count, LANES))
    for level, bit in enumerate(steps[1:]):
        sums = sums + jnp.flip(swap(sums, "dev", bit), axis=1 + level)
    sums = sums.reshape(2, all_queries // 2, LANES)
    quarter = half_rows // 2
    send, rest = call(
        functools.partial(merge_body, length=length),
        [shape((quarter, width), BF16), shape((quarter, width), F32)],
        "merge",
    )(keep, got, sums)
    for bit in steps[1:-1]:
        rest = rest + swap(send, "dev", bit).astype(F32)
        quarter = quarter // 2
        rest, send = rest[:quarter], rest[quarter:].astype(BF16)
    got = swap(send, "dev", steps[-1])
    grad, loss = call(
        functools.partial(last_body, length=length),
        [shape(queries.shape, F32), shape((query_count, LANES), F32)],
        "last",
    )(queries, rest, got, sums[:, :query_count])
    return loss[:, 0], grad


def solution(mesh):
    placed = (
        P(("group", "dev"), None, None),
        P(("group", "dev"), None, None),
        P(("group", "dev"), None),
        P(),
    )
    return jax.shard_map(
        local,
        mesh=mesh,
        in_specs=placed,
        out_specs=(P(("group", "dev")), P(("group", "dev"), None, None)),
        check_vma=False,
    )
```

time: 349 us -> 95.7 us (0.27)
  waiting for transfers between devices: 214 us -> 39.7 us
  local copies, waits for them, and re-layouts: 57 us -> 3.37 us
  matrix products: 32.1 us -> 0 us
  Pallas kernels: 0 us -> 20.5 us
  starting transfers between devices: 35.7 us -> 26.8 us
  other arithmetic: 8.01 us -> 4.29 us
    all_to_all x8 -> x0, waiting for transfers between devices: 214 us -> none  [the longest x1 69.5 us: local(): lax.all_to_all(outgoing, 'dev', split_axis=1, concat_axis=1, tiled=True)]
    ppermute x0 -> x12, waiting for transfers between devices: none -> 39.7 us  [swap(): lax.ppermute(value, axis, [(index, index ^ bit) for index in range(size)])]
    all_to_all x8 -> x0, starting transfers between devices: 35.7 us -> none  [the longest x1 7.28 us: local(): lax.all_to_all(labels, 'dev', split_axis=1, concat_axis=1, tiled=True)]
    dot_general x9 -> x0, matrix products: 32.1 us -> none  [the longest x4 22.1 us: score_block(): jnp.einsum('bqe,bpe->bqp', query_block, passage_block, preferred_element_...]
    gather x10 -> x0, local copies, waits for them, and re-layouts: 29.8 us -> none  [the longest x4 23.7 us: score_block(): passage_block = jnp.take(passage_unit, tag_block, axis=0)]
    ppermute x0 -> x12, starting transfers between devices: none -> 26.8 us  [swap(): lax.ppermute(value, axis, [(index, index ^ bit) for index in range(size)])]
    pallas_call x0 -> x7, Pallas kernels: none -> 20.5 us  [the longest x1 8.77 us: local(): call(functools.partial(far_body, **sizes), [shape((2, half_rows, width),...]
    scatter x2 -> x0, local copies, waits for them, and re-layouts: 11.1 us -> none  [the longest x1 9.71 us: local(): outgoing = outgoing.at[slot_index].set(query_send[query_owner])]
  transfers between devices with their start and end apart: 8 -> 12, of which waited for: 7 -> 8; matrix products, arithmetic and copies ran while one was open for 9% -> 3% of each run, Pallas kernels for 0% -> 9%
where the time goes in v1:
time: 95.7 us; the launch traced here: 95.5 us
  waiting for transfers between devices  39.7 us (41%)
  starting transfers between devices  26.8 us (28%)
  Pallas kernels  20.5 us (21%)
  other arithmetic  4.29 us (4%)
  local copies, waits for them, and re-layouts  3.37 us (4%)
    ppermute x12, waiting for transfers between devices, swap(): lax.ppermute(value, axis, [(index, index ^ bit) for index in range(size)])  39.7 us
    ppermute x12, starting transfers between devices, swap(): lax.ppermute(value, axis, [(index, index ^ bit) for index in range(size)])  26.8 us
    pallas_call x1, Pallas kernels, local(): call(functools.partial(far_body, **sizes), [shape((2, half_rows, width),...  8.77 us
    pallas_call x1, Pallas kernels, local(): call(functools.partial(near_body, **sizes), [shape((2 * all_queries * len...  7.61 us
    unnamed x10, local copies, waits for them, and re-layouts  2.56 us
    concatenate x3, other arithmetic, local(): pay = jnp.concatenate([pay, swap(pay, 'dev', bit)], axis=0)  2.41 us
  transfers between devices with their start and end apart: 12, of which 8 were waited for; matrix products, arithmetic and copies ran while one was open for 3% of the time, Pallas kernels for 9%

profile of v1, /device:TPU:0, one launch (start us, length us, event | category | flops | bytes accessed | tf_op | source)
XLA Modules:
  0.0 95.5 jit_solution(4046850852876224805)
XLA Ops:
  0.6 0.0 copy-start.1
  0.6 1.2 %copy-done.1 = bf16[16,256,128]{2,1,0:T(8,128)(2,1)S(1)} copy-done((bf16[16,256,128]{2,1,0:T(8,128)(2,1)S(1)}, bf16[16,256,128]{2,1,0:T(8,128)(2,1)}, u32[]{:S(2)}) %copy-start.1) | copy-done | bytes 1048600
  1.9 0.0 copy-start.3
  1.9 0.0 copy-start.2
  1.9 0.0 copy-start.4
  1.9 1.9 %passage_units.1 = bf16[16,256,128]{2,1,0:T(8,128)(2,1)S(1)} custom-call(bf16[16,256,128]{2,1,0:T(8,128)(2,1)S(1)} %copy-done.1), custom_call_target="tpu_custom_call" | custom-call | bytes 1048576 | tf_op jit(solution)/shard_map/passage_units/pallas_call | solution.py:214
  3.8 3.0 %collective-permute-start.3 = (bf16[16,256,128]{2,1,0:T(8,128)(2,1)S(1)}, bf16[16,256,128]{2,1,0:T(8,128)(2,1)S(1)}, u32[]{:S(2)}, u32[]{:S(2)}) collective-permute-start(bf16[16,256,128]{2,1,0:T(8,128)(2,1)S(1)} %passage_units.1), channel_id=1, source_target_pairs={{0,16},{8,24},{16,0},{24,8},{1,17},{9,25},{17,1},{25,9},{2,18},{10... | collective-permute-start | bytes 3145736 | tf_op jit(solution)/shard_map/ppermute | solution.py:193
  6.8 0.0 copy-done.3
  6.8 0.1 reshape.34.cand_ref
  6.9 0.0 copy-done.2
  6.9 0.1 query_units.1
  7.0 2.7 %collective-permute-start = (bf16[1,272,128]{2,1,0:T(8,128)(2,1)S(1)}, bf16[1,272,128]{2,1,0:T(8,128)(2,1)S(1)}, u32[]{:S(2)}, u32[]{:S(2)}) collective-permute-start(bf16[1,272,128]{2,1,0:T(8,128)(2,1)S(1)} %bitcast.16), channel_id=1, source_target_pairs={{0,4},{1,5},{2,6},{3,7},{4,0},{5,1},{6,2},{7,3},{8,12},{9,13},{10,... | collective-permute-start | bytes 208904 | tf_op jit(solution)/shard_map/ppermute | solution.py:193
  9.6 0.0 collective-permute-start.5
  9.6 3.0 %collective-permute-done = bf16[1,272,128]{2,1,0:T(8,128)(2,1)S(1)} collective-permute-done((bf16[1,272,128]{2,1,0:T(8,128)(2,1)S(1)}, bf16[1,272,128]{2,1,0:T(8,128)(2,1)S(1)}, u32[]{:S(2)}, u32[]{:S(2)}) %collective-permute-start) | collective-permute-done | bytes 69664 | tf_op jit(solution)/shard_map/ppermute | solution.py:193
  12.6 0.7 pad_maximum_fusion.4
  13.3 1.3 %collective-permute-start.1 = (bf16[2,272,128]{2,1,0:T(8,128)(2,1)}, bf16[2,272,128]{2,1,0:T(8,128)(2,1)S(1)}, u32[]{:S(2)}, u32[]{:S(2)}) collective-permute-start(bf16[2,272,128]{2,1,0:T(8,128)(2,1)} %pad_maximum_fusion.4), channel_id=1, source_target_pairs={{0,2},{1,3},{2,0},{3,1},{4,6},{5,7},{6,4},{7,5},{8,10},{9,11},{10,... | collective-permute-start | bytes 417800 | tf_op jit(solution)/shard_map/ppermute | solution.py:193
  14.6 15.3 %collective-permute-done.3 = bf16[16,256,128]{2,1,0:T(8,128)(2,1)S(1)} collective-permute-done((bf16[16,256,128]{2,1,0:T(8,128)(2,1)S(1)}, bf16[16,256,128]{2,1,0:T(8,128)(2,1)S(1)}, u32[]{:S(2)}, u32[]{:S(2)}) %collective-permute-start.3) | collective-permute-done | bytes 1048608 | tf_op jit(solution)/shard_map/ppermute | solution.py:193
  29.9 0.0 collective-permute-start.4
  29.9 0.0 collective-permute-done.1
  29.9 0.7 pad_maximum_fusion.3
  30.7 1.8 %collective-permute-start.2 = (bf16[4,272,128]{2,1,0:T(8,128)(2,1)}, bf16[4,272,128]{2,1,0:T(8,128)(2,1)}, u32[]{:S(2)}, u32[]{:S(2)}) collective-permute-start(bf16[4,272,128]{2,1,0:T(8,128)(2,1)} %pad_maximum_fusion.3), channel_id=1, source_target_pairs={{0,1},{1,0},{2,3},{3,2},{4,5},{5,4},{6,7},{7,6},{8,9},{9,8},{10,11... | collective-permute-start | bytes 835592 | tf_op jit(solution)/shard_map/ppermute | solution.py:193
  32.4 0.1 iota_add_fusion
  32.5 0.1 add.43
  32.6 0.0 copy-done.4
  32.6 0.2 select_reduce_fusion.docs_ref
  32.8 7.3 %collective-permute-done.2 = bf16[4,272,128]{2,1,0:T(8,128)(2,1)} collective-permute-done((bf16[4,272,128]{2,1,0:T(8,128)(2,1)}, bf16[4,272,128]{2,1,0:T(8,128)(2,1)}, u32[]{:S(2)}, u32[]{:S(2)}) %collective-permute-start.2) | collective-permute-done | bytes 278560 | tf_op jit(solution)/shard_map/ppermute | solution.py:193
  40.1 1.0 %pad_maximum_fusion.2.pay_ref = bf16[8,272,128]{2,1,0:T(8,128)(2,1)S(1)} fusion(bf16[4,272,128]{2,1,0:T(8,128)(2,1)} %collective-permute-done.2, bf16[2,272,128]{2,1,0:T(8,128)(2,1)S(1)} %collective-permute-done.1, bf16[1,272,128]{2,1,0:T(8,128)(2,1)S(1)} %collective-permute-done, bf16[1,272,128]{2,1,0:T(8,128)(2,1)S(1)} %bitcast.19), kind=kLoop, calls=%fused_computation.2 | loop fusion | flops 835584 | bytes 1114112 | tf_op jit(solution)/shard_map/concatenate | solution.py:238
  41.1 1.0 %route.1 = s32[2,3,128]{2,1,0:T(4,128)S(1)} custom-call(s32[64]{0:T(128)S(1)} %select_reduce_fusion.docs_ref, bf16[8,272,128]{2,1,0:T(8,128)(2,1)S(1)} %pad_maximum_fusion.2.pay_ref), custom_call_target="tpu_custom_call" | custom-call | bytes 1048576 | tf_op jit(solution)/shard_map/route/pallas_call | solution.py:243
  42.1 0.0 collective-permute-done.5
  42.2 0.2 pad_maximum_fusion.1.pass_ref
  42.3 7.6 %score_near.1 = (f32[4096,128]{1,0:T(8,128)S(1)}, f32[128,128]{1,0:T(8,128)S(1)}) custom-call(s32[3,128]{1,0:T(4,128)S(1)} %get-tuple-element.20.list_ref, bf16[8,272,128]{2,1,0:T(8,128)(2,1)S(1)} %pad_maximum_fusion.2.pay_ref, bf16[32,256,128]{2,1,0:T(8,128)(2,1)S(1)} %pad_maximum_fusion.1.pass_ref), custom_call_target="tpu_custom_call" | custom-call | flops 1073741824 | bytes 1048576 | tf_op jit(solution)/shard_map/score_near/pallas_call | solution.py:254
  50.0 0.0 copy-start
  50.0 1.3 %copy-done = f32[4096,128]{1,0:T(8,128)} copy-done((f32[4096,128]{1,0:T(8,128)}, f32[4096,128]{1,0:T(8,128)S(1)}, u32[]{:S(2)}) %copy-start) | copy-done | bytes 2097176
  51.3 0.0 collective-permute-done.4
  51.3 1.4 %pad_maximum_fusion.pass_ref = bf16[32,256,128]{2,1,0:T(8,128)(2,1)S(1)} fusion(bf16[16,256,128]{2,1,0:T(8,128)(2,1)} %collective-permute-done.4, bf16[16,256,128]{2,1,0:T(8,128)(2,1)S(1)} %collective-permute-done.3), kind=kLoop, calls=%fused_computation | loop fusion | flops 1048576 | bytes 4194304 | tf_op jit(solution)/shard_map/concatenate | solution.py:228
  52.7 8.8 %score_far.1 = (bf16[2,1024,128]{2,1,0:T(8,128)(2,1)S(1)}, f32[2,1024,128]{2,1,0:T(8,128)S(1)}, f32[128,128]{1,0:T(8,128)S(1)}) custom-call(s32[3,128]{1,0:T(4,128)S(1)} %get-tuple-element.21.list_ref, bf16[8,272,128]{2,1,0:T(8,128)(2,1)S(1)} %pad_maximum_fusion.2.pay_ref, bf16[32,256,128]{2,1,0:T(8,128)(2,1)S(1)} %pad_maximum_fusion.pass_ref, ...), custom_call_target="tpu_custom_call" | custom-call | flops 1073741824 | bytes 1048576 | tf_op jit(solution)/shard_map/score_far/pallas_call | solution.py:262
  61.5 0.1 collective-permute-start.7
  61.6 2.0 %collective-permute-start.6 = (bf16[2,1024,128]{2,1,0:T(8,128)(2,1)S(1)}, bf16[2,1024,128]{2,1,0:T(8,128)(2,1)S(1)}, u32[]{:S(2)}, u32[]{:S(2)}) collective-permute-start(bf16[2,1024,128]{2,1,0:T(8,128)(2,1)S(1)} %get-tuple-element.14), channel_id=1, source_target_pairs={{0,1},{1,0},{2,3},{3,2},{4,5},{5,4},{6,7},{7,6},{8,9},{9,8},{10,11... | collective-permute-start | bytes 1572872 | tf_op jit(solution)/shard_map/ppermute | solution.py:193
  63.6 2.2 %collective-permute-done.7 = f32[2,32,128]{2,1,0:T(8,128)S(1)} collective-permute-done((f32[2,32,128]{2,1,0:T(8,128)S(1)}, f32[2,32,128]{2,1,0:T(8,128)S(1)}, u32[]{:S(2)}, u32[]{:S(2)}) %collective-permute-start.7) | collective-permute-done | bytes 32800 | tf_op jit(solution)/shard_map/ppermute | solution.py:193
  65.8 1.1 %collective-permute-start.8 = (f32[2,2,2,8,128]{4,3,2,1,0:T(8,128)S(1)}, f32[2,2,2,8,128]{4,3,2,1,0:T(8,128)S(1)}, u32[]{:S(2)}, u32[]{:S(2)}) collective-permute-start(f32[2,2,2,8,128]{4,3,2,1,0:T(8,128)S(1)} %bitcast.24), channel_id=1, source_target_pairs={{0,2},{1,3},{2,0},{3,1},{4,6},{5,7},{6,4},{7,5},{8,10},{9,11},{10,... | collective-permute-start | bytes 98312 | tf_op jit(solution)/shard_map/ppermute | solution.py:193
  66.9 2.8 %collective-permute-done.8 = f32[2,2,2,8,128]{4,3,2,1,0:T(8,128)S(1)} collective-permute-done((f32[2,2,2,8,128]{4,3,2,1,0:T(8,128)S(1)}, f32[2,2,2,8,128]{4,3,2,1,0:T(8,128)S(1)}, u32[]{:S(2)}, u32[]{:S(2)}) %collective-permute-start.8) | collective-permute-done | bytes 32800 | tf_op jit(solution)/shard_map/ppermute | solution.py:193
  69.7 8.5 %collective-permute-start.9 = (f32[2,2,2,8,128]{4,3,2,1,0:T(8,128)S(1)}, f32[2,2,2,8,128]{4,3,2,1,0:T(8,128)S(1)}, u32[]{:S(2)}, u32[]{:S(2)}) collective-permute-start(f32[2,2,2,8,128]{4,3,2,1,0:T(8,128)S(1)} %reverse_add_fusion.1), channel_id=1, source_target_pairs={{0,4},{1,5},{2,6},{3,7},{4,0},{5,1},{6,2},{7,3},{8,12},{9,13},{10,... | collective-permute-start | bytes 98312 | tf_op jit(solution)/shard_map/ppermute | solution.py:193
  78.2 1.9 %collective-permute-done.9 = f32[2,2,2,8,128]{4,3,2,1,0:T(8,128)S(1)} collective-permute-done((f32[2,2,2,8,128]{4,3,2,1,0:T(8,128)S(1)}, f32[2,2,2,8,128]{4,3,2,1,0:T(8,128)S(1)}, u32[]{:S(2)}, u32[]{:S(2)}) %collective-permute-start.9) | collective-permute-done | bytes 32800 | tf_op jit(solution)/shard_map/ppermute | solution.py:193
  80.1 0.0 collective-permute-done.6.got_ref
  80.1 0.2 merge.1
  80.4 0.1 collective-permute-start.10
  80.4 5.0 %collective-permute-done.10 = bf16[512,128]{1,0:T(8,128)(2,1)S(1)} collective-permute-done((bf16[512,128]{1,0:T(8,128)(2,1)S(1)}, bf16[512,128]{1,0:T(8,128)(2,1)S(1)}, u32[]{:S(2)}, u32[]{:S(2)}) %collective-permute-start.10) | collective-permute-done | bytes 131104 | tf_op jit(solution)/shard_map/ppermute | solution.py:193
  85.4 6.3 %collective-permute-start.11 = (bf16[256,128]{1,0:T(8,128)(2,1)S(1)}, bf16[256,128]{1,0:T(8,128)(2,1)S(1)}, u32[]{:S(2)}, u32[]{:S(2)}) collective-permute-start(bf16[256,128]{1,0:T(8,128)(2,1)S(1)} %slice.48), channel_id=1, source_target_pairs={{0,4},{1,5},{2,6},{3,7},{4,0},{5,1},{6,2},{7,3},{8,12},{9,13},{10,... | collective-permute-start | bytes 196616 | tf_op jit(solution)/shard_map/ppermute | solution.py:193
  91.8 2.2 %collective-permute-done.11.got_ref = bf16[256,128]{1,0:T(8,128)(2,1)S(1)} collective-permute-done((bf16[256,128]{1,0:T(8,128)(2,1)S(1)}, bf16[256,128]{1,0:T(8,128)(2,1)S(1)}, u32[]{:S(2)}, u32[]{:S(2)}) %collective-permute-start.11) | collective-permute-done | bytes 65568 | tf_op jit(solution)/shard_map/ppermute | solution.py:193
  94.0 0.9 last.1
  94.9 0.6 slice_reduce_fusion
  (10 shorter events, 0.1 us)
Async XLA Ops:
  0.6 1.2 %copy-start.1 = (bf16[16,256,128]{2,1,0:T(8,128)(2,1)S(1)}, bf16[16,256,128]{2,1,0:T(8,128)(2,1)}, u32[]{:S(2)}) copy-start(bf16[16,256,128]{2,1,0:T(8,128)(2,1)} %passages_ref.1) | copy-start | bytes 3145732
  1.9 4.9 %copy-start.3 = (s32[8,16]{1,0:T(8,128)S(1)}, s32[8,16]{1,0:T(8,128)}, u32[]{:S(2)}) copy-start(s32[8,16]{1,0:T(8,128)} %param.7) | copy-start | bytes 1540
  1.9 5.0 %copy-start.2 = (bf16[8,32,128]{2,1,0:T(8,128)(2,1)S(1)}, bf16[8,32,128]{2,1,0:T(8,128)(2,1)}, u32[]{:S(2)}) copy-start(bf16[8,32,128]{2,1,0:T(8,128)(2,1)} %queries_ref.3) | copy-start | bytes 196612
  1.9 30.7 %copy-start.4 = (s32[512]{0:T(512)S(1)}, s32[512]{0:T(512)}, u32[]{:S(2)}) copy-start(s32[512]{0:T(512)} %param.8) | copy-start | bytes 6148
  3.8 26.2 %collective-permute-start.3 = (bf16[16,256,128]{2,1,0:T(8,128)(2,1)S(1)}, bf16[16,256,128]{2,1,0:T(8,128)(2,1)S(1)}, u32[]{:S(2)}, u32[]{:S(2)}) collective-permute-start(bf16[16,256,128]{2,1,0:T(8,128)(2,1)S(1)} %passage_units.1), channel_id=1, source_target_pairs={{0,16},{8,24},{16,0},{24,8},{1,17},{9,25},{17,1},{25,9},{2,18},{10... | collective-permute-start | bytes 3145736 | tf_op jit(solution)/shard_map/ppermute | solution.py:193
  7.0 5.6 %collective-permute-start = (bf16[1,272,128]{2,1,0:T(8,128)(2,1)S(1)}, bf16[1,272,128]{2,1,0:T(8,128)(2,1)S(1)}, u32[]{:S(2)}, u32[]{:S(2)}) collective-permute-start(bf16[1,272,128]{2,1,0:T(8,128)(2,1)S(1)} %bitcast.16), channel_id=1, source_target_pairs={{0,4},{1,5},{2,6},{3,7},{4,0},{5,1},{6,2},{7,3},{8,12},{9,13},{10,... | collective-permute-start | bytes 208904 | tf_op jit(solution)/shard_map/ppermute | solution.py:193
  9.6 32.5 %collective-permute-start.5 = (bf16[16,256,128]{2,1,0:T(8,128)(2,1)S(1)}, bf16[16,256,128]{2,1,0:T(8,128)(2,1)S(1)}, u32[]{:S(2)}, u32[]{:S(2)}) collective-permute-start(bf16[16,256,128]{2,1,0:T(8,128)(2,1)S(1)} %passage_units.1), channel_id=1, source_target_pairs={{0,8},{8,0},{16,24},{24,16},{1,9},{9,1},{17,25},{25,17},{2,10},{10... | collective-permute-start | bytes 3145736 | tf_op jit(solution)/shard_map/ppermute | solution.py:193
  13.3 16.7 %collective-permute-start.1 = (bf16[2,272,128]{2,1,0:T(8,128)(2,1)}, bf16[2,272,128]{2,1,0:T(8,128)(2,1)S(1)}, u32[]{:S(2)}, u32[]{:S(2)}) collective-permute-start(bf16[2,272,128]{2,1,0:T(8,128)(2,1)} %pad_maximum_fusion.4), channel_id=1, source_target_pairs={{0,2},{1,3},{2,0},{3,1},{4,6},{5,7},{6,4},{7,5},{8,10},{9,11},{10,... | collective-permute-start | bytes 417800 | tf_op jit(solution)/shard_map/ppermute | solution.py:193
  29.9 21.4 %collective-permute-start.4 = (bf16[16,256,128]{2,1,0:T(8,128)(2,1)S(1)}, bf16[16,256,128]{2,1,0:T(8,128)(2,1)}, u32[]{:S(2)}, u32[]{:S(2)}) collective-permute-start(bf16[16,256,128]{2,1,0:T(8,128)(2,1)S(1)} %collective-permute-done.3), channel_id=1, source_target_pairs={{0,8},{8,0},{16,24},{24,16},{1,9},{9,1},{17,25},{25,17},{2,10},{10... | collective-permute-start | bytes 3145736 | tf_op jit(solution)/shard_map/ppermute | solution.py:193
  30.7 9.4 %collective-permute-start.2 = (bf16[4,272,128]{2,1,0:T(8,128)(2,1)}, bf16[4,272,128]{2,1,0:T(8,128)(2,1)}, u32[]{:S(2)}, u32[]{:S(2)}) collective-permute-start(bf16[4,272,128]{2,1,0:T(8,128)(2,1)} %pad_maximum_fusion.3), channel_id=1, source_target_pairs={{0,1},{1,0},{2,3},{3,2},{4,5},{5,4},{6,7},{7,6},{8,9},{9,8},{10,11... | collective-permute-start | bytes 835592 | tf_op jit(solution)/shard_map/ppermute | solution.py:193
  50.0 1.3 %copy-start = (f32[4096,128]{1,0:T(8,128)}, f32[4096,128]{1,0:T(8,128)S(1)}, u32[]{:S(2)}) copy-start(f32[4096,128]{1,0:T(8,128)S(1)} %get-tuple-element.11.acc_in) | copy-start | bytes 6291460
  61.5 4.3 %collective-permute-start.7 = (f32[2,32,128]{2,1,0:T(8,128)S(1)}, f32[2,32,128]{2,1,0:T(8,128)S(1)}, u32[]{:S(2)}, u32[]{:S(2)}) collective-permute-start(f32[2,32,128]{2,1,0:T(8,128)S(1)} %slice_bitcast_fusion), channel_id=1, source_target_pairs={{0,1},{1,0},{2,3},{3,2},{4,5},{5,4},{6,7},{7,6},{8,9},{9,8},{10,11... | collective-permute-start | bytes 98312 | tf_op jit(solution)/shard_map/ppermute | solution.py:193
  61.6 18.5 %collective-permute-start.6 = (bf16[2,1024,128]{2,1,0:T(8,128)(2,1)S(1)}, bf16[2,1024,128]{2,1,0:T(8,128)(2,1)S(1)}, u32[]{:S(2)}, u32[]{:S(2)}) collective-permute-start(bf16[2,1024,128]{2,1,0:T(8,128)(2,1)S(1)} %get-tuple-element.14), channel_id=1, source_target_pairs={{0,1},{1,0},{2,3},{3,2},{4,5},{5,4},{6,7},{7,6},{8,9},{9,8},{10,11... | collective-permute-start | bytes 1572872 | tf_op jit(solution)/shard_map/ppermute | solution.py:193
  65.8 3.9 %collective-permute-start.8 = (f32[2,2,2,8,128]{4,3,2,1,0:T(8,128)S(1)}, f32[2,2,2,8,128]{4,3,2,1,0:T(8,128)S(1)}, u32[]{:S(2)}, u32[]{:S(2)}) collective-permute-start(f32[2,2,2,8,128]{4,3,2,1,0:T(8,128)S(1)} %bitcast.24), channel_id=1, source_target_pairs={{0,2},{1,3},{2,0},{3,1},{4,6},{5,7},{6,4},{7,5},{8,10},{9,11},{10,... | collective-permute-start | bytes 98312 | tf_op jit(solution)/shard_map/ppermute | solution.py:193
  69.7 10.4 %collective-permute-start.9 = (f32[2,2,2,8,128]{4,3,2,1,0:T(8,128)S(1)}, f32[2,2,2,8,128]{4,3,2,1,0:T(8,128)S(1)}, u32[]{:S(2)}, u32[]{:S(2)}) collective-permute-start(f32[2,2,2,8,128]{4,3,2,1,0:T(8,128)S(1)} %reverse_add_fusion.1), channel_id=1, source_target_pairs={{0,4},{1,5},{2,6},{3,7},{4,0},{5,1},{6,2},{7,3},{8,12},{9,13},{10,... | collective-permute-start | bytes 98312 | tf_op jit(solution)/shard_map/ppermute | solution.py:193
  80.4 5.0 %collective-permute-start.10 = (bf16[512,128]{1,0:T(8,128)(2,1)S(1)}, bf16[512,128]{1,0:T(8,128)(2,1)S(1)}, u32[]{:S(2)}, u32[]{:S(2)}) collective-permute-start(bf16[512,128]{1,0:T(8,128)(2,1)S(1)} %get-tuple-element.17), channel_id=1, source_target_pairs={{0,2},{1,3},{2,0},{3,1},{4,6},{5,7},{6,4},{7,5},{8,10},{9,11},{10,... | collective-permute-start | bytes 393224 | tf_op jit(solution)/shard_map/ppermute | solution.py:193
  85.4 8.6 %collective-permute-start.11 = (bf16[256,128]{1,0:T(8,128)(2,1)S(1)}, bf16[256,128]{1,0:T(8,128)(2,1)S(1)}, u32[]{:S(2)}, u32[]{:S(2)}) collective-permute-start(bf16[256,128]{1,0:T(8,128)(2,1)S(1)} %slice.48), channel_id=1, source_target_pairs={{0,4},{1,5},{2,6},{3,7},{4,0},{5,1},{6,2},{7,3},{8,12},{9,13},{10,... | collective-permute-start | bytes 196616 | tf_op jit(solution)/shard_map/ppermute | solution.py:193

commit v2 on v1

v2 whole, which is shorter than its diff:
```python
import functools

import jax
import jax.numpy as jnp
from jax import lax
from jax.experimental import pallas as pl
from jax.experimental.pallas import tpu as pltpu
from jax.sharding import PartitionSpec as P

SOFTNESS = 0.02
EPSILON = 1e-06
LANES = 128
TAIL = 16
BASE = 256
UNROLL = 16
CHUNKS = 2
F32 = jnp.float32
BF16 = jnp.bfloat16


def call(body, out_shape, name, flops=0, in_specs=None, aliases={}):
    kwargs = {} if in_specs is None else {"in_specs": in_specs}
    return pl.pallas_call(
        body,
        out_shape=out_shape,
        input_output_aliases=aliases,
        name=name,
        cost_estimate=pl.CostEstimate(flops=flops, bytes_accessed=1 << 20, transcendentals=0),
        compiler_params=pltpu.CompilerParams(vmem_limit_bytes=48 * 1024 * 1024),
        **kwargs,
    )


def unit(values):
    floats = values.astype(F32)
    scale = lax.rsqrt(jnp.sum(floats * floats, axis=-1, keepdims=True) + EPSILON)
    return floats * scale, scale


def pack_body(queries_ref, cand_ref, out_ref):
    count, length, width = queries_ref.shape
    rows = count * length
    out_ref[:rows] = unit(queries_ref[...])[0].astype(BF16).reshape(rows, width)
    ids = jnp.broadcast_to(cand_ref[...], (TAIL, LANES))
    high = ids // BASE
    low = ids - high * BASE
    place = lax.broadcasted_iota(jnp.int32, (TAIL, LANES), 0)
    digits = jnp.where(place == 0, high, jnp.where(place == 1, low, 0))
    out_ref[rows:] = digits.astype(F32).astype(BF16)


def unit_body(passages_ref, out_ref):
    def step(index, carry):
        out_ref[index] = unit(passages_ref[index])[0].astype(BF16)
        return carry

    lax.fori_loop(0, passages_ref.shape[0], step, 0)


def route_body(docs_ref, pay_ref, out_ref, *, rows, pieces):
    blocks = pay_ref.shape[0]
    parts = out_ref.shape[1] - 1
    ids = []
    for block in range(blocks):
        tile = pay_ref[block, rows : rows + TAIL].astype(F32)
        ids.append((tile[0:1] * BASE + tile[1:2]).astype(jnp.int32))
    ids = jnp.concatenate(ids, axis=0)
    pair = lax.broadcasted_iota(jnp.int32, (blocks, LANES), 0) * LANES
    pair = pair + lax.broadcasted_iota(jnp.int32, (blocks, LANES), 1)
    upper = lax.broadcasted_iota(jnp.int32, (LANES, LANES), 0)
    lane = lax.broadcasted_iota(jnp.int32, (LANES, LANES), 1)
    triangle = (upper <= lane).astype(F32)
    diagonal = upper == lane
    place = lax.broadcasted_iota(jnp.int32, (parts * LANES, LANES), 0).astype(F32)
    for piece, (start, size) in enumerate(pieces):
        local = jnp.full((blocks, LANES), -1, jnp.int32)
        for index in range(size):
            local = jnp.where(ids == docs_ref[start + index], index, local)
        mask = local >= 0
        code = (local * (blocks * LANES) + pair).astype(F32)
        ranks = jnp.dot(mask.astype(F32), triangle, preferred_element_type=F32)
        before = jnp.zeros((1, 1), F32)
        found = jnp.zeros((parts * LANES, LANES), F32)
        for block in range(blocks):
            row = ranks[block : block + 1]
            slot = jnp.where(mask[block : block + 1], before + row - 1.0, -1.0)
            found = found + jnp.where(place == slot, code[block : block + 1], 0.0)
            before = before + row[:, LANES - 1 : LANES]
        packed = jnp.sum(found, axis=1, keepdims=True)
        for part in range(parts):
            value = packed[part * LANES : (part + 1) * LANES]
            line = jnp.sum(jnp.where(diagonal, value, 0.0), axis=0, keepdims=True)
            out_ref[piece, part : part + 1] = line.astype(jnp.int32)
        out_ref[piece, parts : parts + 1] = jnp.broadcast_to(before, (1, LANES)).astype(jnp.int32)


def score_pairs(piece, list_ref, pay_ref, pass_ref, acc_ref, sums_ref, length, list_len):
    parts = list_ref.shape[1] - 1
    blocks = pay_ref.shape[0]
    per_block = LANES // list_len
    queries = blocks * per_block
    quarter = queries // 4
    count = list_ref[piece, parts, 0]

    def step(index, carry):
        pairs = []
        for offset in range(UNROLL):
            slot = index * UNROLL + offset
            code = list_ref[piece, slot // LANES, slot % LANES]
            pair = code % (blocks * LANES)
            query = pair // list_len
            weight = jnp.where(slot < count, 1.0, 0.0).astype(F32)
            row = pl.multiple_of((query % per_block) * length, length)
            tokens = pay_ref[query // per_block, pl.ds(row, length)]
            passage = pass_ref[code // (blocks * LANES)]
            pairs.append((query, (pair % list_len) == 0, weight, tokens, passage))
        contract = (((1,), (1,)), ((), ()))
        logits = [
            lax.dot_general(tokens, passage, contract, preferred_element_type=F32)
            for _, _, _, tokens, passage in pairs
        ]
        terms = [jnp.exp(block * (1.0 / SOFTNESS)) for block in logits]
        masses = [jnp.sum(block, axis=1, keepdims=True) for block in terms]
        pulled = [
            jnp.dot(block.astype(BF16), pair[4], preferred_element_type=F32)
            for block, pair in zip(terms, pairs)
        ]
        done = []
        for (query, first, weight, _, _), mass, rows in zip(pairs, masses, pulled):
            score = SOFTNESS * jnp.sum(jnp.log(mass), axis=0, keepdims=True)
            exp_score = jnp.exp(score)
            region = query // quarter
            moved = ((region % 2) * 2 + region // 2) * quarter + query % quarter
            target = jnp.where(first, queries + moved, query)
            factor = jnp.where(first, 1.0, exp_score) * weight
            value = jnp.where(first, score, exp_score) * weight
            entry = jnp.where(first, queries, 0) + query
            done.append((target, (rows / mass) * factor, entry, value))
        for target, product, entry, value in done:
            at = pl.ds(pl.multiple_of(target * length, length), length)
            acc_ref[at] = acc_ref[at] + product
            sums_ref[pl.ds(entry, 1)] = sums_ref[pl.ds(entry, 1)] + value
        return carry

    lax.fori_loop(0, (count + UNROLL - 1) // UNROLL, step, 0)


def first_score_body(list_ref, pay_ref, pass_ref, acc_ref, sums_ref, *, piece, **sizes):
    acc_ref[...] = jnp.zeros_like(acc_ref)
    sums_ref[...] = jnp.zeros_like(sums_ref)
    score_pairs(piece, list_ref, pay_ref, pass_ref, acc_ref, sums_ref, **sizes)


def score_body(list_ref, pay_ref, pass_ref, _, __, acc_ref, sums_ref, *, piece, **sizes):
    score_pairs(piece, list_ref, pay_ref, pass_ref, acc_ref, sums_ref, **sizes)


def last_score_body(
    list_ref, pay_ref, pass_ref, _, __, acc_ref, sums_ref, others_ref, firsts_ref, *, piece, **sizes
):
    score_pairs(piece, list_ref, pay_ref, pass_ref, acc_ref, sums_ref, **sizes)
    half = others_ref.shape[0]
    others_ref[...] = acc_ref[half : 2 * half].astype(BF16)
    firsts_ref[...] = acc_ref[3 * half : 4 * half].astype(BF16)


def halve_body(acc_ref, others_ref, firsts_ref, send_a, send_b, keep_a, keep_b):
    half = others_ref.shape[0]
    quarter = half // 2
    for start, got, send, keep in (
        (0, others_ref, send_a, keep_a),
        (2 * half, firsts_ref, send_b, keep_b),
    ):
        keep[...] = acc_ref[start : start + quarter] + got[:quarter].astype(F32)
        rest = acc_ref[start + quarter : start + half] + got[quarter:].astype(F32)
        send[...] = rest.astype(BF16)


def merge_body(others_ref, got_others, firsts_ref, got_firsts, sums_ref, send_ref, rest_ref, *, length):
    queries = sums_ref.shape[1]

    def part(index):
        at = slice(index * length, (index + 1) * length)
        others = others_ref[at] + got_others[at].astype(F32)
        first = firsts_ref[at] + got_firsts[at].astype(F32)
        return others - sums_ref[0, index : index + 1] * first

    for index in range(queries // 2):
        at = slice(index * length, (index + 1) * length)
        rest_ref[at] = part(index)
        send_ref[at] = part(index + queries // 2).astype(BF16)


def last_body(queries_ref, keep_ref, got_ref, sums_ref, grad_ref, loss_ref, *, length):
    for index in range(queries_ref.shape[0]):
        at = slice(index * length, (index + 1) * length)
        spread = sums_ref[0, index : index + 1]
        score = sums_ref[1, index : index + 1]
        total = spread + jnp.exp(score)
        loss_ref[index : index + 1] = jnp.log(total) - score
        gradient = (keep_ref[at] + got_ref[at].astype(F32)) / total
        query_unit, query_scale = unit(queries_ref[index])
        along = jnp.sum(query_unit * gradient, axis=-1, keepdims=True)
        grad_ref[index] = (gradient - query_unit * along) * query_scale


def swap(value, axis, bit):
    size = lax.axis_size(axis)
    return lax.ppermute(value, axis, [(index, index ^ bit) for index in range(size)])


def bits_of(size):
    return [1 << power for power in reversed(range(size.bit_length() - 1))]


def spread_offsets(size):
    offsets = [0]
    for bit in bits_of(size):
        offsets = offsets + [offset ^ bit for offset in offsets]
    return offsets


def spread(block):
    blocks = [block]
    for bit in bits_of(lax.axis_size("group") // 2):
        blocks = blocks + [swap(held, "group", bit) for held in blocks]
    return blocks


def local(queries, passages, candidates, location):
    group_count = lax.axis_size("group")
    dev_count = lax.axis_size("dev")
    device_total = group_count * dev_count
    query_count, length, width = queries.shape
    pass_count, pass_len, _ = passages.shape
    list_len = candidates.shape[1]
    pair_count = query_count * list_len
    rows = query_count * length
    slot_cap = max(2, (3 * pair_count + device_total - 1) // device_total)
    group = lax.axis_index("group")
    dev = lax.axis_index("dev")
    shape = jax.ShapeDtypeStruct

    half_bit = group_count // 2
    chunk = pass_count // CHUNKS
    far_raw = [
        swap(passages[start : start + chunk], "group", half_bit)
        for start in range(0, pass_count, chunk)
    ]
    payload = call(pack_body, shape((rows + TAIL, width), BF16), "query_units")(
        queries, candidates.reshape(1, pair_count)
    )
    units = call(unit_body, shape(passages.shape, BF16), "passage_units")(passages)
    held = spread(units)
    near_offsets = spread_offsets(half_bit)
    pieces = [(offset, 0, pass_count) for offset in near_offsets]
    pieces += [
        (offset ^ half_bit, start, chunk)
        for start in range(0, pass_count, chunk)
        for offset in near_offsets
    ]
    held_rows = jnp.concatenate(
        [
            ((group ^ offset) * dev_count + dev) * pass_count + start + jnp.arange(size)
            for offset, start, size in pieces
        ]
    )
    hits = location[None, :] == held_rows.astype(jnp.int32)[:, None]
    documents = jnp.arange(location.shape[0], dtype=jnp.int32)
    docs = jnp.sum(jnp.where(hits, documents[None, :], 0), axis=1)

    pay = payload[None]
    for bit in bits_of(dev_count):
        pay = jnp.concatenate([pay, swap(pay, "dev", bit)], axis=0)

    parts = -(-dev_count * min(pair_count, slot_cap) // LANES)
    starts = [sum(piece[2] for piece in pieces[:index]) for index in range(len(pieces))]
    spans = tuple((start, piece[2]) for start, piece in zip(starts, pieces))
    smem, vmem = (pl.BlockSpec(memory_space=space) for space in (pltpu.SMEM, pltpu.VMEM))
    lists = call(
        functools.partial(route_body, rows=rows, pieces=spans),
        shape((len(pieces), parts + 1, LANES), jnp.int32),
        "route",
        in_specs=[smem, vmem],
    )(docs, pay)

    all_queries = dev_count * query_count
    half_rows = all_queries * length // 2
    totals = [shape((4 * half_rows, width), F32), shape((2 * all_queries, LANES), F32)]
    sends = [shape((half_rows, width), BF16)] * 2
    state = None
    piece = 0

    def score(block, last=False):
        body = first_score_body if state is None else last_score_body if last else score_body
        return call(
            functools.partial(body, piece=piece, length=length, list_len=list_len),
            totals + (sends if last else []),
            "score",
            all_queries * list_len // len(pieces) * length * pass_len * width * 4,
            [smem, vmem, vmem] + ([] if state is None else [vmem, vmem]),
            aliases={} if state is None else {3: 0, 4: 1},
        )(lists, pay, block, *(state or ()))

    for block in held:
        state = score(block)
        piece += 1
    for index, raw in enumerate(far_raw):
        raw, *state = lax.optimization_barrier((raw, *state))
        block_units = call(unit_body, shape(raw.shape, BF16), "passage_units")(raw)
        for block in spread(block_units):
            state = score(block, piece == len(pieces) - 1)[: 4 if piece == len(pieces) - 1 else 2]
            piece += 1
    acc, sums, others, firsts = state

    steps = bits_of(dev_count)[::-1]
    got_others = swap(others, "dev", steps[0])
    got_firsts = swap(firsts, "dev", steps[1])
    sums = sums.reshape((2, 2, all_queries // 2, LANES))
    sums = sums[:, 0] + swap(sums[:, 1], "dev", steps[0])
    sums = sums.reshape((2, 2, all_queries // 4, LANES))
    sums = sums[:, 0] + swap(sums[:, 1], "dev", steps[1])
    levels = len(steps) - 2
    sums = sums.reshape((2,) + (2,) * levels + (query_count, LANES))
    for level, bit in enumerate(steps[2:]):
        sums = sums + jnp.flip(swap(sums, "dev", bit), axis=1 + level)
    sums = sums.reshape(2, all_queries // 4, LANES)
    quarter = half_rows // 2
    send_others, send_firsts, others, firsts = call(
        halve_body, [shape((quarter, width), BF16)] * 2 + [shape((quarter, width), F32)] * 2, "halve"
    )(acc, got_others, got_firsts)
    got_others = swap(send_others, "dev", steps[1])
    got_firsts = swap(send_firsts, "dev", steps[0])
    quarter = quarter // 2
    send, rest = call(
        functools.partial(merge_body, length=length),
        [shape((quarter, width), BF16), shape((quarter, width), F32)],
        "merge",
    )(others, got_others, firsts, got_firsts, sums)
    for bit in steps[2:-1]:
        rest = rest + swap(send, "dev", bit).astype(F32)
        quarter = quarter // 2
        rest, send = rest[:quarter], rest[quarter:].astype(BF16)
    got = swap(send, "dev", steps[-1])
    grad, loss = call(
        functools.partial(last_body, length=length),
        [shape(queries.shape, F32), shape((query_count, LANES), F32)],
        "last",
    )(queries, rest, got, sums[:, :query_count])
    return loss[:, 0], grad


def solution(mesh):
    placed = (
        P(("group", "dev"), None, None),
        P(("group", "dev"), None, None),
        P(("group", "dev"), None),
        P(),
    )
    return jax.shard_map(
        local,
        mesh=mesh,
        in_specs=placed,
        out_specs=(P(("group", "dev")), P(("group", "dev"), None, None)),
        check_vma=False,
    )
```

time: 95.7 us -> 80 us (0.84)
  waiting for transfers between devices: 39.7 us -> 29.6 us
  Pallas kernels: 20.5 us -> 17.6 us
  starting transfers between devices: 26.8 us -> 24.9 us
  other arithmetic: 4.29 us -> 2.64 us
  local copies, waits for them, and re-layouts: 3.37 us -> 4.47 us
    ppermute x12 -> x16, waiting for transfers between devices: 39.7 us -> 29.6 us  [swap(): lax.ppermute(value, axis, [(index, index ^ bit) for index in range(size)])]
    pallas_call x3 -> x10, Pallas kernels: 17.4 us -> 14.7 us  [the longest x6 11.5 us: score(): call(functools.partial(body, piece=piece, length=length, list_len=list_le...]
    ppermute x12 -> x16, starting transfers between devices: 26.8 us -> 24.9 us  [swap(): lax.ppermute(value, axis, [(index, index ^ bit) for index in range(size)])]
    concatenate x2 -> x0, other arithmetic: 1.59 us -> none  [the longest x1 1.41 us: local(): jnp.concatenate([held[index] for index in order[near_blocks:]], axis=0)]
    unnamed x10 -> x8, local copies, waits for them, and re-layouts: 2.56 us -> 2.08 us
  transfers between devices with their start and end apart: 12 -> 16, of which waited for: 8 -> 10; matrix products, arithmetic and copies ran while one was open for 3% -> 5% of each run, Pallas kernels for 9% -> 16%
where the time goes in v2:
time: 80 us; the launch traced here: 80.1 us
  waiting for transfers between devices  29.6 us (37%)
  starting transfers between devices  24.9 us (31%)
  Pallas kernels  17.6 us (22%)
  local copies, waits for them, and re-layouts  4.47 us (6%)
  other arithmetic  2.64 us (3%)
  between operations  0.81 us (1%)
    ppermute x16, waiting for transfers between devices, swap(): lax.ppermute(value, axis, [(index, index ^ bit) for index in range(size)])  29.6 us
    ppermute x16, starting transfers between devices, swap(): lax.ppermute(value, axis, [(index, index ^ bit) for index in range(size)])  24.9 us
    pallas_call x6, Pallas kernels, score(): call(functools.partial(body, piece=piece, length=length, list_len=list_le...  11.5 us
    concatenate x3, other arithmetic, local(): pay = jnp.concatenate([pay, swap(pay, 'dev', bit)], axis=0)  2.44 us
    unnamed x8, local copies, waits for them, and re-layouts  2.08 us
    pallas_call x1, Pallas kernels, local(): call(unit_body, shape(passages.shape, BF16), 'passage_units')(passages)  1.9 us
    pallas_call x2, Pallas kernels, local(): block_units = call(unit_body, shape(raw.shape, BF16), 'passage_units')(raw)  1.9 us
  transfers between devices with their start and end apart: 16, of which 10 were waited for; matrix products, arithmetic and copies ran while one was open for 5% of the time, Pallas kernels for 16%

profile of v2, /device:TPU:0, one launch (start us, length us, event | category | flops | bytes accessed | tf_op | source)
XLA Modules:
  0.0 80.1 jit_solution(4386499708289741523)
XLA Ops:
  0.6 0.8 reshape.21.cand_ref
  1.4 0.0 copy-start.1
  1.4 0.8 %copy-done.1 = bf16[8,32,128]{2,1,0:T(8,128)(2,1)S(1)} copy-done((bf16[8,32,128]{2,1,0:T(8,128)(2,1)S(1)}, bf16[8,32,128]{2,1,0:T(8,128)(2,1)}, u32[]{:S(2)}) %copy-start.1) | copy-done | bytes 65560
  2.2 0.1 query_units.1
  2.4 4.1 %collective-permute-start = (bf16[1,272,128]{2,1,0:T(8,128)(2,1)S(1)}, bf16[1,272,128]{2,1,0:T(8,128)(2,1)S(1)}, u32[]{:S(2)}, u32[]{:S(2)}) collective-permute-start(bf16[1,272,128]{2,1,0:T(8,128)(2,1)S(1)} %bitcast.33), channel_id=1, source_target_pairs={{0,4},{1,5},{2,6},{3,7},{4,0},{5,1},{6,2},{7,3},{8,12},{9,13},{10,... | collective-permute-start | bytes 208904 | tf_op jit(solution)/shard_map/ppermute | solution.py:209
  6.5 0.0 copy-start
  6.5 1.2 %copy-done = bf16[16,256,128]{2,1,0:T(8,128)(2,1)S(1)} copy-done((bf16[16,256,128]{2,1,0:T(8,128)(2,1)S(1)}, bf16[16,256,128]{2,1,0:T(8,128)(2,1)}, u32[]{:S(2)}) %copy-start) | copy-done | bytes 1048600
  7.7 0.0 copy-start.3
  7.7 1.9 %passage_units.3.pass_ref = bf16[16,256,128]{2,1,0:T(8,128)(2,1)S(1)} custom-call(bf16[16,256,128]{2,1,0:T(8,128)(2,1)S(1)} %copy-done), custom_call_target="tpu_custom_call" | custom-call | bytes 1048576 | tf_op jit(solution)/shard_map/passage_units/pallas_call | solution.py:253
  9.6 0.1 collective-permute-start.5
  9.7 0.6 collective-permute-done
  10.2 0.7 pad_maximum_fusion.2
  10.9 1.0 %collective-permute-start.1 = (bf16[2,272,128]{2,1,0:T(8,128)(2,1)}, bf16[2,272,128]{2,1,0:T(8,128)(2,1)S(1)}, u32[]{:S(2)}, u32[]{:S(2)}) collective-permute-start(bf16[2,272,128]{2,1,0:T(8,128)(2,1)} %pad_maximum_fusion.2), channel_id=1, source_target_pairs={{0,2},{1,3},{2,0},{3,1},{4,6},{5,7},{6,4},{7,5},{8,10},{9,11},{10,... | collective-permute-start | bytes 417800 | tf_op jit(solution)/shard_map/ppermute | solution.py:209
  11.9 0.9 %fusion.3 = (bf16[8,256,128]{2,1,0:T(8,128)(2,1)}, bf16[8,256,128]{2,1,0:T(8,128)(2,1)S(1)}) fusion(bf16[16,256,128]{2,1,0:T(8,128)(2,1)S(1)} %copy-done), kind=kLoop, calls=%fused_computation.19 | loop fusion | bytes 2097152 | tf_op jit(solution)/shard_map/slice | solution.py:247
  12.8 1.5 %collective-permute-start.4 = (bf16[8,256,128]{2,1,0:T(8,128)(2,1)}, bf16[8,256,128]{2,1,0:T(8,128)(2,1)S(1)}, u32[]{:S(2)}, u32[]{:S(2)}) collective-permute-start(bf16[8,256,128]{2,1,0:T(8,128)(2,1)} %get-tuple-element.58), channel_id=1, source_target_pairs={{0,16},{8,24},{16,0},{24,8},{1,17},{9,25},{17,1},{25,9},{2,18},{10... | collective-permute-start | bytes 1572872 | tf_op jit(solution)/shard_map/ppermute | solution.py:209
  14.3 2.3 %collective-permute-done.1 = bf16[2,272,128]{2,1,0:T(8,128)(2,1)S(1)} collective-permute-done((bf16[2,272,128]{2,1,0:T(8,128)(2,1)}, bf16[2,272,128]{2,1,0:T(8,128)(2,1)S(1)}, u32[]{:S(2)}, u32[]{:S(2)}) %collective-permute-start.1) | collective-permute-done | bytes 139296 | tf_op jit(solution)/shard_map/ppermute | solution.py:209
  16.6 0.7 pad_maximum_fusion.1
  17.4 1.5 %collective-permute-start.2 = (bf16[4,272,128]{2,1,0:T(8,128)(2,1)}, bf16[4,272,128]{2,1,0:T(8,128)(2,1)}, u32[]{:S(2)}, u32[]{:S(2)}) collective-permute-start(bf16[4,272,128]{2,1,0:T(8,128)(2,1)} %pad_maximum_fusion.1), channel_id=1, source_target_pairs={{0,1},{1,0},{2,3},{3,2},{4,5},{5,4},{6,7},{7,6},{8,9},{9,8},{10,11... | collective-permute-start | bytes 835592 | tf_op jit(solution)/shard_map/ppermute | solution.py:209
  18.9 0.1 concatenate.14
  19.0 0.0 copy-done.3
  19.0 0.2 select_reduce_fusion.docs_ref
  19.2 6.2 %collective-permute-done.2 = bf16[4,272,128]{2,1,0:T(8,128)(2,1)} collective-permute-done((bf16[4,272,128]{2,1,0:T(8,128)(2,1)}, bf16[4,272,128]{2,1,0:T(8,128)(2,1)}, u32[]{:S(2)}, u32[]{:S(2)}) %collective-permute-start.2) | collective-permute-done | bytes 278560 | tf_op jit(solution)/shard_map/ppermute | solution.py:209
  25.3 1.0 %pad_maximum_fusion.pay_ref = bf16[8,272,128]{2,1,0:T(8,128)(2,1)S(1)} fusion(bf16[4,272,128]{2,1,0:T(8,128)(2,1)} %collective-permute-done.2, bf16[2,272,128]{2,1,0:T(8,128)(2,1)S(1)} %collective-permute-done.1, bf16[1,272,128]{2,1,0:T(8,128)(2,1)S(1)} %collective-permute-done, bf16[1,272,128]{2,1,0:T(8,128)(2,1)S(1)} %bitcast.36), kind=kLoop, calls=%fused_computation | loop fusion | flops 835584 | bytes 1114112 | tf_op jit(solution)/shard_map/concatenate | solution.py:274
  26.4 1.2 %route.1.list_ref = s32[6,2,128]{2,1,0:T(2,128)S(1)} custom-call(s32[64]{0:T(128)S(1)} %select_reduce_fusion.docs_ref, bf16[8,272,128]{2,1,0:T(8,128)(2,1)S(1)} %pad_maximum_fusion.pay_ref), custom_call_target="tpu_custom_call" | custom-call | bytes 1048576 | tf_op jit(solution)/shard_map/route/pallas_call | solution.py:280
  27.5 2.3 %score.6 = (f32[4096,128]{1,0:T(8,128)S(1)}, f32[128,128]{1,0:T(8,128)S(1)}) custom-call(s32[6,2,128]{2,1,0:T(2,128)S(1)} %route.1.list_ref, bf16[8,272,128]{2,1,0:T(8,128)(2,1)S(1)} %pad_maximum_fusion.pay_ref, bf16[16,256,128]{2,1,0:T(8,128)(2,1)S(1)} %passage_units.3.pass_ref), custom_call_target="tpu_custom_call" | custom-call | flops 713031680 | bytes 1048576 | tf_op jit(solution)/shard_map/score/pallas_call | solution.py:296
  29.8 0.0 collective-permute-done.5.pass_ref
  29.8 2.1 %score.7 = (f32[4096,128]{1,0:T(8,128)S(1)}, f32[128,128]{1,0:T(8,128)S(1)}) custom-call(s32[6,2,128]{2,1,0:T(2,128)S(1)} %route.1.list_ref, bf16[8,272,128]{2,1,0:T(8,128)(2,1)S(1)} %pad_maximum_fusion.pay_ref, bf16[16,256,128]{2,1,0:T(8,128)(2,1)S(1)} %collective-permute-done.5.pass_ref, ...), custom_call_target="tpu_custom_call", output_to_operand_aliasing={{0}: (3, {}), {1}: (4, {})} | custom-call | flops 713031680 | bytes 1048576 | tf_op jit(solution)/shard_map/score/pallas_call | solution.py:296
  31.9 0.0 collective-permute-done.4.passages_ref
  32.0 0.9 %passage_units.4.pass_ref = bf16[8,256,128]{2,1,0:T(8,128)(2,1)S(1)} custom-call(bf16[8,256,128]{2,1,0:T(8,128)(2,1)S(1)} %collective-permute-done.4.passages_ref), custom_call_target="tpu_custom_call" | custom-call | bytes 1048576 | tf_op jit(solution)/shard_map/passage_units/pallas_call | solution.py:310
  32.9 0.1 collective-permute-start.6
  33.0 2.1 %collective-permute-start.3 = (bf16[8,256,128]{2,1,0:T(8,128)(2,1)S(1)}, bf16[8,256,128]{2,1,0:T(8,128)(2,1)S(1)}, u32[]{:S(2)}, u32[]{:S(2)}) collective-permute-start(bf16[8,256,128]{2,1,0:T(8,128)(2,1)S(1)} %get-tuple-element.59), channel_id=1, source_target_pairs={{0,16},{8,24},{16,0},{24,8},{1,17},{9,25},{17,1},{25,9},{2,18},{10... | collective-permute-start | bytes 1572872 | tf_op jit(solution)/shard_map/ppermute | solution.py:209
  35.1 1.4 %score.8 = (f32[4096,128]{1,0:T(8,128)S(1)}, f32[128,128]{1,0:T(8,128)S(1)}) custom-call(s32[6,2,128]{2,1,0:T(2,128)S(1)} %route.1.list_ref, bf16[8,272,128]{2,1,0:T(8,128)(2,1)S(1)} %pad_maximum_fusion.pay_ref, bf16[8,256,128]{2,1,0:T(8,128)(2,1)S(1)} %passage_units.4.pass_ref, ...), custom_call_target="tpu_custom_call", output_to_operand_aliasing={{0}: (3, {}), {1}: (4, {})} | custom-call | flops 713031680 | bytes 1048576 | tf_op jit(solution)/shard_map/score/pallas_call | solution.py:296
  36.5 0.0 collective-permute-done.6.pass_ref
  36.5 2.2 %score.9 = (f32[4096,128]{1,0:T(8,128)S(1)}, f32[128,128]{1,0:T(8,128)S(1)}) custom-call(s32[6,2,128]{2,1,0:T(2,128)S(1)} %route.1.list_ref, bf16[8,272,128]{2,1,0:T(8,128)(2,1)S(1)} %pad_maximum_fusion.pay_ref, bf16[8,256,128]{2,1,0:T(8,128)(2,1)S(1)} %collective-permute-done.6.pass_ref, ...), custom_call_target="tpu_custom_call", output_to_operand_aliasing={{0}: (3, {}), {1}: (4, {})} | custom-call | flops 713031680 | bytes 1048576 | tf_op jit(solution)/shard_map/score/pallas_call | solution.py:296
  38.7 9.0 %collective-permute-done.3.passages_ref = bf16[8,256,128]{2,1,0:T(8,128)(2,1)S(1)} collective-permute-done((bf16[8,256,128]{2,1,0:T(8,128)(2,1)S(1)}, bf16[8,256,128]{2,1,0:T(8,128)(2,1)S(1)}, u32[]{:S(2)}, u32[]{:S(2)}) %collective-permute-start.3) | collective-permute-done | bytes 524320 | tf_op jit(solution)/shard_map/ppermute | solution.py:209
  47.7 0.9 %passage_units.5.pass_ref = bf16[8,256,128]{2,1,0:T(8,128)(2,1)S(1)} custom-call(bf16[8,256,128]{2,1,0:T(8,128)(2,1)S(1)} %collective-permute-done.3.passages_ref), custom_call_target="tpu_custom_call" | custom-call | bytes 1048576 | tf_op jit(solution)/shard_map/passage_units/pallas_call | solution.py:310
  48.6 0.1 collective-permute-start.7
  48.7 1.4 %score.10 = (f32[4096,128]{1,0:T(8,128)S(1)}, f32[128,128]{1,0:T(8,128)S(1)}) custom-call(s32[6,2,128]{2,1,0:T(2,128)S(1)} %route.1.list_ref, bf16[8,272,128]{2,1,0:T(8,128)(2,1)S(1)} %pad_maximum_fusion.pay_ref, bf16[8,256,128]{2,1,0:T(8,128)(2,1)S(1)} %passage_units.5.pass_ref, ...), custom_call_target="tpu_custom_call", output_to_operand_aliasing={{0}: (3, {}), {1}: (4, {})} | custom-call | flops 713031680 | bytes 1048576 | tf_op jit(solution)/shard_map/score/pallas_call | solution.py:296
  50.1 0.5 collective-permute-done.7.pass_ref
  50.6 2.2 %score.11 = (f32[4096,128]{1,0:T(8,128)S(1)}, f32[128,128]{1,0:T(8,128)S(1)}, bf16[1024,128]{1,0:T(8,128)(2,1)S(1)}, bf16[1024,128]{1,0:T(8,128)(2,1)S(1)}) custom-call(s32[6,2,128]{2,1,0:T(2,128)S(1)} %route.1.list_ref, bf16[8,272,128]{2,1,0:T(8,128)(2,1)S(1)} %pad_maximum_fusion.pay_ref, ...), custom_call_target="tpu_custom_call", output_to_operand_aliasing={{0}: (3, {}), {1}: (4, {})} | custom-call | flops 713031680 | bytes 1048576 | tf_op jit(solution)/shard_map/score/pallas_call | solution.py:296
  52.8 0.0 copy-start.2
  52.8 1.1 %collective-permute-start.12 = (f32[2,32,128]{2,1,0:T(8,128)S(1)}, f32[2,32,128]{2,1,0:T(8,128)S(1)}, u32[]{:S(2)}, u32[]{:S(2)}) collective-permute-start(f32[2,32,128]{2,1,0:T(8,128)S(1)} %slice_bitcast_fusion), channel_id=1, source_target_pairs={{0,1},{1,0},{2,3},{3,2},{4,5},{5,4},{6,7},{7,6},{8,9},{9,8},{10,11... | collective-permute-start | bytes 98312 | tf_op jit(solution)/shard_map/ppermute | solution.py:209
  53.9 1.0 %collective-permute-start.8 = (bf16[1024,128]{1,0:T(8,128)(2,1)S(1)}, bf16[1024,128]{1,0:T(8,128)(2,1)S(1)}, u32[]{:S(2)}, u32[]{:S(2)}) collective-permute-start(bf16[1024,128]{1,0:T(8,128)(2,1)S(1)} %get-tuple-element.47), channel_id=1, source_target_pairs={{0,1},{1,0},{2,3},{3,2},{4,5},{5,4},{6,7},{7,6},{8,9},{9,8},{10,11... | collective-permute-start | bytes 786440 | tf_op jit(solution)/shard_map/ppermute | solution.py:209
  54.9 3.7 %collective-permute-start.9 = (bf16[1024,128]{1,0:T(8,128)(2,1)S(1)}, bf16[1024,128]{1,0:T(8,128)(2,1)S(1)}, u32[]{:S(2)}, u32[]{:S(2)}) collective-permute-start(bf16[1024,128]{1,0:T(8,128)(2,1)S(1)} %get-tuple-element.48), channel_id=1, source_target_pairs={{0,2},{1,3},{2,0},{3,1},{4,6},{5,7},{6,4},{7,5},{8,10},{9,11},{10,... | collective-permute-start | bytes 786440 | tf_op jit(solution)/shard_map/ppermute | solution.py:209
  58.6 0.0 collective-permute-done.12
  58.6 2.1 %collective-permute-start.13 = (f32[2,16,128]{2,1,0:T(8,128)S(1)}, f32[2,16,128]{2,1,0:T(8,128)S(1)}, u32[]{:S(2)}, u32[]{:S(2)}) collective-permute-start(f32[2,16,128]{2,1,0:T(8,128)S(1)} %slice_bitcast_fusion.2), channel_id=1, source_target_pairs={{0,2},{1,3},{2,0},{3,1},{4,6},{5,7},{6,4},{7,5},{8,10},{9,11},{10,... | collective-permute-start | bytes 49160 | tf_op jit(solution)/shard_map/ppermute | solution.py:209
  60.8 5.1 %collective-permute-done.13 = f32[2,16,128]{2,1,0:T(8,128)S(1)} collective-permute-done((f32[2,16,128]{2,1,0:T(8,128)S(1)}, f32[2,16,128]{2,1,0:T(8,128)S(1)}, u32[]{:S(2)}, u32[]{:S(2)}) %collective-permute-start.13) | collective-permute-done | bytes 16416 | tf_op jit(solution)/shard_map/ppermute | solution.py:209
  65.9 0.0 collective-permute-start.14
  65.9 0.0 collective-permute-done.8.others_ref
  65.9 0.0 collective-permute-done.9.firsts_ref
  65.9 0.1 halve.1
  66.1 1.8 %collective-permute-start.10 = (bf16[512,128]{1,0:T(8,128)(2,1)S(1)}, bf16[512,128]{1,0:T(8,128)(2,1)S(1)}, u32[]{:S(2)}, u32[]{:S(2)}) collective-permute-start(bf16[512,128]{1,0:T(8,128)(2,1)S(1)} %get-tuple-element.50), channel_id=1, source_target_pairs={{0,2},{1,3},{2,0},{3,1},{4,6},{5,7},{6,4},{7,5},{8,10},{9,11},{10,... | collective-permute-start | bytes 393224 | tf_op jit(solution)/shard_map/ppermute | solution.py:209
  67.9 1.7 %collective-permute-start.11 = (bf16[512,128]{1,0:T(8,128)(2,1)S(1)}, bf16[512,128]{1,0:T(8,128)(2,1)S(1)}, u32[]{:S(2)}, u32[]{:S(2)}) collective-permute-start(bf16[512,128]{1,0:T(8,128)(2,1)S(1)} %get-tuple-element.52), channel_id=1, source_target_pairs={{0,1},{1,0},{2,3},{3,2},{4,5},{5,4},{6,7},{7,6},{8,9},{9,8},{10,11... | collective-permute-start | bytes 393224 | tf_op jit(solution)/shard_map/ppermute | solution.py:209
  69.5 1.2 %collective-permute-done.14 = f32[2,2,8,128]{3,2,1,0:T(8,128)S(1)} collective-permute-done((f32[2,2,8,128]{3,2,1,0:T(8,128)S(1)}, f32[2,2,8,128]{3,2,1,0:T(8,128)S(1)}, u32[]{:S(2)}, u32[]{:S(2)}) %collective-permute-start.14) | collective-permute-done | bytes 16416 | tf_op jit(solution)/shard_map/ppermute | solution.py:209
  70.8 1.0 %collective-permute-done.10.got_others = bf16[512,128]{1,0:T(8,128)(2,1)S(1)} collective-permute-done((bf16[512,128]{1,0:T(8,128)(2,1)S(1)}, bf16[512,128]{1,0:T(8,128)(2,1)S(1)}, u32[]{:S(2)}, u32[]{:S(2)}) %collective-permute-start.10) | collective-permute-done | bytes 131104 | tf_op jit(solution)/shard_map/ppermute | solution.py:209
  71.8 1.1 %collective-permute-done.11.got_firsts = bf16[512,128]{1,0:T(8,128)(2,1)S(1)} collective-permute-done((bf16[512,128]{1,0:T(8,128)(2,1)S(1)}, bf16[512,128]{1,0:T(8,128)(2,1)S(1)}, u32[]{:S(2)}, u32[]{:S(2)}) %collective-permute-start.11) | collective-permute-done | bytes 131104 | tf_op jit(solution)/shard_map/ppermute | solution.py:209
  72.8 0.1 merge.1
  72.9 3.0 %collective-permute-start.15 = (bf16[256,128]{1,0:T(8,128)(2,1)S(1)}, bf16[256,128]{1,0:T(8,128)(2,1)S(1)}, u32[]{:S(2)}, u32[]{:S(2)}) collective-permute-start(bf16[256,128]{1,0:T(8,128)(2,1)S(1)} %get-tuple-element.55), channel_id=1, source_target_pairs={{0,4},{1,5},{2,6},{3,7},{4,0},{5,1},{6,2},{7,3},{8,12},{9,13},{10,... | collective-permute-start | bytes 196616 | tf_op jit(solution)/shard_map/ppermute | solution.py:209
  75.9 2.7 %collective-permute-done.15.got_ref = bf16[256,128]{1,0:T(8,128)(2,1)S(1)} collective-permute-done((bf16[256,128]{1,0:T(8,128)(2,1)S(1)}, bf16[256,128]{1,0:T(8,128)(2,1)S(1)}, u32[]{:S(2)}, u32[]{:S(2)}) %collective-permute-start.15) | collective-permute-done | bytes 65568 | tf_op jit(solution)/shard_map/ppermute | solution.py:209
  78.6 0.0 copy-done.2
  78.6 0.9 %last.1 = (f32[8,32,128]{2,1,0:T(8,128)}, f32[8,128]{1,0:T(8,128)S(1)}) custom-call(bf16[8,32,128]{2,1,0:T(8,128)(2,1)S(1)} %copy-done.2, f32[256,128]{1,0:T(8,128)S(1)} %get-tuple-element.54.keep_ref, bf16[256,128]{1,0:T(8,128)(2,1)S(1)} %collective-permute-done.15.got_ref, f32[2,8,128]{2,1,0:T(8,128)S(1)} %slice.36.sums_ref), custom_call_target="tpu_custom_call" | custom-call | bytes 1048576 | tf_op jit(solution)/shard_map/last/pallas_call | solution.py:345
  79.5 0.6 slice_reduce_fusion
  (9 shorter events, 0.0 us)
Async XLA Ops:
  1.4 0.8 %copy-start.1 = (bf16[8,32,128]{2,1,0:T(8,128)(2,1)S(1)}, bf16[8,32,128]{2,1,0:T(8,128)(2,1)}, u32[]{:S(2)}) copy-start(bf16[8,32,128]{2,1,0:T(8,128)(2,1)} %queries_ref.3) | copy-start | bytes 196612
  2.4 7.9 %collective-permute-start = (bf16[1,272,128]{2,1,0:T(8,128)(2,1)S(1)}, bf16[1,272,128]{2,1,0:T(8,128)(2,1)S(1)}, u32[]{:S(2)}, u32[]{:S(2)}) collective-permute-start(bf16[1,272,128]{2,1,0:T(8,128)(2,1)S(1)} %bitcast.33), channel_id=1, source_target_pairs={{0,4},{1,5},{2,6},{3,7},{4,0},{5,1},{6,2},{7,3},{8,12},{9,13},{10,... | collective-permute-start | bytes 208904 | tf_op jit(solution)/shard_map/ppermute | solution.py:209
  6.5 1.2 %copy-start = (bf16[16,256,128]{2,1,0:T(8,128)(2,1)S(1)}, bf16[16,256,128]{2,1,0:T(8,128)(2,1)}, u32[]{:S(2)}) copy-start(bf16[16,256,128]{2,1,0:T(8,128)(2,1)} %passages_ref.1) | copy-start | bytes 3145732
  7.7 11.3 %copy-start.3 = (s32[512]{0:T(512)S(1)}, s32[512]{0:T(512)}, u32[]{:S(2)}) copy-start(s32[512]{0:T(512)} %param.7) | copy-start | bytes 6148
  9.6 20.2 %collective-permute-start.5 = (bf16[16,256,128]{2,1,0:T(8,128)(2,1)S(1)}, bf16[16,256,128]{2,1,0:T(8,128)(2,1)S(1)}, u32[]{:S(2)}, u32[]{:S(2)}) collective-permute-start(bf16[16,256,128]{2,1,0:T(8,128)(2,1)S(1)} %passage_units.3.pass_ref), channel_id=1, source_target_pairs={{0,8},{8,0},{16,24},{24,16},{1,9},{9,1},{17,25},{25,17},{2,10},{10... | collective-permute-start | bytes 3145736 | tf_op jit(solution)/shard_map/ppermute | solution.py:209
  10.9 5.7 %collective-permute-start.1 = (bf16[2,272,128]{2,1,0:T(8,128)(2,1)}, bf16[2,272,128]{2,1,0:T(8,128)(2,1)S(1)}, u32[]{:S(2)}, u32[]{:S(2)}) collective-permute-start(bf16[2,272,128]{2,1,0:T(8,128)(2,1)} %pad_maximum_fusion.2), channel_id=1, source_target_pairs={{0,2},{1,3},{2,0},{3,1},{4,6},{5,7},{6,4},{7,5},{8,10},{9,11},{10,... | collective-permute-start | bytes 417800 | tf_op jit(solution)/shard_map/ppermute | solution.py:209
  12.8 19.1 %collective-permute-start.4 = (bf16[8,256,128]{2,1,0:T(8,128)(2,1)}, bf16[8,256,128]{2,1,0:T(8,128)(2,1)S(1)}, u32[]{:S(2)}, u32[]{:S(2)}) collective-permute-start(bf16[8,256,128]{2,1,0:T(8,128)(2,1)} %get-tuple-element.58), channel_id=1, source_target_pairs={{0,16},{8,24},{16,0},{24,8},{1,17},{9,25},{17,1},{25,9},{2,18},{10... | collective-permute-start | bytes 1572872 | tf_op jit(solution)/shard_map/ppermute | solution.py:209
  17.4 7.9 %collective-permute-start.2 = (bf16[4,272,128]{2,1,0:T(8,128)(2,1)}, bf16[4,272,128]{2,1,0:T(8,128)(2,1)}, u32[]{:S(2)}, u32[]{:S(2)}) collective-permute-start(bf16[4,272,128]{2,1,0:T(8,128)(2,1)} %pad_maximum_fusion.1), channel_id=1, source_target_pairs={{0,1},{1,0},{2,3},{3,2},{4,5},{5,4},{6,7},{7,6},{8,9},{9,8},{10,11... | collective-permute-start | bytes 835592 | tf_op jit(solution)/shard_map/ppermute | solution.py:209
  32.9 3.6 %collective-permute-start.6 = (bf16[8,256,128]{2,1,0:T(8,128)(2,1)S(1)}, bf16[8,256,128]{2,1,0:T(8,128)(2,1)S(1)}, u32[]{:S(2)}, u32[]{:S(2)}) collective-permute-start(bf16[8,256,128]{2,1,0:T(8,128)(2,1)S(1)} %passage_units.4.pass_ref), channel_id=1, source_target_pairs={{0,8},{8,0},{16,24},{24,16},{1,9},{9,1},{17,25},{25,17},{2,10},{10... | collective-permute-start | bytes 1572872 | tf_op jit(solution)/shard_map/ppermute | solution.py:209
  33.0 14.7 %collective-permute-start.3 = (bf16[8,256,128]{2,1,0:T(8,128)(2,1)S(1)}, bf16[8,256,128]{2,1,0:T(8,128)(2,1)S(1)}, u32[]{:S(2)}, u32[]{:S(2)}) collective-permute-start(bf16[8,256,128]{2,1,0:T(8,128)(2,1)S(1)} %get-tuple-element.59), channel_id=1, source_target_pairs={{0,16},{8,24},{16,0},{24,8},{1,17},{9,25},{17,1},{25,9},{2,18},{10... | collective-permute-start | bytes 1572872 | tf_op jit(solution)/shard_map/ppermute | solution.py:209
  48.6 2.0 %collective-permute-start.7 = (bf16[8,256,128]{2,1,0:T(8,128)(2,1)S(1)}, bf16[8,256,128]{2,1,0:T(8,128)(2,1)S(1)}, u32[]{:S(2)}, u32[]{:S(2)}) collective-permute-start(bf16[8,256,128]{2,1,0:T(8,128)(2,1)S(1)} %passage_units.5.pass_ref), channel_id=1, source_target_pairs={{0,8},{8,0},{16,24},{24,16},{1,9},{9,1},{17,25},{25,17},{2,10},{10... | collective-permute-start | bytes 1572872 | tf_op jit(solution)/shard_map/ppermute | solution.py:209
  52.8 25.8 %copy-start.2 = (bf16[8,32,128]{2,1,0:T(8,128)(2,1)S(1)}, bf16[8,32,128]{2,1,0:T(8,128)(2,1)}, u32[]{:S(2)}) copy-start(bf16[8,32,128]{2,1,0:T(8,128)(2,1)} %queries_ref.3) | copy-start | bytes 196612
  52.8 5.8 %collective-permute-start.12 = (f32[2,32,128]{2,1,0:T(8,128)S(1)}, f32[2,32,128]{2,1,0:T(8,128)S(1)}, u32[]{:S(2)}, u32[]{:S(2)}) collective-permute-start(f32[2,32,128]{2,1,0:T(8,128)S(1)} %slice_bitcast_fusion), channel_id=1, source_target_pairs={{0,1},{1,0},{2,3},{3,2},{4,5},{5,4},{6,7},{7,6},{8,9},{9,8},{10,11... | collective-permute-start | bytes 98312 | tf_op jit(solution)/shard_map/ppermute | solution.py:209
  53.9 12.0 %collective-permute-start.8 = (bf16[1024,128]{1,0:T(8,128)(2,1)S(1)}, bf16[1024,128]{1,0:T(8,128)(2,1)S(1)}, u32[]{:S(2)}, u32[]{:S(2)}) collective-permute-start(bf16[1024,128]{1,0:T(8,128)(2,1)S(1)} %get-tuple-element.47), channel_id=1, source_target_pairs={{0,1},{1,0},{2,3},{3,2},{4,5},{5,4},{6,7},{7,6},{8,9},{9,8},{10,11... | collective-permute-start | bytes 786440 | tf_op jit(solution)/shard_map/ppermute | solution.py:209
  54.9 11.0 %collective-permute-start.9 = (bf16[1024,128]{1,0:T(8,128)(2,1)S(1)}, bf16[1024,128]{1,0:T(8,128)(2,1)S(1)}, u32[]{:S(2)}, u32[]{:S(2)}) collective-permute-start(bf16[1024,128]{1,0:T(8,128)(2,1)S(1)} %get-tuple-element.48), channel_id=1, source_target_pairs={{0,2},{1,3},{2,0},{3,1},{4,6},{5,7},{6,4},{7,5},{8,10},{9,11},{10,... | collective-permute-start | bytes 786440 | tf_op jit(solution)/shard_map/ppermute | solution.py:209
  58.6 7.3 %collective-permute-start.13 = (f32[2,16,128]{2,1,0:T(8,128)S(1)}, f32[2,16,128]{2,1,0:T(8,128)S(1)}, u32[]{:S(2)}, u32[]{:S(2)}) collective-permute-start(f32[2,16,128]{2,1,0:T(8,128)S(1)} %slice_bitcast_fusion.2), channel_id=1, source_target_pairs={{0,2},{1,3},{2,0},{3,1},{4,6},{5,7},{6,4},{7,5},{8,10},{9,11},{10,... | collective-permute-start | bytes 49160 | tf_op jit(solution)/shard_map/ppermute | solution.py:209
  65.9 4.8 %collective-permute-start.14 = (f32[2,2,8,128]{3,2,1,0:T(8,128)S(1)}, f32[2,2,8,128]{3,2,1,0:T(8,128)S(1)}, u32[]{:S(2)}, u32[]{:S(2)}) collective-permute-start(f32[2,2,8,128]{3,2,1,0:T(8,128)S(1)} %fusion.2), channel_id=1, source_target_pairs={{0,4},{1,5},{2,6},{3,7},{4,0},{5,1},{6,2},{7,3},{8,12},{9,13},{10,... | collective-permute-start | bytes 49160 | tf_op jit(solution)/shard_map/ppermute | solution.py:209
  66.1 5.7 %collective-permute-start.10 = (bf16[512,128]{1,0:T(8,128)(2,1)S(1)}, bf16[512,128]{1,0:T(8,128)(2,1)S(1)}, u32[]{:S(2)}, u32[]{:S(2)}) collective-permute-start(bf16[512,128]{1,0:T(8,128)(2,1)S(1)} %get-tuple-element.50), channel_id=1, source_target_pairs={{0,2},{1,3},{2,0},{3,1},{4,6},{5,7},{6,4},{7,5},{8,10},{9,11},{10,... | collective-permute-start | bytes 393224 | tf_op jit(solution)/shard_map/ppermute | solution.py:209
  67.9 5.0 %collective-permute-start.11 = (bf16[512,128]{1,0:T(8,128)(2,1)S(1)}, bf16[512,128]{1,0:T(8,128)(2,1)S(1)}, u32[]{:S(2)}, u32[]{:S(2)}) collective-permute-start(bf16[512,128]{1,0:T(8,128)(2,1)S(1)} %get-tuple-element.52), channel_id=1, source_target_pairs={{0,1},{1,0},{2,3},{3,2},{4,5},{5,4},{6,7},{7,6},{8,9},{9,8},{10,11... | collective-permute-start | bytes 393224 | tf_op jit(solution)/shard_map/ppermute | solution.py:209
  72.9 5.7 %collective-permute-start.15 = (bf16[256,128]{1,0:T(8,128)(2,1)S(1)}, bf16[256,128]{1,0:T(8,128)(2,1)S(1)}, u32[]{:S(2)}, u32[]{:S(2)}) collective-permute-start(bf16[256,128]{1,0:T(8,128)(2,1)S(1)} %get-tuple-element.55), channel_id=1, source_target_pairs={{0,4},{1,5},{2,6},{3,7},{4,0},{5,1},{6,2},{7,3},{8,12},{9,13},{10,... | collective-permute-start | bytes 196616 | tf_op jit(solution)/shard_map/ppermute | solution.py:209

commit v3 on v2

v3 whole, which is shorter than its diff:
```python
import functools

import jax
import jax.numpy as jnp
from jax import lax
from jax.experimental import pallas as pl
from jax.experimental.pallas import tpu as pltpu
from jax.sharding import PartitionSpec as P

SOFTNESS = 0.02
EPSILON = 1e-06
LANES = 128
TAIL = 16
BASE = 256
UNROLL = 16
SHIFT = 1 << 16
F32 = jnp.float32
BF16 = jnp.bfloat16


def call(body, out_shape, name, in_specs=None, aliases={}):
    kwargs = {} if in_specs is None else {"in_specs": in_specs}
    return pl.pallas_call(
        body,
        out_shape=out_shape,
        input_output_aliases=aliases,
        name=name,
        cost_estimate=pl.CostEstimate(flops=0, bytes_accessed=0, transcendentals=0),
        compiler_params=pltpu.CompilerParams(vmem_limit_bytes=48 * 1024 * 1024),
        **kwargs,
    )


def unit(values):
    floats = values.astype(F32)
    scale = lax.rsqrt(jnp.sum(floats * floats, axis=-1, keepdims=True) + EPSILON)
    return floats * scale, scale


def pack_body(queries_ref, cand_ref, out_ref):
    count, length, width = queries_ref.shape
    rows = count * length
    out_ref[:rows] = unit(queries_ref[...])[0].astype(BF16).reshape(rows, width)
    ids = jnp.concatenate([cand_ref[index : index + 1] for index in range(count)], axis=1)
    ids = jnp.broadcast_to(ids, (TAIL, LANES))
    high = ids // BASE
    low = ids - high * BASE
    place = lax.broadcasted_iota(jnp.int32, (TAIL, LANES), 0)
    digits = jnp.where(place == 0, high, jnp.where(place == 1, low, 0))
    out_ref[rows:] = digits.astype(F32).astype(BF16)


def unit_body(*refs):
    half = len(refs) // 2
    for source, out_ref in zip(refs[:half], refs[half:]):
        count = source.shape[0]
        together = min(count, 8)

        def step(index, carry, source=source, out_ref=out_ref, together=together):
            for offset in range(together):
                at = index * together + offset
                out_ref[at] = unit(source[at])[0].astype(BF16)
            return carry

        lax.fori_loop(0, count // together, step, 0)


def route_body(docs_ref, *refs, rows, size, list_len):
    *pay_refs, out_ref, list_ref = refs
    per_ref = pay_refs[0].shape[0]
    blocks = per_ref * len(pay_refs)
    stride = rows + TAIL
    ids = []
    for index, pay_ref in enumerate(pay_refs):
        for block in range(per_ref):
            start = (index * per_ref + block) * stride
            out_ref[start : start + stride] = pay_ref[block]
            tile = pay_ref[block, rows:].astype(F32)
            ids.append((tile[0:1] * BASE + tile[1:2]).astype(jnp.int32))
    ids = jnp.concatenate(ids, axis=0)
    per_block = LANES // list_len
    queries = blocks * per_block
    block = lax.broadcasted_iota(jnp.int32, (blocks, LANES), 0)
    lane = lax.broadcasted_iota(jnp.int32, (blocks, LANES), 1)
    query = lane // list_len
    source = (block * stride + query * (rows // per_block)).astype(F32)
    quarter = blocks // 4
    region = block // quarter
    moved = block + jnp.where(region == 1, quarter, 0) - jnp.where(region == 2, quarter, 0)
    first = lane % list_len == 0
    target = jnp.where(first, queries + moved * per_block, block * per_block) + query
    target = (target - 2 * queries).astype(F32)
    upper = lax.broadcasted_iota(jnp.int32, (LANES, LANES), 0)
    column = lax.broadcasted_iota(jnp.int32, (LANES, LANES), 1)
    triangle = (upper <= column).astype(F32)
    diagonal = upper == column
    parts = list_ref.shape[2]
    place = lax.broadcasted_iota(jnp.int32, (parts * LANES, LANES), 0).astype(F32)
    for piece in range(list_ref.shape[0]):
        held = jnp.full((blocks, LANES), -1, jnp.int32)
        for index in range(size):
            held = jnp.where(ids == docs_ref[piece * size + index], index, held)
        mask = held >= 0
        code = held.astype(F32) * SHIFT + source
        ranks = jnp.dot(mask.astype(F32), triangle, preferred_element_type=F32)
        before = jnp.zeros((1, 1), F32)
        codes = jnp.zeros((parts * LANES, LANES), F32)
        targets = jnp.zeros((parts * LANES, LANES), F32)
        for index in range(blocks):
            row = ranks[index : index + 1]
            slot = jnp.where(mask[index : index + 1], before + row - 1.0, -1.0)
            here = place == slot
            codes = codes + jnp.where(here, code[index : index + 1], 0.0)
            targets = targets + jnp.where(here, target[index : index + 1], 0.0)
            before = before + row[:, LANES - 1 : LANES]
        for kind, found in enumerate((codes, targets + 2.0 * queries / LANES)):
            packed = jnp.sum(found, axis=1, keepdims=True)
            for part in range(parts):
                value = packed[part * LANES : (part + 1) * LANES]
                line = jnp.sum(jnp.where(diagonal, value, 0.0), axis=0, keepdims=True)
                list_ref[piece, kind, part : part + 1] = line.astype(jnp.int32)
        count = jnp.broadcast_to(before, (parts, LANES)).astype(jnp.int32)
        list_ref[piece, 2] = count


def score_pairs(piece, list_ref, pay_ref, pass_ref, acc_ref, sums_ref, length):
    queries = sums_ref.shape[0] // 2
    count = list_ref[piece, 2, 0, 0]
    contract = (((1,), (1,)), ((), ()))

    def step(index, carry):
        pairs = []
        for offset in range(UNROLL):
            slot = index * UNROLL + offset
            part, lane = lax.shift_right_logical(slot, 7), slot & (LANES - 1)
            code = list_ref[piece, 0, part, lane]
            row = pl.multiple_of(code & (SHIFT - 1), 16)
            passage = pass_ref[lax.shift_right_logical(code, SHIFT.bit_length() - 1)]
            pairs.append((list_ref[piece, 1, part, lane], pay_ref[pl.ds(row, length)], passage))
        logits = [
            lax.dot_general(tokens, passage, contract, preferred_element_type=F32)
            for _, tokens, passage in pairs
        ]
        terms = [jnp.exp(block * (1.0 / SOFTNESS)) for block in logits]
        masses = [jnp.sum(block, axis=1, keepdims=True) for block in terms]
        pulled = [
            jnp.dot(block.astype(BF16), pair[2], preferred_element_type=F32)
            for block, pair in zip(terms, pairs)
        ]
        done = []
        for (target, _, _), mass, rows in zip(pairs, masses, pulled):
            score = SOFTNESS * jnp.sum(jnp.log(mass), axis=0, keepdims=True)
            exp_score = jnp.exp(score)
            first = target >= queries
            factor = jnp.where(first, 1.0, exp_score)
            done.append((target, rows * (factor / mass), jnp.where(first, score, exp_score)))
        for target, product, value in done:
            at = pl.ds(pl.multiple_of(target * length, length), length)
            acc_ref[at] = acc_ref[at] + product
            sums_ref[pl.ds(target, 1)] = sums_ref[pl.ds(target, 1)] + value
        return carry

    lax.fori_loop(0, lax.div(count + UNROLL - 1, UNROLL), step, 0)


def near_score_body(list_ref, pay_ref, *refs, length):
    *pass_refs, acc_ref, sums_ref = refs
    acc_ref[...] = jnp.zeros_like(acc_ref)
    sums_ref[...] = jnp.zeros_like(sums_ref)
    for piece, pass_ref in enumerate(pass_refs):
        score_pairs(piece, list_ref, pay_ref, pass_ref, acc_ref, sums_ref, length)


def score_body(list_ref, pay_ref, pass_ref, _, __, acc_ref, sums_ref, *, piece, length):
    score_pairs(piece, list_ref, pay_ref, pass_ref, acc_ref, sums_ref, length)


def last_score_body(
    list_ref, pay_ref, pass_ref, _, __, acc_ref, sums_ref, others_ref, firsts_ref, *, piece, length
):
    score_pairs(piece, list_ref, pay_ref, pass_ref, acc_ref, sums_ref, length)
    half = others_ref.shape[0]
    others_ref[...] = acc_ref[half : 2 * half].astype(BF16)
    firsts_ref[...] = acc_ref[3 * half : 4 * half].astype(BF16)


def halve_body(acc_ref, others_ref, firsts_ref, send_a, send_b, keep_a, keep_b):
    half = others_ref.shape[0]
    quarter = half // 2
    for start, got, send, keep in (
        (0, others_ref, send_a, keep_a),
        (2 * half, firsts_ref, send_b, keep_b),
    ):
        keep[...] = acc_ref[start : start + quarter] + got[:quarter].astype(F32)
        rest = acc_ref[start + quarter : start + half] + got[quarter:].astype(F32)
        send[...] = rest.astype(BF16)


def merge_body(others_ref, got_others, firsts_ref, got_firsts, sums_ref, send_ref, rest_ref, *, length):
    queries = sums_ref.shape[1]

    def part(index):
        at = slice(index * length, (index + 1) * length)
        others = others_ref[at] + got_others[at].astype(F32)
        first = firsts_ref[at] + got_firsts[at].astype(F32)
        return others - sums_ref[0, index : index + 1] * first

    for index in range(queries // 2):
        at = slice(index * length, (index + 1) * length)
        rest_ref[at] = part(index)
        send_ref[at] = part(index + queries // 2).astype(BF16)


def last_body(queries_ref, keep_ref, got_ref, sums_ref, grad_ref, loss_ref, *, length):
    count = queries_ref.shape[0]
    losses = []
    for index in range(count):
        at = slice(index * length, (index + 1) * length)
        spread = sums_ref[0, index : index + 1]
        score = sums_ref[1, index : index + 1]
        total = spread + jnp.exp(score)
        losses.append(jnp.log(total) - score)
        gradient = (keep_ref[at] + got_ref[at].astype(F32)) / total
        query_unit, query_scale = unit(queries_ref[index])
        along = jnp.sum(query_unit * gradient, axis=-1, keepdims=True)
        grad_ref[index] = (gradient - query_unit * along) * query_scale
    losses = jnp.concatenate(losses, axis=0)
    place = lax.broadcasted_iota(jnp.int32, (count, LANES), 0)
    lane = lax.broadcasted_iota(jnp.int32, (count, LANES), 1)
    loss_ref[...] = jnp.sum(jnp.where(place == lane, losses, 0.0), axis=0, keepdims=True)[:, :count]


def swap(value, axis, bit):
    size = lax.axis_size(axis)
    return lax.ppermute(value, axis, [(index, index ^ bit) for index in range(size)])


def bits_of(size):
    return [1 << power for power in reversed(range(size.bit_length() - 1))]


def spread_offsets(size):
    offsets = [0]
    for bit in bits_of(size):
        offsets = offsets + [offset ^ bit for offset in offsets]
    return offsets


def spread(block):
    blocks = [block]
    for bit in bits_of(lax.axis_size("group") // 2):
        blocks = blocks + [swap(held, "group", bit) for held in blocks]
    return blocks


def local(queries, passages, candidates, location):
    group_count = lax.axis_size("group")
    dev_count = lax.axis_size("dev")
    device_total = group_count * dev_count
    query_count, length, width = queries.shape
    pass_count, pass_len, _ = passages.shape
    list_len = candidates.shape[1]
    pair_count = query_count * list_len
    rows = query_count * length
    slot_cap = max(2, (3 * pair_count + device_total - 1) // device_total)
    group = lax.axis_index("group")
    dev = lax.axis_index("dev")
    shape = jax.ShapeDtypeStruct

    half_bit = group_count // 2
    far_raw = swap(passages, "group", half_bit)
    near_raw = spread(passages)
    payload = call(pack_body, shape((rows + TAIL, width), BF16), "query_units")(queries, candidates)

    *first_bits, low, lowest = bits_of(dev_count)
    pay = payload[None]
    for bit in first_bits:
        pay = jnp.concatenate([pay, swap(pay, "dev", bit)], axis=0)
    pay_low = swap(pay, "dev", low)
    pays = [pay, pay_low, swap(pay, "dev", lowest), swap(pay_low, "dev", lowest)]

    near_offsets = spread_offsets(half_bit)
    offsets = near_offsets + [offset ^ half_bit for offset in near_offsets]
    held_rows = jnp.concatenate(
        [
            ((group ^ offset) * dev_count + dev) * pass_count + jnp.arange(pass_count)
            for offset in offsets
        ]
    )
    hits = location[None, :] == held_rows.astype(jnp.int32)[:, None]
    documents = jnp.arange(location.shape[0], dtype=jnp.int32)
    docs = jnp.sum(jnp.where(hits, documents[None, :], 0), axis=1)

    parts = -(-dev_count * min(pair_count, slot_cap) // LANES)
    smem, vmem = (pl.BlockSpec(memory_space=space) for space in (pltpu.SMEM, pltpu.VMEM))
    pay, lists = call(
        functools.partial(route_body, rows=rows, size=pass_count, list_len=list_len),
        [
            shape((dev_count * (rows + TAIL), width), BF16),
            shape((len(offsets), 3, parts, LANES), jnp.int32),
        ],
        "route",
        in_specs=[smem] + [vmem] * len(pays),
    )(docs, *pays)

    all_queries = dev_count * query_count
    half_rows = all_queries * length // 2
    totals = [
        shape(((2 * all_queries + 1) * length, width), F32),
        shape((2 * all_queries + 1, LANES), F32),
    ]
    sends = [shape((half_rows, width), BF16)] * 2
    near = call(unit_body, [shape(passages.shape, BF16)] * len(near_raw), "passage_units")(*near_raw)
    state = call(
        functools.partial(near_score_body, length=length),
        totals,
        "score_near",
        in_specs=[smem] + [vmem] * (1 + len(near)),
    )(lists, pay, *near)
    far_raw, *state = lax.optimization_barrier((far_raw, *state))
    far = spread(call(unit_body, shape(passages.shape, BF16), "passage_units")(far_raw))
    for index, held in enumerate(far):
        last = index == len(far) - 1
        state = call(
            functools.partial(
                last_score_body if last else score_body, piece=len(near) + index, length=length
            ),
            totals + (sends if last else []),
            "score_far",
            in_specs=[smem] + [vmem] * 4,
            aliases={3: 0, 4: 1},
        )(lists, pay, held, *state)
    acc, sums, others, firsts = state

    steps = bits_of(dev_count)[::-1]
    got_others = swap(others, "dev", steps[0])
    got_firsts = swap(firsts, "dev", steps[1])
    sums = sums[: 2 * all_queries].reshape(2, 2, 2, all_queries // 4, LANES)
    spreads, scores = sums[0], jnp.swapaxes(sums[1], 0, 1)
    sums = jnp.stack([spreads[0], scores[0]])
    sums = sums + swap(jnp.stack([spreads[1], scores[1]]), "dev", steps[0])
    sums = sums[:, 0] + swap(sums[:, 1], "dev", steps[1])
    levels = len(steps) - 2
    sums = sums.reshape((2,) + (2,) * levels + (query_count, LANES))
    for level, bit in enumerate(steps[2:]):
        sums = sums + jnp.flip(swap(sums, "dev", bit), axis=1 + level)
    sums = sums.reshape(2, all_queries // 4, LANES)
    quarter = half_rows // 2
    send_others, send_firsts, others, firsts = call(
        halve_body, [shape((quarter, width), BF16)] * 2 + [shape((quarter, width), F32)] * 2, "halve"
    )(acc, got_others, got_firsts)
    got_others = swap(send_others, "dev", steps[1])
    got_firsts = swap(send_firsts, "dev", steps[0])
    quarter = quarter // 2
    send, rest = call(
        functools.partial(merge_body, length=length),
        [shape((quarter, width), BF16), shape((quarter, width), F32)],
        "merge",
    )(others, got_others, firsts, got_firsts, sums)
    for bit in steps[2:-1]:
        rest = rest + swap(send, "dev", bit).astype(F32)
        quarter = quarter // 2
        rest, send = rest[:quarter], rest[quarter:].astype(BF16)
    got = swap(send, "dev", steps[-1])
    grad, loss = call(
        functools.partial(last_body, length=length),
        [shape(queries.shape, F32), shape((1, query_count), F32)],
        "last",
    )(queries, rest, got, sums[:, :query_count])
    return loss.reshape(query_count), grad


def solution(mesh):
    placed = (
        P(("group", "dev"), None, None),
        P(("group", "dev"), None, None),
        P(("group", "dev"), None),
        P(),
    )
    return jax.shard_map(
        local,
        mesh=mesh,
        in_specs=placed,
        out_specs=(P(("group", "dev")), P(("group", "dev"), None, None)),
        check_vma=False,
    )
```

time: 80 us -> 63.1 us (0.79)
  starting transfers between devices: 24.9 us -> 18.8 us
  Pallas kernels: 17.6 us -> 12.4 us
  waiting for transfers between devices: 29.6 us -> 26.8 us
  local copies, waits for them, and re-layouts: 4.47 us -> 2.78 us
  other arithmetic: 2.64 us -> 0.98 us
    ppermute x16 -> x15, starting transfers between devices: 24.9 us -> 18.8 us  [swap(): lax.ppermute(value, axis, [(index, index ^ bit) for index in range(size)])]
    pallas_call x10 -> x6, Pallas kernels: 16.5 us -> 11.2 us  [the longest x2 4.5 us: local(): call(functools.partial(last_score_body if last else score_body, piece=len...]
    ppermute x16 -> x15, waiting for transfers between devices: 29.6 us -> 26.8 us  [swap(): lax.ppermute(value, axis, [(index, index ^ bit) for index in range(size)])]
    concatenate x3 -> x1, other arithmetic: 2.44 us -> 0.01 us  [local(): pay = jnp.concatenate([pay, swap(pay, 'dev', bit)], axis=0)]
    slice x2 -> x3, local copies, waits for them, and re-layouts: 1.53 us -> 0.01 us  [the longest x2 0.01 us: local(): sums = jnp.stack([spreads[0], scores[0]])]
  transfers between devices with their start and end apart: 16 -> 15, of which waited for: 10 -> 10; matrix products, arithmetic and copies ran while one was open for 5% -> 2% of each run, Pallas kernels for 16% -> 13%
where the time goes in v3:
time: 63.1 us; the launch traced here: 62.5 us
  waiting for transfers between devices  26.8 us (42%)
  starting transfers between devices  18.8 us (30%)
  Pallas kernels  12.4 us (20%)
  local copies, waits for them, and re-layouts  2.78 us (4%)
  other arithmetic  0.98 us (2%)
  between operations  0.79 us (1%)
    ppermute x15, waiting for transfers between devices, swap(): lax.ppermute(value, axis, [(index, index ^ bit) for index in range(size)])  26.8 us
    ppermute x15, starting transfers between devices, swap(): lax.ppermute(value, axis, [(index, index ^ bit) for index in range(size)])  18.8 us
    pallas_call x2, Pallas kernels, local(): call(functools.partial(last_score_body if last else score_body, piece=len...  4.5 us
    pallas_call x1, Pallas kernels, local(): call(functools.partial(near_score_body, length=length), totals, 'score_ne...  3.3 us
    unnamed x8, local copies, waits for them, and re-layouts  2.75 us
    pallas_call x1, Pallas kernels, local(): call(unit_body, [shape(passages.shape, BF16)] * len(near_raw), 'passage_u...  1.41 us
    pallas_call x1, Pallas kernels, local(): call(functools.partial(route_body, rows=rows, size=pass_count, list_len=l...  1.3 us
  transfers between devices with their start and end apart: 15, of which 10 were waited for; matrix products, arithmetic and copies ran while one was open for 2% of the time, Pallas kernels for 13%

profile of v3, /device:TPU:0, one launch (start us, length us, event | category | flops | bytes accessed | tf_op | source)
XLA Modules:
  0.0 62.5 jit_solution(3640812060373119725)
XLA Ops:
  0.6 0.5 collective-permute-start.5
  1.1 2.6 %collective-permute-start.4 = (bf16[16,256,128]{2,1,0:T(8,128)(2,1)}, bf16[16,256,128]{2,1,0:T(8,128)(2,1)S(1)}, u32[]{:S(2)}, u32[]{:S(2)}) collective-permute-start(bf16[16,256,128]{2,1,0:T(8,128)(2,1)} %refs_0_.1), channel_id=1, source_target_pairs={{0,16},{8,24},{16,0},{24,8},{1,17},{9,25},{17,1},{25,9},{2,18},{10... | collective-permute-start | bytes 3145736 | tf_op jit(solution)/shard_map/ppermute | solution.py:235
  3.7 0.0 copy-start.1
  3.7 0.8 %copy-done.1 = bf16[8,32,128]{2,1,0:T(8,128)(2,1)S(1)} copy-done((bf16[8,32,128]{2,1,0:T(8,128)(2,1)S(1)}, bf16[8,32,128]{2,1,0:T(8,128)(2,1)}, u32[]{:S(2)}) %copy-start.1) | copy-done | bytes 65560
  4.6 0.0 copy-start.3
  4.6 0.7 %copy-done.3 = s32[8,16]{1,0:T(8,128)S(1)} copy-done((s32[8,16]{1,0:T(8,128)S(1)}, s32[8,16]{1,0:T(8,128)}, u32[]{:S(2)}) %copy-start.3) | copy-done | bytes 536
  5.2 0.1 query_units.1
  5.4 2.7 %collective-permute-start = (bf16[1,272,128]{2,1,0:T(8,128)(2,1)S(1)}, bf16[1,272,128]{2,1,0:T(8,128)(2,1)S(1)}, u32[]{:S(2)}, u32[]{:S(2)}) collective-permute-start(bf16[1,272,128]{2,1,0:T(8,128)(2,1)S(1)} %bitcast.26), channel_id=1, source_target_pairs={{0,4},{1,5},{2,6},{3,7},{4,0},{5,1},{6,2},{7,3},{8,12},{9,13},{10,... | collective-permute-start | bytes 208904 | tf_op jit(solution)/shard_map/ppermute | solution.py:235
  8.0 4.1 %collective-permute-done = bf16[1,272,128]{2,1,0:T(8,128)(2,1)S(1)} collective-permute-done((bf16[1,272,128]{2,1,0:T(8,128)(2,1)S(1)}, bf16[1,272,128]{2,1,0:T(8,128)(2,1)S(1)}, u32[]{:S(2)}, u32[]{:S(2)}) %collective-permute-start) | collective-permute-done | bytes 69664 | tf_op jit(solution)/shard_map/ppermute | solution.py:235
  12.2 0.7 %collective-permute-start.1 = (bf16[2,272,128]{2,1,0:T(8,128)(2,1)S(1)}, bf16[2,272,128]{2,1,0:T(8,128)(2,1)S(1)}, u32[]{:S(2)}, u32[]{:S(2)}) collective-permute-start(bf16[2,272,128]{2,1,0:T(8,128)(2,1)S(1)} %pad_maximum_fusion.refs_0_), channel_id=1, source_target_pairs={{0,2},{1,3},{2,0},{3,1},{4,6},{5,7},{6,4},{7,5},{8,10},{9,11},{10,... | collective-permute-start | bytes 417800 | tf_op jit(solution)/shard_map/ppermute | solution.py:235
  12.9 1.5 %collective-permute-start.2 = (bf16[2,272,128]{2,1,0:T(8,128)(2,1)S(1)}, bf16[2,272,128]{2,1,0:T(8,128)(2,1)S(1)}, u32[]{:S(2)}, u32[]{:S(2)}) collective-permute-start(bf16[2,272,128]{2,1,0:T(8,128)(2,1)S(1)} %pad_maximum_fusion.refs_0_), channel_id=1, source_target_pairs={{0,1},{1,0},{2,3},{3,2},{4,5},{5,4},{6,7},{7,6},{8,9},{9,8},{10,11... | collective-permute-start | bytes 417800 | tf_op jit(solution)/shard_map/ppermute | solution.py:235
  14.4 2.9 %collective-permute-done.1.refs_1_ = bf16[2,272,128]{2,1,0:T(8,128)(2,1)S(1)} collective-permute-done((bf16[2,272,128]{2,1,0:T(8,128)(2,1)S(1)}, bf16[2,272,128]{2,1,0:T(8,128)(2,1)S(1)}, u32[]{:S(2)}, u32[]{:S(2)}) %collective-permute-start.1) | collective-permute-done | bytes 139296 | tf_op jit(solution)/shard_map/ppermute | solution.py:235
  17.3 1.5 %collective-permute-start.3 = (bf16[2,272,128]{2,1,0:T(8,128)(2,1)S(1)}, bf16[2,272,128]{2,1,0:T(8,128)(2,1)S(1)}, u32[]{:S(2)}, u32[]{:S(2)}) collective-permute-start(bf16[2,272,128]{2,1,0:T(8,128)(2,1)S(1)} %collective-permute-done.1.refs_1_), channel_id=1, source_target_pairs={{0,1},{1,0},{2,3},{3,2},{4,5},{5,4},{6,7},{7,6},{8,9},{9,8},{10,11... | collective-permute-start | bytes 417800 | tf_op jit(solution)/shard_map/ppermute | solution.py:235
  18.8 0.1 pad_add_fusion
  18.9 0.9 %select_reduce_fusion.docs_ref = s32[64]{0:T(128)S(1)} fusion(s32[512]{0:T(512)} %param.7, s32[64]{0:T(128)S(1)} %pad_add_fusion), kind=kLoop, calls=%fused_computation.1 | loop fusion | flops 98240 | bytes 2560 | tf_op jit(solution)/shard_map/reduce_sum | solution.py:292
  19.8 0.0 collective-permute-done.2.refs_2_
  19.8 2.6 %collective-permute-done.3.refs_3_ = bf16[2,272,128]{2,1,0:T(8,128)(2,1)S(1)} collective-permute-done((bf16[2,272,128]{2,1,0:T(8,128)(2,1)S(1)}, bf16[2,272,128]{2,1,0:T(8,128)(2,1)S(1)}, u32[]{:S(2)}, u32[]{:S(2)}) %collective-permute-start.3) | collective-permute-done | bytes 139296 | tf_op jit(solution)/shard_map/ppermute | solution.py:235
  22.3 1.3 %route.1 = (bf16[2176,128]{1,0:T(8,128)(2,1)S(1)}, s32[4,3,1,128]{3,2,1,0:T(1,128)S(1)}) custom-call(s32[64]{0:T(128)S(1)} %select_reduce_fusion.docs_ref, bf16[2,272,128]{2,1,0:T(8,128)(2,1)S(1)} %pad_maximum_fusion.refs_0_, bf16[2,272,128]{2,1,0:T(8,128)(2,1)S(1)} %collective-permute-done.1.refs_1_, ...), custom_call_target="tpu_custom_call" | custom-call | tf_op jit(solution)/shard_map/route/pallas_call | solution.py:296
  23.7 0.0 collective-permute-done.5.refs_1_
  23.7 0.0 copy-start
  23.7 1.2 %copy-done = bf16[16,256,128]{2,1,0:T(8,128)(2,1)S(1)} copy-done((bf16[16,256,128]{2,1,0:T(8,128)(2,1)S(1)}, bf16[16,256,128]{2,1,0:T(8,128)(2,1)}, u32[]{:S(2)}) %copy-start) | copy-done | bytes 1048600
  24.9 1.4 %passage_units.2 = (bf16[16,256,128]{2,1,0:T(8,128)(2,1)S(1)}, bf16[16,256,128]{2,1,0:T(8,128)(2,1)S(1)}) custom-call(bf16[16,256,128]{2,1,0:T(8,128)(2,1)S(1)} %copy-done, bf16[16,256,128]{2,1,0:T(8,128)(2,1)S(1)} %collective-permute-done.5.refs_1_), custom_call_target="tpu_custom_call" | custom-call | tf_op jit(solution)/shard_map/passage_units/pallas_call | solution.py:313
  26.3 3.3 %score_near.1 = (f32[4128,128]{1,0:T(8,128)S(1)}, f32[129,128]{1,0:T(8,128)S(1)}) custom-call(s32[4,3,1,128]{3,2,1,0:T(1,128)S(1)} %get-tuple-element.25.list_ref, bf16[2176,128]{1,0:T(8,128)(2,1)S(1)} %get-tuple-element.26.pay_ref, bf16[16,256,128]{2,1,0:T(8,128)(2,1)S(1)} %get-tuple-element.27.refs_0_, bf16[16,256,128]{2,1,0:T(8,128)(2,1)S(1)} %get-tuple-element.28.refs_1_), custom_call_target="tpu_custom_call" | custom-call | tf_op jit(solution)/shard_map/score_near/pallas_call | solution.py:314
  29.6 0.0 collective-permute-done.4.refs_0_
  29.6 0.7 %passage_units.3.pass_ref = bf16[16,256,128]{2,1,0:T(8,128)(2,1)S(1)} custom-call(bf16[16,256,128]{2,1,0:T(8,128)(2,1)S(1)} %collective-permute-done.4.refs_0_), custom_call_target="tpu_custom_call" | custom-call | tf_op jit(solution)/shard_map/passage_units/pallas_call | solution.py:321
  30.3 0.1 collective-permute-start.6
  30.4 1.9 %score_far.2 = (f32[4128,128]{1,0:T(8,128)S(1)}, f32[129,128]{1,0:T(8,128)S(1)}) custom-call(s32[4,3,1,128]{3,2,1,0:T(1,128)S(1)} %get-tuple-element.25.list_ref, bf16[2176,128]{1,0:T(8,128)(2,1)S(1)} %get-tuple-element.26.pay_ref, bf16[16,256,128]{2,1,0:T(8,128)(2,1)S(1)} %passage_units.3.pass_ref, ...), custom_call_target="tpu_custom_call", output_to_operand_aliasing={{0}: (3, {}), {1}: (4, {})} | custom-call | tf_op jit(solution)/shard_map/score_far/pallas_call | solution.py:324
  32.3 0.7 %collective-permute-done.6.pass_ref = bf16[16,256,128]{2,1,0:T(8,128)(2,1)S(1)} collective-permute-done((bf16[16,256,128]{2,1,0:T(8,128)(2,1)S(1)}, bf16[16,256,128]{2,1,0:T(8,128)(2,1)S(1)}, u32[]{:S(2)}, u32[]{:S(2)}) %collective-permute-start.6) | collective-permute-done | bytes 1048608 | tf_op jit(solution)/shard_map/ppermute | solution.py:235
  33.1 2.6 %score_far.3 = (f32[4128,128]{1,0:T(8,128)S(1)}, f32[129,128]{1,0:T(8,128)S(1)}, bf16[1024,128]{1,0:T(8,128)(2,1)S(1)}, bf16[1024,128]{1,0:T(8,128)(2,1)S(1)}) custom-call(s32[4,3,1,128]{3,2,1,0:T(1,128)S(1)} %get-tuple-element.25.list_ref, bf16[2176,128]{1,0:T(8,128)(2,1)S(1)} %get-tuple-element.26.pay_ref, ...), custom_call_target="tpu_custom_call", output_to_operand_aliasing={{0}: (3, {}), {1}: (4, {})} | custom-call | tf_op jit(solution)/shard_map/score_far/pallas_call | solution.py:324
  35.7 0.0 copy-start.2
  35.7 4.0 %collective-permute-start.11 = (f32[2,2,16,128]{3,2,1,0:T(8,128)S(1)}, f32[2,2,16,128]{3,2,1,0:T(8,128)S(1)}, u32[]{:S(2)}, u32[]{:S(2)}) collective-permute-start(f32[2,2,16,128]{3,2,1,0:T(8,128)S(1)} %pad_maximum_fusion.1), channel_id=1, source_target_pairs={{0,1},{1,0},{2,3},{3,2},{4,5},{5,4},{6,7},{7,6},{8,9},{9,8},{10,11... | collective-permute-start | bytes 98312 | tf_op jit(solution)/shard_map/ppermute | solution.py:235
  39.8 0.1 collective-permute-start.7
  39.8 0.0 collective-permute-start.8
  39.8 1.8 %collective-permute-done.11 = f32[2,2,16,128]{3,2,1,0:T(8,128)S(1)} collective-permute-done((f32[2,2,16,128]{3,2,1,0:T(8,128)S(1)}, f32[2,2,16,128]{3,2,1,0:T(8,128)S(1)}, u32[]{:S(2)}, u32[]{:S(2)}) %collective-permute-start.11) | collective-permute-done | bytes 32800 | tf_op jit(solution)/shard_map/ppermute | solution.py:235
  41.7 0.3 collective-permute-start.12
  41.9 6.4 %collective-permute-done.12 = f32[2,16,128]{2,1,0:T(8,128)S(1)} collective-permute-done((f32[2,16,128]{2,1,0:T(8,128)S(1)}, f32[2,16,128]{2,1,0:T(8,128)S(1)}, u32[]{:S(2)}, u32[]{:S(2)}) %collective-permute-start.12) | collective-permute-done | bytes 16416 | tf_op jit(solution)/shard_map/ppermute | solution.py:235
  48.3 1.0 %collective-permute-start.13 = (f32[2,2,8,128]{3,2,1,0:T(8,128)S(1)}, f32[2,2,8,128]{3,2,1,0:T(8,128)S(1)}, u32[]{:S(2)}, u32[]{:S(2)}) collective-permute-start(f32[2,2,8,128]{3,2,1,0:T(8,128)S(1)} %fusion.1), channel_id=1, source_target_pairs={{0,4},{1,5},{2,6},{3,7},{4,0},{5,1},{6,2},{7,3},{8,12},{9,13},{10,... | collective-permute-start | bytes 49160 | tf_op jit(solution)/shard_map/ppermute | solution.py:235
  49.3 0.0 collective-permute-done.7.others_ref
  49.3 0.0 collective-permute-done.8.firsts_ref
  49.3 0.1 halve.1
  49.4 1.3 %collective-permute-start.9 = (bf16[512,128]{1,0:T(8,128)(2,1)S(1)}, bf16[512,128]{1,0:T(8,128)(2,1)S(1)}, u32[]{:S(2)}, u32[]{:S(2)}) collective-permute-start(bf16[512,128]{1,0:T(8,128)(2,1)S(1)} %get-tuple-element.40), channel_id=1, source_target_pairs={{0,2},{1,3},{2,0},{3,1},{4,6},{5,7},{6,4},{7,5},{8,10},{9,11},{10,... | collective-permute-start | bytes 393224 | tf_op jit(solution)/shard_map/ppermute | solution.py:235
  50.7 1.5 %collective-permute-start.10 = (bf16[512,128]{1,0:T(8,128)(2,1)S(1)}, bf16[512,128]{1,0:T(8,128)(2,1)S(1)}, u32[]{:S(2)}, u32[]{:S(2)}) collective-permute-start(bf16[512,128]{1,0:T(8,128)(2,1)S(1)} %get-tuple-element.42), channel_id=1, source_target_pairs={{0,1},{1,0},{2,3},{3,2},{4,5},{5,4},{6,7},{7,6},{8,9},{9,8},{10,11... | collective-permute-start | bytes 393224 | tf_op jit(solution)/shard_map/ppermute | solution.py:235
  52.2 0.8 %collective-permute-done.13 = f32[2,2,8,128]{3,2,1,0:T(8,128)S(1)} collective-permute-done((f32[2,2,8,128]{3,2,1,0:T(8,128)S(1)}, f32[2,2,8,128]{3,2,1,0:T(8,128)S(1)}, u32[]{:S(2)}, u32[]{:S(2)}) %collective-permute-start.13) | collective-permute-done | bytes 16416 | tf_op jit(solution)/shard_map/ppermute | solution.py:235
  53.0 1.4 %collective-permute-done.9.got_others = bf16[512,128]{1,0:T(8,128)(2,1)S(1)} collective-permute-done((bf16[512,128]{1,0:T(8,128)(2,1)S(1)}, bf16[512,128]{1,0:T(8,128)(2,1)S(1)}, u32[]{:S(2)}, u32[]{:S(2)}) %collective-permute-start.9) | collective-permute-done | bytes 131104 | tf_op jit(solution)/shard_map/ppermute | solution.py:235
  54.5 1.2 %collective-permute-done.10.got_firsts = bf16[512,128]{1,0:T(8,128)(2,1)S(1)} collective-permute-done((bf16[512,128]{1,0:T(8,128)(2,1)S(1)}, bf16[512,128]{1,0:T(8,128)(2,1)S(1)}, u32[]{:S(2)}, u32[]{:S(2)}) %collective-permute-start.10) | collective-permute-done | bytes 131104 | tf_op jit(solution)/shard_map/ppermute | solution.py:235
  55.7 0.1 merge.1
  55.7 1.1 %collective-permute-start.14 = (bf16[256,128]{1,0:T(8,128)(2,1)S(1)}, bf16[256,128]{1,0:T(8,128)(2,1)S(1)}, u32[]{:S(2)}, u32[]{:S(2)}) collective-permute-start(bf16[256,128]{1,0:T(8,128)(2,1)S(1)} %get-tuple-element.45), channel_id=1, source_target_pairs={{0,4},{1,5},{2,6},{3,7},{4,0},{5,1},{6,2},{7,3},{8,12},{9,13},{10,... | collective-permute-start | bytes 196616 | tf_op jit(solution)/shard_map/ppermute | solution.py:235
  56.8 4.8 %collective-permute-done.14.got_ref = bf16[256,128]{1,0:T(8,128)(2,1)S(1)} collective-permute-done((bf16[256,128]{1,0:T(8,128)(2,1)S(1)}, bf16[256,128]{1,0:T(8,128)(2,1)S(1)}, u32[]{:S(2)}, u32[]{:S(2)}) %collective-permute-start.14) | collective-permute-done | bytes 65568 | tf_op jit(solution)/shard_map/ppermute | solution.py:235
  61.7 0.0 copy-done.2
  61.7 0.9 %last.1 = (f32[8,32,128]{2,1,0:T(8,128)}, f32[1,8]{1,0:T(1,128)}) custom-call(bf16[8,32,128]{2,1,0:T(8,128)(2,1)S(1)} %copy-done.2, f32[256,128]{1,0:T(8,128)S(1)} %get-tuple-element.44.keep_ref, bf16[256,128]{1,0:T(8,128)(2,1)S(1)} %collective-permute-done.14.got_ref, f32[2,8,128]{2,1,0:T(8,128)S(1)} %slice.52.sums_ref), custom_call_target="tpu_custom_call" | custom-call | tf_op jit(solution)/shard_map/last/pallas_call | solution.py:365
  (13 shorter events, 0.1 us)
Async XLA Ops:
  0.6 23.0 %collective-permute-start.5 = (bf16[16,256,128]{2,1,0:T(8,128)(2,1)}, bf16[16,256,128]{2,1,0:T(8,128)(2,1)S(1)}, u32[]{:S(2)}, u32[]{:S(2)}) collective-permute-start(bf16[16,256,128]{2,1,0:T(8,128)(2,1)} %refs_0_.1), channel_id=1, source_target_pairs={{0,8},{8,0},{16,24},{24,16},{1,9},{9,1},{17,25},{25,17},{2,10},{10... | collective-permute-start | bytes 3145736 | tf_op jit(solution)/shard_map/ppermute | solution.py:235
  1.1 28.5 %collective-permute-start.4 = (bf16[16,256,128]{2,1,0:T(8,128)(2,1)}, bf16[16,256,128]{2,1,0:T(8,128)(2,1)S(1)}, u32[]{:S(2)}, u32[]{:S(2)}) collective-permute-start(bf16[16,256,128]{2,1,0:T(8,128)(2,1)} %refs_0_.1), channel_id=1, source_target_pairs={{0,16},{8,24},{16,0},{24,8},{1,17},{9,25},{17,1},{25,9},{2,18},{10... | collective-permute-start | bytes 3145736 | tf_op jit(solution)/shard_map/ppermute | solution.py:235
  3.7 0.8 %copy-start.1 = (bf16[8,32,128]{2,1,0:T(8,128)(2,1)S(1)}, bf16[8,32,128]{2,1,0:T(8,128)(2,1)}, u32[]{:S(2)}) copy-start(bf16[8,32,128]{2,1,0:T(8,128)(2,1)} %queries_ref.3) | copy-start | bytes 196612
  4.6 0.7 %copy-start.3 = (s32[8,16]{1,0:T(8,128)S(1)}, s32[8,16]{1,0:T(8,128)}, u32[]{:S(2)}) copy-start(s32[8,16]{1,0:T(8,128)} %cand_ref.1) | copy-start | bytes 1540
  5.4 6.8 %collective-permute-start = (bf16[1,272,128]{2,1,0:T(8,128)(2,1)S(1)}, bf16[1,272,128]{2,1,0:T(8,128)(2,1)S(1)}, u32[]{:S(2)}, u32[]{:S(2)}) collective-permute-start(bf16[1,272,128]{2,1,0:T(8,128)(2,1)S(1)} %bitcast.26), channel_id=1, source_target_pairs={{0,4},{1,5},{2,6},{3,7},{4,0},{5,1},{6,2},{7,3},{8,12},{9,13},{10,... | collective-permute-start | bytes 208904 | tf_op jit(solution)/shard_map/ppermute | solution.py:235
  12.2 5.1 %collective-permute-start.1 = (bf16[2,272,128]{2,1,0:T(8,128)(2,1)S(1)}, bf16[2,272,128]{2,1,0:T(8,128)(2,1)S(1)}, u32[]{:S(2)}, u32[]{:S(2)}) collective-permute-start(bf16[2,272,128]{2,1,0:T(8,128)(2,1)S(1)} %pad_maximum_fusion.refs_0_), channel_id=1, source_target_pairs={{0,2},{1,3},{2,0},{3,1},{4,6},{5,7},{6,4},{7,5},{8,10},{9,11},{10,... | collective-permute-start | bytes 417800 | tf_op jit(solution)/shard_map/ppermute | solution.py:235
  12.9 6.9 %collective-permute-start.2 = (bf16[2,272,128]{2,1,0:T(8,128)(2,1)S(1)}, bf16[2,272,128]{2,1,0:T(8,128)(2,1)S(1)}, u32[]{:S(2)}, u32[]{:S(2)}) collective-permute-start(bf16[2,272,128]{2,1,0:T(8,128)(2,1)S(1)} %pad_maximum_fusion.refs_0_), channel_id=1, source_target_pairs={{0,1},{1,0},{2,3},{3,2},{4,5},{5,4},{6,7},{7,6},{8,9},{9,8},{10,11... | collective-permute-start | bytes 417800 | tf_op jit(solution)/shard_map/ppermute | solution.py:235
  17.3 5.1 %collective-permute-start.3 = (bf16[2,272,128]{2,1,0:T(8,128)(2,1)S(1)}, bf16[2,272,128]{2,1,0:T(8,128)(2,1)S(1)}, u32[]{:S(2)}, u32[]{:S(2)}) collective-permute-start(bf16[2,272,128]{2,1,0:T(8,128)(2,1)S(1)} %collective-permute-done.1.refs_1_), channel_id=1, source_target_pairs={{0,1},{1,0},{2,3},{3,2},{4,5},{5,4},{6,7},{7,6},{8,9},{9,8},{10,11... | collective-permute-start | bytes 417800 | tf_op jit(solution)/shard_map/ppermute | solution.py:235
  23.7 1.2 %copy-start = (bf16[16,256,128]{2,1,0:T(8,128)(2,1)S(1)}, bf16[16,256,128]{2,1,0:T(8,128)(2,1)}, u32[]{:S(2)}) copy-start(bf16[16,256,128]{2,1,0:T(8,128)(2,1)} %refs_0_.1) | copy-start | bytes 3145732
  30.3 2.7 %collective-permute-start.6 = (bf16[16,256,128]{2,1,0:T(8,128)(2,1)S(1)}, bf16[16,256,128]{2,1,0:T(8,128)(2,1)S(1)}, u32[]{:S(2)}, u32[]{:S(2)}) collective-permute-start(bf16[16,256,128]{2,1,0:T(8,128)(2,1)S(1)} %passage_units.3.pass_ref), channel_id=1, source_target_pairs={{0,8},{8,0},{16,24},{24,16},{1,9},{9,1},{17,25},{25,17},{2,10},{10... | collective-permute-start | bytes 3145736 | tf_op jit(solution)/shard_map/ppermute | solution.py:235
  35.7 26.0 %copy-start.2 = (bf16[8,32,128]{2,1,0:T(8,128)(2,1)S(1)}, bf16[8,32,128]{2,1,0:T(8,128)(2,1)}, u32[]{:S(2)}) copy-start(bf16[8,32,128]{2,1,0:T(8,128)(2,1)} %queries_ref.3) | copy-start | bytes 196612
  35.7 5.9 %collective-permute-start.11 = (f32[2,2,16,128]{3,2,1,0:T(8,128)S(1)}, f32[2,2,16,128]{3,2,1,0:T(8,128)S(1)}, u32[]{:S(2)}, u32[]{:S(2)}) collective-permute-start(f32[2,2,16,128]{3,2,1,0:T(8,128)S(1)} %pad_maximum_fusion.1), channel_id=1, source_target_pairs={{0,1},{1,0},{2,3},{3,2},{4,5},{5,4},{6,7},{7,6},{8,9},{9,8},{10,11... | collective-permute-start | bytes 98312 | tf_op jit(solution)/shard_map/ppermute | solution.py:235
  39.8 9.6 %collective-permute-start.7 = (bf16[1024,128]{1,0:T(8,128)(2,1)S(1)}, bf16[1024,128]{1,0:T(8,128)(2,1)S(1)}, u32[]{:S(2)}, u32[]{:S(2)}) collective-permute-start(bf16[1024,128]{1,0:T(8,128)(2,1)S(1)} %get-tuple-element.37), channel_id=1, source_target_pairs={{0,1},{1,0},{2,3},{3,2},{4,5},{5,4},{6,7},{7,6},{8,9},{9,8},{10,11... | collective-permute-start | bytes 786440 | tf_op jit(solution)/shard_map/ppermute | solution.py:235
  39.8 9.5 %collective-permute-start.8 = (bf16[1024,128]{1,0:T(8,128)(2,1)S(1)}, bf16[1024,128]{1,0:T(8,128)(2,1)S(1)}, u32[]{:S(2)}, u32[]{:S(2)}) collective-permute-start(bf16[1024,128]{1,0:T(8,128)(2,1)S(1)} %get-tuple-element.38), channel_id=1, source_target_pairs={{0,2},{1,3},{2,0},{3,1},{4,6},{5,7},{6,4},{7,5},{8,10},{9,11},{10,... | collective-permute-start | bytes 786440 | tf_op jit(solution)/shard_map/ppermute | solution.py:235
  41.7 6.7 %collective-permute-start.12 = (f32[2,16,128]{2,1,0:T(8,128)S(1)}, f32[2,16,128]{2,1,0:T(8,128)S(1)}, u32[]{:S(2)}, u32[]{:S(2)}) collective-permute-start(f32[2,16,128]{2,1,0:T(8,128)S(1)} %slice_bitcast_fusion), channel_id=1, source_target_pairs={{0,2},{1,3},{2,0},{3,1},{4,6},{5,7},{6,4},{7,5},{8,10},{9,11},{10,... | collective-permute-start | bytes 49160 | tf_op jit(solution)/shard_map/ppermute | solution.py:235
  48.3 4.7 %collective-permute-start.13 = (f32[2,2,8,128]{3,2,1,0:T(8,128)S(1)}, f32[2,2,8,128]{3,2,1,0:T(8,128)S(1)}, u32[]{:S(2)}, u32[]{:S(2)}) collective-permute-start(f32[2,2,8,128]{3,2,1,0:T(8,128)S(1)} %fusion.1), channel_id=1, source_target_pairs={{0,4},{1,5},{2,6},{3,7},{4,0},{5,1},{6,2},{7,3},{8,12},{9,13},{10,... | collective-permute-start | bytes 49160 | tf_op jit(solution)/shard_map/ppermute | solution.py:235
  49.4 5.0 %collective-permute-start.9 = (bf16[512,128]{1,0:T(8,128)(2,1)S(1)}, bf16[512,128]{1,0:T(8,128)(2,1)S(1)}, u32[]{:S(2)}, u32[]{:S(2)}) collective-permute-start(bf16[512,128]{1,0:T(8,128)(2,1)S(1)} %get-tuple-element.40), channel_id=1, source_target_pairs={{0,2},{1,3},{2,0},{3,1},{4,6},{5,7},{6,4},{7,5},{8,10},{9,11},{10,... | collective-permute-start | bytes 393224 | tf_op jit(solution)/shard_map/ppermute | solution.py:235
  50.7 5.0 %collective-permute-start.10 = (bf16[512,128]{1,0:T(8,128)(2,1)S(1)}, bf16[512,128]{1,0:T(8,128)(2,1)S(1)}, u32[]{:S(2)}, u32[]{:S(2)}) collective-permute-start(bf16[512,128]{1,0:T(8,128)(2,1)S(1)} %get-tuple-element.42), channel_id=1, source_target_pairs={{0,1},{1,0},{2,3},{3,2},{4,5},{5,4},{6,7},{7,6},{8,9},{9,8},{10,11... | collective-permute-start | bytes 393224 | tf_op jit(solution)/shard_map/ppermute | solution.py:235
  55.7 5.9 %collective-permute-start.14 = (bf16[256,128]{1,0:T(8,128)(2,1)S(1)}, bf16[256,128]{1,0:T(8,128)(2,1)S(1)}, u32[]{:S(2)}, u32[]{:S(2)}) collective-permute-start(bf16[256,128]{1,0:T(8,128)(2,1)S(1)} %get-tuple-element.45), channel_id=1, source_target_pairs={{0,4},{1,5},{2,6},{3,7},{4,0},{5,1},{6,2},{7,3},{8,12},{9,13},{10,... | collective-permute-start | bytes 196616 | tf_op jit(solution)/shard_map/ppermute | solution.py:235

commit v4 on v3

--- a/solution.py
+++ b/solution.py
@@ -18,15 +18,16 @@
 BF16 = jnp.bfloat16
 
 
-def call(body, out_shape, name, in_specs=None, aliases={}):
+def call(body, out_shape, name, in_specs=None, aliases={}, scratch=(), cost=0):
     kwargs = {} if in_specs is None else {"in_specs": in_specs}
     return pl.pallas_call(
         body,
         out_shape=out_shape,
         input_output_aliases=aliases,
+        scratch_shapes=list(scratch),
         name=name,
-        cost_estimate=pl.CostEstimate(flops=0, bytes_accessed=0, transcendentals=0),
-        compiler_params=pltpu.CompilerParams(vmem_limit_bytes=48 * 1024 * 1024),
+        cost_estimate=pl.CostEstimate(flops=0, bytes_accessed=cost, transcendentals=0),
+        compiler_params=pltpu.CompilerParams(vmem_limit_bytes=20 * 1024 * 1024),
         **kwargs,
     )
 
@@ -50,19 +51,25 @@
     out_ref[rows:] = digits.astype(F32).astype(BF16)
 
 
+def turn_units(source, units_ref, turned_ref):
+    count = source.shape[0]
+    together = min(count, 8)
+
+    def step(index, carry):
+        for offset in range(together):
+            at = index * together + offset
+            units = unit(source[at])[0].astype(BF16)
+            units_ref[at] = units
+            turned_ref[at] = units.T
+        return carry
+
+    lax.fori_loop(0, count // together, step, 0)
+
+
 def unit_body(*refs):
-    half = len(refs) // 2
-    for source, out_ref in zip(refs[:half], refs[half:]):
-        count = source.shape[0]
-        together = min(count, 8)
-
-        def step(index, carry, source=source, out_ref=out_ref, together=together):
-            for offset in range(together):
-                at = index * together + offset
-                out_ref[at] = unit(source[at])[0].astype(BF16)
-            return carry
-
-        lax.fori_loop(0, count // together, step, 0)
+    half = len(refs) // 3
+    for index, source in enumerate(refs[:half]):
+        turn_units(source, refs[half + 2 * index], refs[half + 2 * index + 1])
 
 
 def route_body(docs_ref, *refs, rows, size, list_len):
@@ -123,28 +130,27 @@
         list_ref[piece, 2] = count
 
 
-def score_pairs(piece, list_ref, pay_ref, pass_ref, acc_ref, sums_ref, length):
+def score_pairs(list_ref, pay_ref, pass_ref, turned_ref, acc_ref, sums_ref, length):
     queries = sums_ref.shape[0] // 2
-    count = list_ref[piece, 2, 0, 0]
-    contract = (((1,), (1,)), ((), ()))
+    count = list_ref[2, 0, 0]
 
     def step(index, carry):
         pairs = []
         for offset in range(UNROLL):
             slot = index * UNROLL + offset
             part, lane = lax.shift_right_logical(slot, 7), slot & (LANES - 1)
-            code = list_ref[piece, 0, part, lane]
+            code = list_ref[0, part, lane]
             row = pl.multiple_of(code & (SHIFT - 1), 16)
-            passage = pass_ref[lax.shift_right_logical(code, SHIFT.bit_length() - 1)]
-            pairs.append((list_ref[piece, 1, part, lane], pay_ref[pl.ds(row, length)], passage))
+            place = lax.shift_right_logical(code, SHIFT.bit_length() - 1)
+            pairs.append((list_ref[1, part, lane], pay_ref[pl.ds(row, length)], place))
         logits = [
-            lax.dot_general(tokens, passage, contract, preferred_element_type=F32)
-            for _, tokens, passage in pairs
+            jnp.dot(tokens, turned_ref[place], preferred_element_type=F32)
+            for _, tokens, place in pairs
         ]
         terms = [jnp.exp(block * (1.0 / SOFTNESS)) for block in logits]
         masses = [jnp.sum(block, axis=1, keepdims=True) for block in terms]
         pulled = [
-            jnp.dot(block.astype(BF16), pair[2], preferred_element_type=F32)
+            jnp.dot(block.astype(BF16), pass_ref[pair[2]], preferred_element_type=F32)
             for block, pair in zip(terms, pairs)
         ]
         done = []
@@ -163,25 +169,37 @@
     lax.fori_loop(0, lax.div(count + UNROLL - 1, UNROLL), step, 0)
 
 
-def near_score_body(list_ref, pay_ref, *refs, length):
-    *pass_refs, acc_ref, sums_ref = refs
+def near_score_body(lists_ref, pay_ref, *refs, length):
+    *pass_refs, acc_ref, sums_ref, list_ref, sem = refs
+    move = pltpu.make_async_copy(lists_ref.at[: len(pass_refs) // 2], list_ref, sem)
+    move.start()
     acc_ref[...] = jnp.zeros_like(acc_ref)
     sums_ref[...] = jnp.zeros_like(sums_ref)
-    for piece, pass_ref in enumerate(pass_refs):
-        score_pairs(piece, list_ref, pay_ref, pass_ref, acc_ref, sums_ref, length)
-
-
-def score_body(list_ref, pay_ref, pass_ref, _, __, acc_ref, sums_ref, *, piece, length):
-    score_pairs(piece, list_ref, pay_ref, pass_ref, acc_ref, sums_ref, length)
-
-
-def last_score_body(
-    list_ref, pay_ref, pass_ref, _, __, acc_ref, sums_ref, others_ref, firsts_ref, *, piece, length
-):
-    score_pairs(piece, list_ref, pay_ref, pass_ref, acc_ref, sums_ref, length)
-    half = others_ref.shape[0]
-    others_ref[...] = acc_ref[half : 2 * half].astype(BF16)
-    firsts_ref[...] = acc_ref[3 * half : 4 * half].astype(BF16)
+    move.wait()
+    for piece in range(len(pass_refs) // 2):
+        score_pairs(
+            list_ref.at[piece],
+            pay_ref,
+            pass_refs[2 * piece],
+            pass_refs[2 * piece + 1],
+            acc_ref,
+            sums_ref,
+            length,
+        )
+
+
+def far_score_body(lists_ref, pay_ref, raw_ref, _, __, acc_ref, sums_ref, *refs, piece, length):
+    *send_refs, pass_ref, turned_ref, list_ref, sem = refs
+    move = pltpu.make_async_copy(lists_ref.at[piece], list_ref, sem)
+    move.start()
+    turn_units(raw_ref, pass_ref, turned_ref)
+    move.wait()
+    score_pairs(list_ref, pay_ref, pass_ref, turned_ref, acc_ref, sums_ref, length)
+    if send_refs:
+        others_ref, firsts_ref = send_refs
+        half = others_ref.shape[0]
+        others_ref[...] = acc_ref[half : 2 * half].astype(BF16)
+        firsts_ref[...] = acc_ref[3 * half : 4 * half].astype(BF16)
 
 
 def halve_body(acc_ref, others_ref, firsts_ref, send_a, send_b, keep_a, keep_b):
@@ -270,14 +288,27 @@
     half_bit = group_count // 2
     far_raw = swap(passages, "group", half_bit)
     near_raw = spread(passages)
-    payload = call(pack_body, shape((rows + TAIL, width), BF16), "query_units")(queries, candidates)
+    hbm, smem, vmem = (
+        pl.BlockSpec(memory_space=space) for space in (pltpu.HBM, pltpu.SMEM, pltpu.VMEM)
+    )
+    payload = call(
+        pack_body,
+        shape((rows + TAIL, width), BF16),
+        "query_units",
+        [vmem, vmem],
+    )(queries, candidates)
 
     *first_bits, low, lowest = bits_of(dev_count)
     pay = payload[None]
     for bit in first_bits:
         pay = jnp.concatenate([pay, swap(pay, "dev", bit)], axis=0)
+    turned = shape((pass_count, width, pass_len), BF16)
+    near = call(unit_body, [shape(passages.shape, BF16), turned] * len(near_raw), "passage_units")(
+        *near_raw
+    )
     pay_low = swap(pay, "dev", low)
     pays = [pay, pay_low, swap(pay, "dev", lowest), swap(pay_low, "dev", lowest)]
+    pays[3], near = lax.optimization_barrier((pays[3], near))
 
     near_offsets = spread_offsets(half_bit)
     offsets = near_offsets + [offset ^ half_bit for offset in near_offsets]
@@ -292,7 +323,6 @@
     docs = jnp.sum(jnp.where(hits, documents[None, :], 0), axis=1)
 
     parts = -(-dev_count * min(pair_count, slot_cap) // LANES)
-    smem, vmem = (pl.BlockSpec(memory_space=space) for space in (pltpu.SMEM, pltpu.VMEM))
     pay, lists = call(
         functools.partial(route_body, rows=rows, size=pass_count, list_len=list_len),
         [
@@ -310,26 +340,33 @@
         shape((2 * all_queries + 1, LANES), F32),
     ]
     sends = [shape((half_rows, width), BF16)] * 2
-    near = call(unit_body, [shape(passages.shape, BF16)] * len(near_raw), "passage_units")(*near_raw)
     state = call(
         functools.partial(near_score_body, length=length),
         totals,
         "score_near",
-        in_specs=[smem] + [vmem] * (1 + len(near)),
+        [vmem] * (2 + len(near)),
+        scratch=[
+            pltpu.SMEM((len(near_raw), 3, parts, LANES), jnp.int32),
+            pltpu.SemaphoreType.DMA(()),
+        ],
     )(lists, pay, *near)
     far_raw, *state = lax.optimization_barrier((far_raw, *state))
-    far = spread(call(unit_body, shape(passages.shape, BF16), "passage_units")(far_raw))
-    for index, held in enumerate(far):
+    far = spread(far_raw)
+    for index, raw in enumerate(far):
         last = index == len(far) - 1
         state = call(
-            functools.partial(
-                last_score_body if last else score_body, piece=len(near) + index, length=length
-            ),
+            functools.partial(far_score_body, piece=len(far) + index, length=length),
             totals + (sends if last else []),
             "score_far",
-            in_specs=[smem] + [vmem] * 4,
-            aliases={3: 0, 4: 1},
-        )(lists, pay, held, *state)
+            [vmem] * 5,
+            {3: 0, 4: 1},
+            [
+                pltpu.VMEM(passages.shape, BF16),
+                pltpu.VMEM(turned.shape, BF16),
+                pltpu.SMEM((3, parts, LANES), jnp.int32),
+                pltpu.SemaphoreType.DMA(()),
+            ],
+        )(lists, pay, raw, *state)
     acc, sums, others, firsts = state
 
     steps = bits_of(dev_count)[::-1]

time: 63.1 us -> 58.6 us (0.929)
  waiting for transfers between devices: 26.8 us -> 21.6 us
    ppermute x15, waiting for transfers between devices: 26.8 us -> 21.6 us  [swap(): lax.ppermute(value, axis, [(index, index ^ bit) for index in range(size)])]
    pallas_call x5 -> x4, Pallas kernels: 6.76 us -> 7.81 us  [the longest x2 5.66 us: local(): call(functools.partial(far_score_body, piece=len(far) + index, length=len...]
  transfers between devices with their start and end apart: 15 -> 15, of which waited for: 10 -> 9; matrix products, arithmetic and copies ran while one was open for 2% -> 2% of each run, Pallas kernels for 13% -> 17%
where the time goes in v4:
time: 58.6 us; the launch traced here: 58.3 us
  waiting for transfers between devices  21.6 us (37%)
  starting transfers between devices  19.2 us (33%)
  Pallas kernels  13 us (22%)
  local copies, waits for them, and re-layouts  2.78 us (5%)
  other arithmetic  0.98 us (2%)
  between operations  0.79 us (1%)
    ppermute x15, waiting for transfers between devices, swap(): lax.ppermute(value, axis, [(index, index ^ bit) for index in range(size)])  21.6 us
    ppermute x15, starting transfers between devices, swap(): lax.ppermute(value, axis, [(index, index ^ bit) for index in range(size)])  19.2 us
    pallas_call x2, Pallas kernels, local(): call(functools.partial(far_score_body, piece=len(far) + index, length=len...  5.66 us
    pallas_call x1, Pallas kernels, local(): call(functools.partial(near_score_body, length=length), totals, 'score_ne...  2.82 us
    unnamed x8, local copies, waits for them, and re-layouts  2.75 us
    pallas_call x1, Pallas kernels, local(): call(unit_body, [shape(passages.shape, BF16), turned] * len(near_raw), 'p...  2.01 us
    pallas_call x1, Pallas kernels, local(): call(functools.partial(route_body, rows=rows, size=pass_count, list_len=l...  1.3 us
  transfers between devices with their start and end apart: 15, of which 9 were waited for; matrix products, arithmetic and copies ran while one was open for 2% of the time, Pallas kernels for 17%

profile of v4, /device:TPU:0, one launch (start us, length us, event | category | flops | bytes accessed | tf_op | source)
XLA Modules:
  0.0 58.3 jit_solution(4140023923495254017)
XLA Ops:
  0.6 0.5 collective-permute-start.4
  1.1 2.6 %collective-permute-start.5 = (bf16[16,256,128]{2,1,0:T(8,128)(2,1)}, bf16[16,256,128]{2,1,0:T(8,128)(2,1)S(1)}, u32[]{:S(2)}, u32[]{:S(2)}) collective-permute-start(bf16[16,256,128]{2,1,0:T(8,128)(2,1)} %refs_0_.1), channel_id=1, source_target_pairs={{0,16},{8,24},{16,0},{24,8},{1,17},{9,25},{17,1},{25,9},{2,18},{10... | collective-permute-start | bytes 3145736 | tf_op jit(solution)/shard_map/ppermute | solution.py:253
  3.7 0.0 copy-start.1
  3.7 0.8 %copy-done.1 = bf16[8,32,128]{2,1,0:T(8,128)(2,1)S(1)} copy-done((bf16[8,32,128]{2,1,0:T(8,128)(2,1)S(1)}, bf16[8,32,128]{2,1,0:T(8,128)(2,1)}, u32[]{:S(2)}) %copy-start.1) | copy-done | bytes 65560
  4.6 0.0 copy-start.3
  4.6 0.7 %copy-done.3 = s32[8,16]{1,0:T(8,128)S(1)} copy-done((s32[8,16]{1,0:T(8,128)S(1)}, s32[8,16]{1,0:T(8,128)}, u32[]{:S(2)}) %copy-start.3) | copy-done | bytes 536
  5.2 0.1 query_units.1
  5.4 2.7 %collective-permute-start = (bf16[1,272,128]{2,1,0:T(8,128)(2,1)S(1)}, bf16[1,272,128]{2,1,0:T(8,128)(2,1)S(1)}, u32[]{:S(2)}, u32[]{:S(2)}) collective-permute-start(bf16[1,272,128]{2,1,0:T(8,128)(2,1)S(1)} %bitcast.26), channel_id=1, source_target_pairs={{0,4},{1,5},{2,6},{3,7},{4,0},{5,1},{6,2},{7,3},{8,12},{9,13},{10,... | collective-permute-start | bytes 208904 | tf_op jit(solution)/shard_map/ppermute | solution.py:253
  8.0 4.1 %collective-permute-done = bf16[1,272,128]{2,1,0:T(8,128)(2,1)S(1)} collective-permute-done((bf16[1,272,128]{2,1,0:T(8,128)(2,1)S(1)}, bf16[1,272,128]{2,1,0:T(8,128)(2,1)S(1)}, u32[]{:S(2)}, u32[]{:S(2)}) %collective-permute-start) | collective-permute-done | bytes 69664 | tf_op jit(solution)/shard_map/ppermute | solution.py:253
  12.2 0.7 %collective-permute-start.1 = (bf16[2,272,128]{2,1,0:T(8,128)(2,1)S(1)}, bf16[2,272,128]{2,1,0:T(8,128)(2,1)S(1)}, u32[]{:S(2)}, u32[]{:S(2)}) collective-permute-start(bf16[2,272,128]{2,1,0:T(8,128)(2,1)S(1)} %pad_maximum_fusion.refs_0_), channel_id=1, source_target_pairs={{0,2},{1,3},{2,0},{3,1},{4,6},{5,7},{6,4},{7,5},{8,10},{9,11},{10,... | collective-permute-start | bytes 417800 | tf_op jit(solution)/shard_map/ppermute | solution.py:253
  12.9 1.5 %collective-permute-start.2 = (bf16[2,272,128]{2,1,0:T(8,128)(2,1)S(1)}, bf16[2,272,128]{2,1,0:T(8,128)(2,1)S(1)}, u32[]{:S(2)}, u32[]{:S(2)}) collective-permute-start(bf16[2,272,128]{2,1,0:T(8,128)(2,1)S(1)} %pad_maximum_fusion.refs_0_), channel_id=1, source_target_pairs={{0,1},{1,0},{2,3},{3,2},{4,5},{5,4},{6,7},{7,6},{8,9},{9,8},{10,11... | collective-permute-start | bytes 417800 | tf_op jit(solution)/shard_map/ppermute | solution.py:253
  14.4 2.9 %collective-permute-done.1.refs_1_ = bf16[2,272,128]{2,1,0:T(8,128)(2,1)S(1)} collective-permute-done((bf16[2,272,128]{2,1,0:T(8,128)(2,1)S(1)}, bf16[2,272,128]{2,1,0:T(8,128)(2,1)S(1)}, u32[]{:S(2)}, u32[]{:S(2)}) %collective-permute-start.1) | collective-permute-done | bytes 139296 | tf_op jit(solution)/shard_map/ppermute | solution.py:253
  17.3 1.5 %collective-permute-start.3 = (bf16[2,272,128]{2,1,0:T(8,128)(2,1)S(1)}, bf16[2,272,128]{2,1,0:T(8,128)(2,1)S(1)}, u32[]{:S(2)}, u32[]{:S(2)}) collective-permute-start(bf16[2,272,128]{2,1,0:T(8,128)(2,1)S(1)} %collective-permute-done.1.refs_1_), channel_id=1, source_target_pairs={{0,1},{1,0},{2,3},{3,2},{4,5},{5,4},{6,7},{7,6},{8,9},{9,8},{10,11... | collective-permute-start | bytes 417800 | tf_op jit(solution)/shard_map/ppermute | solution.py:253
  18.8 0.1 pad_add_fusion
  18.9 0.9 %select_reduce_fusion.docs_ref = s32[64]{0:T(128)S(1)} fusion(s32[512]{0:T(512)} %param.7, s32[64]{0:T(128)S(1)} %pad_add_fusion), kind=kLoop, calls=%fused_computation.1 | loop fusion | flops 98240 | bytes 2560 | tf_op jit(solution)/shard_map/reduce_sum | solution.py:323
  19.8 0.0 collective-permute-done.4.refs_1_
  19.8 0.0 copy-start
  19.8 1.2 %copy-done = bf16[16,256,128]{2,1,0:T(8,128)(2,1)S(1)} copy-done((bf16[16,256,128]{2,1,0:T(8,128)(2,1)S(1)}, bf16[16,256,128]{2,1,0:T(8,128)(2,1)}, u32[]{:S(2)}) %copy-start) | copy-done | bytes 1048600
  21.0 2.0 %passage_units.1 = (bf16[16,256,128]{2,1,0:T(8,128)(2,1)S(1)}, bf16[16,128,256]{2,1,0:T(8,128)(2,1)S(1)}, bf16[16,256,128]{2,1,0:T(8,128)(2,1)S(1)}, bf16[16,128,256]{2,1,0:T(8,128)(2,1)S(1)}) custom-call(bf16[16,256,128]{2,1,0:T(8,128)(2,1)S(1)} %copy-done, bf16[16,256,128]{2,1,0:T(8,128)(2,1)S(1)} %collective-permute-done.4.refs_1_), custom_call_target="tpu_custom_call" | custom-call | tf_op jit(solution)/shard_map/passage_units/pallas_call | solution.py:306
  23.0 0.0 collective-permute-done.3.refs_3_
  23.0 0.0 collective-permute-done.2.refs_2_
  23.0 1.3 %route.1 = (bf16[2176,128]{1,0:T(8,128)(2,1)S(1)}, s32[4,3,1,128]{3,2,1,0:T(1,128)S(1)}) custom-call(s32[64]{0:T(128)S(1)} %select_reduce_fusion.docs_ref, bf16[2,272,128]{2,1,0:T(8,128)(2,1)S(1)} %pad_maximum_fusion.refs_0_, bf16[2,272,128]{2,1,0:T(8,128)(2,1)S(1)} %collective-permute-done.1.refs_1_, ...), custom_call_target="tpu_custom_call" | custom-call | tf_op jit(solution)/shard_map/route/pallas_call | solution.py:326
  24.3 2.8 %score_near.1 = (f32[4128,128]{1,0:T(8,128)S(1)}, f32[129,128]{1,0:T(8,128)S(1)}) custom-call(s32[4,3,1,128]{3,2,1,0:T(1,128)S(1)} %get-tuple-element.37.lists_ref, bf16[2176,128]{1,0:T(8,128)(2,1)S(1)} %get-tuple-element.38.pay_ref, bf16[16,256,128]{2,1,0:T(8,128)(2,1)S(1)} %get-tuple-element.39.refs_0_, ...), custom_call_target="tpu_custom_call" | custom-call | tf_op jit(solution)/shard_map/score_near/pallas_call | solution.py:343
  27.2 0.5 collective-permute-done.5.raw_ref
  27.7 0.0 collective-permute-start.6
  27.7 3.7 %score_far.2 = (f32[4128,128]{1,0:T(8,128)S(1)}, f32[129,128]{1,0:T(8,128)S(1)}) custom-call(s32[4,3,1,128]{3,2,1,0:T(1,128)S(1)} %get-tuple-element.37.lists_ref, bf16[2176,128]{1,0:T(8,128)(2,1)S(1)} %get-tuple-element.38.pay_ref, bf16[16,256,128]{2,1,0:T(8,128)(2,1)S(1)} %collective-permute-done.5.raw_ref, ...), custom_call_target="tpu_custom_call", output_to_operand_aliasing={{0}: (3, {}), {1}: (4, {})} | custom-call | tf_op jit(solution)/shard_map/score_far/pallas_call | solution.py:357
  31.4 0.0 collective-permute-done.6.raw_ref
  31.4 2.0 %score_far.3 = (f32[4128,128]{1,0:T(8,128)S(1)}, f32[129,128]{1,0:T(8,128)S(1)}, bf16[1024,128]{1,0:T(8,128)(2,1)S(1)}, bf16[1024,128]{1,0:T(8,128)(2,1)S(1)}) custom-call(s32[4,3,1,128]{3,2,1,0:T(1,128)S(1)} %get-tuple-element.37.lists_ref, bf16[2176,128]{1,0:T(8,128)(2,1)S(1)} %get-tuple-element.38.pay_ref, ...), custom_call_target="tpu_custom_call", output_to_operand_aliasing={{0}: (3, {}), {1}: (4, {})} | custom-call | tf_op jit(solution)/shard_map/score_far/pallas_call | solution.py:357
  33.4 0.0 copy-start.2
  33.4 0.8 %collective-permute-start.11 = (f32[2,2,16,128]{3,2,1,0:T(8,128)S(1)}, f32[2,2,16,128]{3,2,1,0:T(8,128)S(1)}, u32[]{:S(2)}, u32[]{:S(2)}) collective-permute-start(f32[2,2,16,128]{3,2,1,0:T(8,128)S(1)} %pad_maximum_fusion.1), channel_id=1, source_target_pairs={{0,1},{1,0},{2,3},{3,2},{4,5},{5,4},{6,7},{7,6},{8,9},{9,8},{10,11... | collective-permute-start | bytes 98312 | tf_op jit(solution)/shard_map/ppermute | solution.py:253
  34.3 1.3 %collective-permute-start.7 = (bf16[1024,128]{1,0:T(8,128)(2,1)S(1)}, bf16[1024,128]{1,0:T(8,128)(2,1)S(1)}, u32[]{:S(2)}, u32[]{:S(2)}) collective-permute-start(bf16[1024,128]{1,0:T(8,128)(2,1)S(1)} %get-tuple-element.51), channel_id=1, source_target_pairs={{0,1},{1,0},{2,3},{3,2},{4,5},{5,4},{6,7},{7,6},{8,9},{9,8},{10,11... | collective-permute-start | bytes 786440 | tf_op jit(solution)/shard_map/ppermute | solution.py:253
  35.5 1.2 %collective-permute-start.8 = (bf16[1024,128]{1,0:T(8,128)(2,1)S(1)}, bf16[1024,128]{1,0:T(8,128)(2,1)S(1)}, u32[]{:S(2)}, u32[]{:S(2)}) collective-permute-start(bf16[1024,128]{1,0:T(8,128)(2,1)S(1)} %get-tuple-element.52), channel_id=1, source_target_pairs={{0,2},{1,3},{2,0},{3,1},{4,6},{5,7},{6,4},{7,5},{8,10},{9,11},{10,... | collective-permute-start | bytes 786440 | tf_op jit(solution)/shard_map/ppermute | solution.py:253
  36.8 1.0 %collective-permute-done.11 = f32[2,2,16,128]{3,2,1,0:T(8,128)S(1)} collective-permute-done((f32[2,2,16,128]{3,2,1,0:T(8,128)S(1)}, f32[2,2,16,128]{3,2,1,0:T(8,128)S(1)}, u32[]{:S(2)}, u32[]{:S(2)}) %collective-permute-start.11) | collective-permute-done | bytes 32800 | tf_op jit(solution)/shard_map/ppermute | solution.py:253
  37.8 1.3 %collective-permute-start.12 = (f32[2,16,128]{2,1,0:T(8,128)S(1)}, f32[2,16,128]{2,1,0:T(8,128)S(1)}, u32[]{:S(2)}, u32[]{:S(2)}) collective-permute-start(f32[2,16,128]{2,1,0:T(8,128)S(1)} %slice_bitcast_fusion), channel_id=1, source_target_pairs={{0,2},{1,3},{2,0},{3,1},{4,6},{5,7},{6,4},{7,5},{8,10},{9,11},{10,... | collective-permute-start | bytes 49160 | tf_op jit(solution)/shard_map/ppermute | solution.py:253
  39.1 5.4 %collective-permute-done.12 = f32[2,16,128]{2,1,0:T(8,128)S(1)} collective-permute-done((f32[2,16,128]{2,1,0:T(8,128)S(1)}, f32[2,16,128]{2,1,0:T(8,128)S(1)}, u32[]{:S(2)}, u32[]{:S(2)}) %collective-permute-start.12) | collective-permute-done | bytes 16416 | tf_op jit(solution)/shard_map/ppermute | solution.py:253
  44.5 1.0 %collective-permute-start.13 = (f32[2,2,8,128]{3,2,1,0:T(8,128)S(1)}, f32[2,2,8,128]{3,2,1,0:T(8,128)S(1)}, u32[]{:S(2)}, u32[]{:S(2)}) collective-permute-start(f32[2,2,8,128]{3,2,1,0:T(8,128)S(1)} %fusion.1), channel_id=1, source_target_pairs={{0,4},{1,5},{2,6},{3,7},{4,0},{5,1},{6,2},{7,3},{8,12},{9,13},{10,... | collective-permute-start | bytes 49160 | tf_op jit(solution)/shard_map/ppermute | solution.py:253
  45.5 0.0 collective-permute-done.7.others_ref
  45.5 0.0 collective-permute-done.8.firsts_ref
  45.5 0.1 halve.1
  45.6 1.6 %collective-permute-start.10 = (bf16[512,128]{1,0:T(8,128)(2,1)S(1)}, bf16[512,128]{1,0:T(8,128)(2,1)S(1)}, u32[]{:S(2)}, u32[]{:S(2)}) collective-permute-start(bf16[512,128]{1,0:T(8,128)(2,1)S(1)} %get-tuple-element.56), channel_id=1, source_target_pairs={{0,1},{1,0},{2,3},{3,2},{4,5},{5,4},{6,7},{7,6},{8,9},{9,8},{10,11... | collective-permute-start | bytes 393224 | tf_op jit(solution)/shard_map/ppermute | solution.py:253
  47.2 1.6 %collective-permute-start.9 = (bf16[512,128]{1,0:T(8,128)(2,1)S(1)}, bf16[512,128]{1,0:T(8,128)(2,1)S(1)}, u32[]{:S(2)}, u32[]{:S(2)}) collective-permute-start(bf16[512,128]{1,0:T(8,128)(2,1)S(1)} %get-tuple-element.54), channel_id=1, source_target_pairs={{0,2},{1,3},{2,0},{3,1},{4,6},{5,7},{6,4},{7,5},{8,10},{9,11},{10,... | collective-permute-start | bytes 393224 | tf_op jit(solution)/shard_map/ppermute | solution.py:253
  48.8 0.4 collective-permute-done.13
  49.2 1.4 %collective-permute-done.10.got_firsts = bf16[512,128]{1,0:T(8,128)(2,1)S(1)} collective-permute-done((bf16[512,128]{1,0:T(8,128)(2,1)S(1)}, bf16[512,128]{1,0:T(8,128)(2,1)S(1)}, u32[]{:S(2)}, u32[]{:S(2)}) %collective-permute-start.10) | collective-permute-done | bytes 131104 | tf_op jit(solution)/shard_map/ppermute | solution.py:253
  50.7 1.5 %collective-permute-done.9.got_others = bf16[512,128]{1,0:T(8,128)(2,1)S(1)} collective-permute-done((bf16[512,128]{1,0:T(8,128)(2,1)S(1)}, bf16[512,128]{1,0:T(8,128)(2,1)S(1)}, u32[]{:S(2)}, u32[]{:S(2)}) %collective-permute-start.9) | collective-permute-done | bytes 131104 | tf_op jit(solution)/shard_map/ppermute | solution.py:253
  52.2 0.1 merge.1
  52.2 0.9 %collective-permute-start.14 = (bf16[256,128]{1,0:T(8,128)(2,1)S(1)}, bf16[256,128]{1,0:T(8,128)(2,1)S(1)}, u32[]{:S(2)}, u32[]{:S(2)}) collective-permute-start(bf16[256,128]{1,0:T(8,128)(2,1)S(1)} %get-tuple-element.59), channel_id=1, source_target_pairs={{0,4},{1,5},{2,6},{3,7},{4,0},{5,1},{6,2},{7,3},{8,12},{9,13},{10,... | collective-permute-start | bytes 196616 | tf_op jit(solution)/shard_map/ppermute | solution.py:253
  53.2 4.3 %collective-permute-done.14.got_ref = bf16[256,128]{1,0:T(8,128)(2,1)S(1)} collective-permute-done((bf16[256,128]{1,0:T(8,128)(2,1)S(1)}, bf16[256,128]{1,0:T(8,128)(2,1)S(1)}, u32[]{:S(2)}, u32[]{:S(2)}) %collective-permute-start.14) | collective-permute-done | bytes 65568 | tf_op jit(solution)/shard_map/ppermute | solution.py:253
  57.5 0.0 copy-done.2
  57.5 0.9 %last.1 = (f32[8,32,128]{2,1,0:T(8,128)}, f32[1,8]{1,0:T(1,128)}) custom-call(bf16[8,32,128]{2,1,0:T(8,128)(2,1)S(1)} %copy-done.2, f32[256,128]{1,0:T(8,128)S(1)} %get-tuple-element.58.keep_ref, bf16[256,128]{1,0:T(8,128)(2,1)S(1)} %collective-permute-done.14.got_ref, f32[2,8,128]{2,1,0:T(8,128)S(1)} %slice.52.sums_ref), custom_call_target="tpu_custom_call" | custom-call | tf_op jit(solution)/shard_map/last/pallas_call | solution.py:402
  (13 shorter events, 0.1 us)
Async XLA Ops:
  0.6 19.1 %collective-permute-start.4 = (bf16[16,256,128]{2,1,0:T(8,128)(2,1)}, bf16[16,256,128]{2,1,0:T(8,128)(2,1)S(1)}, u32[]{:S(2)}, u32[]{:S(2)}) collective-permute-start(bf16[16,256,128]{2,1,0:T(8,128)(2,1)} %refs_0_.1), channel_id=1, source_target_pairs={{0,8},{8,0},{16,24},{24,16},{1,9},{9,1},{17,25},{25,17},{2,10},{10... | collective-permute-start | bytes 3145736 | tf_op jit(solution)/shard_map/ppermute | solution.py:253
  1.1 26.5 %collective-permute-start.5 = (bf16[16,256,128]{2,1,0:T(8,128)(2,1)}, bf16[16,256,128]{2,1,0:T(8,128)(2,1)S(1)}, u32[]{:S(2)}, u32[]{:S(2)}) collective-permute-start(bf16[16,256,128]{2,1,0:T(8,128)(2,1)} %refs_0_.1), channel_id=1, source_target_pairs={{0,16},{8,24},{16,0},{24,8},{1,17},{9,25},{17,1},{25,9},{2,18},{10... | collective-permute-start | bytes 3145736 | tf_op jit(solution)/shard_map/ppermute | solution.py:253
  3.7 0.8 %copy-start.1 = (bf16[8,32,128]{2,1,0:T(8,128)(2,1)S(1)}, bf16[8,32,128]{2,1,0:T(8,128)(2,1)}, u32[]{:S(2)}) copy-start(bf16[8,32,128]{2,1,0:T(8,128)(2,1)} %queries_ref.3) | copy-start | bytes 196612
  4.6 0.7 %copy-start.3 = (s32[8,16]{1,0:T(8,128)S(1)}, s32[8,16]{1,0:T(8,128)}, u32[]{:S(2)}) copy-start(s32[8,16]{1,0:T(8,128)} %cand_ref.1) | copy-start | bytes 1540
  5.4 6.8 %collective-permute-start = (bf16[1,272,128]{2,1,0:T(8,128)(2,1)S(1)}, bf16[1,272,128]{2,1,0:T(8,128)(2,1)S(1)}, u32[]{:S(2)}, u32[]{:S(2)}) collective-permute-start(bf16[1,272,128]{2,1,0:T(8,128)(2,1)S(1)} %bitcast.26), channel_id=1, source_target_pairs={{0,4},{1,5},{2,6},{3,7},{4,0},{5,1},{6,2},{7,3},{8,12},{9,13},{10,... | collective-permute-start | bytes 208904 | tf_op jit(solution)/shard_map/ppermute | solution.py:253
  12.2 5.1 %collective-permute-start.1 = (bf16[2,272,128]{2,1,0:T(8,128)(2,1)S(1)}, bf16[2,272,128]{2,1,0:T(8,128)(2,1)S(1)}, u32[]{:S(2)}, u32[]{:S(2)}) collective-permute-start(bf16[2,272,128]{2,1,0:T(8,128)(2,1)S(1)} %pad_maximum_fusion.refs_0_), channel_id=1, source_target_pairs={{0,2},{1,3},{2,0},{3,1},{4,6},{5,7},{6,4},{7,5},{8,10},{9,11},{10,... | collective-permute-start | bytes 417800 | tf_op jit(solution)/shard_map/ppermute | solution.py:253
  12.9 10.2 %collective-permute-start.2 = (bf16[2,272,128]{2,1,0:T(8,128)(2,1)S(1)}, bf16[2,272,128]{2,1,0:T(8,128)(2,1)S(1)}, u32[]{:S(2)}, u32[]{:S(2)}) collective-permute-start(bf16[2,272,128]{2,1,0:T(8,128)(2,1)S(1)} %pad_maximum_fusion.refs_0_), channel_id=1, source_target_pairs={{0,1},{1,0},{2,3},{3,2},{4,5},{5,4},{6,7},{7,6},{8,9},{9,8},{10,11... | collective-permute-start | bytes 417800 | tf_op jit(solution)/shard_map/ppermute | solution.py:253
  17.3 5.7 %collective-permute-start.3 = (bf16[2,272,128]{2,1,0:T(8,128)(2,1)S(1)}, bf16[2,272,128]{2,1,0:T(8,128)(2,1)S(1)}, u32[]{:S(2)}, u32[]{:S(2)}) collective-permute-start(bf16[2,272,128]{2,1,0:T(8,128)(2,1)S(1)} %collective-permute-done.1.refs_1_), channel_id=1, source_target_pairs={{0,1},{1,0},{2,3},{3,2},{4,5},{5,4},{6,7},{7,6},{8,9},{9,8},{10,11... | collective-permute-start | bytes 417800 | tf_op jit(solution)/shard_map/ppermute | solution.py:253
  19.8 1.2 %copy-start = (bf16[16,256,128]{2,1,0:T(8,128)(2,1)S(1)}, bf16[16,256,128]{2,1,0:T(8,128)(2,1)}, u32[]{:S(2)}) copy-start(bf16[16,256,128]{2,1,0:T(8,128)(2,1)} %refs_0_.1) | copy-start | bytes 3145732
  27.7 3.7 %collective-permute-start.6 = (bf16[16,256,128]{2,1,0:T(8,128)(2,1)S(1)}, bf16[16,256,128]{2,1,0:T(8,128)(2,1)S(1)}, u32[]{:S(2)}, u32[]{:S(2)}) collective-permute-start(bf16[16,256,128]{2,1,0:T(8,128)(2,1)S(1)} %collective-permute-done.5.raw_ref), channel_id=1, source_target_pairs={{0,8},{8,0},{16,24},{24,16},{1,9},{9,1},{17,25},{25,17},{2,10},{10... | collective-permute-start | bytes 3145736 | tf_op jit(solution)/shard_map/ppermute | solution.py:253
  33.4 24.1 %copy-start.2 = (bf16[8,32,128]{2,1,0:T(8,128)(2,1)S(1)}, bf16[8,32,128]{2,1,0:T(8,128)(2,1)}, u32[]{:S(2)}) copy-start(bf16[8,32,128]{2,1,0:T(8,128)(2,1)} %queries_ref.3) | copy-start | bytes 196612
  33.4 4.3 %collective-permute-start.11 = (f32[2,2,16,128]{3,2,1,0:T(8,128)S(1)}, f32[2,2,16,128]{3,2,1,0:T(8,128)S(1)}, u32[]{:S(2)}, u32[]{:S(2)}) collective-permute-start(f32[2,2,16,128]{3,2,1,0:T(8,128)S(1)} %pad_maximum_fusion.1), channel_id=1, source_target_pairs={{0,1},{1,0},{2,3},{3,2},{4,5},{5,4},{6,7},{7,6},{8,9},{9,8},{10,11... | collective-permute-start | bytes 98312 | tf_op jit(solution)/shard_map/ppermute | solution.py:253
  34.3 11.2 %collective-permute-start.7 = (bf16[1024,128]{1,0:T(8,128)(2,1)S(1)}, bf16[1024,128]{1,0:T(8,128)(2,1)S(1)}, u32[]{:S(2)}, u32[]{:S(2)}) collective-permute-start(bf16[1024,128]{1,0:T(8,128)(2,1)S(1)} %get-tuple-element.51), channel_id=1, source_target_pairs={{0,1},{1,0},{2,3},{3,2},{4,5},{5,4},{6,7},{7,6},{8,9},{9,8},{10,11... | collective-permute-start | bytes 786440 | tf_op jit(solution)/shard_map/ppermute | solution.py:253
  35.5 10.0 %collective-permute-start.8 = (bf16[1024,128]{1,0:T(8,128)(2,1)S(1)}, bf16[1024,128]{1,0:T(8,128)(2,1)S(1)}, u32[]{:S(2)}, u32[]{:S(2)}) collective-permute-start(bf16[1024,128]{1,0:T(8,128)(2,1)S(1)} %get-tuple-element.52), channel_id=1, source_target_pairs={{0,2},{1,3},{2,0},{3,1},{4,6},{5,7},{6,4},{7,5},{8,10},{9,11},{10,... | collective-permute-start | bytes 786440 | tf_op jit(solution)/shard_map/ppermute | solution.py:253
  37.8 6.7 %collective-permute-start.12 = (f32[2,16,128]{2,1,0:T(8,128)S(1)}, f32[2,16,128]{2,1,0:T(8,128)S(1)}, u32[]{:S(2)}, u32[]{:S(2)}) collective-permute-start(f32[2,16,128]{2,1,0:T(8,128)S(1)} %slice_bitcast_fusion), channel_id=1, source_target_pairs={{0,2},{1,3},{2,0},{3,1},{4,6},{5,7},{6,4},{7,5},{8,10},{9,11},{10,... | collective-permute-start | bytes 49160 | tf_op jit(solution)/shard_map/ppermute | solution.py:253
  44.5 4.7 %collective-permute-start.13 = (f32[2,2,8,128]{3,2,1,0:T(8,128)S(1)}, f32[2,2,8,128]{3,2,1,0:T(8,128)S(1)}, u32[]{:S(2)}, u32[]{:S(2)}) collective-permute-start(f32[2,2,8,128]{3,2,1,0:T(8,128)S(1)} %fusion.1), channel_id=1, source_target_pairs={{0,4},{1,5},{2,6},{3,7},{4,0},{5,1},{6,2},{7,3},{8,12},{9,13},{10,... | collective-permute-start | bytes 49160 | tf_op jit(solution)/shard_map/ppermute | solution.py:253
  45.6 5.0 %collective-permute-start.10 = (bf16[512,128]{1,0:T(8,128)(2,1)S(1)}, bf16[512,128]{1,0:T(8,128)(2,1)S(1)}, u32[]{:S(2)}, u32[]{:S(2)}) collective-permute-start(bf16[512,128]{1,0:T(8,128)(2,1)S(1)} %get-tuple-element.56), channel_id=1, source_target_pairs={{0,1},{1,0},{2,3},{3,2},{4,5},{5,4},{6,7},{7,6},{8,9},{9,8},{10,11... | collective-permute-start | bytes 393224 | tf_op jit(solution)/shard_map/ppermute | solution.py:253
  47.2 5.0 %collective-permute-start.9 = (bf16[512,128]{1,0:T(8,128)(2,1)S(1)}, bf16[512,128]{1,0:T(8,128)(2,1)S(1)}, u32[]{:S(2)}, u32[]{:S(2)}) collective-permute-start(bf16[512,128]{1,0:T(8,128)(2,1)S(1)} %get-tuple-element.54), channel_id=1, source_target_pairs={{0,2},{1,3},{2,0},{3,1},{4,6},{5,7},{6,4},{7,5},{8,10},{9,11},{10,... | collective-permute-start | bytes 393224 | tf_op jit(solution)/shard_map/ppermute | solution.py:253
  52.2 5.2 %collective-permute-start.14 = (bf16[256,128]{1,0:T(8,128)(2,1)S(1)}, bf16[256,128]{1,0:T(8,128)(2,1)S(1)}, u32[]{:S(2)}, u32[]{:S(2)}) collective-permute-start(bf16[256,128]{1,0:T(8,128)(2,1)S(1)} %get-tuple-element.59), channel_id=1, source_target_pairs={{0,4},{1,5},{2,6},{3,7},{4,0},{5,1},{6,2},{7,3},{8,12},{9,13},{10,... | collective-permute-start | bytes 196616 | tf_op jit(solution)/shard_map/ppermute | solution.py:253

commit v5 on v4

--- a/solution.py
+++ b/solution.py
@@ -376,11 +376,14 @@
     spreads, scores = sums[0], jnp.swapaxes(sums[1], 0, 1)
     sums = jnp.stack([spreads[0], scores[0]])
     sums = sums + swap(jnp.stack([spreads[1], scores[1]]), "dev", steps[0])
-    sums = sums[:, 0] + swap(sums[:, 1], "dev", steps[1])
     levels = len(steps) - 2
-    sums = sums.reshape((2,) + (2,) * levels + (query_count, LANES))
-    for level, bit in enumerate(steps[2:]):
-        sums = sums + jnp.flip(swap(sums, "dev", bit), axis=1 + level)
+    halves = [sums[:, index].reshape((2,) + (2,) * levels + (query_count, LANES)) for index in (0, 1)]
+    sums = halves[0]
+    for mask in range(1, 2 << levels):
+        turned_halves = halves[mask & 1]
+        axes = [1 + level for level in range(levels) if mask >> (level + 1) & 1]
+        bits = sum(bit for place, bit in enumerate(steps[1:]) if mask >> place & 1)
+        sums = sums + swap(jnp.flip(turned_halves, axis=axes), "dev", bits)
     sums = sums.reshape(2, all_queries // 4, LANES)
     quarter = half_rows // 2
     send_others, send_firsts, others, firsts = call(

time: 58.6 us -> 57.8 us (0.986)
  starting transfers between devices: 19.2 us -> 25 us
  waiting for transfers between devices: 21.6 us -> 17.4 us
  Pallas kernels: 13 us -> 11.1 us
    ppermute x15 -> x16, starting transfers between devices: 19.2 us -> 25 us  [swap(): lax.ppermute(value, axis, [(index, index ^ bit) for index in range(size)])]
    ppermute x15 -> x16, waiting for transfers between devices: 21.6 us -> 17.4 us  [swap(): lax.ppermute(value, axis, [(index, index ^ bit) for index in range(size)])]
    pallas_call x2, Pallas kernels: 5.66 us -> 3.86 us  [local(): call(functools.partial(far_score_body, piece=len(far) + index, length=len...]
  transfers between devices with their start and end apart: 15 -> 16, of which waited for: 9 -> 11; matrix products, arithmetic and copies ran while one was open for 2% -> 2% of each run, Pallas kernels for 17% -> 14%
where the time goes in v5:
time: 57.8 us; the launch traced here: 58.1 us
  starting transfers between devices  25 us (43%)
  waiting for transfers between devices  17.4 us (30%)
  Pallas kernels  11.1 us (19%)
  local copies, waits for them, and re-layouts  2.78 us (5%)
  other arithmetic  0.98 us (2%)
  between operations  0.8 us (1%)
    ppermute x16, starting transfers between devices, swap(): lax.ppermute(value, axis, [(index, index ^ bit) for index in range(size)])  25 us
    ppermute x16, waiting for transfers between devices, swap(): lax.ppermute(value, axis, [(index, index ^ bit) for index in range(size)])  17.4 us
    pallas_call x2, Pallas kernels, local(): call(functools.partial(far_score_body, piece=len(far) + index, length=len...  3.86 us
    pallas_call x1, Pallas kernels, local(): call(functools.partial(near_score_body, length=length), totals, 'score_ne...  2.83 us
    unnamed x8, local copies, waits for them, and re-layouts  2.75 us
    pallas_call x1, Pallas kernels, local(): call(unit_body, [shape(passages.shape, BF16), turned] * len(near_raw), 'p...  2.01 us
    pallas_call x1, Pallas kernels, local(): call(functools.partial(route_body, rows=rows, size=pass_count, list_len=l...  1.3 us
  transfers between devices with their start and end apart: 16, of which 11 were waited for; matrix products, arithmetic and copies ran while one was open for 2% of the time, Pallas kernels for 14%

profile of v5, /device:TPU:0, one launch (start us, length us, event | category | flops | bytes accessed | tf_op | source)
XLA Modules:
  0.0 58.1 jit_solution(6991973630518160096)
XLA Ops:
  0.6 0.5 collective-permute-start.4
  1.1 2.6 %collective-permute-start.5 = (bf16[16,256,128]{2,1,0:T(8,128)(2,1)}, bf16[16,256,128]{2,1,0:T(8,128)(2,1)S(1)}, u32[]{:S(2)}, u32[]{:S(2)}) collective-permute-start(bf16[16,256,128]{2,1,0:T(8,128)(2,1)} %refs_0_.1), channel_id=1, source_target_pairs={{0,16},{8,24},{16,0},{24,8},{1,17},{9,25},{17,1},{25,9},{2,18},{10... | collective-permute-start | bytes 3145736 | tf_op jit(solution)/shard_map/ppermute | solution.py:253
  3.7 0.0 copy-start.1
  3.7 0.8 %copy-done.1 = bf16[8,32,128]{2,1,0:T(8,128)(2,1)S(1)} copy-done((bf16[8,32,128]{2,1,0:T(8,128)(2,1)S(1)}, bf16[8,32,128]{2,1,0:T(8,128)(2,1)}, u32[]{:S(2)}) %copy-start.1) | copy-done | bytes 65560
  4.6 0.0 copy-start.3
  4.6 0.7 %copy-done.3 = s32[8,16]{1,0:T(8,128)S(1)} copy-done((s32[8,16]{1,0:T(8,128)S(1)}, s32[8,16]{1,0:T(8,128)}, u32[]{:S(2)}) %copy-start.3) | copy-done | bytes 536
  5.2 0.1 query_units.1
  5.4 2.7 %collective-permute-start = (bf16[1,272,128]{2,1,0:T(8,128)(2,1)S(1)}, bf16[1,272,128]{2,1,0:T(8,128)(2,1)S(1)}, u32[]{:S(2)}, u32[]{:S(2)}) collective-permute-start(bf16[1,272,128]{2,1,0:T(8,128)(2,1)S(1)} %bitcast.16), channel_id=1, source_target_pairs={{0,4},{1,5},{2,6},{3,7},{4,0},{5,1},{6,2},{7,3},{8,12},{9,13},{10,... | collective-permute-start | bytes 208904 | tf_op jit(solution)/shard_map/ppermute | solution.py:253
  8.0 4.1 %collective-permute-done = bf16[1,272,128]{2,1,0:T(8,128)(2,1)S(1)} collective-permute-done((bf16[1,272,128]{2,1,0:T(8,128)(2,1)S(1)}, bf16[1,272,128]{2,1,0:T(8,128)(2,1)S(1)}, u32[]{:S(2)}, u32[]{:S(2)}) %collective-permute-start) | collective-permute-done | bytes 69664 | tf_op jit(solution)/shard_map/ppermute | solution.py:253
  12.2 0.7 %collective-permute-start.1 = (bf16[2,272,128]{2,1,0:T(8,128)(2,1)S(1)}, bf16[2,272,128]{2,1,0:T(8,128)(2,1)S(1)}, u32[]{:S(2)}, u32[]{:S(2)}) collective-permute-start(bf16[2,272,128]{2,1,0:T(8,128)(2,1)S(1)} %pad_maximum_fusion.refs_0_), channel_id=1, source_target_pairs={{0,2},{1,3},{2,0},{3,1},{4,6},{5,7},{6,4},{7,5},{8,10},{9,11},{10,... | collective-permute-start | bytes 417800 | tf_op jit(solution)/shard_map/ppermute | solution.py:253
  12.9 1.5 %collective-permute-start.2 = (bf16[2,272,128]{2,1,0:T(8,128)(2,1)S(1)}, bf16[2,272,128]{2,1,0:T(8,128)(2,1)S(1)}, u32[]{:S(2)}, u32[]{:S(2)}) collective-permute-start(bf16[2,272,128]{2,1,0:T(8,128)(2,1)S(1)} %pad_maximum_fusion.refs_0_), channel_id=1, source_target_pairs={{0,1},{1,0},{2,3},{3,2},{4,5},{5,4},{6,7},{7,6},{8,9},{9,8},{10,11... | collective-permute-start | bytes 417800 | tf_op jit(solution)/shard_map/ppermute | solution.py:253
  14.4 2.9 %collective-permute-done.1.refs_1_ = bf16[2,272,128]{2,1,0:T(8,128)(2,1)S(1)} collective-permute-done((bf16[2,272,128]{2,1,0:T(8,128)(2,1)S(1)}, bf16[2,272,128]{2,1,0:T(8,128)(2,1)S(1)}, u32[]{:S(2)}, u32[]{:S(2)}) %collective-permute-start.1) | collective-permute-done | bytes 139296 | tf_op jit(solution)/shard_map/ppermute | solution.py:253
  17.3 1.5 %collective-permute-start.3 = (bf16[2,272,128]{2,1,0:T(8,128)(2,1)S(1)}, bf16[2,272,128]{2,1,0:T(8,128)(2,1)S(1)}, u32[]{:S(2)}, u32[]{:S(2)}) collective-permute-start(bf16[2,272,128]{2,1,0:T(8,128)(2,1)S(1)} %collective-permute-done.1.refs_1_), channel_id=1, source_target_pairs={{0,1},{1,0},{2,3},{3,2},{4,5},{5,4},{6,7},{7,6},{8,9},{9,8},{10,11... | collective-permute-start | bytes 417800 | tf_op jit(solution)/shard_map/ppermute | solution.py:253
  18.8 0.1 pad_add_fusion
  18.9 0.9 %select_reduce_fusion.docs_ref = s32[64]{0:T(128)S(1)} fusion(s32[512]{0:T(512)} %param.7, s32[64]{0:T(128)S(1)} %pad_add_fusion), kind=kLoop, calls=%fused_computation.1 | loop fusion | flops 98240 | bytes 2560 | tf_op jit(solution)/shard_map/reduce_sum | solution.py:323
  19.8 0.0 collective-permute-done.4.refs_1_
  19.8 0.0 copy-start
  19.8 1.2 %copy-done = bf16[16,256,128]{2,1,0:T(8,128)(2,1)S(1)} copy-done((bf16[16,256,128]{2,1,0:T(8,128)(2,1)S(1)}, bf16[16,256,128]{2,1,0:T(8,128)(2,1)}, u32[]{:S(2)}) %copy-start) | copy-done | bytes 1048600
  21.0 2.0 %passage_units.1 = (bf16[16,256,128]{2,1,0:T(8,128)(2,1)S(1)}, bf16[16,128,256]{2,1,0:T(8,128)(2,1)S(1)}, bf16[16,256,128]{2,1,0:T(8,128)(2,1)S(1)}, bf16[16,128,256]{2,1,0:T(8,128)(2,1)S(1)}) custom-call(bf16[16,256,128]{2,1,0:T(8,128)(2,1)S(1)} %copy-done, bf16[16,256,128]{2,1,0:T(8,128)(2,1)S(1)} %collective-permute-done.4.refs_1_), custom_call_target="tpu_custom_call" | custom-call | tf_op jit(solution)/shard_map/passage_units/pallas_call | solution.py:306
  23.0 0.0 collective-permute-done.3.refs_3_
  23.0 0.0 collective-permute-done.2.refs_2_
  23.0 1.3 %route.1 = (bf16[2176,128]{1,0:T(8,128)(2,1)S(1)}, s32[4,3,1,128]{3,2,1,0:T(1,128)S(1)}) custom-call(s32[64]{0:T(128)S(1)} %select_reduce_fusion.docs_ref, bf16[2,272,128]{2,1,0:T(8,128)(2,1)S(1)} %pad_maximum_fusion.refs_0_, bf16[2,272,128]{2,1,0:T(8,128)(2,1)S(1)} %collective-permute-done.1.refs_1_, ...), custom_call_target="tpu_custom_call" | custom-call | tf_op jit(solution)/shard_map/route/pallas_call | solution.py:326
  24.3 2.8 %score_near.1 = (f32[4128,128]{1,0:T(8,128)S(1)}, f32[129,128]{1,0:T(8,128)S(1)}) custom-call(s32[4,3,1,128]{3,2,1,0:T(1,128)S(1)} %get-tuple-element.37.lists_ref, bf16[2176,128]{1,0:T(8,128)(2,1)S(1)} %get-tuple-element.38.pay_ref, bf16[16,256,128]{2,1,0:T(8,128)(2,1)S(1)} %get-tuple-element.39.refs_0_, ...), custom_call_target="tpu_custom_call" | custom-call | tf_op jit(solution)/shard_map/score_near/pallas_call | solution.py:343
  27.2 0.5 collective-permute-done.5.raw_ref
  27.7 0.0 collective-permute-start.6
  27.7 1.9 %score_far.2 = (f32[4128,128]{1,0:T(8,128)S(1)}, f32[129,128]{1,0:T(8,128)S(1)}) custom-call(s32[4,3,1,128]{3,2,1,0:T(1,128)S(1)} %get-tuple-element.37.lists_ref, bf16[2176,128]{1,0:T(8,128)(2,1)S(1)} %get-tuple-element.38.pay_ref, bf16[16,256,128]{2,1,0:T(8,128)(2,1)S(1)} %collective-permute-done.5.raw_ref, ...), custom_call_target="tpu_custom_call", output_to_operand_aliasing={{0}: (3, {}), {1}: (4, {})} | custom-call | tf_op jit(solution)/shard_map/score_far/pallas_call | solution.py:357
  29.6 0.8 %collective-permute-done.6.raw_ref = bf16[16,256,128]{2,1,0:T(8,128)(2,1)S(1)} collective-permute-done((bf16[16,256,128]{2,1,0:T(8,128)(2,1)S(1)}, bf16[16,256,128]{2,1,0:T(8,128)(2,1)S(1)}, u32[]{:S(2)}, u32[]{:S(2)}) %collective-permute-start.6) | collective-permute-done | bytes 1048608 | tf_op jit(solution)/shard_map/ppermute | solution.py:253
  30.3 2.0 %score_far.3 = (f32[4128,128]{1,0:T(8,128)S(1)}, f32[129,128]{1,0:T(8,128)S(1)}, bf16[1024,128]{1,0:T(8,128)(2,1)S(1)}, bf16[1024,128]{1,0:T(8,128)(2,1)S(1)}) custom-call(s32[4,3,1,128]{3,2,1,0:T(1,128)S(1)} %get-tuple-element.37.lists_ref, bf16[2176,128]{1,0:T(8,128)(2,1)S(1)} %get-tuple-element.38.pay_ref, ...), custom_call_target="tpu_custom_call", output_to_operand_aliasing={{0}: (3, {}), {1}: (4, {})} | custom-call | tf_op jit(solution)/shard_map/score_far/pallas_call | solution.py:357
  32.3 0.0 copy-start.2
  32.4 2.3 %collective-permute-start.11 = (f32[2,2,16,128]{3,2,1,0:T(8,128)S(1)}, f32[2,2,16,128]{3,2,1,0:T(8,128)S(1)}, u32[]{:S(2)}, u32[]{:S(2)}) collective-permute-start(f32[2,2,16,128]{3,2,1,0:T(8,128)S(1)} %pad_maximum_fusion.1), channel_id=1, source_target_pairs={{0,1},{1,0},{2,3},{3,2},{4,5},{5,4},{6,7},{7,6},{8,9},{9,8},{10,11... | collective-permute-start | bytes 98312 | tf_op jit(solution)/shard_map/ppermute | solution.py:253
  34.7 0.1 collective-permute-start.7
  34.8 1.5 %collective-permute-start.8 = (bf16[1024,128]{1,0:T(8,128)(2,1)S(1)}, bf16[1024,128]{1,0:T(8,128)(2,1)S(1)}, u32[]{:S(2)}, u32[]{:S(2)}) collective-permute-start(bf16[1024,128]{1,0:T(8,128)(2,1)S(1)} %get-tuple-element.52), channel_id=1, source_target_pairs={{0,2},{1,3},{2,0},{3,1},{4,6},{5,7},{6,4},{7,5},{8,10},{9,11},{10,... | collective-permute-start | bytes 786440 | tf_op jit(solution)/shard_map/ppermute | solution.py:253
  36.3 0.3 collective-permute-done.11
  36.6 3.4 %collective-permute-start.13 = (f32[2,2,8,128]{3,2,1,0:T(8,128)S(1)}, f32[2,2,8,128]{3,2,1,0:T(8,128)S(1)}, u32[]{:S(2)}, u32[]{:S(2)}) collective-permute-start(f32[2,2,8,128]{3,2,1,0:T(8,128)S(1)} %rev.7), channel_id=1, source_target_pairs={{0,4},{1,5},{2,6},{3,7},{4,0},{5,1},{6,2},{7,3},{8,12},{9,13},{10,... | collective-permute-start | bytes 49160 | tf_op jit(solution)/shard_map/ppermute | solution.py:253
  40.1 0.6 %collective-permute-start.14 = (f32[2,2,8,128]{3,2,1,0:T(8,128)S(1)}, f32[2,2,8,128]{3,2,1,0:T(8,128)S(1)}, u32[]{:S(2)}, u32[]{:S(2)}) collective-permute-start(f32[2,2,8,128]{3,2,1,0:T(8,128)S(1)} %rev.8), channel_id=1, source_target_pairs={{0,6},{1,7},{2,4},{3,5},{4,2},{5,3},{6,0},{7,1},{8,14},{9,15},{10,... | collective-permute-start | bytes 49160 | tf_op jit(solution)/shard_map/ppermute | solution.py:253
  40.7 0.2 collective-permute-start.12
  40.9 2.0 %collective-permute-done.7.others_ref = bf16[1024,128]{1,0:T(8,128)(2,1)S(1)} collective-permute-done((bf16[1024,128]{1,0:T(8,128)(2,1)S(1)}, bf16[1024,128]{1,0:T(8,128)(2,1)S(1)}, u32[]{:S(2)}, u32[]{:S(2)}) %collective-permute-start.7) | collective-permute-done | bytes 262176 | tf_op jit(solution)/shard_map/ppermute | solution.py:253
  42.9 0.6 %collective-permute-done.8.firsts_ref = bf16[1024,128]{1,0:T(8,128)(2,1)S(1)} collective-permute-done((bf16[1024,128]{1,0:T(8,128)(2,1)S(1)}, bf16[1024,128]{1,0:T(8,128)(2,1)S(1)}, u32[]{:S(2)}, u32[]{:S(2)}) %collective-permute-start.8) | collective-permute-done | bytes 262176 | tf_op jit(solution)/shard_map/ppermute | solution.py:253
  43.5 0.1 halve.1
  43.6 1.7 %collective-permute-start.10 = (bf16[512,128]{1,0:T(8,128)(2,1)S(1)}, bf16[512,128]{1,0:T(8,128)(2,1)S(1)}, u32[]{:S(2)}, u32[]{:S(2)}) collective-permute-start(bf16[512,128]{1,0:T(8,128)(2,1)S(1)} %get-tuple-element.56), channel_id=1, source_target_pairs={{0,1},{1,0},{2,3},{3,2},{4,5},{5,4},{6,7},{7,6},{8,9},{9,8},{10,11... | collective-permute-start | bytes 393224 | tf_op jit(solution)/shard_map/ppermute | solution.py:253
  45.3 1.0 %collective-permute-start.9 = (bf16[512,128]{1,0:T(8,128)(2,1)S(1)}, bf16[512,128]{1,0:T(8,128)(2,1)S(1)}, u32[]{:S(2)}, u32[]{:S(2)}) collective-permute-start(bf16[512,128]{1,0:T(8,128)(2,1)S(1)} %get-tuple-element.54), channel_id=1, source_target_pairs={{0,2},{1,3},{2,0},{3,1},{4,6},{5,7},{6,4},{7,5},{8,10},{9,11},{10,... | collective-permute-start | bytes 393224 | tf_op jit(solution)/shard_map/ppermute | solution.py:253
  46.3 0.0 collective-permute-done.13
  46.3 0.8 %collective-permute-done.14 = f32[2,2,8,128]{3,2,1,0:T(8,128)S(1)} collective-permute-done((f32[2,2,8,128]{3,2,1,0:T(8,128)S(1)}, f32[2,2,8,128]{3,2,1,0:T(8,128)S(1)}, u32[]{:S(2)}, u32[]{:S(2)}) %collective-permute-start.14) | collective-permute-done | bytes 16416 | tf_op jit(solution)/shard_map/ppermute | solution.py:253
  47.2 0.0 collective-permute-done.12
  47.2 1.4 %collective-permute-done.10.got_firsts = bf16[512,128]{1,0:T(8,128)(2,1)S(1)} collective-permute-done((bf16[512,128]{1,0:T(8,128)(2,1)S(1)}, bf16[512,128]{1,0:T(8,128)(2,1)S(1)}, u32[]{:S(2)}, u32[]{:S(2)}) %collective-permute-start.10) | collective-permute-done | bytes 131104 | tf_op jit(solution)/shard_map/ppermute | solution.py:253
  48.6 1.7 %collective-permute-done.9.got_others = bf16[512,128]{1,0:T(8,128)(2,1)S(1)} collective-permute-done((bf16[512,128]{1,0:T(8,128)(2,1)S(1)}, bf16[512,128]{1,0:T(8,128)(2,1)S(1)}, u32[]{:S(2)}, u32[]{:S(2)}) %collective-permute-start.9) | collective-permute-done | bytes 131104 | tf_op jit(solution)/shard_map/ppermute | solution.py:253
  50.3 0.1 merge.1
  50.3 4.6 %collective-permute-start.15 = (bf16[256,128]{1,0:T(8,128)(2,1)S(1)}, bf16[256,128]{1,0:T(8,128)(2,1)S(1)}, u32[]{:S(2)}, u32[]{:S(2)}) collective-permute-start(bf16[256,128]{1,0:T(8,128)(2,1)S(1)} %get-tuple-element.59), channel_id=1, source_target_pairs={{0,4},{1,5},{2,6},{3,7},{4,0},{5,1},{6,2},{7,3},{8,12},{9,13},{10,... | collective-permute-start | bytes 196616 | tf_op jit(solution)/shard_map/ppermute | solution.py:253
  54.9 2.3 %collective-permute-done.15.got_ref = bf16[256,128]{1,0:T(8,128)(2,1)S(1)} collective-permute-done((bf16[256,128]{1,0:T(8,128)(2,1)S(1)}, bf16[256,128]{1,0:T(8,128)(2,1)S(1)}, u32[]{:S(2)}, u32[]{:S(2)}) %collective-permute-start.15) | collective-permute-done | bytes 65568 | tf_op jit(solution)/shard_map/ppermute | solution.py:253
  57.2 0.0 copy-done.2
  57.2 0.9 %last.1 = (f32[8,32,128]{2,1,0:T(8,128)}, f32[1,8]{1,0:T(1,128)}) custom-call(bf16[8,32,128]{2,1,0:T(8,128)(2,1)S(1)} %copy-done.2, f32[256,128]{1,0:T(8,128)S(1)} %get-tuple-element.58.keep_ref, bf16[256,128]{1,0:T(8,128)(2,1)S(1)} %collective-permute-done.15.got_ref, f32[2,8,128]{2,1,0:T(8,128)S(1)} %slice.52.sums_ref), custom_call_target="tpu_custom_call" | custom-call | tf_op jit(solution)/shard_map/last/pallas_call | solution.py:405
  (14 shorter events, 0.1 us)
Async XLA Ops:
  0.6 19.1 %collective-permute-start.4 = (bf16[16,256,128]{2,1,0:T(8,128)(2,1)}, bf16[16,256,128]{2,1,0:T(8,128)(2,1)S(1)}, u32[]{:S(2)}, u32[]{:S(2)}) collective-permute-start(bf16[16,256,128]{2,1,0:T(8,128)(2,1)} %refs_0_.1), channel_id=1, source_target_pairs={{0,8},{8,0},{16,24},{24,16},{1,9},{9,1},{17,25},{25,17},{2,10},{10... | collective-permute-start | bytes 3145736 | tf_op jit(solution)/shard_map/ppermute | solution.py:253
  1.1 26.5 %collective-permute-start.5 = (bf16[16,256,128]{2,1,0:T(8,128)(2,1)}, bf16[16,256,128]{2,1,0:T(8,128)(2,1)S(1)}, u32[]{:S(2)}, u32[]{:S(2)}) collective-permute-start(bf16[16,256,128]{2,1,0:T(8,128)(2,1)} %refs_0_.1), channel_id=1, source_target_pairs={{0,16},{8,24},{16,0},{24,8},{1,17},{9,25},{17,1},{25,9},{2,18},{10... | collective-permute-start | bytes 3145736 | tf_op jit(solution)/shard_map/ppermute | solution.py:253
  3.7 0.8 %copy-start.1 = (bf16[8,32,128]{2,1,0:T(8,128)(2,1)S(1)}, bf16[8,32,128]{2,1,0:T(8,128)(2,1)}, u32[]{:S(2)}) copy-start(bf16[8,32,128]{2,1,0:T(8,128)(2,1)} %queries_ref.3) | copy-start | bytes 196612
  4.6 0.7 %copy-start.3 = (s32[8,16]{1,0:T(8,128)S(1)}, s32[8,16]{1,0:T(8,128)}, u32[]{:S(2)}) copy-start(s32[8,16]{1,0:T(8,128)} %cand_ref.1) | copy-start | bytes 1540
  5.4 6.8 %collective-permute-start = (bf16[1,272,128]{2,1,0:T(8,128)(2,1)S(1)}, bf16[1,272,128]{2,1,0:T(8,128)(2,1)S(1)}, u32[]{:S(2)}, u32[]{:S(2)}) collective-permute-start(bf16[1,272,128]{2,1,0:T(8,128)(2,1)S(1)} %bitcast.16), channel_id=1, source_target_pairs={{0,4},{1,5},{2,6},{3,7},{4,0},{5,1},{6,2},{7,3},{8,12},{9,13},{10,... | collective-permute-start | bytes 208904 | tf_op jit(solution)/shard_map/ppermute | solution.py:253
  12.2 5.1 %collective-permute-start.1 = (bf16[2,272,128]{2,1,0:T(8,128)(2,1)S(1)}, bf16[2,272,128]{2,1,0:T(8,128)(2,1)S(1)}, u32[]{:S(2)}, u32[]{:S(2)}) collective-permute-start(bf16[2,272,128]{2,1,0:T(8,128)(2,1)S(1)} %pad_maximum_fusion.refs_0_), channel_id=1, source_target_pairs={{0,2},{1,3},{2,0},{3,1},{4,6},{5,7},{6,4},{7,5},{8,10},{9,11},{10,... | collective-permute-start | bytes 417800 | tf_op jit(solution)/shard_map/ppermute | solution.py:253
  12.9 10.2 %collective-permute-start.2 = (bf16[2,272,128]{2,1,0:T(8,128)(2,1)S(1)}, bf16[2,272,128]{2,1,0:T(8,128)(2,1)S(1)}, u32[]{:S(2)}, u32[]{:S(2)}) collective-permute-start(bf16[2,272,128]{2,1,0:T(8,128)(2,1)S(1)} %pad_maximum_fusion.refs_0_), channel_id=1, source_target_pairs={{0,1},{1,0},{2,3},{3,2},{4,5},{5,4},{6,7},{7,6},{8,9},{9,8},{10,11... | collective-permute-start | bytes 417800 | tf_op jit(solution)/shard_map/ppermute | solution.py:253
  17.3 5.7 %collective-permute-start.3 = (bf16[2,272,128]{2,1,0:T(8,128)(2,1)S(1)}, bf16[2,272,128]{2,1,0:T(8,128)(2,1)S(1)}, u32[]{:S(2)}, u32[]{:S(2)}) collective-permute-start(bf16[2,272,128]{2,1,0:T(8,128)(2,1)S(1)} %collective-permute-done.1.refs_1_), channel_id=1, source_target_pairs={{0,1},{1,0},{2,3},{3,2},{4,5},{5,4},{6,7},{7,6},{8,9},{9,8},{10,11... | collective-permute-start | bytes 417800 | tf_op jit(solution)/shard_map/ppermute | solution.py:253
  19.8 1.2 %copy-start = (bf16[16,256,128]{2,1,0:T(8,128)(2,1)S(1)}, bf16[16,256,128]{2,1,0:T(8,128)(2,1)}, u32[]{:S(2)}) copy-start(bf16[16,256,128]{2,1,0:T(8,128)(2,1)} %refs_0_.1) | copy-start | bytes 3145732
  27.7 2.7 %collective-permute-start.6 = (bf16[16,256,128]{2,1,0:T(8,128)(2,1)S(1)}, bf16[16,256,128]{2,1,0:T(8,128)(2,1)S(1)}, u32[]{:S(2)}, u32[]{:S(2)}) collective-permute-start(bf16[16,256,128]{2,1,0:T(8,128)(2,1)S(1)} %collective-permute-done.5.raw_ref), channel_id=1, source_target_pairs={{0,8},{8,0},{16,24},{24,16},{1,9},{9,1},{17,25},{25,17},{2,10},{10... | collective-permute-start | bytes 3145736 | tf_op jit(solution)/shard_map/ppermute | solution.py:253
  32.3 24.9 %copy-start.2 = (bf16[8,32,128]{2,1,0:T(8,128)(2,1)S(1)}, bf16[8,32,128]{2,1,0:T(8,128)(2,1)}, u32[]{:S(2)}) copy-start(bf16[8,32,128]{2,1,0:T(8,128)(2,1)} %queries_ref.3) | copy-start | bytes 196612
  32.4 4.2 %collective-permute-start.11 = (f32[2,2,16,128]{3,2,1,0:T(8,128)S(1)}, f32[2,2,16,128]{3,2,1,0:T(8,128)S(1)}, u32[]{:S(2)}, u32[]{:S(2)}) collective-permute-start(f32[2,2,16,128]{3,2,1,0:T(8,128)S(1)} %pad_maximum_fusion.1), channel_id=1, source_target_pairs={{0,1},{1,0},{2,3},{3,2},{4,5},{5,4},{6,7},{7,6},{8,9},{9,8},{10,11... | collective-permute-start | bytes 98312 | tf_op jit(solution)/shard_map/ppermute | solution.py:253
  34.7 8.2 %collective-permute-start.7 = (bf16[1024,128]{1,0:T(8,128)(2,1)S(1)}, bf16[1024,128]{1,0:T(8,128)(2,1)S(1)}, u32[]{:S(2)}, u32[]{:S(2)}) collective-permute-start(bf16[1024,128]{1,0:T(8,128)(2,1)S(1)} %get-tuple-element.51), channel_id=1, source_target_pairs={{0,1},{1,0},{2,3},{3,2},{4,5},{5,4},{6,7},{7,6},{8,9},{9,8},{10,11... | collective-permute-start | bytes 786440 | tf_op jit(solution)/shard_map/ppermute | solution.py:253
  34.8 8.7 %collective-permute-start.8 = (bf16[1024,128]{1,0:T(8,128)(2,1)S(1)}, bf16[1024,128]{1,0:T(8,128)(2,1)S(1)}, u32[]{:S(2)}, u32[]{:S(2)}) collective-permute-start(bf16[1024,128]{1,0:T(8,128)(2,1)S(1)} %get-tuple-element.52), channel_id=1, source_target_pairs={{0,2},{1,3},{2,0},{3,1},{4,6},{5,7},{6,4},{7,5},{8,10},{9,11},{10,... | collective-permute-start | bytes 786440 | tf_op jit(solution)/shard_map/ppermute | solution.py:253
  36.6 9.7 %collective-permute-start.13 = (f32[2,2,8,128]{3,2,1,0:T(8,128)S(1)}, f32[2,2,8,128]{3,2,1,0:T(8,128)S(1)}, u32[]{:S(2)}, u32[]{:S(2)}) collective-permute-start(f32[2,2,8,128]{3,2,1,0:T(8,128)S(1)} %rev.7), channel_id=1, source_target_pairs={{0,4},{1,5},{2,6},{3,7},{4,0},{5,1},{6,2},{7,3},{8,12},{9,13},{10,... | collective-permute-start | bytes 49160 | tf_op jit(solution)/shard_map/ppermute | solution.py:253
  40.1 7.1 %collective-permute-start.14 = (f32[2,2,8,128]{3,2,1,0:T(8,128)S(1)}, f32[2,2,8,128]{3,2,1,0:T(8,128)S(1)}, u32[]{:S(2)}, u32[]{:S(2)}) collective-permute-start(f32[2,2,8,128]{3,2,1,0:T(8,128)S(1)} %rev.8), channel_id=1, source_target_pairs={{0,6},{1,7},{2,4},{3,5},{4,2},{5,3},{6,0},{7,1},{8,14},{9,15},{10,... | collective-permute-start | bytes 49160 | tf_op jit(solution)/shard_map/ppermute | solution.py:253
  40.7 6.5 %collective-permute-start.12 = (f32[2,2,8,128]{3,2,1,0:T(8,128)S(1)}, f32[2,2,8,128]{3,2,1,0:T(8,128)S(1)}, u32[]{:S(2)}, u32[]{:S(2)}) collective-permute-start(f32[2,2,8,128]{3,2,1,0:T(8,128)S(1)} %get-tuple-element.65), channel_id=1, source_target_pairs={{0,2},{1,3},{2,0},{3,1},{4,6},{5,7},{6,4},{7,5},{8,10},{9,11},{10,... | collective-permute-start | bytes 49160 | tf_op jit(solution)/shard_map/ppermute | solution.py:253
  43.6 5.0 %collective-permute-start.10 = (bf16[512,128]{1,0:T(8,128)(2,1)S(1)}, bf16[512,128]{1,0:T(8,128)(2,1)S(1)}, u32[]{:S(2)}, u32[]{:S(2)}) collective-permute-start(bf16[512,128]{1,0:T(8,128)(2,1)S(1)} %get-tuple-element.56), channel_id=1, source_target_pairs={{0,1},{1,0},{2,3},{3,2},{4,5},{5,4},{6,7},{7,6},{8,9},{9,8},{10,11... | collective-permute-start | bytes 393224 | tf_op jit(solution)/shard_map/ppermute | solution.py:253
  45.3 5.0 %collective-permute-start.9 = (bf16[512,128]{1,0:T(8,128)(2,1)S(1)}, bf16[512,128]{1,0:T(8,128)(2,1)S(1)}, u32[]{:S(2)}, u32[]{:S(2)}) collective-permute-start(bf16[512,128]{1,0:T(8,128)(2,1)S(1)} %get-tuple-element.54), channel_id=1, source_target_pairs={{0,2},{1,3},{2,0},{3,1},{4,6},{5,7},{6,4},{7,5},{8,10},{9,11},{10,... | collective-permute-start | bytes 393224 | tf_op jit(solution)/shard_map/ppermute | solution.py:253
  50.3 6.9 %collective-permute-start.15 = (bf16[256,128]{1,0:T(8,128)(2,1)S(1)}, bf16[256,128]{1,0:T(8,128)(2,1)S(1)}, u32[]{:S(2)}, u32[]{:S(2)}) collective-permute-start(bf16[256,128]{1,0:T(8,128)(2,1)S(1)} %get-tuple-element.59), channel_id=1, source_target_pairs={{0,4},{1,5},{2,6},{3,7},{4,0},{5,1},{6,2},{7,3},{8,12},{9,13},{10,... | collective-permute-start | bytes 196616 | tf_op jit(solution)/shard_map/ppermute | solution.py:253

commit v6 on v5

--- a/solution.py
+++ b/solution.py
@@ -72,7 +72,7 @@
         turn_units(source, refs[half + 2 * index], refs[half + 2 * index + 1])
 
 
-def route_body(docs_ref, *refs, rows, size, list_len):
+def route_body(docs_ref, *refs, rows, size, groups_of, list_len):
     *pay_refs, out_ref, list_ref = refs
     per_ref = pay_refs[0].shape[0]
     blocks = per_ref * len(pay_refs)
@@ -103,31 +103,34 @@
     diagonal = upper == column
     parts = list_ref.shape[2]
     place = lax.broadcasted_iota(jnp.int32, (parts * LANES, LANES), 0).astype(F32)
-    for piece in range(list_ref.shape[0]):
+    leaving = (block >= 2 * quarter) | (first & (region == 1))
+    for index, groups in enumerate(groups_of):
         held = jnp.full((blocks, LANES), -1, jnp.int32)
-        for index in range(size):
-            held = jnp.where(ids == docs_ref[piece * size + index], index, held)
-        mask = held >= 0
+        for place_of in range(size):
+            held = jnp.where(ids == docs_ref[index * size + place_of], place_of, held)
         code = held.astype(F32) * SHIFT + source
-        ranks = jnp.dot(mask.astype(F32), triangle, preferred_element_type=F32)
-        before = jnp.zeros((1, 1), F32)
-        codes = jnp.zeros((parts * LANES, LANES), F32)
-        targets = jnp.zeros((parts * LANES, LANES), F32)
-        for index in range(blocks):
-            row = ranks[index : index + 1]
-            slot = jnp.where(mask[index : index + 1], before + row - 1.0, -1.0)
-            here = place == slot
-            codes = codes + jnp.where(here, code[index : index + 1], 0.0)
-            targets = targets + jnp.where(here, target[index : index + 1], 0.0)
-            before = before + row[:, LANES - 1 : LANES]
-        for kind, found in enumerate((codes, targets + 2.0 * queries / LANES)):
-            packed = jnp.sum(found, axis=1, keepdims=True)
-            for part in range(parts):
-                value = packed[part * LANES : (part + 1) * LANES]
-                line = jnp.sum(jnp.where(diagonal, value, 0.0), axis=0, keepdims=True)
-                list_ref[piece, kind, part : part + 1] = line.astype(jnp.int32)
-        count = jnp.broadcast_to(before, (parts, LANES)).astype(jnp.int32)
-        list_ref[piece, 2] = count
+        for piece, group in groups:
+            mask = held >= 0
+            if group is not None:
+                mask = mask & (leaving if group == 0 else jnp.logical_not(leaving))
+            ranks = jnp.dot(mask.astype(F32), triangle, preferred_element_type=F32)
+            before = jnp.zeros((1, 1), F32)
+            codes = jnp.zeros((parts * LANES, LANES), F32)
+            targets = jnp.zeros((parts * LANES, LANES), F32)
+            for row_of in range(blocks):
+                row = ranks[row_of : row_of + 1]
+                slot = jnp.where(mask[row_of : row_of + 1], before + row - 1.0, -1.0)
+                here = place == slot
+                codes = codes + jnp.where(here, code[row_of : row_of + 1], 0.0)
+                targets = targets + jnp.where(here, target[row_of : row_of + 1], 0.0)
+                before = before + row[:, LANES - 1 : LANES]
+            for kind, found in enumerate((codes, targets + 2.0 * queries / LANES)):
+                packed = jnp.sum(found, axis=1, keepdims=True)
+                for part in range(parts):
+                    value = packed[part * LANES : (part + 1) * LANES]
+                    line = jnp.sum(jnp.where(diagonal, value, 0.0), axis=0, keepdims=True)
+                    list_ref[piece, kind, part : part + 1] = line.astype(jnp.int32)
+            list_ref[piece, 2] = jnp.broadcast_to(before, (parts, LANES)).astype(jnp.int32)
 
 
 def score_pairs(list_ref, pay_ref, pass_ref, turned_ref, acc_ref, sums_ref, length):
@@ -169,27 +172,31 @@
     lax.fori_loop(0, lax.div(count + UNROLL - 1, UNROLL), step, 0)
 
 
-def near_score_body(lists_ref, pay_ref, *refs, length):
-    *pass_refs, acc_ref, sums_ref, list_ref, sem = refs
-    move = pltpu.make_async_copy(lists_ref.at[: len(pass_refs) // 2], list_ref, sem)
+def score_body(lists_ref, pay_ref, *refs, piece, count, begin, length):
+    pass_refs, refs = refs[: 2 * count], refs[2 * count :]
+    acc_ref, sums_ref, list_ref, sem = refs if begin else refs[2:]
+    move = pltpu.make_async_copy(lists_ref.at[piece : piece + count], list_ref, sem)
     move.start()
-    acc_ref[...] = jnp.zeros_like(acc_ref)
-    sums_ref[...] = jnp.zeros_like(sums_ref)
+    if begin:
+        acc_ref[...] = jnp.zeros_like(acc_ref)
+        sums_ref[...] = jnp.zeros_like(sums_ref)
     move.wait()
-    for piece in range(len(pass_refs) // 2):
+    for index in range(count):
         score_pairs(
-            list_ref.at[piece],
+            list_ref.at[index],
             pay_ref,
-            pass_refs[2 * piece],
-            pass_refs[2 * piece + 1],
+            pass_refs[2 * index],
+            pass_refs[2 * index + 1],
             acc_ref,
             sums_ref,
             length,
         )
 
 
-def far_score_body(lists_ref, pay_ref, raw_ref, _, __, acc_ref, sums_ref, *refs, piece, length):
-    *send_refs, pass_ref, turned_ref, list_ref, sem = refs
+def far_score_body(
+    lists_ref, pay_ref, raw_ref, _, __, acc_ref, sums_ref, pass_ref, turned_ref, *refs, piece, length
+):
+    *send_refs, list_ref, sem = refs
     move = pltpu.make_async_copy(lists_ref.at[piece], list_ref, sem)
     move.start()
     turn_units(raw_ref, pass_ref, turned_ref)
@@ -323,11 +330,16 @@
     docs = jnp.sum(jnp.where(hits, documents[None, :], 0), axis=1)
 
     parts = -(-dev_count * min(pair_count, slot_cap) // LANES)
+    near_count = len(near_offsets)
+    groups_of = [((index, None),) for index in range(near_count)]
+    groups_of += [((near_count + i, 0), (2 * near_count + i, 1)) for i in range(near_count)]
     pay, lists = call(
-        functools.partial(route_body, rows=rows, size=pass_count, list_len=list_len),
+        functools.partial(
+            route_body, rows=rows, size=pass_count, groups_of=groups_of, list_len=list_len
+        ),
         [
             shape((dev_count * (rows + TAIL), width), BF16),
-            shape((len(offsets), 3, parts, LANES), jnp.int32),
+            shape((3 * near_count, 3, parts, LANES), jnp.int32),
         ],
         "route",
         in_specs=[smem] + [vmem] * len(pays),
@@ -340,42 +352,49 @@
         shape((2 * all_queries + 1, LANES), F32),
     ]
     sends = [shape((half_rows, width), BF16)] * 2
-    state = call(
-        functools.partial(near_score_body, length=length),
-        totals,
-        "score_near",
-        [vmem] * (2 + len(near)),
-        scratch=[
-            pltpu.SMEM((len(near_raw), 3, parts, LANES), jnp.int32),
-            pltpu.SemaphoreType.DMA(()),
-        ],
-    )(lists, pay, *near)
+    def score(blocks, piece, state=()):
+        return call(
+            functools.partial(
+                score_body, piece=piece, count=near_count, begin=not state, length=length
+            ),
+            totals,
+            "score",
+            [vmem] * (2 + len(blocks) + len(state)),
+            {2 + len(blocks): 0, 3 + len(blocks): 1} if state else {},
+            [
+                pltpu.SMEM((near_count, 3, parts, LANES), jnp.int32),
+                pltpu.SemaphoreType.DMA(()),
+            ],
+        )(lists, pay, *blocks, *state)
+
+    state = score(near, 0)
     far_raw, *state = lax.optimization_barrier((far_raw, *state))
-    far = spread(far_raw)
-    for index, raw in enumerate(far):
-        last = index == len(far) - 1
-        state = call(
-            functools.partial(far_score_body, piece=len(far) + index, length=length),
-            totals + (sends if last else []),
+    far = []
+    for index, raw in enumerate(spread(far_raw)):
+        last = index == near_count - 1
+        acc, sums, *blocks = call(
+            functools.partial(far_score_body, piece=near_count + index, length=length),
+            totals + [shape(passages.shape, BF16), turned] + (sends if last else []),
             "score_far",
             [vmem] * 5,
             {3: 0, 4: 1},
-            [
-                pltpu.VMEM(passages.shape, BF16),
-                pltpu.VMEM(turned.shape, BF16),
-                pltpu.SMEM((3, parts, LANES), jnp.int32),
-                pltpu.SemaphoreType.DMA(()),
-            ],
+            [pltpu.SMEM((3, parts, LANES), jnp.int32), pltpu.SemaphoreType.DMA(())],
         )(lists, pay, raw, *state)
-    acc, sums, others, firsts = state
+        state = (acc, sums)
+        far += blocks[:2]
+    others, firsts = blocks[2:]
 
     steps = bits_of(dev_count)[::-1]
     got_others = swap(others, "dev", steps[0])
     got_firsts = swap(firsts, "dev", steps[1])
-    sums = sums[: 2 * all_queries].reshape(2, 2, 2, all_queries // 4, LANES)
-    spreads, scores = sums[0], jnp.swapaxes(sums[1], 0, 1)
-    sums = jnp.stack([spreads[0], scores[0]])
-    sums = sums + swap(jnp.stack([spreads[1], scores[1]]), "dev", steps[0])
+    def quarters(sums):
+        spreads, scores = sums[: 2 * all_queries].reshape(2, 2, 2, all_queries // 4, LANES)
+        return [jnp.stack([spreads[half], scores[:, half]]) for half in (0, 1)]
+
+    got_sums = swap(quarters(sums)[1], "dev", steps[0])
+    got_sums, *state = lax.optimization_barrier((got_sums, *state))
+    acc, sums = score(far, 2 * near_count, state)
+    sums = quarters(sums)[0] + got_sums
     levels = len(steps) - 2
     halves = [sums[:, index].reshape((2,) + (2,) * levels + (query_count, LANES)) for index in (0, 1)]
     sums = halves[0]

time: 57.8 us -> 56.9 us (0.984)
  waiting for transfers between devices: 17.4 us -> 14.7 us
  starting transfers between devices: 25 us -> 26.4 us
    ppermute x16, waiting for transfers between devices: 17.4 us -> 14.7 us  [swap(): lax.ppermute(value, axis, [(index, index ^ bit) for index in range(size)])]
    ppermute x16, starting transfers between devices: 25 us -> 26.4 us  [swap(): lax.ppermute(value, axis, [(index, index ^ bit) for index in range(size)])]
    pallas_call x4 -> x5, Pallas kernels: 8 us -> 8.49 us  [the longest x2 3.87 us: score(): call(functools.partial(score_body, piece=piece, count=near_count, begin=n...]
  transfers between devices with their start and end apart: 16 -> 16, of which waited for: 11 -> 8; matrix products, arithmetic and copies ran while one was open for 2% -> 2% of each run, Pallas kernels for 14% -> 16%
where the time goes in v6:
time: 56.9 us; the launch traced here: 57.3 us
  starting transfers between devices  26.4 us (46%)
  waiting for transfers between devices  14.7 us (26%)
  Pallas kernels  11.6 us (20%)
  local copies, waits for them, and re-layouts  2.79 us (5%)
  other arithmetic  0.98 us (2%)
  between operations  0.84 us (1%)
    ppermute x16, starting transfers between devices, swap(): lax.ppermute(value, axis, [(index, index ^ bit) for index in range(size)])  26.4 us
    ppermute x16, waiting for transfers between devices, swap(): lax.ppermute(value, axis, [(index, index ^ bit) for index in range(size)])  14.7 us
    pallas_call x2, Pallas kernels, score(): call(functools.partial(score_body, piece=piece, count=near_count, begin=n...  3.87 us
    pallas_call x2, Pallas kernels, local(): call(functools.partial(far_score_body, piece=near_count + index, length=l...  3.02 us
    unnamed x8, local copies, waits for them, and re-layouts  2.75 us
    pallas_call x1, Pallas kernels, local(): call(unit_body, [shape(passages.shape, BF16), turned] * len(near_raw), 'p...  2.01 us
    pallas_call x1, Pallas kernels, local(): call(functools.partial(route_body, rows=rows, size=pass_count, groups_of=...  1.6 us
  transfers between devices with their start and end apart: 16, of which 8 were waited for; matrix products, arithmetic and copies ran while one was open for 2% of the time, Pallas kernels for 16%

profile of v6, /device:TPU:0, one launch (start us, length us, event | category | flops | bytes accessed | tf_op | source)
XLA Modules:
  0.0 57.3 jit_solution(11278794191026320865)
XLA Ops:
  0.6 0.5 collective-permute-start.4
  1.1 2.6 %collective-permute-start.5 = (bf16[16,256,128]{2,1,0:T(8,128)(2,1)}, bf16[16,256,128]{2,1,0:T(8,128)(2,1)S(1)}, u32[]{:S(2)}, u32[]{:S(2)}) collective-permute-start(bf16[16,256,128]{2,1,0:T(8,128)(2,1)} %refs_0_.1), channel_id=1, source_target_pairs={{0,16},{8,24},{16,0},{24,8},{1,17},{9,25},{17,1},{25,9},{2,18},{10... | collective-permute-start | bytes 3145736 | tf_op jit(solution)/shard_map/ppermute | solution.py:260
  3.7 0.0 copy-start.1
  3.7 0.8 %copy-done.1 = bf16[8,32,128]{2,1,0:T(8,128)(2,1)S(1)} copy-done((bf16[8,32,128]{2,1,0:T(8,128)(2,1)S(1)}, bf16[8,32,128]{2,1,0:T(8,128)(2,1)}, u32[]{:S(2)}) %copy-start.1) | copy-done | bytes 65560
  4.6 0.0 copy-start.3
  4.6 0.7 %copy-done.3 = s32[8,16]{1,0:T(8,128)S(1)} copy-done((s32[8,16]{1,0:T(8,128)S(1)}, s32[8,16]{1,0:T(8,128)}, u32[]{:S(2)}) %copy-start.3) | copy-done | bytes 536
  5.2 0.1 query_units.1
  5.4 2.7 %collective-permute-start = (bf16[1,272,128]{2,1,0:T(8,128)(2,1)S(1)}, bf16[1,272,128]{2,1,0:T(8,128)(2,1)S(1)}, u32[]{:S(2)}, u32[]{:S(2)}) collective-permute-start(bf16[1,272,128]{2,1,0:T(8,128)(2,1)S(1)} %bitcast.20), channel_id=1, source_target_pairs={{0,4},{1,5},{2,6},{3,7},{4,0},{5,1},{6,2},{7,3},{8,12},{9,13},{10,... | collective-permute-start | bytes 208904 | tf_op jit(solution)/shard_map/ppermute | solution.py:260
  8.0 4.1 %collective-permute-done = bf16[1,272,128]{2,1,0:T(8,128)(2,1)S(1)} collective-permute-done((bf16[1,272,128]{2,1,0:T(8,128)(2,1)S(1)}, bf16[1,272,128]{2,1,0:T(8,128)(2,1)S(1)}, u32[]{:S(2)}, u32[]{:S(2)}) %collective-permute-start) | collective-permute-done | bytes 69664 | tf_op jit(solution)/shard_map/ppermute | solution.py:260
  12.2 0.7 %collective-permute-start.1 = (bf16[2,272,128]{2,1,0:T(8,128)(2,1)S(1)}, bf16[2,272,128]{2,1,0:T(8,128)(2,1)S(1)}, u32[]{:S(2)}, u32[]{:S(2)}) collective-permute-start(bf16[2,272,128]{2,1,0:T(8,128)(2,1)S(1)} %pad_maximum_fusion.refs_0_), channel_id=1, source_target_pairs={{0,2},{1,3},{2,0},{3,1},{4,6},{5,7},{6,4},{7,5},{8,10},{9,11},{10,... | collective-permute-start | bytes 417800 | tf_op jit(solution)/shard_map/ppermute | solution.py:260
  12.9 1.5 %collective-permute-start.2 = (bf16[2,272,128]{2,1,0:T(8,128)(2,1)S(1)}, bf16[2,272,128]{2,1,0:T(8,128)(2,1)S(1)}, u32[]{:S(2)}, u32[]{:S(2)}) collective-permute-start(bf16[2,272,128]{2,1,0:T(8,128)(2,1)S(1)} %pad_maximum_fusion.refs_0_), channel_id=1, source_target_pairs={{0,1},{1,0},{2,3},{3,2},{4,5},{5,4},{6,7},{7,6},{8,9},{9,8},{10,11... | collective-permute-start | bytes 417800 | tf_op jit(solution)/shard_map/ppermute | solution.py:260
  14.4 2.9 %collective-permute-done.1.refs_1_ = bf16[2,272,128]{2,1,0:T(8,128)(2,1)S(1)} collective-permute-done((bf16[2,272,128]{2,1,0:T(8,128)(2,1)S(1)}, bf16[2,272,128]{2,1,0:T(8,128)(2,1)S(1)}, u32[]{:S(2)}, u32[]{:S(2)}) %collective-permute-start.1) | collective-permute-done | bytes 139296 | tf_op jit(solution)/shard_map/ppermute | solution.py:260
  17.3 1.5 %collective-permute-start.3 = (bf16[2,272,128]{2,1,0:T(8,128)(2,1)S(1)}, bf16[2,272,128]{2,1,0:T(8,128)(2,1)S(1)}, u32[]{:S(2)}, u32[]{:S(2)}) collective-permute-start(bf16[2,272,128]{2,1,0:T(8,128)(2,1)S(1)} %collective-permute-done.1.refs_1_), channel_id=1, source_target_pairs={{0,1},{1,0},{2,3},{3,2},{4,5},{5,4},{6,7},{7,6},{8,9},{9,8},{10,11... | collective-permute-start | bytes 417800 | tf_op jit(solution)/shard_map/ppermute | solution.py:260
  18.8 0.1 pad_add_fusion
  18.9 0.9 %select_reduce_fusion.docs_ref = s32[64]{0:T(128)S(1)} fusion(s32[512]{0:T(512)} %param.7, s32[64]{0:T(128)S(1)} %pad_add_fusion), kind=kLoop, calls=%fused_computation.1 | loop fusion | flops 98240 | bytes 2560 | tf_op jit(solution)/shard_map/reduce_sum | solution.py:330
  19.8 0.0 collective-permute-done.4.refs_1_
  19.8 0.0 copy-start
  19.8 1.2 %copy-done = bf16[16,256,128]{2,1,0:T(8,128)(2,1)S(1)} copy-done((bf16[16,256,128]{2,1,0:T(8,128)(2,1)S(1)}, bf16[16,256,128]{2,1,0:T(8,128)(2,1)}, u32[]{:S(2)}) %copy-start) | copy-done | bytes 1048600
  21.0 2.0 %passage_units.1 = (bf16[16,256,128]{2,1,0:T(8,128)(2,1)S(1)}, bf16[16,128,256]{2,1,0:T(8,128)(2,1)S(1)}, bf16[16,256,128]{2,1,0:T(8,128)(2,1)S(1)}, bf16[16,128,256]{2,1,0:T(8,128)(2,1)S(1)}) custom-call(bf16[16,256,128]{2,1,0:T(8,128)(2,1)S(1)} %copy-done, bf16[16,256,128]{2,1,0:T(8,128)(2,1)S(1)} %collective-permute-done.4.refs_1_), custom_call_target="tpu_custom_call" | custom-call | tf_op jit(solution)/shard_map/passage_units/pallas_call | solution.py:313
  23.0 0.0 collective-permute-done.3.refs_3_
  23.0 0.0 collective-permute-done.2.refs_2_
  23.0 1.6 %route.1 = (bf16[2176,128]{1,0:T(8,128)(2,1)S(1)}, s32[6,3,1,128]{3,2,1,0:T(1,128)S(1)}) custom-call(s32[64]{0:T(128)S(1)} %select_reduce_fusion.docs_ref, bf16[2,272,128]{2,1,0:T(8,128)(2,1)S(1)} %pad_maximum_fusion.refs_0_, bf16[2,272,128]{2,1,0:T(8,128)(2,1)S(1)} %collective-permute-done.1.refs_1_, ...), custom_call_target="tpu_custom_call" | custom-call | tf_op jit(solution)/shard_map/route/pallas_call | solution.py:336
  24.6 2.4 %score.2 = (f32[4128,128]{1,0:T(8,128)S(1)}, f32[129,128]{1,0:T(8,128)S(1)}) custom-call(s32[6,3,1,128]{3,2,1,0:T(1,128)S(1)} %get-tuple-element.46.lists_ref, bf16[2176,128]{1,0:T(8,128)(2,1)S(1)} %get-tuple-element.47.pay_ref, bf16[16,256,128]{2,1,0:T(8,128)(2,1)S(1)} %get-tuple-element.48.refs_0_, bf16[16,128,256]{2,1,0:T(8,128)(2,1)S(1)} %get-tuple-element.49.refs_1_, ...), custom_call_target="tpu_custom_call" | custom-call | tf_op jit(solution)/shard_map/score/pallas_call | solution.py:356
  27.0 0.6 %collective-permute-done.5.raw_ref = bf16[16,256,128]{2,1,0:T(8,128)(2,1)S(1)} collective-permute-done((bf16[16,256,128]{2,1,0:T(8,128)(2,1)}, bf16[16,256,128]{2,1,0:T(8,128)(2,1)S(1)}, u32[]{:S(2)}, u32[]{:S(2)}) %collective-permute-start.5) | collective-permute-done | bytes 1048608 | tf_op jit(solution)/shard_map/ppermute | solution.py:260
  27.7 0.0 collective-permute-start.6
  27.7 1.5 %score_far.2 = (f32[4128,128]{1,0:T(8,128)S(1)}, f32[129,128]{1,0:T(8,128)S(1)}, bf16[16,256,128]{2,1,0:T(8,128)(2,1)S(1)}, bf16[16,128,256]{2,1,0:T(8,128)(2,1)S(1)}) custom-call(s32[6,3,1,128]{3,2,1,0:T(1,128)S(1)} %get-tuple-element.46.lists_ref, bf16[2176,128]{1,0:T(8,128)(2,1)S(1)} %get-tuple-element.47.pay_ref, ...), custom_call_target="tpu_custom_call", output_to_operand_aliasing={{0}: (3, {}), {1}: (4, {})} | custom-call | tf_op jit(solution)/shard_map/score_far/pallas_call | solution.py:375
  29.2 1.2 %collective-permute-done.6.raw_ref = bf16[16,256,128]{2,1,0:T(8,128)(2,1)S(1)} collective-permute-done((bf16[16,256,128]{2,1,0:T(8,128)(2,1)S(1)}, bf16[16,256,128]{2,1,0:T(8,128)(2,1)S(1)}, u32[]{:S(2)}, u32[]{:S(2)}) %collective-permute-start.6) | collective-permute-done | bytes 1048608 | tf_op jit(solution)/shard_map/ppermute | solution.py:260
  30.3 1.5 %score_far.3 = (f32[4128,128]{1,0:T(8,128)S(1)}, f32[129,128]{1,0:T(8,128)S(1)}, bf16[16,256,128]{2,1,0:T(8,128)(2,1)S(1)}, bf16[16,128,256]{2,1,0:T(8,128)(2,1)...) custom-call(s32[6,3,1,128]{3,2,1,0:T(1,128)S(1)} %get-tuple-element., ...), custom_call_target="tpu_custom_call", output_to_operand_aliasing={{0}: (3, {}), {1}: (4, {})} | custom-call | tf_op jit(solution)/shard_map/score_far/pallas_call | solution.py:375
  31.9 1.8 %collective-permute-start.7 = (f32[2,2,16,128]{3,2,1,0:T(8,128)S(1)}, f32[2,2,16,128]{3,2,1,0:T(8,128)S(1)}, u32[]{:S(2)}, u32[]{:S(2)}) collective-permute-start(f32[2,2,16,128]{3,2,1,0:T(8,128)S(1)} %pad_maximum_fusion.1), channel_id=1, source_target_pairs={{0,1},{1,0},{2,3},{3,2},{4,5},{5,4},{6,7},{7,6},{8,9},{9,8},{10,11... | collective-permute-start | bytes 98312 | tf_op jit(solution)/shard_map/ppermute | solution.py:260
  33.8 0.3 collective-permute-start.8
  34.0 2.3 %collective-permute-start.9 = (bf16[1024,128]{1,0:T(8,128)(2,1)S(1)}, bf16[1024,128]{1,0:T(8,128)(2,1)S(1)}, u32[]{:S(2)}, u32[]{:S(2)}) collective-permute-start(bf16[1024,128]{1,0:T(8,128)(2,1)S(1)} %get-tuple-element.69), channel_id=1, source_target_pairs={{0,2},{1,3},{2,0},{3,1},{4,6},{5,7},{6,4},{7,5},{8,10},{9,11},{10,... | collective-permute-start | bytes 786440 | tf_op jit(solution)/shard_map/ppermute | solution.py:260
  36.3 0.0 collective-permute-done.7
  36.3 1.5 %score.3 = (f32[4128,128]{1,0:T(8,128)S(1)}, f32[129,128]{1,0:T(8,128)S(1)}) custom-call(s32[6,3,1,128]{3,2,1,0:T(1,128)S(1)} %get-tuple-element.46.lists_ref, bf16[2176,128]{1,0:T(8,128)(2,1)S(1)} %get-tuple-element.47.pay_ref, bf16[16,256,128]{2,1,0:T(8,128)(2,1)S(1)} %get-tuple-element.57.refs_0_, ...), custom_call_target="tpu_custom_call", output_to_operand_aliasing={{0}: (6, {}), {1}: (7, {})} | custom-call | tf_op jit(solution)/shard_map/score/pallas_call | solution.py:356
  37.8 0.0 copy-start.2
  37.9 5.0 %collective-permute-start.14 = (f32[2,2,8,128]{3,2,1,0:T(8,128)S(1)}, f32[2,2,8,128]{3,2,1,0:T(8,128)S(1)}, u32[]{:S(2)}, u32[]{:S(2)}) collective-permute-start(f32[2,2,8,128]{3,2,1,0:T(8,128)S(1)} %rev.8), channel_id=1, source_target_pairs={{0,6},{1,7},{2,4},{3,5},{4,2},{5,3},{6,0},{7,1},{8,14},{9,15},{10,... | collective-permute-start | bytes 49160 | tf_op jit(solution)/shard_map/ppermute | solution.py:260
  43.0 0.0 collective-permute-start.13
  43.0 0.6 %collective-permute-start.12 = (f32[2,2,8,128]{3,2,1,0:T(8,128)S(1)}, f32[2,2,8,128]{3,2,1,0:T(8,128)S(1)}, u32[]{:S(2)}, u32[]{:S(2)}) collective-permute-start(f32[2,2,8,128]{3,2,1,0:T(8,128)S(1)} %get-tuple-element.81), channel_id=1, source_target_pairs={{0,2},{1,3},{2,0},{3,1},{4,6},{5,7},{6,4},{7,5},{8,10},{9,11},{10,... | collective-permute-start | bytes 49160 | tf_op jit(solution)/shard_map/ppermute | solution.py:260
  43.6 0.0 collective-permute-done.8.others_ref
  43.6 0.0 collective-permute-done.9.firsts_ref
  43.6 0.1 halve.1
  43.7 1.5 %collective-permute-start.10 = (bf16[512,128]{1,0:T(8,128)(2,1)S(1)}, bf16[512,128]{1,0:T(8,128)(2,1)S(1)}, u32[]{:S(2)}, u32[]{:S(2)}) collective-permute-start(bf16[512,128]{1,0:T(8,128)(2,1)S(1)} %get-tuple-element.71), channel_id=1, source_target_pairs={{0,2},{1,3},{2,0},{3,1},{4,6},{5,7},{6,4},{7,5},{8,10},{9,11},{10,... | collective-permute-start | bytes 393224 | tf_op jit(solution)/shard_map/ppermute | solution.py:260
  45.1 2.4 %collective-permute-start.11 = (bf16[512,128]{1,0:T(8,128)(2,1)S(1)}, bf16[512,128]{1,0:T(8,128)(2,1)S(1)}, u32[]{:S(2)}, u32[]{:S(2)}) collective-permute-start(bf16[512,128]{1,0:T(8,128)(2,1)S(1)} %get-tuple-element.73), channel_id=1, source_target_pairs={{0,1},{1,0},{2,3},{3,2},{4,5},{5,4},{6,7},{7,6},{8,9},{9,8},{10,11... | collective-permute-start | bytes 393224 | tf_op jit(solution)/shard_map/ppermute | solution.py:260
  47.5 0.0 collective-permute-done.14
  47.5 0.2 collective-permute-done.13
  47.7 0.0 collective-permute-done.12
  47.7 1.2 %collective-permute-done.10.got_others = bf16[512,128]{1,0:T(8,128)(2,1)S(1)} collective-permute-done((bf16[512,128]{1,0:T(8,128)(2,1)S(1)}, bf16[512,128]{1,0:T(8,128)(2,1)S(1)}, u32[]{:S(2)}, u32[]{:S(2)}) %collective-permute-start.10) | collective-permute-done | bytes 131104 | tf_op jit(solution)/shard_map/ppermute | solution.py:260
  48.9 1.6 %collective-permute-done.11.got_firsts = bf16[512,128]{1,0:T(8,128)(2,1)S(1)} collective-permute-done((bf16[512,128]{1,0:T(8,128)(2,1)S(1)}, bf16[512,128]{1,0:T(8,128)(2,1)S(1)}, u32[]{:S(2)}, u32[]{:S(2)}) %collective-permute-start.11) | collective-permute-done | bytes 131104 | tf_op jit(solution)/shard_map/ppermute | solution.py:260
  50.5 0.1 merge.1
  50.5 3.0 %collective-permute-start.15 = (bf16[256,128]{1,0:T(8,128)(2,1)S(1)}, bf16[256,128]{1,0:T(8,128)(2,1)S(1)}, u32[]{:S(2)}, u32[]{:S(2)}) collective-permute-start(bf16[256,128]{1,0:T(8,128)(2,1)S(1)} %get-tuple-element.77), channel_id=1, source_target_pairs={{0,4},{1,5},{2,6},{3,7},{4,0},{5,1},{6,2},{7,3},{8,12},{9,13},{10,... | collective-permute-start | bytes 196616 | tf_op jit(solution)/shard_map/ppermute | solution.py:260
  53.5 2.9 %collective-permute-done.15.got_ref = bf16[256,128]{1,0:T(8,128)(2,1)S(1)} collective-permute-done((bf16[256,128]{1,0:T(8,128)(2,1)S(1)}, bf16[256,128]{1,0:T(8,128)(2,1)S(1)}, u32[]{:S(2)}, u32[]{:S(2)}) %collective-permute-start.15) | collective-permute-done | bytes 65568 | tf_op jit(solution)/shard_map/ppermute | solution.py:260
  56.5 0.0 copy-done.2
  56.5 0.9 %last.1 = (f32[8,32,128]{2,1,0:T(8,128)}, f32[1,8]{1,0:T(1,128)}) custom-call(bf16[8,32,128]{2,1,0:T(8,128)(2,1)S(1)} %copy-done.2, f32[256,128]{1,0:T(8,128)S(1)} %get-tuple-element.76.keep_ref, bf16[256,128]{1,0:T(8,128)(2,1)S(1)} %collective-permute-done.15.got_ref, f32[2,8,128]{2,1,0:T(8,128)S(1)} %slice.52.sums_ref), custom_call_target="tpu_custom_call" | custom-call | tf_op jit(solution)/shard_map/last/pallas_call | solution.py:424
  (16 shorter events, 0.1 us)
Async XLA Ops:
  0.6 19.1 %collective-permute-start.4 = (bf16[16,256,128]{2,1,0:T(8,128)(2,1)}, bf16[16,256,128]{2,1,0:T(8,128)(2,1)S(1)}, u32[]{:S(2)}, u32[]{:S(2)}) collective-permute-start(bf16[16,256,128]{2,1,0:T(8,128)(2,1)} %refs_0_.1), channel_id=1, source_target_pairs={{0,8},{8,0},{16,24},{24,16},{1,9},{9,1},{17,25},{25,17},{2,10},{10... | collective-permute-start | bytes 3145736 | tf_op jit(solution)/shard_map/ppermute | solution.py:260
  1.1 26.5 %collective-permute-start.5 = (bf16[16,256,128]{2,1,0:T(8,128)(2,1)}, bf16[16,256,128]{2,1,0:T(8,128)(2,1)S(1)}, u32[]{:S(2)}, u32[]{:S(2)}) collective-permute-start(bf16[16,256,128]{2,1,0:T(8,128)(2,1)} %refs_0_.1), channel_id=1, source_target_pairs={{0,16},{8,24},{16,0},{24,8},{1,17},{9,25},{17,1},{25,9},{2,18},{10... | collective-permute-start | bytes 3145736 | tf_op jit(solution)/shard_map/ppermute | solution.py:260
  3.7 0.8 %copy-start.1 = (bf16[8,32,128]{2,1,0:T(8,128)(2,1)S(1)}, bf16[8,32,128]{2,1,0:T(8,128)(2,1)}, u32[]{:S(2)}) copy-start(bf16[8,32,128]{2,1,0:T(8,128)(2,1)} %queries_ref.3) | copy-start | bytes 196612
  4.6 0.7 %copy-start.3 = (s32[8,16]{1,0:T(8,128)S(1)}, s32[8,16]{1,0:T(8,128)}, u32[]{:S(2)}) copy-start(s32[8,16]{1,0:T(8,128)} %cand_ref.1) | copy-start | bytes 1540
  5.4 6.8 %collective-permute-start = (bf16[1,272,128]{2,1,0:T(8,128)(2,1)S(1)}, bf16[1,272,128]{2,1,0:T(8,128)(2,1)S(1)}, u32[]{:S(2)}, u32[]{:S(2)}) collective-permute-start(bf16[1,272,128]{2,1,0:T(8,128)(2,1)S(1)} %bitcast.20), channel_id=1, source_target_pairs={{0,4},{1,5},{2,6},{3,7},{4,0},{5,1},{6,2},{7,3},{8,12},{9,13},{10,... | collective-permute-start | bytes 208904 | tf_op jit(solution)/shard_map/ppermute | solution.py:260
  12.2 5.1 %collective-permute-start.1 = (bf16[2,272,128]{2,1,0:T(8,128)(2,1)S(1)}, bf16[2,272,128]{2,1,0:T(8,128)(2,1)S(1)}, u32[]{:S(2)}, u32[]{:S(2)}) collective-permute-start(bf16[2,272,128]{2,1,0:T(8,128)(2,1)S(1)} %pad_maximum_fusion.refs_0_), channel_id=1, source_target_pairs={{0,2},{1,3},{2,0},{3,1},{4,6},{5,7},{6,4},{7,5},{8,10},{9,11},{10,... | collective-permute-start | bytes 417800 | tf_op jit(solution)/shard_map/ppermute | solution.py:260
  12.9 10.2 %collective-permute-start.2 = (bf16[2,272,128]{2,1,0:T(8,128)(2,1)S(1)}, bf16[2,272,128]{2,1,0:T(8,128)(2,1)S(1)}, u32[]{:S(2)}, u32[]{:S(2)}) collective-permute-start(bf16[2,272,128]{2,1,0:T(8,128)(2,1)S(1)} %pad_maximum_fusion.refs_0_), channel_id=1, source_target_pairs={{0,1},{1,0},{2,3},{3,2},{4,5},{5,4},{6,7},{7,6},{8,9},{9,8},{10,11... | collective-permute-start | bytes 417800 | tf_op jit(solution)/shard_map/ppermute | solution.py:260
  17.3 5.7 %collective-permute-start.3 = (bf16[2,272,128]{2,1,0:T(8,128)(2,1)S(1)}, bf16[2,272,128]{2,1,0:T(8,128)(2,1)S(1)}, u32[]{:S(2)}, u32[]{:S(2)}) collective-permute-start(bf16[2,272,128]{2,1,0:T(8,128)(2,1)S(1)} %collective-permute-done.1.refs_1_), channel_id=1, source_target_pairs={{0,1},{1,0},{2,3},{3,2},{4,5},{5,4},{6,7},{7,6},{8,9},{9,8},{10,11... | collective-permute-start | bytes 417800 | tf_op jit(solution)/shard_map/ppermute | solution.py:260
  19.8 1.2 %copy-start = (bf16[16,256,128]{2,1,0:T(8,128)(2,1)S(1)}, bf16[16,256,128]{2,1,0:T(8,128)(2,1)}, u32[]{:S(2)}) copy-start(bf16[16,256,128]{2,1,0:T(8,128)(2,1)} %refs_0_.1) | copy-start | bytes 3145732
  27.7 2.7 %collective-permute-start.6 = (bf16[16,256,128]{2,1,0:T(8,128)(2,1)S(1)}, bf16[16,256,128]{2,1,0:T(8,128)(2,1)S(1)}, u32[]{:S(2)}, u32[]{:S(2)}) collective-permute-start(bf16[16,256,128]{2,1,0:T(8,128)(2,1)S(1)} %collective-permute-done.5.raw_ref), channel_id=1, source_target_pairs={{0,8},{8,0},{16,24},{24,16},{1,9},{9,1},{17,25},{25,17},{2,10},{10... | collective-permute-start | bytes 3145736 | tf_op jit(solution)/shard_map/ppermute | solution.py:260
  31.9 4.4 %collective-permute-start.7 = (f32[2,2,16,128]{3,2,1,0:T(8,128)S(1)}, f32[2,2,16,128]{3,2,1,0:T(8,128)S(1)}, u32[]{:S(2)}, u32[]{:S(2)}) collective-permute-start(f32[2,2,16,128]{3,2,1,0:T(8,128)S(1)} %pad_maximum_fusion.1), channel_id=1, source_target_pairs={{0,1},{1,0},{2,3},{3,2},{4,5},{5,4},{6,7},{7,6},{8,9},{9,8},{10,11... | collective-permute-start | bytes 98312 | tf_op jit(solution)/shard_map/ppermute | solution.py:260
  33.8 9.8 %collective-permute-start.8 = (bf16[1024,128]{1,0:T(8,128)(2,1)S(1)}, bf16[1024,128]{1,0:T(8,128)(2,1)S(1)}, u32[]{:S(2)}, u32[]{:S(2)}) collective-permute-start(bf16[1024,128]{1,0:T(8,128)(2,1)S(1)} %get-tuple-element.68), channel_id=1, source_target_pairs={{0,1},{1,0},{2,3},{3,2},{4,5},{5,4},{6,7},{7,6},{8,9},{9,8},{10,11... | collective-permute-start | bytes 786440 | tf_op jit(solution)/shard_map/ppermute | solution.py:260
  34.0 9.6 %collective-permute-start.9 = (bf16[1024,128]{1,0:T(8,128)(2,1)S(1)}, bf16[1024,128]{1,0:T(8,128)(2,1)S(1)}, u32[]{:S(2)}, u32[]{:S(2)}) collective-permute-start(bf16[1024,128]{1,0:T(8,128)(2,1)S(1)} %get-tuple-element.69), channel_id=1, source_target_pairs={{0,2},{1,3},{2,0},{3,1},{4,6},{5,7},{6,4},{7,5},{8,10},{9,11},{10,... | collective-permute-start | bytes 786440 | tf_op jit(solution)/shard_map/ppermute | solution.py:260
  37.8 18.7 %copy-start.2 = (bf16[8,32,128]{2,1,0:T(8,128)(2,1)S(1)}, bf16[8,32,128]{2,1,0:T(8,128)(2,1)}, u32[]{:S(2)}) copy-start(bf16[8,32,128]{2,1,0:T(8,128)(2,1)} %queries_ref.3) | copy-start | bytes 196612
  37.9 9.6 %collective-permute-start.14 = (f32[2,2,8,128]{3,2,1,0:T(8,128)S(1)}, f32[2,2,8,128]{3,2,1,0:T(8,128)S(1)}, u32[]{:S(2)}, u32[]{:S(2)}) collective-permute-start(f32[2,2,8,128]{3,2,1,0:T(8,128)S(1)} %rev.8), channel_id=1, source_target_pairs={{0,6},{1,7},{2,4},{3,5},{4,2},{5,3},{6,0},{7,1},{8,14},{9,15},{10,... | collective-permute-start | bytes 49160 | tf_op jit(solution)/shard_map/ppermute | solution.py:260
  43.0 4.7 %collective-permute-start.13 = (f32[2,2,8,128]{3,2,1,0:T(8,128)S(1)}, f32[2,2,8,128]{3,2,1,0:T(8,128)S(1)}, u32[]{:S(2)}, u32[]{:S(2)}) collective-permute-start(f32[2,2,8,128]{3,2,1,0:T(8,128)S(1)} %rev.7), channel_id=1, source_target_pairs={{0,4},{1,5},{2,6},{3,7},{4,0},{5,1},{6,2},{7,3},{8,12},{9,13},{10,... | collective-permute-start | bytes 49160 | tf_op jit(solution)/shard_map/ppermute | solution.py:260
  43.0 4.7 %collective-permute-start.12 = (f32[2,2,8,128]{3,2,1,0:T(8,128)S(1)}, f32[2,2,8,128]{3,2,1,0:T(8,128)S(1)}, u32[]{:S(2)}, u32[]{:S(2)}) collective-permute-start(f32[2,2,8,128]{3,2,1,0:T(8,128)S(1)} %get-tuple-element.81), channel_id=1, source_target_pairs={{0,2},{1,3},{2,0},{3,1},{4,6},{5,7},{6,4},{7,5},{8,10},{9,11},{10,... | collective-permute-start | bytes 49160 | tf_op jit(solution)/shard_map/ppermute | solution.py:260
  43.7 5.2 %collective-permute-start.10 = (bf16[512,128]{1,0:T(8,128)(2,1)S(1)}, bf16[512,128]{1,0:T(8,128)(2,1)S(1)}, u32[]{:S(2)}, u32[]{:S(2)}) collective-permute-start(bf16[512,128]{1,0:T(8,128)(2,1)S(1)} %get-tuple-element.71), channel_id=1, source_target_pairs={{0,2},{1,3},{2,0},{3,1},{4,6},{5,7},{6,4},{7,5},{8,10},{9,11},{10,... | collective-permute-start | bytes 393224 | tf_op jit(solution)/shard_map/ppermute | solution.py:260
  45.1 5.3 %collective-permute-start.11 = (bf16[512,128]{1,0:T(8,128)(2,1)S(1)}, bf16[512,128]{1,0:T(8,128)(2,1)S(1)}, u32[]{:S(2)}, u32[]{:S(2)}) collective-permute-start(bf16[512,128]{1,0:T(8,128)(2,1)S(1)} %get-tuple-element.73), channel_id=1, source_target_pairs={{0,1},{1,0},{2,3},{3,2},{4,5},{5,4},{6,7},{7,6},{8,9},{9,8},{10,11... | collective-permute-start | bytes 393224 | tf_op jit(solution)/shard_map/ppermute | solution.py:260
  50.5 5.9 %collective-permute-start.15 = (bf16[256,128]{1,0:T(8,128)(2,1)S(1)}, bf16[256,128]{1,0:T(8,128)(2,1)S(1)}, u32[]{:S(2)}, u32[]{:S(2)}) collective-permute-start(bf16[256,128]{1,0:T(8,128)(2,1)S(1)} %get-tuple-element.77), channel_id=1, source_target_pairs={{0,4},{1,5},{2,6},{3,7},{4,0},{5,1},{6,2},{7,3},{8,12},{9,13},{10,... | collective-permute-start | bytes 196616 | tf_op jit(solution)/shard_map/ppermute | solution.py:260

commit v7 on v6

--- a/solution.py
+++ b/solution.py
@@ -12,13 +12,13 @@
 LANES = 128
 TAIL = 16
 BASE = 256
-UNROLL = 16
+UNROLL = 20
 SHIFT = 1 << 16
 F32 = jnp.float32
 BF16 = jnp.bfloat16
 
 
-def call(body, out_shape, name, in_specs=None, aliases={}, scratch=(), cost=0):
+def call(body, out_shape, name, in_specs=None, aliases={}, scratch=()):
     kwargs = {} if in_specs is None else {"in_specs": in_specs}
     return pl.pallas_call(
         body,
@@ -26,7 +26,7 @@
         input_output_aliases=aliases,
         scratch_shapes=list(scratch),
         name=name,
-        cost_estimate=pl.CostEstimate(flops=0, bytes_accessed=cost, transcendentals=0),
+        cost_estimate=pl.CostEstimate(flops=0, bytes_accessed=0, transcendentals=0),
         compiler_params=pltpu.CompilerParams(vmem_limit_bytes=20 * 1024 * 1024),
         **kwargs,
     )
@@ -53,7 +53,7 @@
 
 def turn_units(source, units_ref, turned_ref):
     count = source.shape[0]
-    together = min(count, 8)
+    together = min(count, 16)
 
     def step(index, carry):
         for offset in range(together):
@@ -209,31 +209,26 @@
         firsts_ref[...] = acc_ref[3 * half : 4 * half].astype(BF16)
 
 
-def halve_body(acc_ref, others_ref, firsts_ref, send_a, send_b, keep_a, keep_b):
-    half = others_ref.shape[0]
-    quarter = half // 2
-    for start, got, send, keep in (
-        (0, others_ref, send_a, keep_a),
-        (2 * half, firsts_ref, send_b, keep_b),
-    ):
-        keep[...] = acc_ref[start : start + quarter] + got[:quarter].astype(F32)
-        rest = acc_ref[start + quarter : start + half] + got[quarter:].astype(F32)
-        send[...] = rest.astype(BF16)
-
-
-def merge_body(others_ref, got_others, firsts_ref, got_firsts, sums_ref, send_ref, rest_ref, *, length):
-    queries = sums_ref.shape[1]
-
-    def part(index):
+def halve_body(acc_ref, got_others, got_firsts, *send_refs):
+    for index, send_ref in enumerate(send_refs):
+        got, region = ((got_others, 1), (got_firsts, 5))[index % 2]
+        size = send_ref.shape[0]
+        at = (1 - index // 2) * size
+        own = acc_ref[region * 2 * size + at : region * 2 * size + at + size]
+        rest = got[2 * size + at : 2 * size + at + size].astype(F32)
+        send_ref[...] = (own + rest).astype(BF16)
+
+
+def merge_body(acc_ref, others_ref, firsts_ref, got_others, got_firsts, sums_ref, out_ref, *, part, length):
+    rows = out_ref.shape[0]
+    for index in range(rows // length):
         at = slice(index * length, (index + 1) * length)
-        others = others_ref[at] + got_others[at].astype(F32)
-        first = firsts_ref[at] + got_firsts[at].astype(F32)
-        return others - sums_ref[0, index : index + 1] * first
-
-    for index in range(queries // 2):
-        at = slice(index * length, (index + 1) * length)
-        rest_ref[at] = part(index)
-        send_ref[at] = part(index + queries // 2).astype(BF16)
+        here = slice(part * rows + index * length, part * rows + (index + 1) * length)
+        behind = slice(8 * rows + here.start, 8 * rows + here.stop)
+        others = acc_ref[here] + others_ref[here].astype(F32) + got_others[at].astype(F32)
+        first = acc_ref[behind] + firsts_ref[here].astype(F32) + got_firsts[at].astype(F32)
+        query = part * (rows // length) + index
+        out_ref[at] = (others - sums_ref[0, query : query + 1] * first).astype(out_ref.dtype)
 
 
 def last_body(queries_ref, keep_ref, got_ref, sums_ref, grad_ref, loss_ref, *, length):
@@ -329,7 +324,8 @@
     documents = jnp.arange(location.shape[0], dtype=jnp.int32)
     docs = jnp.sum(jnp.where(hits, documents[None, :], 0), axis=1)
 
-    parts = -(-dev_count * min(pair_count, slot_cap) // LANES)
+    most = -(-dev_count * min(pair_count, slot_cap) // UNROLL) * UNROLL
+    parts = -(-most // LANES)
     near_count = len(near_offsets)
     groups_of = [((index, None),) for index in range(near_count)]
     groups_of += [((near_count + i, 0), (2 * near_count + i, 1)) for i in range(near_count)]
@@ -404,18 +400,19 @@
         bits = sum(bit for place, bit in enumerate(steps[1:]) if mask >> place & 1)
         sums = sums + swap(jnp.flip(turned_halves, axis=axes), "dev", bits)
     sums = sums.reshape(2, all_queries // 4, LANES)
-    quarter = half_rows // 2
-    send_others, send_firsts, others, firsts = call(
-        halve_body, [shape((quarter, width), BF16)] * 2 + [shape((quarter, width), F32)] * 2, "halve"
-    )(acc, got_others, got_firsts)
-    got_others = swap(send_others, "dev", steps[1])
-    got_firsts = swap(send_firsts, "dev", steps[0])
-    quarter = quarter // 2
-    send, rest = call(
-        functools.partial(merge_body, length=length),
-        [shape((quarter, width), BF16), shape((quarter, width), F32)],
-        "merge",
-    )(others, got_others, firsts, got_firsts, sums)
+    quarter = half_rows // 4
+    leaving = call(halve_body, [shape((quarter, width), BF16)] * 4, "halve")(
+        acc, got_others, got_firsts
+    )
+    arrived = [swap(rows, "dev", bit) for rows, bit in zip(leaving, steps[1::-1] * 2)]
+    send, rest = (
+        call(
+            functools.partial(merge_body, part=part, length=length),
+            shape((quarter, width), kind),
+            "merge",
+        )(acc, got_others, got_firsts, *arrived[2 * index : 2 * index + 2], sums)
+        for index, (part, kind) in enumerate(((1, BF16), (0, F32)))
+    )
     for bit in steps[2:-1]:
         rest = rest + swap(send, "dev", bit).astype(F32)
         quarter = quarter // 2

time: 56.9 us -> 56 us (0.984)
  starting transfers between devices: 26.4 us -> 24.4 us
  waiting for transfers between devices: 14.7 us -> 15.3 us
    ppermute x16 -> x18, starting transfers between devices: 26.4 us -> 24.4 us  [swap(): lax.ppermute(value, axis, [(index, index ^ bit) for index in range(size)])]
    ppermute x16 -> x18, waiting for transfers between devices: 14.7 us -> 15.3 us  [swap(): lax.ppermute(value, axis, [(index, index ^ bit) for index in range(size)])]
  transfers between devices with their start and end apart: 16 -> 18, of which waited for: 8 -> 7; matrix products, arithmetic and copies ran while one was open for 2% -> 2% of each run, Pallas kernels for 16% -> 17%
where the time goes in v7:
time: 56 us; the launch traced here: 56.1 us
  starting transfers between devices  24.4 us (44%)
  waiting for transfers between devices  15.3 us (27%)
  Pallas kernels  11.8 us (21%)
  local copies, waits for them, and re-layouts  2.79 us (5%)
  other arithmetic  0.98 us (2%)
  between operations  0.86 us (2%)
    ppermute x18, starting transfers between devices, swap(): lax.ppermute(value, axis, [(index, index ^ bit) for index in range(size)])  24.4 us
    ppermute x18, waiting for transfers between devices, swap(): lax.ppermute(value, axis, [(index, index ^ bit) for index in range(size)])  15.3 us
    pallas_call x2, Pallas kernels, score(): call(functools.partial(score_body, piece=piece, count=near_count, begin=n...  4.36 us
    pallas_call x2, Pallas kernels, local(): call(functools.partial(far_score_body, piece=near_count + index, length=l...  2.99 us
    unnamed x8, local copies, waits for them, and re-layouts  2.75 us
    pallas_call x1, Pallas kernels, local(): call(unit_body, [shape(passages.shape, BF16), turned] * len(near_raw), 'p...  1.71 us
    pallas_call x1, Pallas kernels, local(): call(functools.partial(route_body, rows=rows, size=pass_count, groups_of=...  1.6 us
  transfers between devices with their start and end apart: 18, of which 7 were waited for; matrix products, arithmetic and copies ran while one was open for 2% of the time, Pallas kernels for 17%

profile of v7, /device:TPU:0, one launch (start us, length us, event | category | flops | bytes accessed | tf_op | source)
XLA Modules:
  0.0 56.1 jit_solution(6994841987292578907)
XLA Ops:
  0.6 0.5 collective-permute-start.4
  1.1 2.6 %collective-permute-start.5 = (bf16[16,256,128]{2,1,0:T(8,128)(2,1)}, bf16[16,256,128]{2,1,0:T(8,128)(2,1)S(1)}, u32[]{:S(2)}, u32[]{:S(2)}) collective-permute-start(bf16[16,256,128]{2,1,0:T(8,128)(2,1)} %refs_0_.1), channel_id=1, source_target_pairs={{0,16},{8,24},{16,0},{24,8},{1,17},{9,25},{17,1},{25,9},{2,18},{10... | collective-permute-start | bytes 3145736 | tf_op jit(solution)/shard_map/ppermute | solution.py:255
  3.7 0.0 copy-start.1
  3.7 0.8 %copy-done.1 = bf16[8,32,128]{2,1,0:T(8,128)(2,1)S(1)} copy-done((bf16[8,32,128]{2,1,0:T(8,128)(2,1)S(1)}, bf16[8,32,128]{2,1,0:T(8,128)(2,1)}, u32[]{:S(2)}) %copy-start.1) | copy-done | bytes 65560
  4.6 0.0 copy-start.3
  4.6 0.7 %copy-done.3 = s32[8,16]{1,0:T(8,128)S(1)} copy-done((s32[8,16]{1,0:T(8,128)S(1)}, s32[8,16]{1,0:T(8,128)}, u32[]{:S(2)}) %copy-start.3) | copy-done | bytes 536
  5.2 0.1 query_units.1
  5.4 2.7 %collective-permute-start = (bf16[1,272,128]{2,1,0:T(8,128)(2,1)S(1)}, bf16[1,272,128]{2,1,0:T(8,128)(2,1)S(1)}, u32[]{:S(2)}, u32[]{:S(2)}) collective-permute-start(bf16[1,272,128]{2,1,0:T(8,128)(2,1)S(1)} %bitcast.20), channel_id=1, source_target_pairs={{0,4},{1,5},{2,6},{3,7},{4,0},{5,1},{6,2},{7,3},{8,12},{9,13},{10,... | collective-permute-start | bytes 208904 | tf_op jit(solution)/shard_map/ppermute | solution.py:255
  8.0 4.1 %collective-permute-done = bf16[1,272,128]{2,1,0:T(8,128)(2,1)S(1)} collective-permute-done((bf16[1,272,128]{2,1,0:T(8,128)(2,1)S(1)}, bf16[1,272,128]{2,1,0:T(8,128)(2,1)S(1)}, u32[]{:S(2)}, u32[]{:S(2)}) %collective-permute-start) | collective-permute-done | bytes 69664 | tf_op jit(solution)/shard_map/ppermute | solution.py:255
  12.2 0.7 %collective-permute-start.1 = (bf16[2,272,128]{2,1,0:T(8,128)(2,1)S(1)}, bf16[2,272,128]{2,1,0:T(8,128)(2,1)S(1)}, u32[]{:S(2)}, u32[]{:S(2)}) collective-permute-start(bf16[2,272,128]{2,1,0:T(8,128)(2,1)S(1)} %pad_maximum_fusion.refs_0_), channel_id=1, source_target_pairs={{0,2},{1,3},{2,0},{3,1},{4,6},{5,7},{6,4},{7,5},{8,10},{9,11},{10,... | collective-permute-start | bytes 417800 | tf_op jit(solution)/shard_map/ppermute | solution.py:255
  12.9 1.5 %collective-permute-start.2 = (bf16[2,272,128]{2,1,0:T(8,128)(2,1)S(1)}, bf16[2,272,128]{2,1,0:T(8,128)(2,1)S(1)}, u32[]{:S(2)}, u32[]{:S(2)}) collective-permute-start(bf16[2,272,128]{2,1,0:T(8,128)(2,1)S(1)} %pad_maximum_fusion.refs_0_), channel_id=1, source_target_pairs={{0,1},{1,0},{2,3},{3,2},{4,5},{5,4},{6,7},{7,6},{8,9},{9,8},{10,11... | collective-permute-start | bytes 417800 | tf_op jit(solution)/shard_map/ppermute | solution.py:255
  14.4 2.9 %collective-permute-done.1.refs_1_ = bf16[2,272,128]{2,1,0:T(8,128)(2,1)S(1)} collective-permute-done((bf16[2,272,128]{2,1,0:T(8,128)(2,1)S(1)}, bf16[2,272,128]{2,1,0:T(8,128)(2,1)S(1)}, u32[]{:S(2)}, u32[]{:S(2)}) %collective-permute-start.1) | collective-permute-done | bytes 139296 | tf_op jit(solution)/shard_map/ppermute | solution.py:255
  17.3 1.5 %collective-permute-start.3 = (bf16[2,272,128]{2,1,0:T(8,128)(2,1)S(1)}, bf16[2,272,128]{2,1,0:T(8,128)(2,1)S(1)}, u32[]{:S(2)}, u32[]{:S(2)}) collective-permute-start(bf16[2,272,128]{2,1,0:T(8,128)(2,1)S(1)} %collective-permute-done.1.refs_1_), channel_id=1, source_target_pairs={{0,1},{1,0},{2,3},{3,2},{4,5},{5,4},{6,7},{7,6},{8,9},{9,8},{10,11... | collective-permute-start | bytes 417800 | tf_op jit(solution)/shard_map/ppermute | solution.py:255
  18.8 0.1 pad_add_fusion
  18.9 0.9 %select_reduce_fusion.docs_ref = s32[64]{0:T(128)S(1)} fusion(s32[512]{0:T(512)} %param.7, s32[64]{0:T(128)S(1)} %pad_add_fusion), kind=kLoop, calls=%fused_computation.1 | loop fusion | flops 98240 | bytes 2560 | tf_op jit(solution)/shard_map/reduce_sum | solution.py:325
  19.8 0.0 collective-permute-done.4.refs_1_
  19.8 0.0 copy-start
  19.8 1.2 %copy-done = bf16[16,256,128]{2,1,0:T(8,128)(2,1)S(1)} copy-done((bf16[16,256,128]{2,1,0:T(8,128)(2,1)S(1)}, bf16[16,256,128]{2,1,0:T(8,128)(2,1)}, u32[]{:S(2)}) %copy-start) | copy-done | bytes 1048600
  21.0 1.7 %passage_units.1 = (bf16[16,256,128]{2,1,0:T(8,128)(2,1)S(1)}, bf16[16,128,256]{2,1,0:T(8,128)(2,1)S(1)}, bf16[16,256,128]{2,1,0:T(8,128)(2,1)S(1)}, bf16[16,128,256]{2,1,0:T(8,128)(2,1)S(1)}) custom-call(bf16[16,256,128]{2,1,0:T(8,128)(2,1)S(1)} %copy-done, bf16[16,256,128]{2,1,0:T(8,128)(2,1)S(1)} %collective-permute-done.4.refs_1_), custom_call_target="tpu_custom_call" | custom-call | tf_op jit(solution)/shard_map/passage_units/pallas_call | solution.py:308
  22.7 0.0 collective-permute-done.3.refs_3_
  22.7 0.0 collective-permute-done.2.refs_2_
  22.7 1.6 %route.1 = (bf16[2176,128]{1,0:T(8,128)(2,1)S(1)}, s32[6,3,1,128]{3,2,1,0:T(1,128)S(1)}) custom-call(s32[64]{0:T(128)S(1)} %select_reduce_fusion.docs_ref, bf16[2,272,128]{2,1,0:T(8,128)(2,1)S(1)} %pad_maximum_fusion.refs_0_, bf16[2,272,128]{2,1,0:T(8,128)(2,1)S(1)} %collective-permute-done.1.refs_1_, ...), custom_call_target="tpu_custom_call" | custom-call | tf_op jit(solution)/shard_map/route/pallas_call | solution.py:332
  24.3 2.7 %score.2 = (f32[4128,128]{1,0:T(8,128)S(1)}, f32[129,128]{1,0:T(8,128)S(1)}) custom-call(s32[6,3,1,128]{3,2,1,0:T(1,128)S(1)} %get-tuple-element.44.lists_ref, bf16[2176,128]{1,0:T(8,128)(2,1)S(1)} %get-tuple-element.45.pay_ref, bf16[16,256,128]{2,1,0:T(8,128)(2,1)S(1)} %get-tuple-element.46.refs_0_, bf16[16,128,256]{2,1,0:T(8,128)(2,1)S(1)} %get-tuple-element.47.refs_1_, ...), custom_call_target="tpu_custom_call" | custom-call | tf_op jit(solution)/shard_map/score/pallas_call | solution.py:352
  27.0 0.6 %collective-permute-done.5.raw_ref = bf16[16,256,128]{2,1,0:T(8,128)(2,1)S(1)} collective-permute-done((bf16[16,256,128]{2,1,0:T(8,128)(2,1)}, bf16[16,256,128]{2,1,0:T(8,128)(2,1)S(1)}, u32[]{:S(2)}, u32[]{:S(2)}) %collective-permute-start.5) | collective-permute-done | bytes 1048608 | tf_op jit(solution)/shard_map/ppermute | solution.py:255
  27.7 0.0 collective-permute-start.6
  27.7 1.5 %score_far.2 = (f32[4128,128]{1,0:T(8,128)S(1)}, f32[129,128]{1,0:T(8,128)S(1)}, bf16[16,256,128]{2,1,0:T(8,128)(2,1)S(1)}, bf16[16,128,256]{2,1,0:T(8,128)(2,1)S(1)}) custom-call(s32[6,3,1,128]{3,2,1,0:T(1,128)S(1)} %get-tuple-element.44.lists_ref, bf16[2176,128]{1,0:T(8,128)(2,1)S(1)} %get-tuple-element.45.pay_ref, ...), custom_call_target="tpu_custom_call", output_to_operand_aliasing={{0}: (3, {}), {1}: (4, {})} | custom-call | tf_op jit(solution)/shard_map/score_far/pallas_call | solution.py:371
  29.2 1.2 %collective-permute-done.6.raw_ref = bf16[16,256,128]{2,1,0:T(8,128)(2,1)S(1)} collective-permute-done((bf16[16,256,128]{2,1,0:T(8,128)(2,1)S(1)}, bf16[16,256,128]{2,1,0:T(8,128)(2,1)S(1)}, u32[]{:S(2)}, u32[]{:S(2)}) %collective-permute-start.6) | collective-permute-done | bytes 1048608 | tf_op jit(solution)/shard_map/ppermute | solution.py:255
  30.3 1.5 %score_far.3 = (f32[4128,128]{1,0:T(8,128)S(1)}, f32[129,128]{1,0:T(8,128)S(1)}, bf16[16,256,128]{2,1,0:T(8,128)(2,1)S(1)}, bf16[16,128,256]{2,1,0:T(8,128)(2,1)...) custom-call(s32[6,3,1,128]{3,2,1,0:T(1,128)S(1)} %get-tuple-element., ...), custom_call_target="tpu_custom_call", output_to_operand_aliasing={{0}: (3, {}), {1}: (4, {})} | custom-call | tf_op jit(solution)/shard_map/score_far/pallas_call | solution.py:371
  31.9 1.8 %collective-permute-start.7 = (f32[2,2,16,128]{3,2,1,0:T(8,128)S(1)}, f32[2,2,16,128]{3,2,1,0:T(8,128)S(1)}, u32[]{:S(2)}, u32[]{:S(2)}) collective-permute-start(f32[2,2,16,128]{3,2,1,0:T(8,128)S(1)} %pad_maximum_fusion.1), channel_id=1, source_target_pairs={{0,1},{1,0},{2,3},{3,2},{4,5},{5,4},{6,7},{7,6},{8,9},{9,8},{10,11... | collective-permute-start | bytes 98312 | tf_op jit(solution)/shard_map/ppermute | solution.py:255
  33.8 0.2 collective-permute-start.8
  34.0 1.8 %collective-permute-start.9 = (bf16[1024,128]{1,0:T(8,128)(2,1)S(1)}, bf16[1024,128]{1,0:T(8,128)(2,1)S(1)}, u32[]{:S(2)}, u32[]{:S(2)}) collective-permute-start(bf16[1024,128]{1,0:T(8,128)(2,1)S(1)} %get-tuple-element.67), channel_id=1, source_target_pairs={{0,2},{1,3},{2,0},{3,1},{4,6},{5,7},{6,4},{7,5},{8,10},{9,11},{10,... | collective-permute-start | bytes 786440 | tf_op jit(solution)/shard_map/ppermute | solution.py:255
  35.8 0.0 collective-permute-done.7
  35.9 1.7 %score.3 = (f32[4128,128]{1,0:T(8,128)S(1)}, f32[129,128]{1,0:T(8,128)S(1)}) custom-call(s32[6,3,1,128]{3,2,1,0:T(1,128)S(1)} %get-tuple-element.44.lists_ref, bf16[2176,128]{1,0:T(8,128)(2,1)S(1)} %get-tuple-element.45.pay_ref, bf16[16,256,128]{2,1,0:T(8,128)(2,1)S(1)} %get-tuple-element.55.refs_0_, ...), custom_call_target="tpu_custom_call", output_to_operand_aliasing={{0}: (6, {}), {1}: (7, {})} | custom-call | tf_op jit(solution)/shard_map/score/pallas_call | solution.py:352
  37.6 5.1 %collective-permute-start.14 = (f32[2,2,8,128]{3,2,1,0:T(8,128)S(1)}, f32[2,2,8,128]{3,2,1,0:T(8,128)S(1)}, u32[]{:S(2)}, u32[]{:S(2)}) collective-permute-start(f32[2,2,8,128]{3,2,1,0:T(8,128)S(1)} %rev.8), channel_id=1, source_target_pairs={{0,6},{1,7},{2,4},{3,5},{4,2},{5,3},{6,0},{7,1},{8,14},{9,15},{10,... | collective-permute-start | bytes 49160 | tf_op jit(solution)/shard_map/ppermute | solution.py:255
  42.8 0.0 collective-permute-start.13
  42.8 0.6 %collective-permute-start.12 = (f32[2,2,8,128]{3,2,1,0:T(8,128)S(1)}, f32[2,2,8,128]{3,2,1,0:T(8,128)S(1)}, u32[]{:S(2)}, u32[]{:S(2)}) collective-permute-start(f32[2,2,8,128]{3,2,1,0:T(8,128)S(1)} %get-tuple-element.77), channel_id=1, source_target_pairs={{0,2},{1,3},{2,0},{3,1},{4,6},{5,7},{6,4},{7,5},{8,10},{9,11},{10,... | collective-permute-start | bytes 49160 | tf_op jit(solution)/shard_map/ppermute | solution.py:255
  43.4 0.0 collective-permute-done.8.got_others.others_ref
  43.4 0.0 collective-permute-done.9.got_firsts.firsts_ref
  43.5 1.5 %collective-permute-start.15 = (bf16[256,128]{1,0:T(8,128)(2,1)S(1)}, bf16[256,128]{1,0:T(8,128)(2,1)S(1)}, u32[]{:S(2)}, u32[]{:S(2)}) collective-permute-start(bf16[256,128]{1,0:T(8,128)(2,1)S(1)} %get-tuple-element.72), channel_id=1, source_target_pairs={{0,2},{1,3},{2,0},{3,1},{4,6},{5,7},{6,4},{7,5},{8,10},{9,11},{10,... | collective-permute-start | bytes 196616 | tf_op jit(solution)/shard_map/ppermute | solution.py:255
  44.9 0.7 %collective-permute-start.16 = (bf16[256,128]{1,0:T(8,128)(2,1)S(1)}, bf16[256,128]{1,0:T(8,128)(2,1)S(1)}, u32[]{:S(2)}, u32[]{:S(2)}) collective-permute-start(bf16[256,128]{1,0:T(8,128)(2,1)S(1)} %get-tuple-element.73), channel_id=1, source_target_pairs={{0,1},{1,0},{2,3},{3,2},{4,5},{5,4},{6,7},{7,6},{8,9},{9,8},{10,11... | collective-permute-start | bytes 196616 | tf_op jit(solution)/shard_map/ppermute | solution.py:255
  45.7 0.0 collective-permute-done.14
  45.7 1.9 %collective-permute-done.13 = f32[2,2,8,128]{3,2,1,0:T(8,128)S(1)} collective-permute-done((f32[2,2,8,128]{3,2,1,0:T(8,128)S(1)}, f32[2,2,8,128]{3,2,1,0:T(8,128)S(1)}, u32[]{:S(2)}, u32[]{:S(2)}) %collective-permute-start.13) | collective-permute-done | bytes 16416 | tf_op jit(solution)/shard_map/ppermute | solution.py:255
  47.5 0.0 collective-permute-done.12
  47.5 0.1 collective-permute-start.10
  47.6 0.3 collective-permute-start.11
  48.0 0.0 collective-permute-done.15.got_others
  48.0 1.6 %collective-permute-done.16.got_firsts = bf16[256,128]{1,0:T(8,128)(2,1)S(1)} collective-permute-done((bf16[256,128]{1,0:T(8,128)(2,1)S(1)}, bf16[256,128]{1,0:T(8,128)(2,1)S(1)}, u32[]{:S(2)}, u32[]{:S(2)}) %collective-permute-start.16) | collective-permute-done | bytes 65568 | tf_op jit(solution)/shard_map/ppermute | solution.py:255
  49.6 0.1 merge.3
  49.6 0.0 copy-start.2
  49.6 2.7 %collective-permute-start.17 = (bf16[256,128]{1,0:T(8,128)(2,1)S(1)}, bf16[256,128]{1,0:T(8,128)(2,1)S(1)}, u32[]{:S(2)}, u32[]{:S(2)}) collective-permute-start(bf16[256,128]{1,0:T(8,128)(2,1)S(1)} %merge.3), channel_id=1, source_target_pairs={{0,4},{1,5},{2,6},{3,7},{4,0},{5,1},{6,2},{7,3},{8,12},{9,13},{10,... | collective-permute-start | bytes 196616 | tf_op jit(solution)/shard_map/ppermute | solution.py:255
  52.3 0.0 collective-permute-done.10.got_others
  52.3 0.0 collective-permute-done.11.got_firsts
  52.3 0.1 merge.2.keep_ref
  52.3 2.9 %collective-permute-done.17.got_ref = bf16[256,128]{1,0:T(8,128)(2,1)S(1)} collective-permute-done((bf16[256,128]{1,0:T(8,128)(2,1)S(1)}, bf16[256,128]{1,0:T(8,128)(2,1)S(1)}, u32[]{:S(2)}, u32[]{:S(2)}) %collective-permute-start.17) | collective-permute-done | bytes 65568 | tf_op jit(solution)/shard_map/ppermute | solution.py:255
  55.3 0.0 copy-done.2
  55.3 0.9 %last.1 = (f32[8,32,128]{2,1,0:T(8,128)}, f32[1,8]{1,0:T(1,128)}) custom-call(bf16[8,32,128]{2,1,0:T(8,128)(2,1)S(1)} %copy-done.2, f32[256,128]{1,0:T(8,128)S(1)} %merge.2.keep_ref, bf16[256,128]{1,0:T(8,128)(2,1)S(1)} %collective-permute-done.17.got_ref, f32[2,8,128]{2,1,0:T(8,128)S(1)} %slice.52.sums_ref), custom_call_target="tpu_custom_call" | custom-call | tf_op jit(solution)/shard_map/last/pallas_call | solution.py:421
  (17 shorter events, 0.1 us)
Async XLA Ops:
  0.6 19.1 %collective-permute-start.4 = (bf16[16,256,128]{2,1,0:T(8,128)(2,1)}, bf16[16,256,128]{2,1,0:T(8,128)(2,1)S(1)}, u32[]{:S(2)}, u32[]{:S(2)}) collective-permute-start(bf16[16,256,128]{2,1,0:T(8,128)(2,1)} %refs_0_.1), channel_id=1, source_target_pairs={{0,8},{8,0},{16,24},{24,16},{1,9},{9,1},{17,25},{25,17},{2,10},{10... | collective-permute-start | bytes 3145736 | tf_op jit(solution)/shard_map/ppermute | solution.py:255
  1.1 26.5 %collective-permute-start.5 = (bf16[16,256,128]{2,1,0:T(8,128)(2,1)}, bf16[16,256,128]{2,1,0:T(8,128)(2,1)S(1)}, u32[]{:S(2)}, u32[]{:S(2)}) collective-permute-start(bf16[16,256,128]{2,1,0:T(8,128)(2,1)} %refs_0_.1), channel_id=1, source_target_pairs={{0,16},{8,24},{16,0},{24,8},{1,17},{9,25},{17,1},{25,9},{2,18},{10... | collective-permute-start | bytes 3145736 | tf_op jit(solution)/shard_map/ppermute | solution.py:255
  3.7 0.8 %copy-start.1 = (bf16[8,32,128]{2,1,0:T(8,128)(2,1)S(1)}, bf16[8,32,128]{2,1,0:T(8,128)(2,1)}, u32[]{:S(2)}) copy-start(bf16[8,32,128]{2,1,0:T(8,128)(2,1)} %queries_ref.3) | copy-start | bytes 196612
  4.6 0.7 %copy-start.3 = (s32[8,16]{1,0:T(8,128)S(1)}, s32[8,16]{1,0:T(8,128)}, u32[]{:S(2)}) copy-start(s32[8,16]{1,0:T(8,128)} %cand_ref.1) | copy-start | bytes 1540
  5.4 6.8 %collective-permute-start = (bf16[1,272,128]{2,1,0:T(8,128)(2,1)S(1)}, bf16[1,272,128]{2,1,0:T(8,128)(2,1)S(1)}, u32[]{:S(2)}, u32[]{:S(2)}) collective-permute-start(bf16[1,272,128]{2,1,0:T(8,128)(2,1)S(1)} %bitcast.20), channel_id=1, source_target_pairs={{0,4},{1,5},{2,6},{3,7},{4,0},{5,1},{6,2},{7,3},{8,12},{9,13},{10,... | collective-permute-start | bytes 208904 | tf_op jit(solution)/shard_map/ppermute | solution.py:255
  12.2 5.1 %collective-permute-start.1 = (bf16[2,272,128]{2,1,0:T(8,128)(2,1)S(1)}, bf16[2,272,128]{2,1,0:T(8,128)(2,1)S(1)}, u32[]{:S(2)}, u32[]{:S(2)}) collective-permute-start(bf16[2,272,128]{2,1,0:T(8,128)(2,1)S(1)} %pad_maximum_fusion.refs_0_), channel_id=1, source_target_pairs={{0,2},{1,3},{2,0},{3,1},{4,6},{5,7},{6,4},{7,5},{8,10},{9,11},{10,... | collective-permute-start | bytes 417800 | tf_op jit(solution)/shard_map/ppermute | solution.py:255
  12.9 9.9 %collective-permute-start.2 = (bf16[2,272,128]{2,1,0:T(8,128)(2,1)S(1)}, bf16[2,272,128]{2,1,0:T(8,128)(2,1)S(1)}, u32[]{:S(2)}, u32[]{:S(2)}) collective-permute-start(bf16[2,272,128]{2,1,0:T(8,128)(2,1)S(1)} %pad_maximum_fusion.refs_0_), channel_id=1, source_target_pairs={{0,1},{1,0},{2,3},{3,2},{4,5},{5,4},{6,7},{7,6},{8,9},{9,8},{10,11... | collective-permute-start | bytes 417800 | tf_op jit(solution)/shard_map/ppermute | solution.py:255
  17.3 5.4 %collective-permute-start.3 = (bf16[2,272,128]{2,1,0:T(8,128)(2,1)S(1)}, bf16[2,272,128]{2,1,0:T(8,128)(2,1)S(1)}, u32[]{:S(2)}, u32[]{:S(2)}) collective-permute-start(bf16[2,272,128]{2,1,0:T(8,128)(2,1)S(1)} %collective-permute-done.1.refs_1_), channel_id=1, source_target_pairs={{0,1},{1,0},{2,3},{3,2},{4,5},{5,4},{6,7},{7,6},{8,9},{9,8},{10,11... | collective-permute-start | bytes 417800 | tf_op jit(solution)/shard_map/ppermute | solution.py:255
  19.8 1.2 %copy-start = (bf16[16,256,128]{2,1,0:T(8,128)(2,1)S(1)}, bf16[16,256,128]{2,1,0:T(8,128)(2,1)}, u32[]{:S(2)}) copy-start(bf16[16,256,128]{2,1,0:T(8,128)(2,1)} %refs_0_.1) | copy-start | bytes 3145732
  27.7 2.7 %collective-permute-start.6 = (bf16[16,256,128]{2,1,0:T(8,128)(2,1)S(1)}, bf16[16,256,128]{2,1,0:T(8,128)(2,1)S(1)}, u32[]{:S(2)}, u32[]{:S(2)}) collective-permute-start(bf16[16,256,128]{2,1,0:T(8,128)(2,1)S(1)} %collective-permute-done.5.raw_ref), channel_id=1, source_target_pairs={{0,8},{8,0},{16,24},{24,16},{1,9},{9,1},{17,25},{25,17},{2,10},{10... | collective-permute-start | bytes 3145736 | tf_op jit(solution)/shard_map/ppermute | solution.py:255
  31.9 4.0 %collective-permute-start.7 = (f32[2,2,16,128]{3,2,1,0:T(8,128)S(1)}, f32[2,2,16,128]{3,2,1,0:T(8,128)S(1)}, u32[]{:S(2)}, u32[]{:S(2)}) collective-permute-start(f32[2,2,16,128]{3,2,1,0:T(8,128)S(1)} %pad_maximum_fusion.1), channel_id=1, source_target_pairs={{0,1},{1,0},{2,3},{3,2},{4,5},{5,4},{6,7},{7,6},{8,9},{9,8},{10,11... | collective-permute-start | bytes 98312 | tf_op jit(solution)/shard_map/ppermute | solution.py:255
  33.8 9.7 %collective-permute-start.8 = (bf16[1024,128]{1,0:T(8,128)(2,1)S(1)}, bf16[1024,128]{1,0:T(8,128)(2,1)S(1)}, u32[]{:S(2)}, u32[]{:S(2)}) collective-permute-start(bf16[1024,128]{1,0:T(8,128)(2,1)S(1)} %get-tuple-element.66), channel_id=1, source_target_pairs={{0,1},{1,0},{2,3},{3,2},{4,5},{5,4},{6,7},{7,6},{8,9},{9,8},{10,11... | collective-permute-start | bytes 786440 | tf_op jit(solution)/shard_map/ppermute | solution.py:255
  34.0 9.4 %collective-permute-start.9 = (bf16[1024,128]{1,0:T(8,128)(2,1)S(1)}, bf16[1024,128]{1,0:T(8,128)(2,1)S(1)}, u32[]{:S(2)}, u32[]{:S(2)}) collective-permute-start(bf16[1024,128]{1,0:T(8,128)(2,1)S(1)} %get-tuple-element.67), channel_id=1, source_target_pairs={{0,2},{1,3},{2,0},{3,1},{4,6},{5,7},{6,4},{7,5},{8,10},{9,11},{10,... | collective-permute-start | bytes 786440 | tf_op jit(solution)/shard_map/ppermute | solution.py:255
  37.6 8.0 %collective-permute-start.14 = (f32[2,2,8,128]{3,2,1,0:T(8,128)S(1)}, f32[2,2,8,128]{3,2,1,0:T(8,128)S(1)}, u32[]{:S(2)}, u32[]{:S(2)}) collective-permute-start(f32[2,2,8,128]{3,2,1,0:T(8,128)S(1)} %rev.8), channel_id=1, source_target_pairs={{0,6},{1,7},{2,4},{3,5},{4,2},{5,3},{6,0},{7,1},{8,14},{9,15},{10,... | collective-permute-start | bytes 49160 | tf_op jit(solution)/shard_map/ppermute | solution.py:255
  42.8 4.7 %collective-permute-start.13 = (f32[2,2,8,128]{3,2,1,0:T(8,128)S(1)}, f32[2,2,8,128]{3,2,1,0:T(8,128)S(1)}, u32[]{:S(2)}, u32[]{:S(2)}) collective-permute-start(f32[2,2,8,128]{3,2,1,0:T(8,128)S(1)} %rev.7), channel_id=1, source_target_pairs={{0,4},{1,5},{2,6},{3,7},{4,0},{5,1},{6,2},{7,3},{8,12},{9,13},{10,... | collective-permute-start | bytes 49160 | tf_op jit(solution)/shard_map/ppermute | solution.py:255
  42.8 4.7 %collective-permute-start.12 = (f32[2,2,8,128]{3,2,1,0:T(8,128)S(1)}, f32[2,2,8,128]{3,2,1,0:T(8,128)S(1)}, u32[]{:S(2)}, u32[]{:S(2)}) collective-permute-start(f32[2,2,8,128]{3,2,1,0:T(8,128)S(1)} %get-tuple-element.77), channel_id=1, source_target_pairs={{0,2},{1,3},{2,0},{3,1},{4,6},{5,7},{6,4},{7,5},{8,10},{9,11},{10,... | collective-permute-start | bytes 49160 | tf_op jit(solution)/shard_map/ppermute | solution.py:255
  43.5 4.5 %collective-permute-start.15 = (bf16[256,128]{1,0:T(8,128)(2,1)S(1)}, bf16[256,128]{1,0:T(8,128)(2,1)S(1)}, u32[]{:S(2)}, u32[]{:S(2)}) collective-permute-start(bf16[256,128]{1,0:T(8,128)(2,1)S(1)} %get-tuple-element.72), channel_id=1, source_target_pairs={{0,2},{1,3},{2,0},{3,1},{4,6},{5,7},{6,4},{7,5},{8,10},{9,11},{10,... | collective-permute-start | bytes 196616 | tf_op jit(solution)/shard_map/ppermute | solution.py:255
  44.9 4.6 %collective-permute-start.16 = (bf16[256,128]{1,0:T(8,128)(2,1)S(1)}, bf16[256,128]{1,0:T(8,128)(2,1)S(1)}, u32[]{:S(2)}, u32[]{:S(2)}) collective-permute-start(bf16[256,128]{1,0:T(8,128)(2,1)S(1)} %get-tuple-element.73), channel_id=1, source_target_pairs={{0,1},{1,0},{2,3},{3,2},{4,5},{5,4},{6,7},{7,6},{8,9},{9,8},{10,11... | collective-permute-start | bytes 196616 | tf_op jit(solution)/shard_map/ppermute | solution.py:255
  47.5 4.7 %collective-permute-start.10 = (bf16[256,128]{1,0:T(8,128)(2,1)S(1)}, bf16[256,128]{1,0:T(8,128)(2,1)S(1)}, u32[]{:S(2)}, u32[]{:S(2)}) collective-permute-start(bf16[256,128]{1,0:T(8,128)(2,1)S(1)} %get-tuple-element.68), channel_id=1, source_target_pairs={{0,2},{1,3},{2,0},{3,1},{4,6},{5,7},{6,4},{7,5},{8,10},{9,11},{10,... | collective-permute-start | bytes 196616 | tf_op jit(solution)/shard_map/ppermute | solution.py:255
  47.6 4.7 %collective-permute-start.11 = (bf16[256,128]{1,0:T(8,128)(2,1)S(1)}, bf16[256,128]{1,0:T(8,128)(2,1)S(1)}, u32[]{:S(2)}, u32[]{:S(2)}) collective-permute-start(bf16[256,128]{1,0:T(8,128)(2,1)S(1)} %get-tuple-element.69), channel_id=1, source_target_pairs={{0,1},{1,0},{2,3},{3,2},{4,5},{5,4},{6,7},{7,6},{8,9},{9,8},{10,11... | collective-permute-start | bytes 196616 | tf_op jit(solution)/shard_map/ppermute | solution.py:255
  49.6 5.7 %copy-start.2 = (bf16[8,32,128]{2,1,0:T(8,128)(2,1)S(1)}, bf16[8,32,128]{2,1,0:T(8,128)(2,1)}, u32[]{:S(2)}) copy-start(bf16[8,32,128]{2,1,0:T(8,128)(2,1)} %queries_ref.3) | copy-start | bytes 196612
  49.6 5.7 %collective-permute-start.17 = (bf16[256,128]{1,0:T(8,128)(2,1)S(1)}, bf16[256,128]{1,0:T(8,128)(2,1)S(1)}, u32[]{:S(2)}, u32[]{:S(2)}) collective-permute-start(bf16[256,128]{1,0:T(8,128)(2,1)S(1)} %merge.3), channel_id=1, source_target_pairs={{0,4},{1,5},{2,6},{3,7},{4,0},{5,1},{6,2},{7,3},{8,12},{9,13},{10,... | collective-permute-start | bytes 196616 | tf_op jit(solution)/shard_map/ppermute | solution.py:255

commit v8 on v7

--- a/solution.py
+++ b/solution.py
@@ -231,23 +231,27 @@
         out_ref[at] = (others - sums_ref[0, query : query + 1] * first).astype(out_ref.dtype)
 
 
-def last_body(queries_ref, keep_ref, got_ref, sums_ref, grad_ref, loss_ref, *, length):
+def query_body(queries_ref, sums_ref, unit_ref, scale_ref, loss_ref):
     count = queries_ref.shape[0]
     losses = []
     for index in range(count):
-        at = slice(index * length, (index + 1) * length)
-        spread = sums_ref[0, index : index + 1]
         score = sums_ref[1, index : index + 1]
-        total = spread + jnp.exp(score)
+        total = sums_ref[0, index : index + 1] + jnp.exp(score)
         losses.append(jnp.log(total) - score)
-        gradient = (keep_ref[at] + got_ref[at].astype(F32)) / total
-        query_unit, query_scale = unit(queries_ref[index])
-        along = jnp.sum(query_unit * gradient, axis=-1, keepdims=True)
-        grad_ref[index] = (gradient - query_unit * along) * query_scale
+        units, scale = unit(queries_ref[index])
+        unit_ref[index] = units
+        scale_ref[index] = scale / total
     losses = jnp.concatenate(losses, axis=0)
     place = lax.broadcasted_iota(jnp.int32, (count, LANES), 0)
     lane = lax.broadcasted_iota(jnp.int32, (count, LANES), 1)
     loss_ref[...] = jnp.sum(jnp.where(place == lane, losses, 0.0), axis=0, keepdims=True)[:, :count]
+
+
+def last_body(keep_ref, got_ref, unit_ref, scale_ref, grad_ref):
+    gradient = (keep_ref[...] + got_ref[...].astype(F32)).reshape(unit_ref.shape)
+    units = unit_ref[...]
+    along = jnp.sum(units * gradient, axis=-1, keepdims=True)
+    grad_ref[...] = (gradient - units * along) * scale_ref[...]
 
 
 def swap(value, axis, bit):
@@ -418,11 +422,12 @@
         quarter = quarter // 2
         rest, send = rest[:quarter], rest[quarter:].astype(BF16)
     got = swap(send, "dev", steps[-1])
-    grad, loss = call(
-        functools.partial(last_body, length=length),
-        [shape(queries.shape, F32), shape((1, query_count), F32)],
-        "last",
-    )(queries, rest, got, sums[:, :query_count])
+    units, scale, loss = call(
+        query_body,
+        [shape(queries.shape, F32)] * 2 + [shape((1, query_count), F32)],
+        "query_side",
+    )(queries, sums[:, :query_count])
+    grad = call(last_body, shape(queries.shape, F32), "last")(rest, got, units, scale)
     return loss.reshape(query_count), grad
 
 

time: 56 us -> 55.2 us (0.986); the launches traced: 56.1 us -> 54.6 us
  waiting for transfers between devices: 15.3 us -> 11.6 us
  starting transfers between devices: 24.4 us -> 26.2 us
    ppermute x18, waiting for transfers between devices: 15.3 us -> 11.6 us  [swap(): lax.ppermute(value, axis, [(index, index ^ bit) for index in range(size)])]
    ppermute x18, starting transfers between devices: 24.4 us -> 26.2 us  [swap(): lax.ppermute(value, axis, [(index, index ^ bit) for index in range(size)])]
    pallas_call x1 -> x2, Pallas kernels: 0.86 us -> 1.33 us  [the longest x1 0.77 us: local(): call(last_body, shape(queries.shape, F32), 'last')(rest, got, units, scale)]
  transfers between devices with their start and end apart: 18 -> 18, of which waited for: 7 -> 8; matrix products, arithmetic and copies ran while one was open for 2% -> 2% of each run, Pallas kernels for 17% -> 18%
where the time goes in v8:
time: 55.2 us; the launch traced here: 54.6 us
  starting transfers between devices  26.2 us (47%)
  Pallas kernels  12.3 us (22%)
  waiting for transfers between devices  11.6 us (21%)
  local copies, waits for them, and re-layouts  2.79 us (5%)
  other arithmetic  0.98 us (2%)
  between operations  0.85 us (2%)
    ppermute x18, starting transfers between devices, swap(): lax.ppermute(value, axis, [(index, index ^ bit) for index in range(size)])  26.2 us
    ppermute x18, waiting for transfers between devices, swap(): lax.ppermute(value, axis, [(index, index ^ bit) for index in range(size)])  11.6 us
    pallas_call x2, Pallas kernels, score(): call(functools.partial(score_body, piece=piece, count=near_count, begin=n...  4.35 us
    pallas_call x2, Pallas kernels, local(): call(functools.partial(far_score_body, piece=near_count + index, length=l...  3 us
    unnamed x8, local copies, waits for them, and re-layouts  2.75 us
    pallas_call x1, Pallas kernels, local(): call(unit_body, [shape(passages.shape, BF16), turned] * len(near_raw), 'p...  1.71 us
    pallas_call x1, Pallas kernels, local(): call(functools.partial(route_body, rows=rows, size=pass_count, groups_of=...  1.6 us
  transfers between devices with their start and end apart: 18, of which 8 were waited for; matrix products, arithmetic and copies ran while one was open for 2% of the time, Pallas kernels for 18%

profile of v8, /device:TPU:0, one launch (start us, length us, event | category | flops | bytes accessed | tf_op | source)
XLA Modules:
  0.0 54.6 jit_solution(14367366160229015357)
XLA Ops:
  0.6 0.5 collective-permute-start.4
  1.1 2.6 %collective-permute-start.5 = (bf16[16,256,128]{2,1,0:T(8,128)(2,1)}, bf16[16,256,128]{2,1,0:T(8,128)(2,1)S(1)}, u32[]{:S(2)}, u32[]{:S(2)}) collective-permute-start(bf16[16,256,128]{2,1,0:T(8,128)(2,1)} %refs_0_.1), channel_id=1, source_target_pairs={{0,16},{8,24},{16,0},{24,8},{1,17},{9,25},{17,1},{25,9},{2,18},{10... | collective-permute-start | bytes 3145736 | tf_op jit(solution)/shard_map/ppermute | solution.py:259
  3.7 0.0 copy-start.1
  3.7 0.8 %copy-done.1 = bf16[8,32,128]{2,1,0:T(8,128)(2,1)S(1)} copy-done((bf16[8,32,128]{2,1,0:T(8,128)(2,1)S(1)}, bf16[8,32,128]{2,1,0:T(8,128)(2,1)}, u32[]{:S(2)}) %copy-start.1) | copy-done | bytes 65560
  4.6 0.0 copy-start.3
  4.6 0.7 %copy-done.3 = s32[8,16]{1,0:T(8,128)S(1)} copy-done((s32[8,16]{1,0:T(8,128)S(1)}, s32[8,16]{1,0:T(8,128)}, u32[]{:S(2)}) %copy-start.3) | copy-done | bytes 536
  5.2 0.1 query_units.1
  5.4 2.7 %collective-permute-start = (bf16[1,272,128]{2,1,0:T(8,128)(2,1)S(1)}, bf16[1,272,128]{2,1,0:T(8,128)(2,1)S(1)}, u32[]{:S(2)}, u32[]{:S(2)}) collective-permute-start(bf16[1,272,128]{2,1,0:T(8,128)(2,1)S(1)} %bitcast.20), channel_id=1, source_target_pairs={{0,4},{1,5},{2,6},{3,7},{4,0},{5,1},{6,2},{7,3},{8,12},{9,13},{10,... | collective-permute-start | bytes 208904 | tf_op jit(solution)/shard_map/ppermute | solution.py:259
  8.0 4.1 %collective-permute-done = bf16[1,272,128]{2,1,0:T(8,128)(2,1)S(1)} collective-permute-done((bf16[1,272,128]{2,1,0:T(8,128)(2,1)S(1)}, bf16[1,272,128]{2,1,0:T(8,128)(2,1)S(1)}, u32[]{:S(2)}, u32[]{:S(2)}) %collective-permute-start) | collective-permute-done | bytes 69664 | tf_op jit(solution)/shard_map/ppermute | solution.py:259
  12.2 0.7 %collective-permute-start.1 = (bf16[2,272,128]{2,1,0:T(8,128)(2,1)S(1)}, bf16[2,272,128]{2,1,0:T(8,128)(2,1)S(1)}, u32[]{:S(2)}, u32[]{:S(2)}) collective-permute-start(bf16[2,272,128]{2,1,0:T(8,128)(2,1)S(1)} %pad_maximum_fusion.refs_0_), channel_id=1, source_target_pairs={{0,2},{1,3},{2,0},{3,1},{4,6},{5,7},{6,4},{7,5},{8,10},{9,11},{10,... | collective-permute-start | bytes 417800 | tf_op jit(solution)/shard_map/ppermute | solution.py:259
  12.9 1.5 %collective-permute-start.2 = (bf16[2,272,128]{2,1,0:T(8,128)(2,1)S(1)}, bf16[2,272,128]{2,1,0:T(8,128)(2,1)S(1)}, u32[]{:S(2)}, u32[]{:S(2)}) collective-permute-start(bf16[2,272,128]{2,1,0:T(8,128)(2,1)S(1)} %pad_maximum_fusion.refs_0_), channel_id=1, source_target_pairs={{0,1},{1,0},{2,3},{3,2},{4,5},{5,4},{6,7},{7,6},{8,9},{9,8},{10,11... | collective-permute-start | bytes 417800 | tf_op jit(solution)/shard_map/ppermute | solution.py:259
  14.4 2.9 %collective-permute-done.1.refs_1_ = bf16[2,272,128]{2,1,0:T(8,128)(2,1)S(1)} collective-permute-done((bf16[2,272,128]{2,1,0:T(8,128)(2,1)S(1)}, bf16[2,272,128]{2,1,0:T(8,128)(2,1)S(1)}, u32[]{:S(2)}, u32[]{:S(2)}) %collective-permute-start.1) | collective-permute-done | bytes 139296 | tf_op jit(solution)/shard_map/ppermute | solution.py:259
  17.3 1.5 %collective-permute-start.3 = (bf16[2,272,128]{2,1,0:T(8,128)(2,1)S(1)}, bf16[2,272,128]{2,1,0:T(8,128)(2,1)S(1)}, u32[]{:S(2)}, u32[]{:S(2)}) collective-permute-start(bf16[2,272,128]{2,1,0:T(8,128)(2,1)S(1)} %collective-permute-done.1.refs_1_), channel_id=1, source_target_pairs={{0,1},{1,0},{2,3},{3,2},{4,5},{5,4},{6,7},{7,6},{8,9},{9,8},{10,11... | collective-permute-start | bytes 417800 | tf_op jit(solution)/shard_map/ppermute | solution.py:259
  18.8 0.1 pad_add_fusion
  18.9 0.9 %select_reduce_fusion.docs_ref = s32[64]{0:T(128)S(1)} fusion(s32[512]{0:T(512)} %param.7, s32[64]{0:T(128)S(1)} %pad_add_fusion), kind=kLoop, calls=%fused_computation.1 | loop fusion | flops 98240 | bytes 2560 | tf_op jit(solution)/shard_map/reduce_sum | solution.py:329
  19.8 0.0 collective-permute-done.4.refs_1_
  19.8 0.0 copy-start
  19.8 1.2 %copy-done = bf16[16,256,128]{2,1,0:T(8,128)(2,1)S(1)} copy-done((bf16[16,256,128]{2,1,0:T(8,128)(2,1)S(1)}, bf16[16,256,128]{2,1,0:T(8,128)(2,1)}, u32[]{:S(2)}) %copy-start) | copy-done | bytes 1048600
  21.0 1.7 %passage_units.1 = (bf16[16,256,128]{2,1,0:T(8,128)(2,1)S(1)}, bf16[16,128,256]{2,1,0:T(8,128)(2,1)S(1)}, bf16[16,256,128]{2,1,0:T(8,128)(2,1)S(1)}, bf16[16,128,256]{2,1,0:T(8,128)(2,1)S(1)}) custom-call(bf16[16,256,128]{2,1,0:T(8,128)(2,1)S(1)} %copy-done, bf16[16,256,128]{2,1,0:T(8,128)(2,1)S(1)} %collective-permute-done.4.refs_1_), custom_call_target="tpu_custom_call" | custom-call | tf_op jit(solution)/shard_map/passage_units/pallas_call | solution.py:312
  22.7 0.0 collective-permute-done.3.refs_3_
  22.7 0.0 collective-permute-done.2.refs_2_
  22.7 1.6 %route.1 = (bf16[2176,128]{1,0:T(8,128)(2,1)S(1)}, s32[6,3,1,128]{3,2,1,0:T(1,128)S(1)}) custom-call(s32[64]{0:T(128)S(1)} %select_reduce_fusion.docs_ref, bf16[2,272,128]{2,1,0:T(8,128)(2,1)S(1)} %pad_maximum_fusion.refs_0_, bf16[2,272,128]{2,1,0:T(8,128)(2,1)S(1)} %collective-permute-done.1.refs_1_, ...), custom_call_target="tpu_custom_call" | custom-call | tf_op jit(solution)/shard_map/route/pallas_call | solution.py:336
  24.3 2.7 %score.2 = (f32[4128,128]{1,0:T(8,128)S(1)}, f32[129,128]{1,0:T(8,128)S(1)}) custom-call(s32[6,3,1,128]{3,2,1,0:T(1,128)S(1)} %get-tuple-element.45.lists_ref, bf16[2176,128]{1,0:T(8,128)(2,1)S(1)} %get-tuple-element.46.pay_ref, bf16[16,256,128]{2,1,0:T(8,128)(2,1)S(1)} %get-tuple-element.47.refs_0_, bf16[16,128,256]{2,1,0:T(8,128)(2,1)S(1)} %get-tuple-element.48.refs_1_, ...), custom_call_target="tpu_custom_call" | custom-call | tf_op jit(solution)/shard_map/score/pallas_call | solution.py:356
  27.0 0.6 %collective-permute-done.5.raw_ref = bf16[16,256,128]{2,1,0:T(8,128)(2,1)S(1)} collective-permute-done((bf16[16,256,128]{2,1,0:T(8,128)(2,1)}, bf16[16,256,128]{2,1,0:T(8,128)(2,1)S(1)}, u32[]{:S(2)}, u32[]{:S(2)}) %collective-permute-start.5) | collective-permute-done | bytes 1048608 | tf_op jit(solution)/shard_map/ppermute | solution.py:259
  27.7 0.0 collective-permute-start.6
  27.7 1.5 %score_far.2 = (f32[4128,128]{1,0:T(8,128)S(1)}, f32[129,128]{1,0:T(8,128)S(1)}, bf16[16,256,128]{2,1,0:T(8,128)(2,1)S(1)}, bf16[16,128,256]{2,1,0:T(8,128)(2,1)S(1)}) custom-call(s32[6,3,1,128]{3,2,1,0:T(1,128)S(1)} %get-tuple-element.45.lists_ref, bf16[2176,128]{1,0:T(8,128)(2,1)S(1)} %get-tuple-element.46.pay_ref, ...), custom_call_target="tpu_custom_call", output_to_operand_aliasing={{0}: (3, {}), {1}: (4, {})} | custom-call | tf_op jit(solution)/shard_map/score_far/pallas_call | solution.py:375
  29.2 1.2 %collective-permute-done.6.raw_ref = bf16[16,256,128]{2,1,0:T(8,128)(2,1)S(1)} collective-permute-done((bf16[16,256,128]{2,1,0:T(8,128)(2,1)S(1)}, bf16[16,256,128]{2,1,0:T(8,128)(2,1)S(1)}, u32[]{:S(2)}, u32[]{:S(2)}) %collective-permute-start.6) | collective-permute-done | bytes 1048608 | tf_op jit(solution)/shard_map/ppermute | solution.py:259
  30.3 1.5 %score_far.3 = (f32[4128,128]{1,0:T(8,128)S(1)}, f32[129,128]{1,0:T(8,128)S(1)}, bf16[16,256,128]{2,1,0:T(8,128)(2,1)S(1)}, bf16[16,128,256]{2,1,0:T(8,128)(2,1)...) custom-call(s32[6,3,1,128]{3,2,1,0:T(1,128)S(1)} %get-tuple-element., ...), custom_call_target="tpu_custom_call", output_to_operand_aliasing={{0}: (3, {}), {1}: (4, {})} | custom-call | tf_op jit(solution)/shard_map/score_far/pallas_call | solution.py:375
  31.9 1.8 %collective-permute-start.7 = (f32[2,2,16,128]{3,2,1,0:T(8,128)S(1)}, f32[2,2,16,128]{3,2,1,0:T(8,128)S(1)}, u32[]{:S(2)}, u32[]{:S(2)}) collective-permute-start(f32[2,2,16,128]{3,2,1,0:T(8,128)S(1)} %pad_maximum_fusion.1), channel_id=1, source_target_pairs={{0,1},{1,0},{2,3},{3,2},{4,5},{5,4},{6,7},{7,6},{8,9},{9,8},{10,11... | collective-permute-start | bytes 98312 | tf_op jit(solution)/shard_map/ppermute | solution.py:259
  33.7 0.2 collective-permute-start.11
  34.0 1.8 %collective-permute-start.12 = (bf16[1024,128]{1,0:T(8,128)(2,1)S(1)}, bf16[1024,128]{1,0:T(8,128)(2,1)S(1)}, u32[]{:S(2)}, u32[]{:S(2)}) collective-permute-start(bf16[1024,128]{1,0:T(8,128)(2,1)S(1)} %get-tuple-element.71), channel_id=1, source_target_pairs={{0,2},{1,3},{2,0},{3,1},{4,6},{5,7},{6,4},{7,5},{8,10},{9,11},{10,... | collective-permute-start | bytes 786440 | tf_op jit(solution)/shard_map/ppermute | solution.py:259
  35.8 0.0 collective-permute-done.7
  35.9 1.7 %score.3 = (f32[4128,128]{1,0:T(8,128)S(1)}, f32[129,128]{1,0:T(8,128)S(1)}) custom-call(s32[6,3,1,128]{3,2,1,0:T(1,128)S(1)} %get-tuple-element.45.lists_ref, bf16[2176,128]{1,0:T(8,128)(2,1)S(1)} %get-tuple-element.46.pay_ref, bf16[16,256,128]{2,1,0:T(8,128)(2,1)S(1)} %get-tuple-element.56.refs_0_, ...), custom_call_target="tpu_custom_call", output_to_operand_aliasing={{0}: (6, {}), {1}: (7, {})} | custom-call | tf_op jit(solution)/shard_map/score/pallas_call | solution.py:356
  37.6 3.9 %collective-permute-start.10 = (f32[2,2,8,128]{3,2,1,0:T(8,128)S(1)}, f32[2,2,8,128]{3,2,1,0:T(8,128)S(1)}, u32[]{:S(2)}, u32[]{:S(2)}) collective-permute-start(f32[2,2,8,128]{3,2,1,0:T(8,128)S(1)} %rev.8), channel_id=1, source_target_pairs={{0,6},{1,7},{2,4},{3,5},{4,2},{5,3},{6,0},{7,1},{8,14},{9,15},{10,... | collective-permute-start | bytes 49160 | tf_op jit(solution)/shard_map/ppermute | solution.py:259
  41.6 0.0 collective-permute-start.9
  41.6 0.6 %collective-permute-start.8 = (f32[2,2,8,128]{3,2,1,0:T(8,128)S(1)}, f32[2,2,8,128]{3,2,1,0:T(8,128)S(1)}, u32[]{:S(2)}, u32[]{:S(2)}) collective-permute-start(f32[2,2,8,128]{3,2,1,0:T(8,128)S(1)} %get-tuple-element.79), channel_id=1, source_target_pairs={{0,2},{1,3},{2,0},{3,1},{4,6},{5,7},{6,4},{7,5},{8,10},{9,11},{10,... | collective-permute-start | bytes 49160 | tf_op jit(solution)/shard_map/ppermute | solution.py:259
  42.2 0.0 collective-permute-done.11.got_others.others_ref
  42.2 0.0 collective-permute-done.12.got_firsts.firsts_ref
  42.3 0.0 copy-start.2
  42.3 1.7 %collective-permute-start.15 = (bf16[256,128]{1,0:T(8,128)(2,1)S(1)}, bf16[256,128]{1,0:T(8,128)(2,1)S(1)}, u32[]{:S(2)}, u32[]{:S(2)}) collective-permute-start(bf16[256,128]{1,0:T(8,128)(2,1)S(1)} %get-tuple-element.74), channel_id=1, source_target_pairs={{0,2},{1,3},{2,0},{3,1},{4,6},{5,7},{6,4},{7,5},{8,10},{9,11},{10,... | collective-permute-start | bytes 196616 | tf_op jit(solution)/shard_map/ppermute | solution.py:259
  44.0 1.6 %collective-permute-start.16 = (bf16[256,128]{1,0:T(8,128)(2,1)S(1)}, bf16[256,128]{1,0:T(8,128)(2,1)S(1)}, u32[]{:S(2)}, u32[]{:S(2)}) collective-permute-start(bf16[256,128]{1,0:T(8,128)(2,1)S(1)} %get-tuple-element.75), channel_id=1, source_target_pairs={{0,1},{1,0},{2,3},{3,2},{4,5},{5,4},{6,7},{7,6},{8,9},{9,8},{10,11... | collective-permute-start | bytes 196616 | tf_op jit(solution)/shard_map/ppermute | solution.py:259
  45.6 0.1 collective-permute-done.10
  45.7 0.6 %collective-permute-done.9 = f32[2,2,8,128]{3,2,1,0:T(8,128)S(1)} collective-permute-done((f32[2,2,8,128]{3,2,1,0:T(8,128)S(1)}, f32[2,2,8,128]{3,2,1,0:T(8,128)S(1)}, u32[]{:S(2)}, u32[]{:S(2)}) %collective-permute-start.9) | collective-permute-done | bytes 16416 | tf_op jit(solution)/shard_map/ppermute | solution.py:259
  46.3 0.0 collective-permute-done.8
  46.3 0.2 collective-permute-start.13
  46.6 1.8 %collective-permute-start.14 = (bf16[256,128]{1,0:T(8,128)(2,1)S(1)}, bf16[256,128]{1,0:T(8,128)(2,1)S(1)}, u32[]{:S(2)}, u32[]{:S(2)}) collective-permute-start(bf16[256,128]{1,0:T(8,128)(2,1)S(1)} %get-tuple-element.73), channel_id=1, source_target_pairs={{0,1},{1,0},{2,3},{3,2},{4,5},{5,4},{6,7},{7,6},{8,9},{9,8},{10,11... | collective-permute-start | bytes 196616 | tf_op jit(solution)/shard_map/ppermute | solution.py:259
  48.3 0.0 collective-permute-done.15.got_others
  48.3 0.2 collective-permute-done.16.got_firsts
  48.6 0.1 merge.3
  48.6 2.9 %collective-permute-start.17 = (bf16[256,128]{1,0:T(8,128)(2,1)S(1)}, bf16[256,128]{1,0:T(8,128)(2,1)S(1)}, u32[]{:S(2)}, u32[]{:S(2)}) collective-permute-start(bf16[256,128]{1,0:T(8,128)(2,1)S(1)} %merge.3), channel_id=1, source_target_pairs={{0,4},{1,5},{2,6},{3,7},{4,0},{5,1},{6,2},{7,3},{8,12},{9,13},{10,... | collective-permute-start | bytes 196616 | tf_op jit(solution)/shard_map/ppermute | solution.py:259
  51.5 0.0 copy-done.2
  51.5 0.6 %query_side.1 = (f32[8,32,128]{2,1,0:T(8,128)S(1)}, f32[8,32,128]{2,1,0:T(8,128)S(1)}, f32[1,8]{1,0:T(1,128)}) custom-call(bf16[8,32,128]{2,1,0:T(8,128)(2,1)S(1)} %copy-done.2, f32[2,8,128]{2,1,0:T(8,128)S(1)} %slice.52.sums_ref), custom_call_target="tpu_custom_call" | custom-call | tf_op jit(solution)/shard_map/query_side/pallas_call | solution.py:425
  52.1 0.0 collective-permute-done.13.got_others
  52.1 0.0 collective-permute-done.14.got_firsts
  52.1 1.7 %collective-permute-done.17.got_ref = bf16[256,128]{1,0:T(8,128)(2,1)S(1)} collective-permute-done((bf16[256,128]{1,0:T(8,128)(2,1)S(1)}, bf16[256,128]{1,0:T(8,128)(2,1)S(1)}, u32[]{:S(2)}, u32[]{:S(2)}) %collective-permute-start.17) | collective-permute-done | bytes 65568 | tf_op jit(solution)/shard_map/ppermute | solution.py:259
  53.9 0.8 %last.1 = f32[8,32,128]{2,1,0:T(8,128)} custom-call(f32[256,128]{1,0:T(8,128)S(1)} %merge.2.keep_ref, bf16[256,128]{1,0:T(8,128)(2,1)S(1)} %collective-permute-done.17.got_ref, f32[8,32,128]{2,1,0:T(8,128)S(1)} %get-tuple-element.76.unit_ref, f32[8,32,128]{2,1,0:T(8,128)S(1)} %get-tuple-element.77.scale_ref), custom_call_target="tpu_custom_call" | custom-call | tf_op jit(solution)/shard_map/last/pallas_call | solution.py:430
  (18 shorter events, 0.2 us)
Async XLA Ops:
  0.6 19.1 %collective-permute-start.4 = (bf16[16,256,128]{2,1,0:T(8,128)(2,1)}, bf16[16,256,128]{2,1,0:T(8,128)(2,1)S(1)}, u32[]{:S(2)}, u32[]{:S(2)}) collective-permute-start(bf16[16,256,128]{2,1,0:T(8,128)(2,1)} %refs_0_.1), channel_id=1, source_target_pairs={{0,8},{8,0},{16,24},{24,16},{1,9},{9,1},{17,25},{25,17},{2,10},{10... | collective-permute-start | bytes 3145736 | tf_op jit(solution)/shard_map/ppermute | solution.py:259
  1.1 26.5 %collective-permute-start.5 = (bf16[16,256,128]{2,1,0:T(8,128)(2,1)}, bf16[16,256,128]{2,1,0:T(8,128)(2,1)S(1)}, u32[]{:S(2)}, u32[]{:S(2)}) collective-permute-start(bf16[16,256,128]{2,1,0:T(8,128)(2,1)} %refs_0_.1), channel_id=1, source_target_pairs={{0,16},{8,24},{16,0},{24,8},{1,17},{9,25},{17,1},{25,9},{2,18},{10... | collective-permute-start | bytes 3145736 | tf_op jit(solution)/shard_map/ppermute | solution.py:259
  3.7 0.8 %copy-start.1 = (bf16[8,32,128]{2,1,0:T(8,128)(2,1)S(1)}, bf16[8,32,128]{2,1,0:T(8,128)(2,1)}, u32[]{:S(2)}) copy-start(bf16[8,32,128]{2,1,0:T(8,128)(2,1)} %queries_ref.3) | copy-start | bytes 196612
  4.6 0.7 %copy-start.3 = (s32[8,16]{1,0:T(8,128)S(1)}, s32[8,16]{1,0:T(8,128)}, u32[]{:S(2)}) copy-start(s32[8,16]{1,0:T(8,128)} %cand_ref.1) | copy-start | bytes 1540
  5.4 6.8 %collective-permute-start = (bf16[1,272,128]{2,1,0:T(8,128)(2,1)S(1)}, bf16[1,272,128]{2,1,0:T(8,128)(2,1)S(1)}, u32[]{:S(2)}, u32[]{:S(2)}) collective-permute-start(bf16[1,272,128]{2,1,0:T(8,128)(2,1)S(1)} %bitcast.20), channel_id=1, source_target_pairs={{0,4},{1,5},{2,6},{3,7},{4,0},{5,1},{6,2},{7,3},{8,12},{9,13},{10,... | collective-permute-start | bytes 208904 | tf_op jit(solution)/shard_map/ppermute | solution.py:259
  12.2 5.1 %collective-permute-start.1 = (bf16[2,272,128]{2,1,0:T(8,128)(2,1)S(1)}, bf16[2,272,128]{2,1,0:T(8,128)(2,1)S(1)}, u32[]{:S(2)}, u32[]{:S(2)}) collective-permute-start(bf16[2,272,128]{2,1,0:T(8,128)(2,1)S(1)} %pad_maximum_fusion.refs_0_), channel_id=1, source_target_pairs={{0,2},{1,3},{2,0},{3,1},{4,6},{5,7},{6,4},{7,5},{8,10},{9,11},{10,... | collective-permute-start | bytes 417800 | tf_op jit(solution)/shard_map/ppermute | solution.py:259
  12.9 9.9 %collective-permute-start.2 = (bf16[2,272,128]{2,1,0:T(8,128)(2,1)S(1)}, bf16[2,272,128]{2,1,0:T(8,128)(2,1)S(1)}, u32[]{:S(2)}, u32[]{:S(2)}) collective-permute-start(bf16[2,272,128]{2,1,0:T(8,128)(2,1)S(1)} %pad_maximum_fusion.refs_0_), channel_id=1, source_target_pairs={{0,1},{1,0},{2,3},{3,2},{4,5},{5,4},{6,7},{7,6},{8,9},{9,8},{10,11... | collective-permute-start | bytes 417800 | tf_op jit(solution)/shard_map/ppermute | solution.py:259
  17.3 5.4 %collective-permute-start.3 = (bf16[2,272,128]{2,1,0:T(8,128)(2,1)S(1)}, bf16[2,272,128]{2,1,0:T(8,128)(2,1)S(1)}, u32[]{:S(2)}, u32[]{:S(2)}) collective-permute-start(bf16[2,272,128]{2,1,0:T(8,128)(2,1)S(1)} %collective-permute-done.1.refs_1_), channel_id=1, source_target_pairs={{0,1},{1,0},{2,3},{3,2},{4,5},{5,4},{6,7},{7,6},{8,9},{9,8},{10,11... | collective-permute-start | bytes 417800 | tf_op jit(solution)/shard_map/ppermute | solution.py:259
  19.8 1.2 %copy-start = (bf16[16,256,128]{2,1,0:T(8,128)(2,1)S(1)}, bf16[16,256,128]{2,1,0:T(8,128)(2,1)}, u32[]{:S(2)}) copy-start(bf16[16,256,128]{2,1,0:T(8,128)(2,1)} %refs_0_.1) | copy-start | bytes 3145732
  27.7 2.7 %collective-permute-start.6 = (bf16[16,256,128]{2,1,0:T(8,128)(2,1)S(1)}, bf16[16,256,128]{2,1,0:T(8,128)(2,1)S(1)}, u32[]{:S(2)}, u32[]{:S(2)}) collective-permute-start(bf16[16,256,128]{2,1,0:T(8,128)(2,1)S(1)} %collective-permute-done.5.raw_ref), channel_id=1, source_target_pairs={{0,8},{8,0},{16,24},{24,16},{1,9},{9,1},{17,25},{25,17},{2,10},{10... | collective-permute-start | bytes 3145736 | tf_op jit(solution)/shard_map/ppermute | solution.py:259
  31.9 4.0 %collective-permute-start.7 = (f32[2,2,16,128]{3,2,1,0:T(8,128)S(1)}, f32[2,2,16,128]{3,2,1,0:T(8,128)S(1)}, u32[]{:S(2)}, u32[]{:S(2)}) collective-permute-start(f32[2,2,16,128]{3,2,1,0:T(8,128)S(1)} %pad_maximum_fusion.1), channel_id=1, source_target_pairs={{0,1},{1,0},{2,3},{3,2},{4,5},{5,4},{6,7},{7,6},{8,9},{9,8},{10,11... | collective-permute-start | bytes 98312 | tf_op jit(solution)/shard_map/ppermute | solution.py:259
  33.7 8.5 %collective-permute-start.11 = (bf16[1024,128]{1,0:T(8,128)(2,1)S(1)}, bf16[1024,128]{1,0:T(8,128)(2,1)S(1)}, u32[]{:S(2)}, u32[]{:S(2)}) collective-permute-start(bf16[1024,128]{1,0:T(8,128)(2,1)S(1)} %get-tuple-element.70), channel_id=1, source_target_pairs={{0,1},{1,0},{2,3},{3,2},{4,5},{5,4},{6,7},{7,6},{8,9},{9,8},{10,11... | collective-permute-start | bytes 786440 | tf_op jit(solution)/shard_map/ppermute | solution.py:259
  34.0 8.2 %collective-permute-start.12 = (bf16[1024,128]{1,0:T(8,128)(2,1)S(1)}, bf16[1024,128]{1,0:T(8,128)(2,1)S(1)}, u32[]{:S(2)}, u32[]{:S(2)}) collective-permute-start(bf16[1024,128]{1,0:T(8,128)(2,1)S(1)} %get-tuple-element.71), channel_id=1, source_target_pairs={{0,2},{1,3},{2,0},{3,1},{4,6},{5,7},{6,4},{7,5},{8,10},{9,11},{10,... | collective-permute-start | bytes 786440 | tf_op jit(solution)/shard_map/ppermute | solution.py:259
  37.6 8.1 %collective-permute-start.10 = (f32[2,2,8,128]{3,2,1,0:T(8,128)S(1)}, f32[2,2,8,128]{3,2,1,0:T(8,128)S(1)}, u32[]{:S(2)}, u32[]{:S(2)}) collective-permute-start(f32[2,2,8,128]{3,2,1,0:T(8,128)S(1)} %rev.8), channel_id=1, source_target_pairs={{0,6},{1,7},{2,4},{3,5},{4,2},{5,3},{6,0},{7,1},{8,14},{9,15},{10,... | collective-permute-start | bytes 49160 | tf_op jit(solution)/shard_map/ppermute | solution.py:259
  41.6 4.7 %collective-permute-start.9 = (f32[2,2,8,128]{3,2,1,0:T(8,128)S(1)}, f32[2,2,8,128]{3,2,1,0:T(8,128)S(1)}, u32[]{:S(2)}, u32[]{:S(2)}) collective-permute-start(f32[2,2,8,128]{3,2,1,0:T(8,128)S(1)} %rev.7), channel_id=1, source_target_pairs={{0,4},{1,5},{2,6},{3,7},{4,0},{5,1},{6,2},{7,3},{8,12},{9,13},{10,... | collective-permute-start | bytes 49160 | tf_op jit(solution)/shard_map/ppermute | solution.py:259
  41.6 4.7 %collective-permute-start.8 = (f32[2,2,8,128]{3,2,1,0:T(8,128)S(1)}, f32[2,2,8,128]{3,2,1,0:T(8,128)S(1)}, u32[]{:S(2)}, u32[]{:S(2)}) collective-permute-start(f32[2,2,8,128]{3,2,1,0:T(8,128)S(1)} %get-tuple-element.79), channel_id=1, source_target_pairs={{0,2},{1,3},{2,0},{3,1},{4,6},{5,7},{6,4},{7,5},{8,10},{9,11},{10,... | collective-permute-start | bytes 49160 | tf_op jit(solution)/shard_map/ppermute | solution.py:259
  42.3 9.2 %copy-start.2 = (bf16[8,32,128]{2,1,0:T(8,128)(2,1)S(1)}, bf16[8,32,128]{2,1,0:T(8,128)(2,1)}, u32[]{:S(2)}) copy-start(bf16[8,32,128]{2,1,0:T(8,128)(2,1)} %queries_ref.3) | copy-start | bytes 196612
  42.3 6.0 %collective-permute-start.15 = (bf16[256,128]{1,0:T(8,128)(2,1)S(1)}, bf16[256,128]{1,0:T(8,128)(2,1)S(1)}, u32[]{:S(2)}, u32[]{:S(2)}) collective-permute-start(bf16[256,128]{1,0:T(8,128)(2,1)S(1)} %get-tuple-element.74), channel_id=1, source_target_pairs={{0,2},{1,3},{2,0},{3,1},{4,6},{5,7},{6,4},{7,5},{8,10},{9,11},{10,... | collective-permute-start | bytes 196616 | tf_op jit(solution)/shard_map/ppermute | solution.py:259
  44.0 4.6 %collective-permute-start.16 = (bf16[256,128]{1,0:T(8,128)(2,1)S(1)}, bf16[256,128]{1,0:T(8,128)(2,1)S(1)}, u32[]{:S(2)}, u32[]{:S(2)}) collective-permute-start(bf16[256,128]{1,0:T(8,128)(2,1)S(1)} %get-tuple-element.75), channel_id=1, source_target_pairs={{0,1},{1,0},{2,3},{3,2},{4,5},{5,4},{6,7},{7,6},{8,9},{9,8},{10,11... | collective-permute-start | bytes 196616 | tf_op jit(solution)/shard_map/ppermute | solution.py:259
  46.3 5.7 %collective-permute-start.13 = (bf16[256,128]{1,0:T(8,128)(2,1)S(1)}, bf16[256,128]{1,0:T(8,128)(2,1)S(1)}, u32[]{:S(2)}, u32[]{:S(2)}) collective-permute-start(bf16[256,128]{1,0:T(8,128)(2,1)S(1)} %get-tuple-element.72), channel_id=1, source_target_pairs={{0,2},{1,3},{2,0},{3,1},{4,6},{5,7},{6,4},{7,5},{8,10},{9,11},{10,... | collective-permute-start | bytes 196616 | tf_op jit(solution)/shard_map/ppermute | solution.py:259
  46.6 5.5 %collective-permute-start.14 = (bf16[256,128]{1,0:T(8,128)(2,1)S(1)}, bf16[256,128]{1,0:T(8,128)(2,1)S(1)}, u32[]{:S(2)}, u32[]{:S(2)}) collective-permute-start(bf16[256,128]{1,0:T(8,128)(2,1)S(1)} %get-tuple-element.73), channel_id=1, source_target_pairs={{0,1},{1,0},{2,3},{3,2},{4,5},{5,4},{6,7},{7,6},{8,9},{9,8},{10,11... | collective-permute-start | bytes 196616 | tf_op jit(solution)/shard_map/ppermute | solution.py:259
  48.6 5.2 %collective-permute-start.17 = (bf16[256,128]{1,0:T(8,128)(2,1)S(1)}, bf16[256,128]{1,0:T(8,128)(2,1)S(1)}, u32[]{:S(2)}, u32[]{:S(2)}) collective-permute-start(bf16[256,128]{1,0:T(8,128)(2,1)S(1)} %merge.3), channel_id=1, source_target_pairs={{0,4},{1,5},{2,6},{3,7},{4,0},{5,1},{6,2},{7,3},{8,12},{9,13},{10,... | collective-permute-start | bytes 196616 | tf_op jit(solution)/shard_map/ppermute | solution.py:259

commit v9 on v8

--- a/solution.py
+++ b/solution.py
@@ -51,7 +51,7 @@
     out_ref[rows:] = digits.astype(F32).astype(BF16)
 
 
-def turn_units(source, units_ref, turned_ref):
+def turn_units(source, units_ref, turned_ref=None):
     count = source.shape[0]
     together = min(count, 16)
 
@@ -60,7 +60,8 @@
             at = index * together + offset
             units = unit(source[at])[0].astype(BF16)
             units_ref[at] = units
-            turned_ref[at] = units.T
+            if turned_ref is not None:
+                turned_ref[at] = units.T
         return carry
 
     lax.fori_loop(0, count // together, step, 0)
@@ -136,6 +137,7 @@
 def score_pairs(list_ref, pay_ref, pass_ref, turned_ref, acc_ref, sums_ref, length):
     queries = sums_ref.shape[0] // 2
     count = list_ref[2, 0, 0]
+    contract = (((1,), (1,)), ((), ()))
 
     def step(index, carry):
         pairs = []
@@ -147,7 +149,9 @@
             place = lax.shift_right_logical(code, SHIFT.bit_length() - 1)
             pairs.append((list_ref[1, part, lane], pay_ref[pl.ds(row, length)], place))
         logits = [
-            jnp.dot(tokens, turned_ref[place], preferred_element_type=F32)
+            lax.dot_general(tokens, pass_ref[place], contract, preferred_element_type=F32)
+            if turned_ref is None
+            else jnp.dot(tokens, turned_ref[place], preferred_element_type=F32)
             for _, tokens, place in pairs
         ]
         terms = [jnp.exp(block * (1.0 / SOFTNESS)) for block in logits]
@@ -173,7 +177,8 @@
 
 
 def score_body(lists_ref, pay_ref, *refs, piece, count, begin, length):
-    pass_refs, refs = refs[: 2 * count], refs[2 * count :]
+    kinds = 2 if begin else 1
+    pass_refs, refs = refs[: kinds * count], refs[kinds * count :]
     acc_ref, sums_ref, list_ref, sem = refs if begin else refs[2:]
     move = pltpu.make_async_copy(lists_ref.at[piece : piece + count], list_ref, sem)
     move.start()
@@ -185,8 +190,8 @@
         score_pairs(
             list_ref.at[index],
             pay_ref,
-            pass_refs[2 * index],
-            pass_refs[2 * index + 1],
+            pass_refs[kinds * index],
+            pass_refs[kinds * index + 1] if begin else None,
             acc_ref,
             sums_ref,
             length,
@@ -194,14 +199,14 @@
 
 
 def far_score_body(
-    lists_ref, pay_ref, raw_ref, _, __, acc_ref, sums_ref, pass_ref, turned_ref, *refs, piece, length
+    lists_ref, pay_ref, raw_ref, _, __, acc_ref, sums_ref, pass_ref, *refs, piece, length
 ):
     *send_refs, list_ref, sem = refs
     move = pltpu.make_async_copy(lists_ref.at[piece], list_ref, sem)
     move.start()
-    turn_units(raw_ref, pass_ref, turned_ref)
+    turn_units(raw_ref, pass_ref)
     move.wait()
-    score_pairs(list_ref, pay_ref, pass_ref, turned_ref, acc_ref, sums_ref, length)
+    score_pairs(list_ref, pay_ref, pass_ref, None, acc_ref, sums_ref, length)
     if send_refs:
         others_ref, firsts_ref = send_refs
         half = others_ref.shape[0]
@@ -374,15 +379,15 @@
         last = index == near_count - 1
         acc, sums, *blocks = call(
             functools.partial(far_score_body, piece=near_count + index, length=length),
-            totals + [shape(passages.shape, BF16), turned] + (sends if last else []),
+            totals + [shape(passages.shape, BF16)] + (sends if last else []),
             "score_far",
             [vmem] * 5,
             {3: 0, 4: 1},
             [pltpu.SMEM((3, parts, LANES), jnp.int32), pltpu.SemaphoreType.DMA(())],
         )(lists, pay, raw, *state)
         state = (acc, sums)
-        far += blocks[:2]
-    others, firsts = blocks[2:]
+        far += blocks[:1]
+    others, firsts = blocks[1:]
 
     steps = bits_of(dev_count)[::-1]
     got_others = swap(others, "dev", steps[0])

time: 55.2 us -> 56.3 us (1.020)
  Pallas kernels: 12.3 us -> 13.1 us
  transfers between devices with their start and end apart: 18 -> 18, of which waited for: 8 -> 6; matrix products, arithmetic and copies ran while one was open for 2% -> 2% of each run, Pallas kernels for 18% -> 19%
where the time goes in v9:
time: 56.3 us; the launch traced here: 55.3 us
  starting transfers between devices  25.9 us (46%)
  Pallas kernels  13.1 us (23%)
  waiting for transfers between devices  11.8 us (21%)
  local copies, waits for them, and re-layouts  2.79 us (5%)
  other arithmetic  0.98 us (2%)
  between operations  0.85 us (2%)
    ppermute x18, starting transfers between devices, swap(): lax.ppermute(value, axis, [(index, index ^ bit) for index in range(size)])  25.9 us
    ppermute x18, waiting for transfers between devices, swap(): lax.ppermute(value, axis, [(index, index ^ bit) for index in range(size)])  11.8 us
    pallas_call x2, Pallas kernels, score(): call(functools.partial(score_body, piece=piece, count=near_count, begin=n...  4.82 us
    pallas_call x2, Pallas kernels, local(): call(functools.partial(far_score_body, piece=near_count + index, length=l...  3.34 us
    unnamed x8, local copies, waits for them, and re-layouts  2.75 us
    pallas_call x1, Pallas kernels, local(): call(unit_body, [shape(passages.shape, BF16), turned] * len(near_raw), 'p...  1.71 us
    pallas_call x1, Pallas kernels, local(): call(functools.partial(route_body, rows=rows, size=pass_count, groups_of=...  1.6 us
  transfers between devices with their start and end apart: 18, of which 6 were waited for; matrix products, arithmetic and copies ran while one was open for 2% of the time, Pallas kernels for 19%

profile of v9, /device:TPU:0, one launch (start us, length us, event | category | flops | bytes accessed | tf_op | source)
XLA Modules:
  0.0 55.3 jit_solution(16365267590926195613)
XLA Ops:
  0.6 0.5 collective-permute-start.4
  1.1 2.6 %collective-permute-start.5 = (bf16[16,256,128]{2,1,0:T(8,128)(2,1)}, bf16[16,256,128]{2,1,0:T(8,128)(2,1)S(1)}, u32[]{:S(2)}, u32[]{:S(2)}) collective-permute-start(bf16[16,256,128]{2,1,0:T(8,128)(2,1)} %refs_0_.1), channel_id=1, source_target_pairs={{0,16},{8,24},{16,0},{24,8},{1,17},{9,25},{17,1},{25,9},{2,18},{10... | collective-permute-start | bytes 3145736 | tf_op jit(solution)/shard_map/ppermute | solution.py:264
  3.7 0.0 copy-start.1
  3.7 0.8 %copy-done.1 = bf16[8,32,128]{2,1,0:T(8,128)(2,1)S(1)} copy-done((bf16[8,32,128]{2,1,0:T(8,128)(2,1)S(1)}, bf16[8,32,128]{2,1,0:T(8,128)(2,1)}, u32[]{:S(2)}) %copy-start.1) | copy-done | bytes 65560
  4.6 0.0 copy-start.3
  4.6 0.7 %copy-done.3 = s32[8,16]{1,0:T(8,128)S(1)} copy-done((s32[8,16]{1,0:T(8,128)S(1)}, s32[8,16]{1,0:T(8,128)}, u32[]{:S(2)}) %copy-start.3) | copy-done | bytes 536
  5.2 0.1 query_units.1
  5.4 2.7 %collective-permute-start = (bf16[1,272,128]{2,1,0:T(8,128)(2,1)S(1)}, bf16[1,272,128]{2,1,0:T(8,128)(2,1)S(1)}, u32[]{:S(2)}, u32[]{:S(2)}) collective-permute-start(bf16[1,272,128]{2,1,0:T(8,128)(2,1)S(1)} %bitcast.20), channel_id=1, source_target_pairs={{0,4},{1,5},{2,6},{3,7},{4,0},{5,1},{6,2},{7,3},{8,12},{9,13},{10,... | collective-permute-start | bytes 208904 | tf_op jit(solution)/shard_map/ppermute | solution.py:264
  8.0 4.1 %collective-permute-done = bf16[1,272,128]{2,1,0:T(8,128)(2,1)S(1)} collective-permute-done((bf16[1,272,128]{2,1,0:T(8,128)(2,1)S(1)}, bf16[1,272,128]{2,1,0:T(8,128)(2,1)S(1)}, u32[]{:S(2)}, u32[]{:S(2)}) %collective-permute-start) | collective-permute-done | bytes 69664 | tf_op jit(solution)/shard_map/ppermute | solution.py:264
  12.2 0.7 %collective-permute-start.1 = (bf16[2,272,128]{2,1,0:T(8,128)(2,1)S(1)}, bf16[2,272,128]{2,1,0:T(8,128)(2,1)S(1)}, u32[]{:S(2)}, u32[]{:S(2)}) collective-permute-start(bf16[2,272,128]{2,1,0:T(8,128)(2,1)S(1)} %pad_maximum_fusion.refs_0_), channel_id=1, source_target_pairs={{0,2},{1,3},{2,0},{3,1},{4,6},{5,7},{6,4},{7,5},{8,10},{9,11},{10,... | collective-permute-start | bytes 417800 | tf_op jit(solution)/shard_map/ppermute | solution.py:264
  12.9 1.5 %collective-permute-start.2 = (bf16[2,272,128]{2,1,0:T(8,128)(2,1)S(1)}, bf16[2,272,128]{2,1,0:T(8,128)(2,1)S(1)}, u32[]{:S(2)}, u32[]{:S(2)}) collective-permute-start(bf16[2,272,128]{2,1,0:T(8,128)(2,1)S(1)} %pad_maximum_fusion.refs_0_), channel_id=1, source_target_pairs={{0,1},{1,0},{2,3},{3,2},{4,5},{5,4},{6,7},{7,6},{8,9},{9,8},{10,11... | collective-permute-start | bytes 417800 | tf_op jit(solution)/shard_map/ppermute | solution.py:264
  14.4 2.9 %collective-permute-done.1.refs_1_ = bf16[2,272,128]{2,1,0:T(8,128)(2,1)S(1)} collective-permute-done((bf16[2,272,128]{2,1,0:T(8,128)(2,1)S(1)}, bf16[2,272,128]{2,1,0:T(8,128)(2,1)S(1)}, u32[]{:S(2)}, u32[]{:S(2)}) %collective-permute-start.1) | collective-permute-done | bytes 139296 | tf_op jit(solution)/shard_map/ppermute | solution.py:264
  17.3 1.5 %collective-permute-start.3 = (bf16[2,272,128]{2,1,0:T(8,128)(2,1)S(1)}, bf16[2,272,128]{2,1,0:T(8,128)(2,1)S(1)}, u32[]{:S(2)}, u32[]{:S(2)}) collective-permute-start(bf16[2,272,128]{2,1,0:T(8,128)(2,1)S(1)} %collective-permute-done.1.refs_1_), channel_id=1, source_target_pairs={{0,1},{1,0},{2,3},{3,2},{4,5},{5,4},{6,7},{7,6},{8,9},{9,8},{10,11... | collective-permute-start | bytes 417800 | tf_op jit(solution)/shard_map/ppermute | solution.py:264
  18.8 0.1 pad_add_fusion
  18.9 0.9 %select_reduce_fusion.docs_ref = s32[64]{0:T(128)S(1)} fusion(s32[512]{0:T(512)} %param.7, s32[64]{0:T(128)S(1)} %pad_add_fusion), kind=kLoop, calls=%fused_computation.1 | loop fusion | flops 98240 | bytes 2560 | tf_op jit(solution)/shard_map/reduce_sum | solution.py:334
  19.8 0.0 collective-permute-done.4.refs_1_
  19.8 0.0 copy-start
  19.8 1.2 %copy-done = bf16[16,256,128]{2,1,0:T(8,128)(2,1)S(1)} copy-done((bf16[16,256,128]{2,1,0:T(8,128)(2,1)S(1)}, bf16[16,256,128]{2,1,0:T(8,128)(2,1)}, u32[]{:S(2)}) %copy-start) | copy-done | bytes 1048600
  21.0 1.7 %passage_units.1 = (bf16[16,256,128]{2,1,0:T(8,128)(2,1)S(1)}, bf16[16,128,256]{2,1,0:T(8,128)(2,1)S(1)}, bf16[16,256,128]{2,1,0:T(8,128)(2,1)S(1)}, bf16[16,128,256]{2,1,0:T(8,128)(2,1)S(1)}) custom-call(bf16[16,256,128]{2,1,0:T(8,128)(2,1)S(1)} %copy-done, bf16[16,256,128]{2,1,0:T(8,128)(2,1)S(1)} %collective-permute-done.4.refs_1_), custom_call_target="tpu_custom_call" | custom-call | tf_op jit(solution)/shard_map/passage_units/pallas_call | solution.py:317
  22.7 0.0 collective-permute-done.3.refs_3_
  22.7 0.0 collective-permute-done.2.refs_2_
  22.7 1.6 %route.1 = (bf16[2176,128]{1,0:T(8,128)(2,1)S(1)}, s32[6,3,1,128]{3,2,1,0:T(1,128)S(1)}) custom-call(s32[64]{0:T(128)S(1)} %select_reduce_fusion.docs_ref, bf16[2,272,128]{2,1,0:T(8,128)(2,1)S(1)} %pad_maximum_fusion.refs_0_, bf16[2,272,128]{2,1,0:T(8,128)(2,1)S(1)} %collective-permute-done.1.refs_1_, ...), custom_call_target="tpu_custom_call" | custom-call | tf_op jit(solution)/shard_map/route/pallas_call | solution.py:341
  24.3 2.7 %score.2 = (f32[4128,128]{1,0:T(8,128)S(1)}, f32[129,128]{1,0:T(8,128)S(1)}) custom-call(s32[6,3,1,128]{3,2,1,0:T(1,128)S(1)} %get-tuple-element.43.lists_ref, bf16[2176,128]{1,0:T(8,128)(2,1)S(1)} %get-tuple-element.44.pay_ref, bf16[16,256,128]{2,1,0:T(8,128)(2,1)S(1)} %get-tuple-element.45.refs_0_, bf16[16,128,256]{2,1,0:T(8,128)(2,1)S(1)} %get-tuple-element.46.refs_1_, ...), custom_call_target="tpu_custom_call" | custom-call | tf_op jit(solution)/shard_map/score/pallas_call | solution.py:361
  27.0 0.6 %collective-permute-done.5.raw_ref = bf16[16,256,128]{2,1,0:T(8,128)(2,1)S(1)} collective-permute-done((bf16[16,256,128]{2,1,0:T(8,128)(2,1)}, bf16[16,256,128]{2,1,0:T(8,128)(2,1)S(1)}, u32[]{:S(2)}, u32[]{:S(2)}) %collective-permute-start.5) | collective-permute-done | bytes 1048608 | tf_op jit(solution)/shard_map/ppermute | solution.py:264
  27.7 0.0 collective-permute-start.6
  27.7 1.4 %score_far.2 = (f32[4128,128]{1,0:T(8,128)S(1)}, f32[129,128]{1,0:T(8,128)S(1)}, bf16[16,256,128]{2,1,0:T(8,128)(2,1)S(1)}) custom-call(s32[6,3,1,128]{3,2,1,0:T(1,128)S(1)} %get-tuple-element.43.lists_ref, bf16[2176,128]{1,0:T(8,128)(2,1)S(1)} %get-tuple-element.44.pay_ref, ...), custom_call_target="tpu_custom_call", output_to_operand_aliasing={{0}: (3, {}), {1}: (4, {})} | custom-call | tf_op jit(solution)/shard_map/score_far/pallas_call | solution.py:380
  29.1 1.2 %collective-permute-done.6.raw_ref = bf16[16,256,128]{2,1,0:T(8,128)(2,1)S(1)} collective-permute-done((bf16[16,256,128]{2,1,0:T(8,128)(2,1)S(1)}, bf16[16,256,128]{2,1,0:T(8,128)(2,1)S(1)}, u32[]{:S(2)}, u32[]{:S(2)}) %collective-permute-start.6) | collective-permute-done | bytes 1048608 | tf_op jit(solution)/shard_map/ppermute | solution.py:264
  30.3 1.9 %score_far.3 = (f32[4128,128]{1,0:T(8,128)S(1)}, f32[129,128]{1,0:T(8,128)S(1)}, bf16[16,256,128]{2,1,0:T(8,128)(2,1)S(1)}, bf16[1024,128]{1,0:T(8,128)(2,1)S(1)}, bf16[1024,128]{1,0:T(8,128)(2,1)S(1)}) custom-call(s32[6,3,1,128]{3,2,1,0:T(1,128)S(1)} %get-tuple-element.43.lists_ref, ...), custom_call_target="tpu_custom_call", output_to_operand_aliasing={{0}: (3, {}), {1}: (4, {})} | custom-call | tf_op jit(solution)/shard_map/score_far/pallas_call | solution.py:380
  32.3 1.9 %collective-permute-start.7 = (f32[2,2,16,128]{3,2,1,0:T(8,128)S(1)}, f32[2,2,16,128]{3,2,1,0:T(8,128)S(1)}, u32[]{:S(2)}, u32[]{:S(2)}) collective-permute-start(f32[2,2,16,128]{3,2,1,0:T(8,128)S(1)} %pad_maximum_fusion.1), channel_id=1, source_target_pairs={{0,1},{1,0},{2,3},{3,2},{4,5},{5,4},{6,7},{7,6},{8,9},{9,8},{10,11... | collective-permute-start | bytes 98312 | tf_op jit(solution)/shard_map/ppermute | solution.py:264
  34.2 0.2 collective-permute-start.11
  34.4 1.9 %collective-permute-start.12 = (bf16[1024,128]{1,0:T(8,128)(2,1)S(1)}, bf16[1024,128]{1,0:T(8,128)(2,1)S(1)}, u32[]{:S(2)}, u32[]{:S(2)}) collective-permute-start(bf16[1024,128]{1,0:T(8,128)(2,1)S(1)} %get-tuple-element.67), channel_id=1, source_target_pairs={{0,2},{1,3},{2,0},{3,1},{4,6},{5,7},{6,4},{7,5},{8,10},{9,11},{10,... | collective-permute-start | bytes 786440 | tf_op jit(solution)/shard_map/ppermute | solution.py:264
  36.3 0.0 collective-permute-done.7
  36.3 2.1 %score.3 = (f32[4128,128]{1,0:T(8,128)S(1)}, f32[129,128]{1,0:T(8,128)S(1)}) custom-call(s32[6,3,1,128]{3,2,1,0:T(1,128)S(1)} %get-tuple-element.43.lists_ref, bf16[2176,128]{1,0:T(8,128)(2,1)S(1)} %get-tuple-element.44.pay_ref, bf16[16,256,128]{2,1,0:T(8,128)(2,1)S(1)} %get-tuple-element.54.refs_0_, ...), custom_call_target="tpu_custom_call", output_to_operand_aliasing={{0}: (4, {}), {1}: (5, {})} | custom-call | tf_op jit(solution)/shard_map/score/pallas_call | solution.py:361
  38.5 4.0 %collective-permute-start.10 = (f32[2,2,8,128]{3,2,1,0:T(8,128)S(1)}, f32[2,2,8,128]{3,2,1,0:T(8,128)S(1)}, u32[]{:S(2)}, u32[]{:S(2)}) collective-permute-start(f32[2,2,8,128]{3,2,1,0:T(8,128)S(1)} %rev.8), channel_id=1, source_target_pairs={{0,6},{1,7},{2,4},{3,5},{4,2},{5,3},{6,0},{7,1},{8,14},{9,15},{10,... | collective-permute-start | bytes 49160 | tf_op jit(solution)/shard_map/ppermute | solution.py:264
  42.5 0.0 collective-permute-start.9
  42.5 0.6 %collective-permute-start.8 = (f32[2,2,8,128]{3,2,1,0:T(8,128)S(1)}, f32[2,2,8,128]{3,2,1,0:T(8,128)S(1)}, u32[]{:S(2)}, u32[]{:S(2)}) collective-permute-start(f32[2,2,8,128]{3,2,1,0:T(8,128)S(1)} %get-tuple-element.75), channel_id=1, source_target_pairs={{0,2},{1,3},{2,0},{3,1},{4,6},{5,7},{6,4},{7,5},{8,10},{9,11},{10,... | collective-permute-start | bytes 49160 | tf_op jit(solution)/shard_map/ppermute | solution.py:264
  43.1 0.0 collective-permute-done.11.got_others.others_ref
  43.1 0.0 collective-permute-done.12.got_firsts.firsts_ref
  43.2 0.0 copy-start.2
  43.2 1.5 %collective-permute-start.15 = (bf16[256,128]{1,0:T(8,128)(2,1)S(1)}, bf16[256,128]{1,0:T(8,128)(2,1)S(1)}, u32[]{:S(2)}, u32[]{:S(2)}) collective-permute-start(bf16[256,128]{1,0:T(8,128)(2,1)S(1)} %get-tuple-element.70), channel_id=1, source_target_pairs={{0,2},{1,3},{2,0},{3,1},{4,6},{5,7},{6,4},{7,5},{8,10},{9,11},{10,... | collective-permute-start | bytes 196616 | tf_op jit(solution)/shard_map/ppermute | solution.py:264
  44.6 1.9 %collective-permute-start.16 = (bf16[256,128]{1,0:T(8,128)(2,1)S(1)}, bf16[256,128]{1,0:T(8,128)(2,1)S(1)}, u32[]{:S(2)}, u32[]{:S(2)}) collective-permute-start(bf16[256,128]{1,0:T(8,128)(2,1)S(1)} %get-tuple-element.71), channel_id=1, source_target_pairs={{0,1},{1,0},{2,3},{3,2},{4,5},{5,4},{6,7},{7,6},{8,9},{9,8},{10,11... | collective-permute-start | bytes 196616 | tf_op jit(solution)/shard_map/ppermute | solution.py:264
  46.5 0.0 collective-permute-done.10
  46.5 0.8 %collective-permute-done.9 = f32[2,2,8,128]{3,2,1,0:T(8,128)S(1)} collective-permute-done((f32[2,2,8,128]{3,2,1,0:T(8,128)S(1)}, f32[2,2,8,128]{3,2,1,0:T(8,128)S(1)}, u32[]{:S(2)}, u32[]{:S(2)}) %collective-permute-start.9) | collective-permute-done | bytes 16416 | tf_op jit(solution)/shard_map/ppermute | solution.py:264
  47.3 0.0 collective-permute-done.8
  47.3 0.5 collective-permute-start.13
  47.8 1.5 %collective-permute-start.14 = (bf16[256,128]{1,0:T(8,128)(2,1)S(1)}, bf16[256,128]{1,0:T(8,128)(2,1)S(1)}, u32[]{:S(2)}, u32[]{:S(2)}) collective-permute-start(bf16[256,128]{1,0:T(8,128)(2,1)S(1)} %get-tuple-element.69), channel_id=1, source_target_pairs={{0,1},{1,0},{2,3},{3,2},{4,5},{5,4},{6,7},{7,6},{8,9},{9,8},{10,11... | collective-permute-start | bytes 196616 | tf_op jit(solution)/shard_map/ppermute | solution.py:264
  49.3 0.0 collective-permute-done.15.got_others
  49.3 0.0 collective-permute-done.16.got_firsts
  49.3 0.1 merge.3
  49.3 2.6 %collective-permute-start.17 = (bf16[256,128]{1,0:T(8,128)(2,1)S(1)}, bf16[256,128]{1,0:T(8,128)(2,1)S(1)}, u32[]{:S(2)}, u32[]{:S(2)}) collective-permute-start(bf16[256,128]{1,0:T(8,128)(2,1)S(1)} %merge.3), channel_id=1, source_target_pairs={{0,4},{1,5},{2,6},{3,7},{4,0},{5,1},{6,2},{7,3},{8,12},{9,13},{10,... | collective-permute-start | bytes 196616 | tf_op jit(solution)/shard_map/ppermute | solution.py:264
  52.0 0.0 copy-done.2
  52.0 0.6 %query_side.1 = (f32[8,32,128]{2,1,0:T(8,128)S(1)}, f32[8,32,128]{2,1,0:T(8,128)S(1)}, f32[1,8]{1,0:T(1,128)}) custom-call(bf16[8,32,128]{2,1,0:T(8,128)(2,1)S(1)} %copy-done.2, f32[2,8,128]{2,1,0:T(8,128)S(1)} %slice.52.sums_ref), custom_call_target="tpu_custom_call" | custom-call | tf_op jit(solution)/shard_map/query_side/pallas_call | solution.py:430
  52.5 0.0 collective-permute-done.13.got_others
  52.5 0.0 collective-permute-done.14.got_firsts
  52.6 2.0 %collective-permute-done.17.got_ref = bf16[256,128]{1,0:T(8,128)(2,1)S(1)} collective-permute-done((bf16[256,128]{1,0:T(8,128)(2,1)S(1)}, bf16[256,128]{1,0:T(8,128)(2,1)S(1)}, u32[]{:S(2)}, u32[]{:S(2)}) %collective-permute-start.17) | collective-permute-done | bytes 65568 | tf_op jit(solution)/shard_map/ppermute | solution.py:264
  54.6 0.8 %last.1 = f32[8,32,128]{2,1,0:T(8,128)} custom-call(f32[256,128]{1,0:T(8,128)S(1)} %merge.2.keep_ref, bf16[256,128]{1,0:T(8,128)(2,1)S(1)} %collective-permute-done.17.got_ref, f32[8,32,128]{2,1,0:T(8,128)S(1)} %get-tuple-element.72.unit_ref, f32[8,32,128]{2,1,0:T(8,128)S(1)} %get-tuple-element.73.scale_ref), custom_call_target="tpu_custom_call" | custom-call | tf_op jit(solution)/shard_map/last/pallas_call | solution.py:435
  (18 shorter events, 0.2 us)
Async XLA Ops:
  0.6 19.1 %collective-permute-start.4 = (bf16[16,256,128]{2,1,0:T(8,128)(2,1)}, bf16[16,256,128]{2,1,0:T(8,128)(2,1)S(1)}, u32[]{:S(2)}, u32[]{:S(2)}) collective-permute-start(bf16[16,256,128]{2,1,0:T(8,128)(2,1)} %refs_0_.1), channel_id=1, source_target_pairs={{0,8},{8,0},{16,24},{24,16},{1,9},{9,1},{17,25},{25,17},{2,10},{10... | collective-permute-start | bytes 3145736 | tf_op jit(solution)/shard_map/ppermute | solution.py:264
  1.1 26.5 %collective-permute-start.5 = (bf16[16,256,128]{2,1,0:T(8,128)(2,1)}, bf16[16,256,128]{2,1,0:T(8,128)(2,1)S(1)}, u32[]{:S(2)}, u32[]{:S(2)}) collective-permute-start(bf16[16,256,128]{2,1,0:T(8,128)(2,1)} %refs_0_.1), channel_id=1, source_target_pairs={{0,16},{8,24},{16,0},{24,8},{1,17},{9,25},{17,1},{25,9},{2,18},{10... | collective-permute-start | bytes 3145736 | tf_op jit(solution)/shard_map/ppermute | solution.py:264
  3.7 0.8 %copy-start.1 = (bf16[8,32,128]{2,1,0:T(8,128)(2,1)S(1)}, bf16[8,32,128]{2,1,0:T(8,128)(2,1)}, u32[]{:S(2)}) copy-start(bf16[8,32,128]{2,1,0:T(8,128)(2,1)} %queries_ref.3) | copy-start | bytes 196612
  4.6 0.7 %copy-start.3 = (s32[8,16]{1,0:T(8,128)S(1)}, s32[8,16]{1,0:T(8,128)}, u32[]{:S(2)}) copy-start(s32[8,16]{1,0:T(8,128)} %cand_ref.1) | copy-start | bytes 1540
  5.4 6.8 %collective-permute-start = (bf16[1,272,128]{2,1,0:T(8,128)(2,1)S(1)}, bf16[1,272,128]{2,1,0:T(8,128)(2,1)S(1)}, u32[]{:S(2)}, u32[]{:S(2)}) collective-permute-start(bf16[1,272,128]{2,1,0:T(8,128)(2,1)S(1)} %bitcast.20), channel_id=1, source_target_pairs={{0,4},{1,5},{2,6},{3,7},{4,0},{5,1},{6,2},{7,3},{8,12},{9,13},{10,... | collective-permute-start | bytes 208904 | tf_op jit(solution)/shard_map/ppermute | solution.py:264
  12.2 5.1 %collective-permute-start.1 = (bf16[2,272,128]{2,1,0:T(8,128)(2,1)S(1)}, bf16[2,272,128]{2,1,0:T(8,128)(2,1)S(1)}, u32[]{:S(2)}, u32[]{:S(2)}) collective-permute-start(bf16[2,272,128]{2,1,0:T(8,128)(2,1)S(1)} %pad_maximum_fusion.refs_0_), channel_id=1, source_target_pairs={{0,2},{1,3},{2,0},{3,1},{4,6},{5,7},{6,4},{7,5},{8,10},{9,11},{10,... | collective-permute-start | bytes 417800 | tf_op jit(solution)/shard_map/ppermute | solution.py:264
  12.9 9.9 %collective-permute-start.2 = (bf16[2,272,128]{2,1,0:T(8,128)(2,1)S(1)}, bf16[2,272,128]{2,1,0:T(8,128)(2,1)S(1)}, u32[]{:S(2)}, u32[]{:S(2)}) collective-permute-start(bf16[2,272,128]{2,1,0:T(8,128)(2,1)S(1)} %pad_maximum_fusion.refs_0_), channel_id=1, source_target_pairs={{0,1},{1,0},{2,3},{3,2},{4,5},{5,4},{6,7},{7,6},{8,9},{9,8},{10,11... | collective-permute-start | bytes 417800 | tf_op jit(solution)/shard_map/ppermute | solution.py:264
  17.3 5.4 %collective-permute-start.3 = (bf16[2,272,128]{2,1,0:T(8,128)(2,1)S(1)}, bf16[2,272,128]{2,1,0:T(8,128)(2,1)S(1)}, u32[]{:S(2)}, u32[]{:S(2)}) collective-permute-start(bf16[2,272,128]{2,1,0:T(8,128)(2,1)S(1)} %collective-permute-done.1.refs_1_), channel_id=1, source_target_pairs={{0,1},{1,0},{2,3},{3,2},{4,5},{5,4},{6,7},{7,6},{8,9},{9,8},{10,11... | collective-permute-start | bytes 417800 | tf_op jit(solution)/shard_map/ppermute | solution.py:264
  19.8 1.2 %copy-start = (bf16[16,256,128]{2,1,0:T(8,128)(2,1)S(1)}, bf16[16,256,128]{2,1,0:T(8,128)(2,1)}, u32[]{:S(2)}) copy-start(bf16[16,256,128]{2,1,0:T(8,128)(2,1)} %refs_0_.1) | copy-start | bytes 3145732
  27.7 2.7 %collective-permute-start.6 = (bf16[16,256,128]{2,1,0:T(8,128)(2,1)S(1)}, bf16[16,256,128]{2,1,0:T(8,128)(2,1)S(1)}, u32[]{:S(2)}, u32[]{:S(2)}) collective-permute-start(bf16[16,256,128]{2,1,0:T(8,128)(2,1)S(1)} %collective-permute-done.5.raw_ref), channel_id=1, source_target_pairs={{0,8},{8,0},{16,24},{24,16},{1,9},{9,1},{17,25},{25,17},{2,10},{10... | collective-permute-start | bytes 3145736 | tf_op jit(solution)/shard_map/ppermute | solution.py:264
  32.3 4.0 %collective-permute-start.7 = (f32[2,2,16,128]{3,2,1,0:T(8,128)S(1)}, f32[2,2,16,128]{3,2,1,0:T(8,128)S(1)}, u32[]{:S(2)}, u32[]{:S(2)}) collective-permute-start(f32[2,2,16,128]{3,2,1,0:T(8,128)S(1)} %pad_maximum_fusion.1), channel_id=1, source_target_pairs={{0,1},{1,0},{2,3},{3,2},{4,5},{5,4},{6,7},{7,6},{8,9},{9,8},{10,11... | collective-permute-start | bytes 98312 | tf_op jit(solution)/shard_map/ppermute | solution.py:264
  34.2 8.9 %collective-permute-start.11 = (bf16[1024,128]{1,0:T(8,128)(2,1)S(1)}, bf16[1024,128]{1,0:T(8,128)(2,1)S(1)}, u32[]{:S(2)}, u32[]{:S(2)}) collective-permute-start(bf16[1024,128]{1,0:T(8,128)(2,1)S(1)} %get-tuple-element.66), channel_id=1, source_target_pairs={{0,1},{1,0},{2,3},{3,2},{4,5},{5,4},{6,7},{7,6},{8,9},{9,8},{10,11... | collective-permute-start | bytes 786440 | tf_op jit(solution)/shard_map/ppermute | solution.py:264
  34.4 8.7 %collective-permute-start.12 = (bf16[1024,128]{1,0:T(8,128)(2,1)S(1)}, bf16[1024,128]{1,0:T(8,128)(2,1)S(1)}, u32[]{:S(2)}, u32[]{:S(2)}) collective-permute-start(bf16[1024,128]{1,0:T(8,128)(2,1)S(1)} %get-tuple-element.67), channel_id=1, source_target_pairs={{0,2},{1,3},{2,0},{3,1},{4,6},{5,7},{6,4},{7,5},{8,10},{9,11},{10,... | collective-permute-start | bytes 786440 | tf_op jit(solution)/shard_map/ppermute | solution.py:264
  38.5 8.0 %collective-permute-start.10 = (f32[2,2,8,128]{3,2,1,0:T(8,128)S(1)}, f32[2,2,8,128]{3,2,1,0:T(8,128)S(1)}, u32[]{:S(2)}, u32[]{:S(2)}) collective-permute-start(f32[2,2,8,128]{3,2,1,0:T(8,128)S(1)} %rev.8), channel_id=1, source_target_pairs={{0,6},{1,7},{2,4},{3,5},{4,2},{5,3},{6,0},{7,1},{8,14},{9,15},{10,... | collective-permute-start | bytes 49160 | tf_op jit(solution)/shard_map/ppermute | solution.py:264
  42.5 4.9 %collective-permute-start.9 = (f32[2,2,8,128]{3,2,1,0:T(8,128)S(1)}, f32[2,2,8,128]{3,2,1,0:T(8,128)S(1)}, u32[]{:S(2)}, u32[]{:S(2)}) collective-permute-start(f32[2,2,8,128]{3,2,1,0:T(8,128)S(1)} %rev.7), channel_id=1, source_target_pairs={{0,4},{1,5},{2,6},{3,7},{4,0},{5,1},{6,2},{7,3},{8,12},{9,13},{10,... | collective-permute-start | bytes 49160 | tf_op jit(solution)/shard_map/ppermute | solution.py:264
  42.5 4.9 %collective-permute-start.8 = (f32[2,2,8,128]{3,2,1,0:T(8,128)S(1)}, f32[2,2,8,128]{3,2,1,0:T(8,128)S(1)}, u32[]{:S(2)}, u32[]{:S(2)}) collective-permute-start(f32[2,2,8,128]{3,2,1,0:T(8,128)S(1)} %get-tuple-element.75), channel_id=1, source_target_pairs={{0,2},{1,3},{2,0},{3,1},{4,6},{5,7},{6,4},{7,5},{8,10},{9,11},{10,... | collective-permute-start | bytes 49160 | tf_op jit(solution)/shard_map/ppermute | solution.py:264
  43.2 8.8 %copy-start.2 = (bf16[8,32,128]{2,1,0:T(8,128)(2,1)S(1)}, bf16[8,32,128]{2,1,0:T(8,128)(2,1)}, u32[]{:S(2)}) copy-start(bf16[8,32,128]{2,1,0:T(8,128)(2,1)} %queries_ref.3) | copy-start | bytes 196612
  43.2 6.1 %collective-permute-start.15 = (bf16[256,128]{1,0:T(8,128)(2,1)S(1)}, bf16[256,128]{1,0:T(8,128)(2,1)S(1)}, u32[]{:S(2)}, u32[]{:S(2)}) collective-permute-start(bf16[256,128]{1,0:T(8,128)(2,1)S(1)} %get-tuple-element.70), channel_id=1, source_target_pairs={{0,2},{1,3},{2,0},{3,1},{4,6},{5,7},{6,4},{7,5},{8,10},{9,11},{10,... | collective-permute-start | bytes 196616 | tf_op jit(solution)/shard_map/ppermute | solution.py:264
  44.6 4.6 %collective-permute-start.16 = (bf16[256,128]{1,0:T(8,128)(2,1)S(1)}, bf16[256,128]{1,0:T(8,128)(2,1)S(1)}, u32[]{:S(2)}, u32[]{:S(2)}) collective-permute-start(bf16[256,128]{1,0:T(8,128)(2,1)S(1)} %get-tuple-element.71), channel_id=1, source_target_pairs={{0,1},{1,0},{2,3},{3,2},{4,5},{5,4},{6,7},{7,6},{8,9},{9,8},{10,11... | collective-permute-start | bytes 196616 | tf_op jit(solution)/shard_map/ppermute | solution.py:264
  47.3 5.2 %collective-permute-start.13 = (bf16[256,128]{1,0:T(8,128)(2,1)S(1)}, bf16[256,128]{1,0:T(8,128)(2,1)S(1)}, u32[]{:S(2)}, u32[]{:S(2)}) collective-permute-start(bf16[256,128]{1,0:T(8,128)(2,1)S(1)} %get-tuple-element.68), channel_id=1, source_target_pairs={{0,2},{1,3},{2,0},{3,1},{4,6},{5,7},{6,4},{7,5},{8,10},{9,11},{10,... | collective-permute-start | bytes 196616 | tf_op jit(solution)/shard_map/ppermute | solution.py:264
  47.8 4.7 %collective-permute-start.14 = (bf16[256,128]{1,0:T(8,128)(2,1)S(1)}, bf16[256,128]{1,0:T(8,128)(2,1)S(1)}, u32[]{:S(2)}, u32[]{:S(2)}) collective-permute-start(bf16[256,128]{1,0:T(8,128)(2,1)S(1)} %get-tuple-element.69), channel_id=1, source_target_pairs={{0,1},{1,0},{2,3},{3,2},{4,5},{5,4},{6,7},{7,6},{8,9},{9,8},{10,11... | collective-permute-start | bytes 196616 | tf_op jit(solution)/shard_map/ppermute | solution.py:264
  49.3 5.2 %collective-permute-start.17 = (bf16[256,128]{1,0:T(8,128)(2,1)S(1)}, bf16[256,128]{1,0:T(8,128)(2,1)S(1)}, u32[]{:S(2)}, u32[]{:S(2)}) collective-permute-start(bf16[256,128]{1,0:T(8,128)(2,1)S(1)} %merge.3), channel_id=1, source_target_pairs={{0,4},{1,5},{2,6},{3,7},{4,0},{5,1},{6,2},{7,3},{8,12},{9,13},{10,... | collective-permute-start | bytes 196616 | tf_op jit(solution)/shard_map/ppermute | solution.py:264
